TPU v7x, 32 devices: a whole 2x2x4 slice. The times are simulated.
32 devices in a mesh: section: 2 (over core), expert: 8 (over z, y), tensor: 2 (over x).
Axes of the slice: x: 2, y: 2, z: 4, core: 2. Of those that a mesh axis runs over, the one named last changes fastest.
Arguments:
- ends_in: bfloat16 [2, 2, 512, 2048], P('section', None, 'expert'), may hold values from -6 to 6
- attn_gain: bfloat16 [2, 2048], P('section', 'expert'), may hold values from 0.5 to 1.5
- w_query: bfloat16 [2, 2048, 4096], P('section', 'expert', 'tensor'), may hold values from -0.125 to 0.125
- key_matrix: bfloat16 [2, 2048, 512], P('section', 'expert', 'tensor'), may hold values from -0.125 to 0.125
- value_matrix: bfloat16 [2, 2048, 512], P('section', 'expert', 'tensor'), may hold values from -0.125 to 0.125
- query_gain: bfloat16 [2, 128], P('section', 'expert'), may hold values from 0.5 to 1.5
- key_gain: bfloat16 [2, 128], P('section', 'expert'), may hold values from 0.5 to 1.5
- w_out: bfloat16 [2, 4096, 2048], P('section', 'tensor', 'expert'), may hold values from -0.375 to 0.375
- ffn_gain: bfloat16 [2, 2048], P('section', 'expert'), may hold values from 0.5 to 1.5
- router: bfloat16 [2, 2048, 16], P('section', 'expert'), may hold values from -0.0625 to 0.0625
- w_gate: bfloat16 [2, 16, 2048, 768], P('section', 'expert', None, 'tensor'), may hold values from -0.125 to 0.125
- w_up: bfloat16 [2, 16, 2048, 768], P('section', 'expert', None, 'tensor'), may hold values from -0.125 to 0.125
- w_down: bfloat16 [2, 16, 768, 2048], P('section', 'expert', 'tensor'), may hold values from -0.625 to 0.625
- routes: int32 [2, 2, 512, 8], P('section', None, 'expert'), may hold values from 0 to 15, all different within a row; in each aligned block of 64 rows (0 to 63, 64 to 127, ..., all dimensions but the last counted through in order) at most 64 rows name the same one
- lengths: int32 [2, 8, 3], P(None, 'expert'), may hold values from 1 to 48, 64 in all within a row
Outputs:
- ends_out: bfloat16 [2, 2, 512, 2048], P('section', None, 'expert')
- grad_attn_gain: float32 [2, 2048], P('section', 'expert')
- grad_w_query: float32 [2, 2048, 4096], P('section', 'expert', 'tensor')
- grad_w_key: float32 [2, 2048, 512], P('section', 'expert', 'tensor')
- grad_w_value: float32 [2, 2048, 512], P('section', 'expert', 'tensor')
- grad_query_gain: float32 [2, 128], P('section', 'expert')
- grad_key_gain: float32 [2, 128], P('section', 'expert')
- grad_w_out: float32 [2, 4096, 2048], P('section', 'tensor', 'expert')
- grad_ffn_gain: float32 [2, 2048], P('section', 'expert')
- grad_router: float32 [2, 2048, 16], P('section', 'expert')
- grad_w_gate: float32 [2, 16, 2048, 768], P('section', 'expert', None, 'tensor')
- grad_w_up: float32 [2, 16, 2048, 768], P('section', 'expert', None, 'tensor')
- grad_w_down: float32 [2, 16, 768, 2048], P('section', 'expert', 'tensor')
Inputs may be any that keep to these rules, and one draw needn't show every extreme that they name: `routes`: in each layer and micro-batch, the 64 rows of one block name 8 different experts each, no expert more than 64 times in the block, and in some blocks an expert exactly 64 times. Each row holds 3 lengths that sum to 64.
All inputs are finite; a program needn't handle non-finite values.
Results may differ from a plain program's by a relative error of at most 0.025.
Values may be sent and summed in bfloat16 or wider, within the bound.
No kernel may reach another device: no remote copies, remote signals or barrier semaphores. Data moves between devices by JAX's collectives and lax.ppermute only.
A program may use at most 256 MiB of HBM per device.

v0:
```python
import jax
import jax.numpy as jnp
from jax import lax
from jax.sharding import PartitionSpec as P

epsilon = 1e-06
rope_base = 1000000.0
masked_score = -1e30


def from_behind(value, axis, steps):
    count = lax.axis_size(axis)
    leading, last = (max(0, -steps), min(count, count - steps))
    return lax.ppermute(value, axis, [(source, source + steps) for source in range(leading, last)])


def rms_norm(tensor_in, gain_vec):
    return (
        tensor_in
        * lax.rsqrt(jnp.mean(tensor_in * tensor_in, axis=-1, keepdims=True) + epsilon)
        * gain_vec
    )


def rotary(tensor_in, cosine_table, sine_table):
    half_size = tensor_in.shape[-1] // 2
    first_half = tensor_in[..., :half_size]
    second_half = tensor_in[..., half_size:]
    return jnp.concatenate(
        [
            first_half * cosine_table - second_half * sine_table,
            second_half * cosine_table + first_half * sine_table,
        ],
        axis=-1,
    )


def prepare(raw_proj, gain_vec, cosine_table, sine_table, factor):
    return rotary(rms_norm(raw_proj, gain_vec), cosine_table, sine_table) * factor


def swiglu(gate_act, up_act):
    return jax.nn.silu(gate_act) * up_act


def layout(lengths_row, count_of_rows):
    seq_ends = jnp.cumsum(lengths_row, dtype=jnp.int32)
    row_index = jnp.arange(count_of_rows, dtype=jnp.int32)
    segment_ids = jnp.sum(
        (row_index[:, None] >= seq_ends[None, :]).astype(jnp.int32), axis=1, dtype=jnp.int32
    )
    seq_starts = seq_ends - lengths_row
    membership = segment_ids[:, None] == jnp.arange(seq_ends.shape[0], dtype=jnp.int32)[None, :]
    row_start = jnp.sum(jnp.where(membership, seq_starts[None, :], 0), axis=1, dtype=jnp.int32)
    return (segment_ids, row_index - row_start)


def tables(position, head_size):
    half_size = head_size // 2
    inverse = rope_base ** (-(jnp.arange(half_size, dtype=jnp.float32) * 2.0) / head_size)
    angles = position.astype(jnp.float32)[:, None] * inverse[None, :]
    return (jnp.cos(angles)[:, None, :], jnp.sin(angles)[:, None, :])


def slot_ranks(flat_routes, experts):
    one_hot = (flat_routes[:, None] == jnp.arange(experts, dtype=jnp.int32)[None, :]).astype(
        jnp.int32
    )
    before = jnp.cumsum(one_hot, axis=0, dtype=jnp.int32) - 1
    return jnp.sum(before * one_hot, axis=1, dtype=jnp.int32)


def causal_mask(segment_ids):
    row_index = jnp.arange(segment_ids.shape[0], dtype=jnp.int32)
    return (segment_ids[:, None] == segment_ids[None, :]) & (
        row_index[None, :] <= row_index[:, None]
    )


def contract_rows(left_arg, right_arg):
    return lax.dot_general(
        left_arg, right_arg, (((0,), (0,)), ((), ())), preferred_element_type=jnp.float32
    )


def contract_cols(left_arg, right_arg):
    return lax.dot_general(
        left_arg, right_arg, (((1,), (1,)), ((), ())), preferred_element_type=jnp.float32
    )


def slots_away(buffer):
    arrived = lax.all_to_all(buffer, "expert", split_axis=0, concat_axis=0, tiled=True)
    arrived = arrived.reshape(lax.axis_size("expert"), -1, arrived.shape[1], arrived.shape[2])
    return arrived


def slots_home(partial_value):
    shared = lax.psum_scatter(partial_value, "tensor", scatter_dimension=2, tiled=True).astype(
        jnp.bfloat16
    )
    shared = lax.all_gather(shared, "tensor", axis=2, tiled=True)
    return lax.all_to_all(
        shared.reshape(-1, shared.shape[2], shared.shape[3]),
        "expert",
        split_axis=0,
        concat_axis=0,
        tiled=True,
    )


def pick_slots(returned, slot_index, count_of_rows, top_count):
    model_width = returned.shape[2]
    flat_rows = returned.reshape(-1, model_width)
    rows = flat_rows[slot_index].astype(jnp.float32)
    return rows.reshape(count_of_rows, top_count, model_width)


def forward_layer(resid_in, weights, routes_now, lengths_now):
    (
        attn_gain,
        w_query,
        key_matrix,
        value_matrix,
        query_gain,
        key_gain,
        w_out,
        ffn_gain,
        router,
        w_gate,
        w_up,
        w_down,
    ) = weights
    count_of_rows = resid_in.shape[0]
    model_width = resid_in.shape[1]
    head_size = query_gain.shape[0]
    heads_q = w_query.shape[1] // head_size
    heads_kv = key_matrix.shape[1] // head_size
    group_size = heads_q // heads_kv
    top_count = routes_now.shape[1]
    experts = router.shape[1]
    capacity = 2 * top_count * count_of_rows // experts
    segment_ids, position = layout(lengths_now, count_of_rows)
    cosine_table, sine_table = tables(position, head_size)
    normed_rows = rms_norm(resid_in, attn_gain.astype(jnp.float32)).astype(jnp.bfloat16)
    q_raw = jnp.dot(normed_rows, w_query, preferred_element_type=jnp.float32).reshape(
        count_of_rows, heads_q, head_size
    )
    key_unrotated = jnp.dot(normed_rows, key_matrix, preferred_element_type=jnp.float32).reshape(
        count_of_rows, heads_kv, head_size
    )
    values = (
        jnp.dot(normed_rows, value_matrix, preferred_element_type=jnp.float32)
        .astype(jnp.bfloat16)
        .reshape(count_of_rows, heads_kv, head_size)
    )
    queries = prepare(
        q_raw, query_gain.astype(jnp.float32), cosine_table, sine_table, head_size ** (-0.5)
    )
    queries = queries.astype(jnp.bfloat16).reshape(count_of_rows, heads_kv, group_size, head_size)
    key_rotated = prepare(
        key_unrotated, key_gain.astype(jnp.float32), cosine_table, sine_table, 1.0
    ).astype(jnp.bfloat16)
    allowed = causal_mask(segment_ids)
    scores = jnp.einsum("rkgd,skd->kgrs", queries, key_rotated, preferred_element_type=jnp.float32)
    scores = jnp.where(allowed, scores, masked_score)
    row_peak = jnp.max(scores, axis=-1, keepdims=True)
    total_log = row_peak + jnp.log(jnp.sum(jnp.exp(scores - row_peak), axis=-1, keepdims=True))
    probabilities = jnp.exp(scores - total_log).astype(jnp.bfloat16)
    mixed_rows = jnp.einsum(
        "kgrs,skd->rkgd", probabilities, values, preferred_element_type=jnp.float32
    )
    mixed_rows = mixed_rows.astype(jnp.bfloat16).reshape(count_of_rows, -1)
    attn_total = lax.psum(jnp.dot(mixed_rows, w_out, preferred_element_type=jnp.float32), "tensor")
    resid_mid = resid_in + attn_total
    normed_ffn = rms_norm(resid_mid, ffn_gain.astype(jnp.float32)).astype(jnp.bfloat16)
    logits = jnp.dot(normed_ffn, router, preferred_element_type=jnp.float32)
    route_match = routes_now[:, :, None] == jnp.arange(experts, dtype=jnp.int32)[None, None, :]
    chosen = jnp.sum(jnp.where(route_match, logits[:, None, :], 0.0), axis=2)
    gates = jax.nn.softmax(chosen, axis=-1)
    flat_routes = routes_now.reshape(-1)
    slot_index = flat_routes * capacity + slot_ranks(flat_routes, experts)
    buffer = jnp.zeros((experts * capacity, model_width), jnp.bfloat16)
    buffer = (
        buffer.at[slot_index]
        .set(jnp.repeat(normed_ffn, top_count, axis=0))
        .reshape(experts, capacity, model_width)
    )
    arrived = slots_away(buffer)
    gate_act = jnp.einsum("secd,edf->secf", arrived, w_gate, preferred_element_type=jnp.float32)
    up_act = jnp.einsum("secd,edf->secf", arrived, w_up, preferred_element_type=jnp.float32)
    hidden = swiglu(gate_act, up_act).astype(jnp.bfloat16)
    result = jnp.einsum("secf,efd->secd", hidden, w_down, preferred_element_type=jnp.float32)
    returned = slots_home(result)
    picked = pick_slots(returned, slot_index, count_of_rows, top_count)
    ffn_total = jnp.sum(gates[:, :, None] * picked, axis=1)
    saved_state = (
        resid_in,
        normed_rows,
        q_raw,
        key_unrotated,
        queries,
        key_rotated,
        values,
        total_log,
        mixed_rows,
        resid_mid,
        normed_ffn,
        gates,
        slot_index,
        arrived,
        gate_act,
        up_act,
        hidden,
        picked,
    )
    return (resid_mid + ffn_total, saved_state)


def backward_layer(grad_out, saved_state, weights, routes_now, lengths_now):
    (
        attn_gain,
        w_query,
        key_matrix,
        value_matrix,
        query_gain,
        key_gain,
        w_out,
        ffn_gain,
        router,
        w_gate,
        w_up,
        w_down,
    ) = weights
    (
        resid_in,
        normed_rows,
        q_raw,
        key_unrotated,
        queries,
        key_rotated,
        values,
        total_log,
        mixed_rows,
        resid_mid,
        normed_ffn,
        gates,
        slot_index,
        arrived,
        gate_act,
        up_act,
        hidden,
        picked,
    ) = saved_state
    count_of_rows = resid_in.shape[0]
    model_width = resid_in.shape[1]
    head_size = query_gain.shape[0]
    heads_q = w_query.shape[1] // head_size
    heads_kv = key_matrix.shape[1] // head_size
    group_size = heads_q // heads_kv
    top_count = routes_now.shape[1]
    experts = router.shape[1]
    capacity = 2 * top_count * count_of_rows // experts
    segment_ids, position = layout(lengths_now, count_of_rows)
    cosine_table, sine_table = tables(position, head_size)
    to_slots = (gates[:, :, None] * grad_out[:, None, :]).astype(jnp.bfloat16)
    gate_dots = jnp.sum(picked * grad_out[:, None, :], axis=2)
    buffer = jnp.zeros((experts * capacity, model_width), jnp.bfloat16)
    buffer = (
        buffer.at[slot_index]
        .set(to_slots.reshape(-1, model_width))
        .reshape(experts, capacity, model_width)
    )
    slot_grads = slots_away(buffer)
    d_hidden = jnp.einsum("secd,efd->secf", slot_grads, w_down, preferred_element_type=jnp.float32)
    g_down = jnp.einsum("secf,secd->efd", hidden, slot_grads, preferred_element_type=jnp.float32)
    unused, pullback = jax.vjp(swiglu, gate_act, up_act)
    d_gate, d_up = pullback(d_hidden)
    d_gate = d_gate.astype(jnp.bfloat16)
    d_up = d_up.astype(jnp.bfloat16)
    g_gate = jnp.einsum("secd,secf->edf", arrived, d_gate, preferred_element_type=jnp.float32)
    g_up = jnp.einsum("secd,secf->edf", arrived, d_up, preferred_element_type=jnp.float32)
    d_rows = jnp.einsum(
        "secf,edf->secd", d_gate, w_gate, preferred_element_type=jnp.float32
    ) + jnp.einsum("secf,edf->secd", d_up, w_up, preferred_element_type=jnp.float32)
    returned = slots_home(d_rows)
    d_pairs = pick_slots(returned, slot_index, count_of_rows, top_count)
    d_normed_ffn, gate_dots = (jnp.sum(d_pairs, axis=1), gate_dots)
    d_chosen = gates * (gate_dots - jnp.sum(gates * gate_dots, axis=-1, keepdims=True))
    route_match = routes_now[:, :, None] == jnp.arange(experts, dtype=jnp.int32)[None, None, :]
    d_logits = jnp.sum(jnp.where(route_match, d_chosen[:, :, None], 0.0), axis=1).astype(
        jnp.bfloat16
    )
    g_router = contract_rows(normed_ffn, d_logits)
    d_normed_ffn = d_normed_ffn + contract_cols(d_logits, router)
    unused, pullback = jax.vjp(rms_norm, resid_mid, ffn_gain.astype(jnp.float32))
    d_mid, g_ffn_gain = pullback(d_normed_ffn)
    d_mid = d_mid + grad_out
    d_attn = d_mid.astype(jnp.bfloat16)
    g_out = contract_rows(mixed_rows, d_attn)
    d_mixed = (
        contract_cols(d_attn, w_out)
        .astype(jnp.bfloat16)
        .reshape(count_of_rows, heads_kv, group_size, head_size)
    )
    allowed = causal_mask(segment_ids)
    scores = jnp.einsum("rkgd,skd->kgrs", queries, key_rotated, preferred_element_type=jnp.float32)
    scores = jnp.where(allowed, scores, masked_score)
    probabilities = jnp.exp(scores - total_log)
    d_probs = jnp.einsum("rkgd,skd->kgrs", d_mixed, values, preferred_element_type=jnp.float32)
    d_scores = (
        probabilities * (d_probs - jnp.sum(probabilities * d_probs, axis=-1, keepdims=True))
    ).astype(jnp.bfloat16)
    d_values = jnp.einsum(
        "kgrs,rkgd->skd",
        probabilities.astype(jnp.bfloat16),
        d_mixed,
        preferred_element_type=jnp.float32,
    )
    d_values = d_values.astype(jnp.bfloat16).reshape(count_of_rows, -1)
    d_queries = jnp.einsum(
        "kgrs,skd->rkgd", d_scores, key_rotated, preferred_element_type=jnp.float32
    ).reshape(count_of_rows, heads_q, head_size)
    d_keys = jnp.einsum("kgrs,rkgd->skd", d_scores, queries, preferred_element_type=jnp.float32)
    unused, pullback = jax.vjp(
        lambda raw_proj, gain_vec: prepare(
            raw_proj, gain_vec, cosine_table, sine_table, head_size ** (-0.5)
        ),
        q_raw,
        query_gain.astype(jnp.float32),
    )
    d_qraw, g_query_gain = pullback(d_queries)
    unused, pullback = jax.vjp(
        lambda raw_proj, gain_vec: prepare(raw_proj, gain_vec, cosine_table, sine_table, 1.0),
        key_unrotated,
        key_gain.astype(jnp.float32),
    )
    d_kraw, g_key_gain = pullback(d_keys)
    d_qraw = d_qraw.astype(jnp.bfloat16).reshape(count_of_rows, -1)
    d_kraw = d_kraw.astype(jnp.bfloat16).reshape(count_of_rows, -1)
    g_query = contract_rows(normed_rows, d_qraw)
    g_key = contract_rows(normed_rows, d_kraw)
    g_value = contract_rows(normed_rows, d_values)
    d_normed = (
        contract_cols(d_qraw, w_query)
        + contract_cols(d_kraw, key_matrix)
        + contract_cols(d_values, value_matrix)
    )
    d_normed, g_query_gain, g_key_gain = lax.psum((d_normed, g_query_gain, g_key_gain), "tensor")
    unused, pullback = jax.vjp(rms_norm, resid_in, attn_gain.astype(jnp.float32))
    d_resid, g_attn_gain = pullback(d_normed)
    grads = (
        g_attn_gain,
        g_query,
        g_key,
        g_value,
        g_query_gain,
        g_key_gain,
        g_out,
        g_ffn_gain,
        g_router,
        g_gate,
        g_up,
        g_down,
    )
    return (d_mid + d_resid, grads)


def body(
    ends_in,
    attn_gain,
    w_query,
    key_matrix,
    value_matrix,
    query_gain,
    key_gain,
    w_out,
    ffn_gain,
    router,
    w_gate,
    w_up,
    w_down,
    routes,
    lengths,
):
    shared = (
        lax.all_gather(attn_gain[0], "expert", axis=0, tiled=True),
        lax.all_gather(w_query[0], "expert", axis=0, tiled=True),
        lax.all_gather(key_matrix[0], "expert", axis=0, tiled=True),
        lax.all_gather(value_matrix[0], "expert", axis=0, tiled=True),
        lax.all_gather(query_gain[0], "expert", axis=0, tiled=True),
        lax.all_gather(key_gain[0], "expert", axis=0, tiled=True),
        lax.all_gather(w_out[0], "expert", axis=1, tiled=True),
        lax.all_gather(ffn_gain[0], "expert", axis=0, tiled=True),
        lax.all_gather(router[0], "expert", axis=0, tiled=True),
    )
    weights = tuple(shared) + (w_gate[0], w_up[0], w_down[0])
    micro_count = ends_in.shape[1]
    is_last = lax.axis_index("section") == 1
    received = jnp.zeros(ends_in.shape[2:], jnp.bfloat16)
    stored = []
    produced = []
    for time_step in range(micro_count + 1):
        early_mb = min(time_step, micro_count - 1)
        late_mb = max(time_step - 1, 0)
        source = jnp.where(is_last, received, ends_in[0, early_mb])
        routes_now = jnp.where(is_last, routes[0, late_mb], routes[0, early_mb])
        lengths_now = jnp.where(is_last, lengths[late_mb, 0], lengths[early_mb, 0])
        output, saved_state = forward_layer(
            source.astype(jnp.float32), weights, routes_now, lengths_now
        )
        output = output.astype(jnp.bfloat16)
        stored.append((saved_state, routes_now, lengths_now))
        produced.append(output)
        if time_step < micro_count:
            received = from_behind(output, "section", 1)
    totals = None
    received = jnp.zeros(ends_in.shape[2:], jnp.bfloat16)
    returned = []
    for time_step in range(micro_count + 1):
        is_valid = jnp.where(is_last, float(time_step < micro_count), float(time_step >= 1))
        seed_grad = (
            jnp.where(is_last, ends_in[0, min(time_step, micro_count - 1)], received).astype(
                jnp.float32
            )
            * is_valid
        )
        chosen_state = jax.tree.map(
            lambda left_arg, right_arg: jnp.where(is_last, left_arg, right_arg),
            stored[min(time_step + 1, micro_count)],
            stored[max(time_step - 1, 0)],
        )
        saved_state, routes_now, lengths_now = chosen_state
        d_input, grads = backward_layer(seed_grad, saved_state, weights, routes_now, lengths_now)
        if totals is None:
            totals = grads
        else:
            totals = tuple((left_arg + right_arg for left_arg, right_arg in zip(totals, grads)))
        d_input = d_input.astype(jnp.bfloat16)
        returned.append(d_input)
        if time_step < micro_count:
            received = from_behind(d_input, "section", -1)
    (
        g_attn_gain,
        g_query,
        g_key,
        g_value,
        g_query_gain,
        g_key_gain,
        g_out,
        g_ffn_gain,
        g_router,
        g_gate,
        g_up,
        g_down,
    ) = totals
    reduced = (
        lax.psum_scatter(g_attn_gain, "expert", scatter_dimension=0, tiled=True),
        lax.psum_scatter(g_query, "expert", scatter_dimension=0, tiled=True),
        lax.psum_scatter(g_key, "expert", scatter_dimension=0, tiled=True),
        lax.psum_scatter(g_value, "expert", scatter_dimension=0, tiled=True),
        lax.psum_scatter(g_query_gain, "expert", scatter_dimension=0, tiled=True),
        lax.psum_scatter(g_key_gain, "expert", scatter_dimension=0, tiled=True),
        lax.psum_scatter(g_out, "expert", scatter_dimension=1, tiled=True),
        lax.psum_scatter(g_ffn_gain, "expert", scatter_dimension=0, tiled=True),
        lax.psum_scatter(g_router, "expert", scatter_dimension=0, tiled=True),
    )
    ends_out = jnp.stack(
        [
            jnp.where(is_last, produced[micro_idx + 1], returned[micro_idx + 1])
            for micro_idx in range(micro_count)
        ]
    )[None]
    return (
        (ends_out,)
        + tuple((piece[None] for piece in reduced))
        + (g_gate[None], g_up[None], g_down[None])
    )


def solution(mesh):
    return jax.shard_map(
        body,
        mesh=mesh,
        in_specs=(
            P("section", None, "expert", None),
            P("section", "expert"),
            P("section", "expert", "tensor"),
            P("section", "expert", "tensor"),
            P("section", "expert", "tensor"),
            P("section", "expert"),
            P("section", "expert"),
            P("section", "tensor", "expert"),
            P("section", "expert"),
            P("section", "expert", None),
            P("section", "expert", None, "tensor"),
            P("section", "expert", None, "tensor"),
            P("section", "expert", "tensor", None),
            P("section", None, "expert", None),
            P(None, "expert", None),
        ),
        out_specs=(
            P("section", None, "expert", None),
            P("section", "expert"),
            P("section", "expert", "tensor"),
            P("section", "expert", "tensor"),
            P("section", "expert", "tensor"),
            P("section", "expert"),
            P("section", "expert"),
            P("section", "tensor", "expert"),
            P("section", "expert"),
            P("section", "expert", None),
            P("section", "expert", None, "tensor"),
            P("section", "expert", None, "tensor"),
            P("section", "expert", "tensor", None),
        ),
        check_vma=False,
    )
```

profile of v0, /device:TPU:0, one launch (start us, length us, event | category | flops | bytes accessed | tf_op | source)
XLA Modules:
  0.0 3856.3 jit_solution(2040310064506712941)
XLA Ops:
  11.9 22.5 all-gather
  41.0 16.6 all-gather.7
  61.3 19.0 all-reduce.21
  98.2 122.1 %all-gather.36.cloned.1.call-done = bf16[1,2048,2048]{2,1,0:T(8,128)(2,1)} async-done(((bf16[1,256,2048]{2,1,0:T(8,128)(2,1)}), bf16[1,2048,2048]{2,1,0:T(8,128)(2,1)}) %all-gather.36.cloned.1.call-update) | async-done | bytes 8388624 | tf_op jit(solution)/shard_map/all_gather | solution.py:388
  220.2 12.4 copy.342
  240.7 105.0 %all-gather.38.cloned.1.call-done = bf16[1,2048,2048]{2,1,0:T(8,128)(2,1)} async-done(((bf16[1,2048,256]{2,1,0:T(8,128)(2,1)}), bf16[1,2048,2048]{2,1,0:T(8,128)(2,1)}) %all-gather.38.cloned.1.call-update) | async-done | bytes 8388624 | tf_op jit(solution)/shard_map/all_gather | solution.py:393
  352.7 25.9 all-reduce.28.cloned.1.call-done
  387.4 99.0 %all_to_all.60 = bf16[16,64,2048]{2,1,0:T(8,128)(2,1)S(1)} all-to-all(bf16[16,64,2048]{2,1,0:T(8,128)(2,1)} %bitcast.1075), channel_id=1, replica_groups=mesh['section'=2,'expert'=8,'tensor'=2] {'expert'}, dimensions={0} | all-to-all | bytes 8388608 | tf_op jit(solution)/shard_map/all_to_all | solution.py:93
  499.9 97.4 %reduce-scatter.12.cloned.1.call-done = f32[8,2,32,2048]{3,2,0,1:T(8,128)} async-done(((f32[8,2,64,2048]{3,2,0,1:T(8,128)}), f32[8,2,32,2048]{3,2,0,1:T(8,128)}) %reduce-scatter.12.cloned.1.call-update) | async-done | bytes 4194320 | tf_op jit(solution)/shard_map/reduce_scatter | solution.py:99
  601.1 56.9 %all-gather.20.cloned.1.call-done = bf16[8,2,64,2048]{3,2,0,1:T(8,128)(2,1)} async-done(((bf16[8,2,32,2048]{3,2,0,1:T(8,128)(2,1)}), bf16[8,2,64,2048]{3,2,0,1:T(8,128)(2,1)}) %all-gather.20.cloned.1.call-update) | async-done | bytes 4194320 | tf_op jit(solution)/shard_map/all_gather | solution.py:102
  668.4 113.2 %all-gather.8 = bf16[1,2048,16]{1,2,0:T(8,128)(2,1)S(1)} all-gather(bf16[1,256,16]{1,2,0:T(8,128)(2,1)} %param.24), channel_id=10, replica_groups=mesh['section'=2,'expert'=8,'tensor'=2] {'expert'}, dimensions={1}, use_global_device_ids=true | all-gather | bytes 73728 | tf_op jit(solution)/shard_map/all_gather | solution.py:395
  785.0 8.1 gather_fusion
  835.7 26.7 all-reduce.30.cloned.1.call-done
  867.1 6.7 scatter_custom_fusion.1
  873.8 99.0 %all_to_all.61 = bf16[16,64,2048]{2,1,0:T(8,128)(2,1)S(1)} all-to-all(bf16[16,64,2048]{2,1,0:T(8,128)(2,1)} %bitcast.1076), channel_id=1, replica_groups=mesh['section'=2,'expert'=8,'tensor'=2] {'expert'}, dimensions={0} | all-to-all | bytes 8388608 | tf_op jit(solution)/shard_map/all_to_all | solution.py:93
  986.2 97.4 %reduce-scatter.14.cloned.1.call-done = f32[8,2,32,2048]{3,2,0,1:T(8,128)} async-done(((f32[8,2,64,2048]{3,2,0,1:T(8,128)}), f32[8,2,32,2048]{3,2,0,1:T(8,128)}) %reduce-scatter.14.cloned.1.call-update) | async-done | bytes 4194320 | tf_op jit(solution)/shard_map/reduce_scatter | solution.py:99
  1087.5 56.9 %all-gather.22.cloned.1.call-done = bf16[8,2,64,2048]{3,2,0,1:T(8,128)(2,1)} async-done(((bf16[8,2,32,2048]{3,2,0,1:T(8,128)(2,1)}), bf16[8,2,64,2048]{3,2,0,1:T(8,128)(2,1)}) %all-gather.22.cloned.1.call-update) | async-done | bytes 4194320 | tf_op jit(solution)/shard_map/all_gather | solution.py:102
  1166.3 81.7 %all-to-all-done.3 = bf16[16,64,2048]{2,1,0:T(8,128)(2,1)} async-done(((bf16[16,64,2048]{2,1,0:T(8,128)(2,1)}), bf16[16,64,2048]{2,1,0:T(8,128)(2,1)}, u32[]{:S(2)}, u32[]{:S(2)}) %all-to-all-start.3) | async-done | bytes 4194336 | tf_op jit(solution)/shard_map/all_to_all | solution.py:103
  1248.0 8.1 gather_fusion.1
  1256.1 7.4 fusion.28
  1269.5 6.8 scatter_custom_fusion.2
  1276.4 97.7 %all_to_all.62 = bf16[16,64,2048]{2,1,0:T(8,128)(2,1)S(1)} all-to-all(bf16[16,64,2048]{2,1,0:T(8,128)(2,1)} %bitcast.1072), channel_id=1, replica_groups=mesh['section'=2,'expert'=8,'tensor'=2] {'expert'}, dimensions={0} | all-to-all | bytes 8388608 | tf_op jit(solution)/shard_map/all_to_all | solution.py:93
  1385.5 97.4 %reduce-scatter.16.cloned.1.call-done = f32[8,2,32,2048]{3,2,0,1:T(8,128)} async-done(((f32[8,2,64,2048]{3,2,0,1:T(8,128)}), f32[8,2,32,2048]{3,2,0,1:T(8,128)}) %reduce-scatter.16.cloned.1.call-update) | async-done | bytes 4194320 | tf_op jit(solution)/shard_map/reduce_scatter | solution.py:99
  1486.8 56.9 %all-gather.24.cloned.1.call-done = bf16[8,2,64,2048]{3,2,0,1:T(8,128)(2,1)} async-done(((bf16[8,2,32,2048]{3,2,0,1:T(8,128)(2,1)}), bf16[8,2,64,2048]{3,2,0,1:T(8,128)(2,1)}) %all-gather.24.cloned.1.call-update) | async-done | bytes 4194320 | tf_op jit(solution)/shard_map/all_gather | solution.py:102
  1565.4 81.9 %all-to-all-done.5 = bf16[16,64,2048]{2,1,0:T(8,128)(2,1)} async-done(((bf16[16,64,2048]{2,1,0:T(8,128)(2,1)}), bf16[16,64,2048]{2,1,0:T(8,128)(2,1)}, u32[]{:S(2)}, u32[]{:S(2)}) %all-to-all-start.5) | async-done | bytes 4194336 | tf_op jit(solution)/shard_map/all_to_all | solution.py:103
  1647.3 8.2 gather_fusion.2
  1661.2 6.4 fusion.162
  1708.1 6.4 fusion.14
  1723.4 37.9 all-reduce.36.cloned.1.call-done
  1767.1 6.7 scatter_custom_fusion.4
  1773.8 99.2 %all_to_all.63 = bf16[16,64,2048]{2,1,0:T(8,128)(2,1)S(1)} all-to-all(bf16[16,64,2048]{2,1,0:T(8,128)(2,1)} %bitcast.1077), channel_id=1, replica_groups=mesh['section'=2,'expert'=8,'tensor'=2] {'expert'}, dimensions={0} | all-to-all | bytes 8388608 | tf_op jit(solution)/shard_map/all_to_all | solution.py:93
  1886.5 97.4 %reduce-scatter.20.cloned.1.call-done = f32[8,2,32,2048]{3,2,0,1:T(8,128)} async-done(((f32[8,2,64,2048]{3,2,0,1:T(8,128)}), f32[8,2,32,2048]{3,2,0,1:T(8,128)}) %reduce-scatter.20.cloned.1.call-update) | async-done | bytes 4194320 | tf_op jit(solution)/shard_map/reduce_scatter | solution.py:99
  1987.8 56.9 %all-gather.28.cloned.1.call-done = bf16[8,2,64,2048]{3,2,0,1:T(8,128)(2,1)} async-done(((bf16[8,2,32,2048]{3,2,0,1:T(8,128)(2,1)}), bf16[8,2,64,2048]{3,2,0,1:T(8,128)(2,1)}) %all-gather.28.cloned.1.call-update) | async-done | bytes 4194320 | tf_op jit(solution)/shard_map/all_gather | solution.py:102
  2067.3 81.0 %all-to-all-done.9 = bf16[16,64,2048]{2,1,0:T(8,128)(2,1)} async-done(((bf16[16,64,2048]{2,1,0:T(8,128)(2,1)}), bf16[16,64,2048]{2,1,0:T(8,128)(2,1)}, u32[]{:S(2)}, u32[]{:S(2)}) %all-to-all-start.9) | async-done | bytes 4194336 | tf_op jit(solution)/shard_map/all_to_all | solution.py:103
  2148.3 8.5 gather_fusion.4
  2166.6 6.8 scatter_custom_fusion.3
  2173.4 97.4 %all_to_all.64 = bf16[16,64,2048]{2,1,0:T(8,128)(2,1)S(1)} all-to-all(bf16[16,64,2048]{2,1,0:T(8,128)(2,1)} %bitcast.1074), channel_id=1, replica_groups=mesh['section'=2,'expert'=8,'tensor'=2] {'expert'}, dimensions={0} | all-to-all | bytes 8388608 | tf_op jit(solution)/shard_map/all_to_all | solution.py:93
  2282.3 97.4 %reduce-scatter.18.cloned.1.call-done = f32[8,2,32,2048]{3,2,0,1:T(8,128)} async-done(((f32[8,2,64,2048]{3,2,0,1:T(8,128)}), f32[8,2,32,2048]{3,2,0,1:T(8,128)}) %reduce-scatter.18.cloned.1.call-update) | async-done | bytes 4194320 | tf_op jit(solution)/shard_map/reduce_scatter | solution.py:99
  2383.6 56.9 %all-gather.26.cloned.1.call-done = bf16[8,2,64,2048]{3,2,0,1:T(8,128)(2,1)} async-done(((bf16[8,2,32,2048]{3,2,0,1:T(8,128)(2,1)}), bf16[8,2,64,2048]{3,2,0,1:T(8,128)(2,1)}) %all-gather.26.cloned.1.call-update) | async-done | bytes 4194320 | tf_op jit(solution)/shard_map/all_gather | solution.py:102
  2460.6 83.5 %all-to-all-done.8 = bf16[16,64,2048]{2,1,0:T(8,128)(2,1)} async-done(((bf16[16,64,2048]{2,1,0:T(8,128)(2,1)}), bf16[16,64,2048]{2,1,0:T(8,128)(2,1)}, u32[]{:S(2)}, u32[]{:S(2)}) %all-to-all-start.8) | async-done | bytes 4194336 | tf_op jit(solution)/shard_map/all_to_all | solution.py:103
  2544.1 8.3 gather_fusion.3
  2582.4 26.2 all-reduce.32.cloned.1.call-done
  2619.3 7.4 fusion.33
  2630.1 6.8 scatter_custom_fusion.5
  2637.0 100.3 %all_to_all.65 = bf16[16,64,2048]{2,1,0:T(8,128)(2,1)S(1)} all-to-all(bf16[16,64,2048]{2,1,0:T(8,128)(2,1)} %bitcast.1073), channel_id=1, replica_groups=mesh['section'=2,'expert'=8,'tensor'=2] {'expert'}, dimensions={0} | all-to-all | bytes 8388608 | tf_op jit(solution)/shard_map/all_to_all | solution.py:93
  2748.8 97.7 %reduce-scatter.22.cloned.1.call-done = f32[8,2,32,2048]{3,2,0,1:T(8,128)} async-done(((f32[8,2,64,2048]{3,2,0,1:T(8,128)}), f32[8,2,32,2048]{3,2,0,1:T(8,128)}) %reduce-scatter.22.cloned.1.call-update) | async-done | bytes 4194320 | tf_op jit(solution)/shard_map/reduce_scatter | solution.py:99
  2850.4 56.9 %all-gather.30.cloned.1.call-done = bf16[8,2,64,2048]{3,2,0,1:T(8,128)(2,1)} async-done(((bf16[8,2,32,2048]{3,2,0,1:T(8,128)(2,1)}), bf16[8,2,64,2048]{3,2,0,1:T(8,128)(2,1)}) %all-gather.30.cloned.1.call-update) | async-done | bytes 4194320 | tf_op jit(solution)/shard_map/all_gather | solution.py:102
  2923.3 87.9 %all-to-all-done.11 = bf16[16,64,2048]{2,1,0:T(8,128)(2,1)} async-done(((bf16[16,64,2048]{2,1,0:T(8,128)(2,1)}), bf16[16,64,2048]{2,1,0:T(8,128)(2,1)}, u32[]{:S(2)}, u32[]{:S(2)}) %all-to-all-start.11) | async-done | bytes 4194336 | tf_op jit(solution)/shard_map/all_to_all | solution.py:103
  3011.2 7.3 gather_fusion.5
  3046.3 22.6 all-reduce.34.cloned.1.call-done
  3080.4 9.3 fusion.243
  3089.7 8.1 fusion.240
  3097.8 18.3 add_add_fusion
  3117.1 8.2 fusion.252
  3125.3 8.2 fusion.249
  3133.5 18.7 add_add_fusion.1
  3153.7 6.9 fusion.48
  3186.0 9.6 fusion.22
  3195.5 10.4 fusion.24
  3206.0 10.1 fusion.23
  3216.3 37.3 all-reduce.18
  3262.2 15.2 reduce-scatter.28.cloned.1.call-done
  3277.3 286.5 %reduce-scatter.30.cloned.1.call-done = f32[2048,256]{1,0:T(8,128)} async-done(((f32[2048,2048]{1,0:T(8,128)}), f32[2048,256]{1,0:T(8,128)}) %reduce-scatter.30.cloned.1.call-update) | async-done | bytes 2097168 | tf_op jit(solution)/shard_map/reduce_scatter | solution.py:464
  3563.8 285.5 %reduce-scatter.24.cloned.1.call-done = f32[256,2048]{1,0:T(8,128)} async-done(((f32[2048,2048]{1,0:T(8,128)}), f32[256,2048]{1,0:T(8,128)}) %reduce-scatter.24.cloned.1.call-update) | async-done | bytes 2097168 | tf_op jit(solution)/shard_map/reduce_scatter | solution.py:459
  (918 shorter events, 509.5 us)
Async XLA Ops:
  7.2 487.0 %copy-start = (bf16[1,2,384,2048]{3,2,1,0:T(8,128)(2,1)S(1)}, bf16[1,2,384,2048]{3,2,1,0:T(8,128)(2,1)}, u32[]{:S(2)}) copy-start(bf16[1,2,384,2048]{3,2,1,0:T(8,128)(2,1)} %param.27) | copy-start | bytes 9437188
  7.2 81.1 %all-gather.34.cloned.1.call-start = ((), (), s32[]{:S(2)}) async-start(), calls=%async_computation.45 | async-start | bytes 1179648 | tf_op jit(solution)/shard_map/all_gather | solution.py:389
  7.9 86.4 %all-gather.32.cloned.1.call-start = ((), (), s32[]{:S(2)}) async-start(), calls=%async_computation.44 | async-start | bytes 1179648 | tf_op jit(solution)/shard_map/all_gather | solution.py:390
  8.7 211.6 %all-gather.36.cloned.1.call-start = ((), (), s32[]{:S(2)}) async-start(), calls=%async_computation.46 | async-start | bytes 9437184 | tf_op jit(solution)/shard_map/all_gather | solution.py:388
  9.4 336.3 %all-gather.38.cloned.1.call-start = ((), (), s32[]{:S(2)}) async-start(), calls=%async_computation.47 | async-start | bytes 9437184 | tf_op jit(solution)/shard_map/all_gather | solution.py:393
  10.0 368.6 %all-reduce.28.cloned.1.call-start = ((), (), s32[]{:S(2)}) async-start(), calls=%async_computation.23 | async-start | bytes 1048576 | tf_op jit(solution)/shard_map/psum | solution.py:174
  38.8 193.8 %copy-start.198 = (s32[16,5]{0,1:T(8,128)}, s32[16,5]{0,1:T(8,128)S(1)}, u32[]{:S(2)}) copy-start(s32[16,5]{0,1:T(8,128)S(1)} %reduce-window.77) | copy-start | bytes 964
  80.3 158.6 %copy-start.163 = (f32[128]{0:T(128)}, f32[128]{0:T(128)S(1)}, u32[]{:S(2)}) copy-start(f32[128]{0:T(128)S(1)} %convert_element_type.559) | copy-start | bytes 1540
  82.8 149.9 %copy-start.160 = (f32[128]{0:T(128)}, f32[128]{0:T(128)S(1)}, u32[]{:S(2)}) copy-start(f32[128]{0:T(128)S(1)} %convert_element_type.558) | copy-start | bytes 1540
  82.9 149.8 %copy-start.209 = (s32[64]{0:T(128)}, s32[64]{0:T(128)S(1)}, u32[]{:S(2)}) copy-start(s32[64]{0:T(128)S(1)} %convert_reduce_fusion.3) | copy-start | bytes 772
  86.7 145.9 %copy-start.157 = (f32[64]{0:T(128)}, f32[64]{0:T(128)S(1)}, u32[]{:S(2)}) copy-start(f32[64]{0:T(128)S(1)} %add_rsqrt_fusion.11) | copy-start | bytes 772
  97.9 134.8 %copy-start.138 = (f32[64,2,128]{2,0,1:T(8,128)}, f32[64,2,128]{2,0,1:T(8,128)S(1)}, u32[]{:S(2)}) copy-start(f32[64,2,128]{2,0,1:T(8,128)S(1)} %get-tuple-element.205) | copy-start | bytes 196612
  240.2 105.6 %copy-start.141 = (f32[2,8,64]{2,1,0:T(8,128)}, f32[2,8,64]{2,1,0:T(8,128)S(1)}, u32[]{:S(2)}) copy-start(f32[2,8,64]{2,1,0:T(8,128)S(1)} %log_add_fusion.2) | copy-start | bytes 12292
  240.7 110.9 %copy-start.50 = (bf16[64,2,8,128]{3,2,1,0:T(8,128)(2,1)}, bf16[64,2,8,128]{3,2,1,0:T(8,128)(2,1)S(1)}, u32[]{:S(2)}) copy-start(bf16[64,2,8,128]{3,2,1,0:T(8,128)(2,1)S(1)} %copy.345) | copy-start | bytes 786436
  351.6 245.6 %reduce-scatter.12.cloned.1.call-start = ((), (), s32[]{:S(2)}) async-start(), calls=%async_computation.24 | async-start | bytes 12582912 | tf_op jit(solution)/shard_map/reduce_scatter | solution.py:99
  352.7 133.6 %copy-start.205 = (s32[512,1]{0,1:T(1,128)}, s32[512,1]{0,1:T(1,128)S(1)}, u32[]{:S(2)}) copy-start(s32[512,1]{0,1:T(1,128)S(1)} %get-tuple-element.165) | copy-start | bytes 6148
  381.1 401.8 %copy-start.45 = (bf16[64,2048]{1,0:T(8,128)(2,1)}, bf16[64,2048]{1,0:T(8,128)(2,1)S(1)}, u32[]{:S(2)}) copy-start(bf16[64,2048]{1,0:T(8,128)(2,1)S(1)} %multiply_convert_fusion.5) | copy-start | bytes 786436
  387.4 99.0 %copy-start.23 = (bf16[1,2,2048,384]{3,2,1,0:T(8,128)(2,1)S(1)}, bf16[1,2,2048,384]{3,2,1,0:T(8,128)(2,1)}, u32[]{:S(2)}) copy-start(bf16[1,2,2048,384]{3,2,1,0:T(8,128)(2,1)} %param.25) | copy-start | bytes 9437188
  499.8 158.2 %all-gather.20.cloned.1.call-start = ((), (), s32[]{:S(2)}) async-start(), calls=%async_computation.25 | async-start | bytes 6291456 | tf_op jit(solution)/shard_map/all_gather | solution.py:102
  662.8 122.2 %all-to-all-start.1 = ((bf16[16,64,2048]{2,1,0:T(8,128)(2,1)}), bf16[16,64,2048]{2,1,0:T(8,128)(2,1)}, u32[]{:S(2)}, u32[]{:S(2)}) async-start(bf16[16,64,2048]{2,1,0:T(8,128)(2,1)} %bitcast.1071), calls=%async_computation.2 | async-start | bytes 8388608 | tf_op jit(solution)/shard_map/all_to_all | solution.py:103
  668.3 194.0 %all-reduce.30.cloned.1.call-start = ((), (), s32[]{:S(2)}) async-start(), calls=%async_computation.26 | async-start | bytes 1048576 | tf_op jit(solution)/shard_map/psum | solution.py:174
  797.9 2.4 collective-permute-start
  835.5 248.2 %reduce-scatter.14.cloned.1.call-start = ((), (), s32[]{:S(2)}) async-start(), calls=%async_computation.27 | async-start | bytes 12582912 | tf_op jit(solution)/shard_map/reduce_scatter | solution.py:99
  873.8 99.0 %copy-start.24 = (bf16[1,2,2048,384]{3,2,1,0:T(8,128)(2,1)S(1)}, bf16[1,2,2048,384]{3,2,1,0:T(8,128)(2,1)}, u32[]{:S(2)}) copy-start(bf16[1,2,2048,384]{3,2,1,0:T(8,128)(2,1)} %param.25) | copy-start | bytes 9437188
  986.2 158.2 %all-gather.22.cloned.1.call-start = ((), (), s32[]{:S(2)}) async-start(), calls=%async_computation.28 | async-start | bytes 6291456 | tf_op jit(solution)/shard_map/all_gather | solution.py:102
  1149.2 98.8 %all-to-all-start.3 = ((bf16[16,64,2048]{2,1,0:T(8,128)(2,1)}), bf16[16,64,2048]{2,1,0:T(8,128)(2,1)}, u32[]{:S(2)}, u32[]{:S(2)}) async-start(bf16[16,64,2048]{2,1,0:T(8,128)(2,1)} %bitcast.1069), calls=%async_computation.5 | async-start | bytes 8388608 | tf_op jit(solution)/shard_map/all_to_all | solution.py:103
  1154.7 328.3 %reduce-scatter.16.cloned.1.call-start = ((), (), s32[]{:S(2)}) async-start(), calls=%async_computation.29 | async-start | bytes 12582912 | tf_op jit(solution)/shard_map/reduce_scatter | solution.py:99
  1276.4 97.7 %copy-start.231 = (f32[2,8,64,384]{3,2,1,0:T(8,128)S(1)}, f32[2,8,64,384]{3,2,1,0:T(8,128)}, u32[]{:S(2)}) copy-start(f32[2,8,64,384]{3,2,1,0:T(8,128)} %copy-done.230) | copy-start | bytes 4718596
  1276.4 97.7 %copy-start.234 = (f32[2,8,64,384]{3,2,1,0:T(8,128)S(1)}, f32[2,8,64,384]{3,2,1,0:T(8,128)}, u32[]{:S(2)}) copy-start(f32[2,8,64,384]{3,2,1,0:T(8,128)} %copy-done.233) | copy-start | bytes 4718596
  1276.4 97.7 %copy-start.239 = (f32[2,8,64,384]{3,2,1,0:T(8,128)S(1)}, f32[2,8,64,384]{3,2,1,0:T(8,128)}, u32[]{:S(2)}) copy-start(f32[2,8,64,384]{3,2,1,0:T(8,128)} %get-tuple-element.213) | copy-start | bytes 4718596
  1276.4 97.7 %copy-start.241 = (f32[2,8,64,384]{3,2,1,0:T(8,128)S(1)}, f32[2,8,64,384]{3,2,1,0:T(8,128)}, u32[]{:S(2)}) copy-start(f32[2,8,64,384]{3,2,1,0:T(8,128)} %get-tuple-element.209) | copy-start | bytes 4718596
  1385.5 158.2 %all-gather.24.cloned.1.call-start = ((), (), s32[]{:S(2)}) async-start(), calls=%async_computation.30 | async-start | bytes 6291456 | tf_op jit(solution)/shard_map/all_gather | solution.py:102
  1548.5 98.8 %all-to-all-start.5 = ((bf16[16,64,2048]{2,1,0:T(8,128)(2,1)}), bf16[16,64,2048]{2,1,0:T(8,128)(2,1)}, u32[]{:S(2)}, u32[]{:S(2)}) async-start(bf16[16,64,2048]{2,1,0:T(8,128)(2,1)} %bitcast.1068), calls=%async_computation.8 | async-start | bytes 8388608 | tf_op jit(solution)/shard_map/all_to_all | solution.py:103
  1554.0 207.3 %all-reduce.36.cloned.1.call-start = ((), (), s32[]{:S(2)}) async-start(), calls=%async_computation.48 | async-start | bytes 2097152 | tf_op jit(solution)/shard_map/psum | solution.py:349
  1561.3 99.4 %collective-permute-start.1 = (bf16[64,2048]{1,0:T(8,128)(2,1)}, bf16[64,2048]{1,0:T(8,128)(2,1)}, u32[]{:S(2)}, u32[]{:S(2)}) collective-permute-start(bf16[64,2048]{1,0:T(8,128)(2,1)} %add_convert_fusion.1), channel_id=1, source_target_pairs={{0,16},{1,17},{2,18},{3,19},{4,20},{5,21},{6,22},{7,23},{8,24},{9,... | collective-permute-start | bytes 786440 | tf_op jit(solution)/shard_map/ppermute | solution.py:14
  1722.2 261.7 %reduce-scatter.20.cloned.1.call-start = ((), (), s32[]{:S(2)}) async-start(), calls=%async_computation.33 | async-start | bytes 12582912 | tf_op jit(solution)/shard_map/reduce_scatter | solution.py:99
  1773.8 99.2 %copy-start.26 = (bf16[1,2,2048,384]{3,2,1,0:T(8,128)(2,1)S(1)}, bf16[1,2,2048,384]{3,2,1,0:T(8,128)(2,1)}, u32[]{:S(2)}) copy-start(bf16[1,2,2048,384]{3,2,1,0:T(8,128)(2,1)} %param.25) | copy-start | bytes 9437188
  1886.4 158.2 %all-gather.28.cloned.1.call-start = ((), (), s32[]{:S(2)}) async-start(), calls=%async_computation.34 | async-start | bytes 6291456 | tf_op jit(solution)/shard_map/all_gather | solution.py:102
  2049.5 98.8 %all-to-all-start.9 = ((bf16[16,64,2048]{2,1,0:T(8,128)(2,1)}), bf16[16,64,2048]{2,1,0:T(8,128)(2,1)}, u32[]{:S(2)}, u32[]{:S(2)}) async-start(bf16[16,64,2048]{2,1,0:T(8,128)(2,1)} %bitcast.1066), calls=%async_computation.14 | async-start | bytes 8388608 | tf_op jit(solution)/shard_map/all_to_all | solution.py:103
  2055.0 324.8 %reduce-scatter.18.cloned.1.call-start = ((), (), s32[]{:S(2)}) async-start(), calls=%async_computation.31 | async-start | bytes 12582912 | tf_op jit(solution)/shard_map/reduce_scatter | solution.py:99
  2059.2 6.3 collective-permute-start.2
  2173.4 97.4 %copy-start.235 = (f32[2,8,64,384]{3,2,1,0:T(8,128)S(1)}, f32[2,8,64,384]{3,2,1,0:T(8,128)}, u32[]{:S(2)}) copy-start(f32[2,8,64,384]{3,2,1,0:T(8,128)} %copy-done.233) | copy-start | bytes 4718596
  2173.4 97.4 %copy-start.237 = (f32[2,8,64,384]{3,2,1,0:T(8,128)S(1)}, f32[2,8,64,384]{3,2,1,0:T(8,128)}, u32[]{:S(2)}) copy-start(f32[2,8,64,384]{3,2,1,0:T(8,128)} %copy-done.236) | copy-start | bytes 4718596
  2173.4 97.4 %copy-start.242 = (f32[2,8,64,384]{3,2,1,0:T(8,128)S(1)}, f32[2,8,64,384]{3,2,1,0:T(8,128)}, u32[]{:S(2)}) copy-start(f32[2,8,64,384]{3,2,1,0:T(8,128)} %get-tuple-element.209) | copy-start | bytes 4718596
  2173.4 97.5 %copy-start.243 = (f32[2,8,64,384]{3,2,1,0:T(8,128)S(1)}, f32[2,8,64,384]{3,2,1,0:T(8,128)}, u32[]{:S(2)}) copy-start(f32[2,8,64,384]{3,2,1,0:T(8,128)} %get-tuple-element.220) | copy-start | bytes 4718596
  2282.3 158.2 %all-gather.26.cloned.1.call-start = ((), (), s32[]{:S(2)}) async-start(), calls=%async_computation.32 | async-start | bytes 6291456 | tf_op jit(solution)/shard_map/all_gather | solution.py:102
  2445.3 98.8 %all-to-all-start.8 = ((bf16[16,64,2048]{2,1,0:T(8,128)(2,1)}), bf16[16,64,2048]{2,1,0:T(8,128)(2,1)}, u32[]{:S(2)}, u32[]{:S(2)}) async-start(bf16[16,64,2048]{2,1,0:T(8,128)(2,1)} %bitcast.1070), calls=%async_computation.12 | async-start | bytes 8388608 | tf_op jit(solution)/shard_map/all_to_all | solution.py:103
  2450.8 157.7 %all-reduce.32.cloned.1.call-start = ((), (), s32[]{:S(2)}) async-start(), calls=%async_computation.35 | async-start | bytes 1048576 | tf_op jit(solution)/shard_map/psum | solution.py:349
  2581.7 264.9 %reduce-scatter.22.cloned.1.call-start = ((), (), s32[]{:S(2)}) async-start(), calls=%async_computation.36 | async-start | bytes 12582912 | tf_op jit(solution)/shard_map/reduce_scatter | solution.py:99
  2613.6 3.8 collective-permute-start.3
  2637.0 100.3 %copy-start.232 = (f32[2,8,64,384]{3,2,1,0:T(8,128)S(1)}, f32[2,8,64,384]{3,2,1,0:T(8,128)}, u32[]{:S(2)}) copy-start(f32[2,8,64,384]{3,2,1,0:T(8,128)} %copy-done.230) | copy-start | bytes 4718596
  2637.0 100.3 %copy-start.238 = (f32[2,8,64,384]{3,2,1,0:T(8,128)S(1)}, f32[2,8,64,384]{3,2,1,0:T(8,128)}, u32[]{:S(2)}) copy-start(f32[2,8,64,384]{3,2,1,0:T(8,128)} %copy-done.236) | copy-start | bytes 4718596
  2637.0 100.3 %copy-start.240 = (f32[2,8,64,384]{3,2,1,0:T(8,128)S(1)}, f32[2,8,64,384]{3,2,1,0:T(8,128)}, u32[]{:S(2)}) copy-start(f32[2,8,64,384]{3,2,1,0:T(8,128)} %get-tuple-element.213) | copy-start | bytes 4718596
  2637.0 100.3 %copy-start.244 = (f32[2,8,64,384]{3,2,1,0:T(8,128)S(1)}, f32[2,8,64,384]{3,2,1,0:T(8,128)}, u32[]{:S(2)}) copy-start(f32[2,8,64,384]{3,2,1,0:T(8,128)} %get-tuple-element.220) | copy-start | bytes 4718596
  2748.8 158.5 %all-gather.30.cloned.1.call-start = ((), (), s32[]{:S(2)}) async-start(), calls=%async_computation.37 | async-start | bytes 6291456 | tf_op jit(solution)/shard_map/all_gather | solution.py:102
  2912.2 98.9 %all-to-all-start.11 = ((bf16[16,64,2048]{2,1,0:T(8,128)(2,1)}), bf16[16,64,2048]{2,1,0:T(8,128)(2,1)}, u32[]{:S(2)}, u32[]{:S(2)}) async-start(bf16[16,64,2048]{2,1,0:T(8,128)(2,1)} %bitcast.1067), calls=%async_computation.17 | async-start | bytes 8388608 | tf_op jit(solution)/shard_map/all_to_all | solution.py:103
  2917.9 151.0 %all-reduce.34.cloned.1.call-start = ((), (), s32[]{:S(2)}) async-start(), calls=%async_computation.38 | async-start | bytes 1048576 | tf_op jit(solution)/shard_map/psum | solution.py:349
  2923.3 96.7 %copy-start.169 = (bf16[64,16]{0,1:T(8,128)(2,1)}, bf16[64,16]{0,1:T(8,128)(2,1)S(1)}, u32[]{:S(2)}) copy-start(bf16[64,16]{0,1:T(8,128)(2,1)S(1)} %select_reduce_fusion) | copy-start | bytes 6148
  3042.0 220.2 %reduce-scatter.32.cloned.1.call-start = ((), (), s32[]{:S(2)}) async-start(), calls=%async_computation.43 | async-start | bytes 147456 | tf_op jit(solution)/shard_map/reduce_scatter | solution.py:466
  3045.8 216.4 %reduce-scatter.26.cloned.1.call-start = ((), (), s32[]{:S(2)}) async-start(), calls=%async_computation.40 | async-start | bytes 2359296 | tf_op jit(solution)/shard_map/reduce_scatter | solution.py:460
  3076.2 201.1 %reduce-scatter.28.cloned.1.call-start = ((), (), s32[]{:S(2)}) async-start(), calls=%async_computation.41 | async-start | bytes 2359296 | tf_op jit(solution)/shard_map/reduce_scatter | solution.py:461
  3080.3 483.5 %reduce-scatter.30.cloned.1.call-start = ((), (), s32[]{:S(2)}) async-start(), calls=%async_computation.42 | async-start | bytes 18874368 | tf_op jit(solution)/shard_map/reduce_scatter | solution.py:464
  3116.2 733.1 %reduce-scatter.24.cloned.1.call-start = ((), (), s32[]{:S(2)}) async-start(), calls=%async_computation.39 | async-start | bytes 18874368 | tf_op jit(solution)/shard_map/reduce_scatter | solution.py:459
  3206.0 643.3 %copy-start.1 = (bf16[1,2,384,2048]{3,2,1,0:T(8,128)(2,1)S(1)}, bf16[1,2,384,2048]{3,2,1,0:T(8,128)(2,1)}, u32[]{:S(2)}) copy-start(bf16[1,2,384,2048]{3,2,1,0:T(8,128)(2,1)} %param.27) | copy-start | bytes 9437188
  (220 other events, 1457.2 us)
Sparse Core Ops, SparseCore 0:
  10.2 42.9 all-gather.33
  55.3 39.0 all-gather.31
  96.5 123.7 all-gather.35
  222.1 123.5 all-gather.37
  351.7 26.7 all-reduce.27
  499.9 97.2 reduce-scatter.11
  601.2 56.7 all-gather.19
  835.6 26.7 all-reduce.29
  986.3 97.2 reduce-scatter.13
  1087.6 56.7 all-gather.21
  1385.6 97.3 reduce-scatter.15
  1487.0 56.7 all-gather.23
  1722.3 38.9 all-reduce.35
  1886.6 97.3 reduce-scatter.19
  1987.9 56.7 all-gather.27
  2282.4 97.3 reduce-scatter.17
  2383.7 56.7 all-gather.25
  2581.8 26.7 all-reduce.31
  2748.9 97.5 reduce-scatter.21
  2850.5 56.7 all-gather.29
  3042.1 26.7 all-reduce.33
  3073.1 61.2 reduce-scatter.31
  3139.0 66.9 reduce-scatter.25
  3210.3 66.9 reduce-scatter.27
  3282.2 281.5 reduce-scatter.29
  3568.0 281.2 reduce-scatter.23
where the time goes:
time: 3870 us; the launch traced here: 3860 us
  waiting for transfers between devices  2300 us (59%)
  blocking collectives  807 us (21%)
  matrix products  317 us (8%)
  other arithmetic  202 us (5%)
  local copies, waits for them, and re-layouts  165 us (4%)
  starting transfers between devices  41.9 us (1%)
    all_to_all x6, blocking collectives, slots_away(): lax.all_to_all(buffer, 'expert', split_axis=0, concat_axis=0, tiled=True)  593 us
    reduce_scatter x6, waiting for transfers between devices, slots_home(): lax.psum_scatter(partial_value, 'tensor', scatter_dimension=2, tiled=True)  585 us
    all_to_all x6, waiting for transfers between devices, slots_home(): lax.all_to_all(shared.reshape(-1, shared.shape[2], shared.shape[3]), 'exp...  416 us
    all_gather x6, waiting for transfers between devices, slots_home(): shared = lax.all_gather(shared, 'tensor', axis=2, tiled=True)  341 us
    reduce_scatter x1, waiting for transfers between devices, body(): lax.psum_scatter(g_out, 'expert', scatter_dimension=1, tiled=True)  286 us
    reduce_scatter x1, waiting for transfers between devices, body(): lax.psum_scatter(g_query, 'expert', scatter_dimension=0, tiled=True)  285 us
    all_gather x1, waiting for transfers between devices, body(): lax.all_gather(w_query[0], 'expert', axis=0, tiled=True)  122 us
    all_gather x1, blocking collectives, body(): lax.all_gather(router[0], 'expert', axis=0, tiled=True)  113 us
  transfers between devices with their start and end apart: 36, of which 30 were waited for; matrix products, arithmetic and copies ran while one was open for 7% of the time, Pallas kernels for 0%

commit v1 on v0

v1 whole, which is shorter than its diff:
```python
import jax
import jax.numpy as jnp
from jax import lax
from jax.sharding import PartitionSpec as P

epsilon = 1e-06
rope_base = 1000000.0
masked_score = -1e30
bf16 = jnp.bfloat16
f32 = jnp.float32


def dot(left, right):
    return jnp.dot(left, right, preferred_element_type=f32)


def dot_rows(left, right):
    return lax.dot_general(left, right, (((0,), (0,)), ((), ())), preferred_element_type=f32)


def dot_cols(left, right):
    return lax.dot_general(left, right, (((1,), (1,)), ((), ())), preferred_element_type=f32)


def cat(*pieces, axis=0):
    return jnp.concatenate(pieces, axis=axis)


def swap_core(value):
    return lax.ppermute(value, "section", [(0, 1), (1, 0)])


def swap_x(value):
    return lax.ppermute(value, "tensor", [(0, 1), (1, 0)])


def swap_e(value, bits):
    count = lax.axis_size("expert")
    return lax.ppermute(value, "expert", [(i, i ^ bits) for i in range(count)])


def small_grid():
    return lax.axis_size("expert") == 8


def gather_rows(shard):
    if not small_grid():
        return lax.all_gather(shard, ("expert", "tensor"), axis=0, tiled=True)
    own = cat(shard, swap_e(shard, 2), swap_e(shard, 4), swap_e(shard, 6))
    half = own.shape[0] // 2
    from_x = swap_x(own)
    from_y = swap_e(own, 1)
    far_top = swap_e(from_x[:half], 1)
    far_bottom = swap_x(from_y[half:])
    return cat(own, from_x, from_y, far_top, far_bottom)


def scatter_rows(partial):
    if not small_grid():
        return lax.psum_scatter(partial, ("expert", "tensor"), scatter_dimension=0, tiled=True)
    quarter = partial.shape[0] // 4
    half = quarter // 2
    own, to_x, to_y, far = [partial[i * quarter : (i + 1) * quarter] for i in range(4)]
    top = swap_e(far[:half].astype(bf16), 1)
    bottom = swap_x(far[half:].astype(bf16))
    to_x = cat(to_x[:half] + top, to_x[half:]).astype(bf16)
    to_y = cat(to_y[:half], to_y[half:] + bottom).astype(bf16)
    total = own + swap_x(to_x) + swap_e(to_y, 1)
    step = quarter // 4
    for position, bits in ((1, 2), (2, 4), (3, 6)):
        block = total[position * step : (position + 1) * step].astype(bf16)
        if position == 1:
            result = total[:step] + swap_e(block, bits)
        else:
            result = result + swap_e(block, bits)
    return result


def gather_expert(shard):
    return lax.all_gather(shard, "expert", axis=0, tiled=True)


def normalize(value):
    return value * lax.rsqrt(jnp.mean(value * value, axis=-1, keepdims=True) + epsilon)


def rms_norm(value, gain):
    return normalize(value) * gain


def rotary(value, cosine, sine):
    half = value.shape[-1] // 2
    first = value[..., :half]
    second = value[..., half:]
    return cat(first * cosine - second * sine, second * cosine + first * sine, axis=-1)


def prepare(raw, gain, cosine, sine, factor):
    return rotary(rms_norm(raw, gain), cosine, sine) * factor


def layout(lengths_row, row_index):
    ends = jnp.cumsum(lengths_row, dtype=jnp.int32)
    starts = ends - lengths_row
    segment = jnp.sum((row_index[:, None] >= ends[None, :]).astype(jnp.int32), axis=1)
    member = segment[:, None] == jnp.arange(ends.shape[0], dtype=jnp.int32)[None, :]
    return segment, row_index - jnp.sum(jnp.where(member, starts[None, :], 0), axis=1)


def positions(lengths_row, row_index, head):
    segment, position = layout(lengths_row, row_index)
    half = head // 2
    inverse = rope_base ** (-(jnp.arange(half, dtype=f32) * 2.0) / head)
    angles = position.astype(f32)[:, None] * inverse[None, :]
    allowed = (segment[:, None] == segment[None, :]) & (row_index[None, :] <= row_index[:, None])
    return jnp.cos(angles), jnp.sin(angles), allowed


def attend(normed, w_qkv, query_gain, key_gain, tables):
    cosine, sine, allowed = tables
    head = query_gain.shape[0]
    rows = normed.shape[0] // 2
    group = w_qkv.shape[1] // head - 2
    raw = dot(normed, w_qkv).reshape(2, rows, group + 2, head)
    q_raw, k_raw, values = raw[:, :, :group], raw[:, :, group], raw[:, :, group + 1].astype(bf16)
    queries = prepare(
        q_raw, query_gain, cosine[:, :, None], sine[:, :, None], head ** (-0.5)
    ).astype(bf16)
    keys = prepare(k_raw, key_gain, cosine, sine, 1.0).astype(bf16)
    scores = jnp.einsum("mrgd,msd->mgrs", queries, keys, preferred_element_type=f32)
    scores = jnp.where(allowed[:, None], scores, masked_score)
    weights = jnp.exp(scores - jnp.max(scores, axis=-1, keepdims=True))
    probs = weights / jnp.sum(weights, axis=-1, keepdims=True)
    mixed = jnp.einsum("mgrs,msd->mrgd", probs.astype(bf16), values, preferred_element_type=f32)
    mixed = mixed.astype(bf16).reshape(2 * rows, group * head)
    return mixed, (q_raw, k_raw, values, queries, keys, probs)


def attend_back(d_mixed, state, query_gain, key_gain, tables):
    cosine, sine, allowed = tables
    q_raw, k_raw, values, queries, keys, probs = state
    mb, rows, group, head = q_raw.shape
    d_mixed = d_mixed.astype(bf16).reshape(mb, rows, group, head)
    d_probs = jnp.einsum("mrgd,msd->mgrs", d_mixed, values, preferred_element_type=f32)
    d_scores = probs * (d_probs - jnp.sum(probs * d_probs, axis=-1, keepdims=True))
    d_scores = d_scores.astype(bf16)
    d_values = jnp.einsum(
        "mgrs,mrgd->msd", probs.astype(bf16), d_mixed, preferred_element_type=f32
    ).astype(bf16)
    d_queries = jnp.einsum("mgrs,msd->mrgd", d_scores, keys, preferred_element_type=f32)
    d_keys = jnp.einsum("mgrs,mrgd->msd", d_scores, queries, preferred_element_type=f32)
    _, pull = jax.vjp(
        lambda raw, gain: prepare(
            raw, gain, cosine[:, :, None], sine[:, :, None], head ** (-0.5)
        ),
        q_raw,
        query_gain,
    )
    d_q, g_query_gain = pull(d_queries)
    _, pull = jax.vjp(
        lambda raw, gain: prepare(raw, gain, cosine, sine, 1.0), k_raw, key_gain
    )
    d_k, g_key_gain = pull(d_keys)
    d_qkv = cat(
        d_q.astype(bf16).reshape(mb * rows, group * head),
        d_k.astype(bf16).reshape(mb * rows, head),
        d_values.reshape(mb * rows, head),
        axis=1,
    )
    return d_qkv, g_query_gain, g_key_gain


def both_rows(shard):
    block = cat(shard, swap_x(shard))
    return cat(block, swap_core(block))


def own_rows(partial):
    rows = partial.shape[0] // 2
    block = partial[:rows] + swap_core(partial[rows:].astype(bf16))
    half = rows // 2
    return block[:half] + swap_x(block[half:].astype(bf16))


def router_gates(normed, router, mask):
    logits = jnp.where(mask, dot(normed, router), masked_score)
    weights = jnp.exp(logits - jnp.max(logits, axis=-1, keepdims=True))
    return weights / jnp.sum(weights, axis=-1, keepdims=True)


def forward_layer(x, weights, mask, tables, local_experts):
    attn_gain, w_qkv, query_gain, key_gain, w_out, ffn_gain, router, w_gate, w_up, w_down = weights
    width = x.shape[1]
    experts = router.shape[1]
    normed = both_rows(rms_norm(x, attn_gain).astype(bf16))
    mixed, attn_state = attend(normed, w_qkv, query_gain, key_gain, tables)
    mid = x + own_rows(dot_cols(mixed, w_out))
    normed_ffn = rms_norm(mid, ffn_gain).astype(bf16)
    gates = router_gates(normed_ffn, router, mask)
    high = gates.astype(bf16)
    low = (gates - high.astype(f32)).astype(bf16)
    extra = jnp.zeros((x.shape[0], 128 - 2 * experts), bf16)
    gathered = gather_rows(cat(normed_ffn, high, low, extra, axis=1))
    rows_in = gathered[:, :width]
    all_gates = gathered[:, width : width + experts].astype(f32) + gathered[
        :, width + experts : width + 2 * experts
    ].astype(f32)
    local = jnp.stack(
        [jnp.sum(jnp.where(one[None, :], all_gates, 0.0), axis=1) for one in local_experts], axis=1
    )
    hidden_units = w_gate.shape[1] // len(local_experts)
    wide = jnp.repeat(local, hidden_units, axis=1)
    gate_act = dot(rows_in, w_gate)
    up_act = dot(rows_in, w_up)
    hidden = (jax.nn.silu(gate_act) * up_act).astype(bf16)
    scaled = (hidden.astype(f32) * wide).astype(bf16)
    out = mid + scatter_rows(dot(scaled, w_down))
    state = (x, normed, mixed, attn_state, mid, normed_ffn, gates, wide)
    state = state + (rows_in, gate_act, up_act, hidden, scaled)
    return out, state


def backward_layer(grad, state, weights, mask, tables, local_experts):
    attn_gain, w_qkv, query_gain, key_gain, w_out, ffn_gain, router, w_gate, w_up, w_down = weights
    x, normed, mixed, attn_state, mid, normed_ffn, gates, wide = state[:8]
    rows_in, gate_act, up_act, hidden, scaled = state[8:]
    width = x.shape[1]
    experts = router.shape[1]
    grad_rows = gather_rows(grad)
    plain = dot_cols(grad_rows, w_down)
    hidden_units = w_gate.shape[1] // len(local_experts)
    products = (hidden.astype(f32) * plain).reshape(plain.shape[0], -1, hidden_units)
    gate_grads = jnp.sum(products, axis=2)
    placed = sum(
        gate_grads[:, i : i + 1] * one.astype(f32)[None, :] for i, one in enumerate(local_experts)
    )
    d_hidden = plain * wide
    sigmoid = jax.nn.sigmoid(gate_act)
    d_up = (d_hidden * gate_act * sigmoid).astype(bf16)
    d_gate = (d_hidden * up_act * sigmoid * (1.0 + gate_act * (1.0 - sigmoid))).astype(bf16)
    d_rows = dot_cols(d_gate, w_gate) + dot_cols(d_up, w_up)
    extra = jnp.zeros((d_rows.shape[0], 128 - experts), f32)
    back = scatter_rows(cat(d_rows, placed, extra, axis=1))
    gate_grad = back[:, width : width + experts]
    d_logits = gates * (gate_grad - jnp.sum(gates * gate_grad, axis=-1, keepdims=True))
    d_logits = d_logits.astype(bf16)
    d_normed_ffn = back[:, :width] + dot_cols(d_logits, router)
    _, pull = jax.vjp(rms_norm, mid, ffn_gain)
    d_mid, g_ffn_gain = pull(d_normed_ffn)
    d_mid = d_mid + grad.astype(f32)
    d_attn = both_rows(d_mid.astype(bf16))
    d_mixed = dot(d_attn, w_out)
    d_qkv, g_query_gain, g_key_gain = attend_back(
        d_mixed, attn_state, query_gain, key_gain, tables
    )
    d_normed = own_rows(dot_cols(d_qkv, w_qkv))
    _, pull = jax.vjp(rms_norm, x, attn_gain)
    d_x, g_attn_gain = pull(d_normed)
    g_router = dot_rows(d_logits, normed_ffn)
    small = (g_router, g_attn_gain, g_ffn_gain, g_query_gain, g_key_gain)
    heavy = (grad_rows, d_gate, d_up, d_attn, d_qkv)
    return d_mid + d_x, small, heavy


def sum_small(own, other):
    value = own + swap_core(other)
    if not small_grid():
        value = lax.psum(value, "tensor")
        return lax.psum_scatter(value, "expert", scatter_dimension=0, tiled=True)[0]
    value = value + swap_x(value)
    index = lax.axis_index("expert")
    for bit in (4, 2, 1):
        pair = value.reshape(2, value.shape[0] // 2, *value.shape[1:])
        upper = (index & bit) != 0
        keep = jnp.where(upper, pair[1], pair[0])
        give = jnp.where(upper, pair[0], pair[1])
        value = keep + swap_e(give, bit)
    return value[0]


def body(
    ends_in,
    attn_gain,
    w_query,
    key_matrix,
    value_matrix,
    query_gain,
    key_gain,
    w_out,
    ffn_gain,
    router,
    w_gate,
    w_up,
    w_down,
    routes,
    lengths,
):
    core = lax.axis_index("section")
    first = core == 0
    side = lax.axis_index("tensor")
    index = lax.axis_index("expert")
    split = lax.axis_size("expert")
    rows, width = ends_in.shape[2:]
    half = rows // 2
    experts = router.shape[2]
    head = query_gain.shape[1] * split

    def pick(zero, one):
        return jnp.where(first, zero, one)

    def mine(pair):
        return pick(pair[0], pair[1])

    def theirs(pair):
        return pick(pair[1], pair[0])

    def by_layer(own):
        got = swap_core(own)
        return pick(own, got), pick(got, own)

    def half_rows(block):
        return pick_side(block[:half], block[half:])

    def pick_side(zero, one):
        return jnp.where(side == 0, zero, one)

    columns = w_query.shape[2] // 2
    part = w_query.shape[1]
    transposed = w_out[0].T
    groups = [
        (
            cat(
                w_query[0][:, g * columns : (g + 1) * columns],
                key_matrix[0][:, g * head : (g + 1) * head],
                value_matrix[0][:, g * head : (g + 1) * head],
                axis=1,
            ),
            transposed[:, g * columns : (g + 1) * columns],
        )
        for g in range(2)
    ]
    kept = [mine(pair) for pair in zip(*groups)]
    got = [swap_core(theirs(pair)) for pair in zip(*groups)]
    slices = [[pick(k, g) for k, g in zip(kept, got)], [pick(g, k) for k, g in zip(kept, got)]]
    tiny = cat(
        attn_gain[0],
        ffn_gain[0],
        query_gain[0],
        key_gain[0],
        router[0].T.reshape(-1),
    )
    tiny_layers = jnp.stack(by_layer(tiny))
    tiny_all = lax.all_gather(tiny_layers[None], "expert", axis=0, tiled=True)
    full = [gather_expert(slices[0][0]), gather_expert(slices[0][1])]
    full = full + [gather_expert(slices[1][0]), gather_expert(slices[1][1])]
    gates_both = by_layer(w_gate[0].transpose(1, 0, 2).reshape(width, -1))
    ups_both = by_layer(w_up[0].transpose(1, 0, 2).reshape(width, -1))
    downs_both = by_layer(w_down[0].reshape(-1, width))
    layers = []
    for number in range(2):
        one = tiny_all[:, number]
        sizes = (part, part, head // split, head // split)
        vectors, start = [], 0
        for size in sizes:
            vectors.append(one[:, start : start + size].reshape(-1).astype(f32))
            start += size
        router_all = one[:, start:].reshape(split, experts, part).transpose(0, 2, 1)
        layers.append(
            (
                vectors[0],
                full[2 * number],
                vectors[2],
                vectors[3],
                full[2 * number + 1],
                vectors[1],
                router_all.reshape(width, experts),
                gates_both[number],
                ups_both[number],
                downs_both[number],
            )
        )

    crossed = swap_core(pick(ends_in[0, 1], ends_in[0, 0]))
    x_in = half_rows(pick(ends_in[0, 0], crossed)).astype(f32)
    grad_last = half_rows(pick(crossed, ends_in[0, 1]))
    routes_crossed = swap_core(pick(routes[0, 1], routes[0, 0]))
    routes_own = [pick(routes[0, 0], routes_crossed), pick(routes_crossed, routes[0, 1])]
    expert_ids = jnp.arange(experts, dtype=jnp.int32)
    masks = [
        jnp.any(half_rows(r)[:, :, None] == expert_ids[None, None, :], axis=1) for r in routes_own
    ]
    per_device = w_gate.shape[1]
    local_experts = [expert_ids == index * per_device + i for i in range(per_device)]
    row_index = (jnp.arange(rows, dtype=jnp.int32) + side * half) % rows
    length_pair = [pick(lengths[0, 0], lengths[1, 0]), pick(lengths[1, 0], lengths[0, 0])]
    tables = [positions(one, row_index, head) for one in length_pair]
    tables = tuple(jnp.stack(one) for one in zip(*tables))

    out0, state0 = forward_layer(x_in, layers[0], masks[0], tables, local_experts)
    x_mid = out0.astype(bf16).astype(f32)
    out1, state1 = forward_layer(x_mid, layers[1], masks[1], tables, local_experts)
    out1 = out1.astype(bf16)
    d_one, small1, heavy1 = backward_layer(
        grad_last, state1, layers[1], masks[1], tables, local_experts
    )
    d_one = d_one.astype(bf16)
    d_zero, small0, heavy0 = backward_layer(
        d_one, state0, layers[0], masks[0], tables, local_experts
    )
    d_zero = d_zero.astype(bf16)

    def both_batches(zero, one):
        own = pick(zero, one)
        return own, swap_core(pick(one, zero))

    rows_pair = both_batches(state0[8], state1[8])
    scaled_pair = both_batches(state0[12], state1[12])
    grad_pair = both_batches(heavy0[0], heavy1[0])
    gate_pair = both_batches(heavy0[1], heavy1[1])
    up_pair = both_batches(heavy0[2], heavy1[2])

    def both_dots(left, right):
        return dot_rows(left[0], right[0]) + dot_rows(left[1], right[1])

    units = w_gate.shape[3]
    g_gate = both_dots(rows_pair, gate_pair).reshape(width, per_device, units).transpose(1, 0, 2)
    g_up = both_dots(rows_pair, up_pair).reshape(width, per_device, units).transpose(1, 0, 2)
    g_down = both_dots(scaled_pair, grad_pair).reshape(per_device, units, width)

    def spread(value):
        return lax.all_to_all(value, "expert", split_axis=1, concat_axis=0, tiled=True)

    def swap_batches(value):
        return cat(value[rows:], value[:rows])

    normed_cols = spread(pick(state0[1], state1[1]))
    d_attn_cols = spread(pick(heavy0[3], heavy1[3]))
    mixed_own = pick(state0[2], state1[2])
    mixed_got = swap_batches(swap_core(pick(state1[2], state0[2])))
    mixed_all = gather_expert(
        cat(pick(mixed_own, mixed_got), pick(mixed_got, mixed_own), axis=1)
    )
    g_out = dot_rows(mixed_all, d_attn_cols)
    qkv_own = pick(heavy0[4], heavy1[4])
    qkv_got = swap_batches(swap_core(pick(heavy1[4], heavy0[4])))
    qkv_all = gather_expert(cat(pick(qkv_own, qkv_got), pick(qkv_got, qkv_own), axis=1))
    g_qkv = dot_rows(normed_cols, qkv_all)
    wide = g_qkv.shape[1] // 2
    g_query = cat(g_qkv[:, :columns], g_qkv[:, wide : wide + columns], axis=1)
    g_key = cat(
        g_qkv[:, columns : columns + head],
        g_qkv[:, wide + columns : wide + columns + head],
        axis=1,
    )
    g_value = cat(g_qkv[:, columns + head : wide], g_qkv[:, wide + columns + head :], axis=1)

    def by_owner(small):
        g_router, g_attn_gain, g_ffn_gain, g_query_gain, g_key_gain = small
        owned = [
            g_router.reshape(experts, split, part).transpose(1, 0, 2),
            g_attn_gain.reshape(split, 1, part),
            g_ffn_gain.reshape(split, 1, part),
        ]
        heads = cat(g_query_gain.reshape(split, 1, -1), g_key_gain.reshape(split, 1, -1), axis=2)
        owned.append(jnp.pad(heads, ((0, 0), (0, 0), (0, part - heads.shape[2]))))
        return cat(*owned, axis=1)

    small = (by_owner(small0), by_owner(small1))
    summed = sum_small(mine(small), theirs(small))
    g_router = summed[:experts].T
    g_attn_gain = summed[experts]
    g_ffn_gain = summed[experts + 1]
    g_query_gain = summed[experts + 2, : head // split]
    g_key_gain = summed[experts + 2, head // split : 2 * (head // split)]

    end_own = pick(d_zero, out1)
    end_got = swap_core(pick(out1, d_zero))
    ends = jnp.stack([pick(end_own, end_got), pick(end_got, end_own)])
    ends_far = swap_x(ends)
    ends_out = cat(pick_side(ends, ends_far), pick_side(ends_far, ends), axis=1)

    outs = (
        ends_out,
        g_attn_gain,
        g_query,
        g_key,
        g_value,
        g_query_gain,
        g_key_gain,
        g_out,
        g_ffn_gain,
        g_router,
        g_gate,
        g_up,
        g_down,
    )
    return tuple(one[None] for one in outs)


def solution(mesh):
    return jax.shard_map(
        body,
        mesh=mesh,
        in_specs=(
            P("section", None, "expert", None),
            P("section", "expert"),
            P("section", "expert", "tensor"),
            P("section", "expert", "tensor"),
            P("section", "expert", "tensor"),
            P("section", "expert"),
            P("section", "expert"),
            P("section", "tensor", "expert"),
            P("section", "expert"),
            P("section", "expert", None),
            P("section", "expert", None, "tensor"),
            P("section", "expert", None, "tensor"),
            P("section", "expert", "tensor", None),
            P("section", None, "expert", None),
            P(None, "expert", None),
        ),
        out_specs=(
            P("section", None, "expert", None),
            P("section", "expert"),
            P("section", "expert", "tensor"),
            P("section", "expert", "tensor"),
            P("section", "expert", "tensor"),
            P("section", "expert"),
            P("section", "expert"),
            P("section", "tensor", "expert"),
            P("section", "expert"),
            P("section", "expert", None),
            P("section", "expert", None, "tensor"),
            P("section", "expert", None, "tensor"),
            P("section", "expert", "tensor", None),
        ),
        check_vma=False,
    )
```

time: 3870 us -> 864 us (0.22)
  waiting for transfers between devices: 2300 us -> 355 us
  blocking collectives: 807 us -> 33 us
  matrix products: 317 us -> 141 us
  other arithmetic: 202 us -> 79.7 us
  starting transfers between devices: 41.9 us -> 120 us
  local copies, waits for them, and re-layouts: 165 us -> 110 us
    reduce_scatter x11 -> x0, waiting for transfers between devices: 1170 us -> none  [the longest x6 585 us: slots_home(): lax.psum_scatter(partial_value, 'tensor', scatter_dimension=2, tiled=True)]
    all_to_all x6 -> x0, blocking collectives: 593 us -> none  [slots_away(): lax.all_to_all(buffer, 'expert', split_axis=0, concat_axis=0, tiled=True)]
    all_gather x10 -> x6, waiting for transfers between devices: 572 us -> 129 us  [gather_expert(): return lax.all_gather(shard, 'expert', axis=0, tiled=True)]
    all_to_all x6 -> x2, waiting for transfers between devices: 416 us -> 5.54 us  [spread(): lax.all_to_all(value, 'expert', split_axis=1, concat_axis=0, tiled=True)]
    ppermute x4 -> x94, waiting for transfers between devices: 1.14 us -> 220 us  [the longest x43 142 us: swap_e(): return lax.ppermute(value, 'expert', [(i, i ^ bits) for i in range(count)])]
    dot_general x93 -> x44, matrix products: 317 us -> 137 us  [the longest x12 45.6 us: dot_cols(): lax.dot_general(left, right, (((1,), (1,)), ((), ())), preferred_element_...]
    psum x5 -> x0, waiting for transfers between devices: 139 us -> none  [the longest x3 86.7 us: backward_layer(): lax.psum((d_normed, g_query_gain, g_key_gain), 'tensor')]
    all_gather x3 -> x1, blocking collectives: 152 us -> 33 us  [body(): tiny_all = lax.all_gather(tiny_layers[None], 'expert', axis=0, tiled=True)]
  transfers between devices with their start and end apart: 36 -> 102, of which waited for: 30 -> 52; matrix products, arithmetic and copies ran while one was open for 7% -> 29% of each run, Pallas kernels for 0% -> 0%
where the time goes in v1:
time: 864 us; the launch traced here: 857 us
  waiting for transfers between devices  355 us (41%)
  matrix products  141 us (16%)
  starting transfers between devices  120 us (14%)
  local copies, waits for them, and re-layouts  110 us (13%)
  other arithmetic  79.7 us (9%)
  blocking collectives  33 us (4%)
  between operations  18.4 us (2%)
    ppermute x43, waiting for transfers between devices, swap_e(): return lax.ppermute(value, 'expert', [(i, i ^ bits) for i in range(count)])  142 us
    all_gather x6, waiting for transfers between devices, gather_expert(): return lax.all_gather(shard, 'expert', axis=0, tiled=True)  129 us
    ppermute x43, starting transfers between devices, swap_e(): return lax.ppermute(value, 'expert', [(i, i ^ bits) for i in range(count)])  83.8 us
    ppermute x26, waiting for transfers between devices, swap_x(): return lax.ppermute(value, 'tensor', [(0, 1), (1, 0)])  72.2 us
    dot_general x12, matrix products, dot_cols(): lax.dot_general(left, right, (((1,), (1,)), ((), ())), preferred_element_...  45.6 us
    dot_general x10, matrix products, dot_rows(): lax.dot_general(left, right, (((0,), (0,)), ((), ())), preferred_element_...  44.7 us
    dot_general x12, matrix products, dot(): return jnp.dot(left, right, preferred_element_type=f32)  37.1 us
    all_gather x1, blocking collectives, body(): tiny_all = lax.all_gather(tiny_layers[None], 'expert', axis=0, tiled=True)  33 us
  transfers between devices with their start and end apart: 102, of which 52 were waited for; matrix products, arithmetic and copies ran while one was open for 29% of the time, Pallas kernels for 0%

profile of v1, /device:TPU:0, one launch (start us, length us, event | category | flops | bytes accessed | tf_op | source)
XLA Modules:
  0.0 857.4 jit_solution(2119140393882105230)
XLA Ops:
  14.2 4.8 copy.237
  19.3 4.8 copy.238
  27.2 33.0 %all-gather.1 = bf16[8,2,4640]{2,1,0:T(2,128)(2,1)S(1)} all-gather(bf16[1,2,4640]{2,1,0:T(2,128)(2,1)S(1)} %maximum_bitcast_fusion.6), channel_id=2, replica_groups=mesh['section'=2,'expert'=8,'tensor'=2] {'expert'}, dimensions={0}, use_global_device_ids=true | all-gather | bytes 167040 | tf_op jit(solution)/shard_map/all_gather | solution.py:353
  68.2 34.6 %all-gather.9.cloned.1.call-done = bf16[2048,1280]{1,0:T(8,128)(2,1)} async-done(((bf16[256,1280]{1,0:T(8,128)(2,1)}), bf16[2048,1280]{1,0:T(8,128)(2,1)}) %all-gather.9.cloned.1.call-update) | async-done | bytes 5242896 | tf_op jit(solution)/shard_map/all_gather | solution.py:80
  102.8 3.3 fusion.54
  110.7 68.2 %all-gather.11.cloned.1.call-done = bf16[2048,1024]{0,1:T(8,128)(2,1)} async-done(((bf16[256,1024]{0,1:T(8,128)(2,1)}), bf16[2048,1024]{0,1:T(8,128)(2,1)}) %all-gather.11.cloned.1.call-update) | async-done | bytes 4194320 | tf_op jit(solution)/shard_map/all_gather | solution.py:80
  185.2 3.8 collective-permute-done.15
  195.4 10.6 %collective-permute-done.17 = bf16[32,2176]{1,0:T(8,128)(2,1)S(1)} collective-permute-done((bf16[32,2176]{1,0:T(8,128)(2,1)S(1)}, bf16[32,2176]{1,0:T(8,128)(2,1)S(1)}, u32[]{:S(2)}, u32[]{:S(2)}) %collective-permute-start.17) | collective-permute-done | bytes 139296 | tf_op jit(solution)/shard_map/ppermute | solution.py:39
  206.0 4.9 collective-permute-done.18
  215.0 10.6 %collective-permute-done.20 = bf16[128,2176]{1,0:T(8,128)(2,1)S(1)} collective-permute-done((bf16[128,2176]{1,0:T(8,128)(2,1)S(1)}, bf16[128,2176]{1,0:T(8,128)(2,1)S(1)}, u32[]{:S(2)}, u32[]{:S(2)}) %collective-permute-start.20) | collective-permute-done | bytes 557088 | tf_op jit(solution)/shard_map/ppermute | solution.py:34
  228.3 6.2 collective-permute-done.22
  235.8 4.3 fusion.12
  240.2 3.5 fusion.4
  243.8 3.9 fusion.200
  253.4 10.0 %collective-permute-done.26 = bf16[64,2048]{1,0:T(8,128)(2,1)} collective-permute-done((bf16[64,2048]{1,0:T(8,128)(2,1)}, bf16[64,2048]{1,0:T(8,128)(2,1)}, u32[]{:S(2)}, u32[]{:S(2)}) %collective-permute-start.26) | collective-permute-done | bytes 262176 | tf_op jit(solution)/shard_map/ppermute | solution.py:39
  269.0 12.5 %collective-permute-start.1 = (bf16[32,2048]{1,0:T(8,128)(2,1)S(1)}, bf16[32,2048]{1,0:T(8,128)(2,1)S(1)}, u32[]{:S(2)}, u32[]{:S(2)}) collective-permute-start(bf16[32,2048]{1,0:T(8,128)(2,1)S(1)} %get-tuple-element.56), channel_id=1, source_target_pairs={{0,4},{2,6},{4,0},{6,2},{8,12},{10,14},{12,8},{14,10},{1,5},{3,7},... | collective-permute-start | bytes 393224 | tf_op jit(solution)/shard_map/ppermute | solution.py:39
  291.1 3.9 collective-permute-done.1
  305.4 11.4 %collective-permute-done.31 = bf16[32,2048]{1,0:T(8,128)(2,1)S(1)} collective-permute-done((bf16[32,2048]{1,0:T(8,128)(2,1)S(1)}, bf16[32,2048]{1,0:T(8,128)(2,1)S(1)}, u32[]{:S(2)}, u32[]{:S(2)}) %collective-permute-start.31) | collective-permute-done | bytes 131104 | tf_op jit(solution)/shard_map/ppermute | solution.py:39
  330.2 4.3 fusion.61
  352.1 26.4 %all-gather.15.cloned.1.call-done = bf16[2048,1024]{0,1:T(8,128)(2,1)} async-done(((bf16[256,1024]{0,1:T(8,128)(2,1)}), bf16[2048,1024]{0,1:T(8,128)(2,1)}) %all-gather.15.cloned.1.call-update) | async-done | bytes 4194320 | tf_op jit(solution)/shard_map/all_gather | solution.py:80
  386.7 3.6 collective-permute-done.36
  402.5 6.3 collective-permute-done.38
  411.9 9.4 %collective-permute-done.40 = bf16[128,2176]{1,0:T(8,128)(2,1)S(1)} collective-permute-done((bf16[128,2176]{1,0:T(8,128)(2,1)S(1)}, bf16[128,2176]{1,0:T(8,128)(2,1)S(1)}, u32[]{:S(2)}, u32[]{:S(2)}) %collective-permute-start.40) | collective-permute-done | bytes 557088 | tf_op jit(solution)/shard_map/ppermute | solution.py:34
  424.6 3.6 collective-permute-done.42
  436.8 3.9 fusion.6
  440.8 5.4 broadcast_select_fusion.21
  446.2 7.0 multiply_convert_fusion.4
  463.3 4.0 fusion.27
  467.3 5.7 convolution_add_fusion.4
  473.7 5.9 concatenate.222
  483.3 8.5 collective-permute-done.44
  512.9 3.7 collective-permute-done.48
  516.6 7.1 collective-permute-done.49
  527.7 3.3 collective-permute-done.51
  532.1 3.3 broadcast_select_fusion.7
  552.6 3.8 fusion.203
  567.4 7.6 collective-permute-start.56
  578.0 12.8 %collective-permute-done.56 = bf16[32,2048]{1,0:T(8,128)(2,1)S(1)} collective-permute-done((bf16[32,2048]{1,0:T(8,128)(2,1)S(1)}, bf16[32,2048]{1,0:T(8,128)(2,1)S(1)}, u32[]{:S(2)}, u32[]{:S(2)}) %collective-permute-start.56) | collective-permute-done | bytes 131104 | tf_op jit(solution)/shard_map/ppermute | solution.py:39
  592.2 10.7 %collective-permute-done.58 = bf16[128,2048]{1,0:T(8,128)(2,1)S(1)} collective-permute-done((bf16[128,2048]{1,0:T(8,128)(2,1)S(1)}, bf16[128,2048]{1,0:T(8,128)(2,1)S(1)}, u32[]{:S(2)}, u32[]{:S(2)}) %collective-permute-start.58) | collective-permute-done | bytes 524320 | tf_op jit(solution)/shard_map/ppermute | solution.py:34
  604.4 5.0 collective-permute-done.60
  610.2 4.4 broadcast_select_fusion.23
  623.9 4.0 fusion.26
  627.9 5.7 convolution_add_fusion.3
  633.6 6.3 concatenate.230
  646.3 6.1 collective-permute-done.62
  654.4 9.1 %collective-permute-done.74 = bf16[128,2048]{1,0:T(8,128)(2,1)S(1)} collective-permute-done((bf16[128,2048]{1,0:T(8,128)(2,1)S(1)}, bf16[128,2048]{1,0:T(8,128)(2,1)S(1)}, u32[]{:S(2)}, u32[]{:S(2)}) %collective-permute-start.74) | collective-permute-done | bytes 524320 | tf_op jit(solution)/shard_map/ppermute | solution.py:34
  669.5 3.6 collective-permute-done.65
  675.0 9.9 %collective-permute-start.66 = (bf16[32,2176]{1,0:T(8,128)(2,1)}, bf16[32,2176]{1,0:T(8,128)(2,1)}, u32[]{:S(2)}, u32[]{:S(2)}) collective-permute-start(bf16[32,2176]{1,0:T(8,128)(2,1)} %get-tuple-element.126), channel_id=1, source_target_pairs={{0,4},{2,6},{4,0},{6,2},{8,12},{10,14},{12,8},{14,10},{1,5},{3,7},... | collective-permute-start | bytes 417800 | tf_op jit(solution)/shard_map/ppermute | solution.py:39
  711.0 6.1 fusion.206
  725.4 6.1 fusion.205
  732.7 9.2 %convolution_add_fusion.1 = f32[2048,768]{0,1:T(8,128)} fusion(f32[2048,768]{0,1:T(8,128)} %fusion.206, bf16[512,768]{1,0:T(8,128)(2,1)} %get-tuple-element.72, bf16[512,768]{1,0:T(8,128)(2,1)} %get-tuple-element.74, pred[]{:T(512)S(6)} %eq.132, bf16[512,2176]{1,0:T(8,128)(2,1)} %copy-done.2, bf16[512,2176]{1,0:T(8,128)(2,1)} %copy-done), kind=kOutput, calls=%fused_computation.3 | convolution fusion | flops 1613627392 | bytes 18351104 | tf_op jit(solution)/shard_map/dot_general | solution.py:18
  741.9 4.4 fusion.166
  748.6 4.7 convolution_add_fusion.2
  753.3 6.6 copy.276
  759.9 6.7 copy.275
  769.4 3.8 all-to-all-start.1
  780.3 5.6 collective-permute-done.83
  792.1 4.8 convolution_add_fusion
  796.9 16.9 %collective-permute-done.84 = f32[4,19,256]{2,1,0:T(8,128)S(1)} collective-permute-done((f32[4,19,256]{2,1,0:T(8,128)S(1)}, f32[4,19,256]{2,1,0:T(8,128)S(1)}, u32[]{:S(2)}, u32[]{:S(2)}) %collective-permute-start.84) | collective-permute-done | bytes 77856 | tf_op jit(solution)/shard_map/ppermute | solution.py:39
  813.9 7.2 collective-permute-done.85
  825.1 5.8 all-to-all-start
  832.7 4.8 convolution_bitcast_fusion
  837.5 5.5 all-to-all-done
  843.1 4.0 fusion.204
  (991 shorter events, 302.2 us)
Async XLA Ops:
  7.2 95.6 %all-gather.9.cloned.1.call-start = ((), (), s32[]{:S(2)}) async-start(), calls=%async_computation.2 | async-start | bytes 5898240 | tf_op jit(solution)/shard_map/all_gather | solution.py:80
  12.6 166.2 %all-gather.11.cloned.1.call-start = ((), (), s32[]{:S(2)}) async-start(), calls=%async_computation.3 | async-start | bytes 4718592 | tf_op jit(solution)/shard_map/all_gather | solution.py:80
  12.9 14.2 %collective-permute-start.9 = (bf16[4640]{0:T(1024)(128)(2,1)S(1)}, bf16[4640]{0:T(1024)(128)(2,1)S(1)}, u32[]{:S(2)}, u32[]{:S(2)}) collective-permute-start(bf16[4640]{0:T(1024)(128)(2,1)S(1)} %concatenate.203), channel_id=1, source_target_pairs={{0,16},{16,0},{1,17},{17,1},{2,18},{18,2},{3,19},{19,3},{4,20},{20... | collective-permute-start | bytes 27848 | tf_op jit(solution)/shard_map/ppermute | solution.py:30
  13.4 10.8 %collective-permute-start.13 = (bf16[256,1024]{0,1:T(8,128)(2,1)S(1)}, bf16[256,1024]{0,1:T(8,128)(2,1)S(1)}, u32[]{:S(2)}, u32[]{:S(2)}) collective-permute-start(bf16[256,1024]{0,1:T(8,128)(2,1)S(1)} %broadcast_select_fusion.30), channel_id=1, source_target_pairs={{0,16},{16,0},{1,17},{17,1},{2,18},{18,2},{3,19},{19,3},{4,20},{20... | collective-permute-start | bytes 1572872 | tf_op jit(solution)/shard_map/ppermute | solution.py:30
  13.6 46.9 %collective-permute-start = (bf16[64,2048]{1,0:T(8,128)(2,1)S(1)}, bf16[64,2048]{1,0:T(8,128)(2,1)S(1)}, u32[]{:S(2)}, u32[]{:S(2)}) collective-permute-start(bf16[64,2048]{1,0:T(8,128)(2,1)S(1)} %bitcast_select_fusion.3), channel_id=1, source_target_pairs={{0,16},{16,0},{1,17},{17,1},{2,18},{18,2},{3,19},{19,3},{4,20},{20... | collective-permute-start | bytes 786440 | tf_op jit(solution)/shard_map/ppermute | solution.py:30
  14.1 52.6 %collective-permute-start.16 = (s32[64,8]{0,1:T(8,128)S(1)}, s32[64,8]{0,1:T(8,128)S(1)}, u32[]{:S(2)}, u32[]{:S(2)}) collective-permute-start(s32[64,8]{0,1:T(8,128)S(1)} %bitcast_select_fusion.6), channel_id=1, source_target_pairs={{0,16},{16,0},{1,17},{17,1},{2,18},{18,2},{3,19},{19,3},{4,20},{20... | collective-permute-start | bytes 6152 | tf_op jit(solution)/shard_map/ppermute | solution.py:30
  18.9 216.9 %collective-permute-start.24 = (bf16[2048,768]{0,1:T(8,128)(2,1)}, bf16[2048,768]{0,1:T(8,128)(2,1)}, u32[]{:S(2)}, u32[]{:S(2)}) collective-permute-start(bf16[2048,768]{0,1:T(8,128)(2,1)} %bitcast.35), channel_id=1, source_target_pairs={{0,16},{16,0},{1,17},{17,1},{2,18},{18,2},{3,19},{19,3},{4,20},{20... | collective-permute-start | bytes 9437192 | tf_op jit(solution)/shard_map/ppermute | solution.py:30
  24.1 216.0 %collective-permute-start.25 = (bf16[2048,768]{0,1:T(8,128)(2,1)}, bf16[2048,768]{0,1:T(8,128)(2,1)}, u32[]{:S(2)}, u32[]{:S(2)}) collective-permute-start(bf16[2048,768]{0,1:T(8,128)(2,1)} %bitcast.459), channel_id=1, source_target_pairs={{0,16},{16,0},{1,17},{17,1},{2,18},{18,2},{3,19},{19,3},{4,20},{20... | collective-permute-start | bytes 9437192 | tf_op jit(solution)/shard_map/ppermute | solution.py:30
  25.4 304.8 %all-gather.13.cloned.1.call-start = ((), (), s32[]{:S(2)}) async-start(), calls=%async_computation.4 | async-start | bytes 5898240 | tf_op jit(solution)/shard_map/all_gather | solution.py:80
  67.0 311.5 %all-gather.15.cloned.1.call-start = ((), (), s32[]{:S(2)}) async-start(), calls=%async_computation.5 | async-start | bytes 4718592 | tf_op jit(solution)/shard_map/all_gather | solution.py:80
  190.9 15.0 %collective-permute-start.17 = (bf16[32,2176]{1,0:T(8,128)(2,1)S(1)}, bf16[32,2176]{1,0:T(8,128)(2,1)S(1)}, u32[]{:S(2)}, u32[]{:S(2)}) collective-permute-start(bf16[32,2176]{1,0:T(8,128)(2,1)S(1)} %concatenate.210), channel_id=1, source_target_pairs={{0,4},{2,6},{4,0},{6,2},{8,12},{10,14},{12,8},{14,10},{1,5},{3,7},... | collective-permute-start | bytes 417800 | tf_op jit(solution)/shard_map/ppermute | solution.py:39
  191.0 19.8 %collective-permute-start.18 = (bf16[32,2176]{1,0:T(8,128)(2,1)S(1)}, bf16[32,2176]{1,0:T(8,128)(2,1)S(1)}, u32[]{:S(2)}, u32[]{:S(2)}) collective-permute-start(bf16[32,2176]{1,0:T(8,128)(2,1)S(1)} %concatenate.210), channel_id=1, source_target_pairs={{0,8},{2,10},{4,12},{6,14},{8,0},{10,2},{12,4},{14,6},{1,9},{3,11}... | collective-permute-start | bytes 417800 | tf_op jit(solution)/shard_map/ppermute | solution.py:39
  193.0 19.7 %collective-permute-start.19 = (bf16[32,2176]{1,0:T(8,128)(2,1)S(1)}, bf16[32,2176]{1,0:T(8,128)(2,1)S(1)}, u32[]{:S(2)}, u32[]{:S(2)}) collective-permute-start(bf16[32,2176]{1,0:T(8,128)(2,1)S(1)} %concatenate.210), channel_id=1, source_target_pairs={{0,12},{2,14},{4,8},{6,10},{8,4},{10,6},{12,0},{14,2},{1,13},{3,15... | collective-permute-start | bytes 417800 | tf_op jit(solution)/shard_map/ppermute | solution.py:39
  206.0 37.8 %collective-permute-start.8 = (bf16[768,2048]{1,0:T(8,128)(2,1)}, bf16[768,2048]{1,0:T(8,128)(2,1)}, u32[]{:S(2)}, u32[]{:S(2)}) collective-permute-start(bf16[768,2048]{1,0:T(8,128)(2,1)} %bitcast.434), channel_id=1, source_target_pairs={{0,16},{16,0},{1,17},{17,1},{2,18},{18,2},{3,19},{19,3},{4,20},{20... | collective-permute-start | bytes 9437192 | tf_op jit(solution)/shard_map/ppermute | solution.py:30
  212.8 12.8 %collective-permute-start.20 = (bf16[128,2176]{1,0:T(8,128)(2,1)S(1)}, bf16[128,2176]{1,0:T(8,128)(2,1)S(1)}, u32[]{:S(2)}, u32[]{:S(2)}) collective-permute-start(bf16[128,2176]{1,0:T(8,128)(2,1)S(1)} %pad_maximum_fusion.3), channel_id=1, source_target_pairs={{0,1},{1,0},{2,3},{3,2},{4,5},{5,4},{6,7},{7,6},{8,9},{9,8},{10,11... | collective-permute-start | bytes 1671176 | tf_op jit(solution)/shard_map/ppermute | solution.py:34
  214.3 13.5 %collective-permute-start.21 = (bf16[128,2176]{1,0:T(8,128)(2,1)S(1)}, bf16[128,2176]{1,0:T(8,128)(2,1)S(1)}, u32[]{:S(2)}, u32[]{:S(2)}) collective-permute-start(bf16[128,2176]{1,0:T(8,128)(2,1)S(1)} %pad_maximum_fusion.3), channel_id=1, source_target_pairs={{0,2},{2,0},{4,6},{6,4},{8,10},{10,8},{12,14},{14,12},{1,3},{3,1},... | collective-permute-start | bytes 1671176 | tf_op jit(solution)/shard_map/ppermute | solution.py:39
  248.5 14.9 %collective-permute-start.26 = (bf16[64,2048]{1,0:T(8,128)(2,1)}, bf16[64,2048]{1,0:T(8,128)(2,1)}, u32[]{:S(2)}, u32[]{:S(2)}) collective-permute-start(bf16[64,2048]{1,0:T(8,128)(2,1)} %get-tuple-element.101), channel_id=1, source_target_pairs={{0,2},{2,0},{4,6},{6,4},{8,10},{10,8},{12,14},{14,12},{1,3},{3,1},... | collective-permute-start | bytes 786440 | tf_op jit(solution)/shard_map/ppermute | solution.py:39
  250.6 12.9 %collective-permute-start.28 = (bf16[64,2048]{1,0:T(8,128)(2,1)S(1)}, bf16[64,2048]{1,0:T(8,128)(2,1)}, u32[]{:S(2)}, u32[]{:S(2)}) collective-permute-start(bf16[64,2048]{1,0:T(8,128)(2,1)S(1)} %get-tuple-element.102), channel_id=1, source_target_pairs={{0,1},{1,0},{2,3},{3,2},{4,5},{5,4},{6,7},{7,6},{8,9},{9,8},{10,11... | collective-permute-start | bytes 786440 | tf_op jit(solution)/shard_map/ppermute | solution.py:34
  253.2 579.5 %all-gather.19.cloned.1.call-start = ((), (), s32[]{:S(2)}) async-start(), calls=%async_computation.7 | async-start | bytes 4718592 | tf_op jit(solution)/shard_map/all_gather | solution.py:80
  265.8 31.4 %collective-permute-start.27 = (bf16[128,2048]{1,0:T(8,128)(2,1)}, bf16[128,2048]{1,0:T(8,128)(2,1)}, u32[]{:S(2)}, u32[]{:S(2)}) collective-permute-start(bf16[128,2048]{1,0:T(8,128)(2,1)} %pad_maximum_fusion.10), channel_id=1, source_target_pairs={{0,1},{1,0},{2,3},{3,2},{4,5},{5,4},{6,7},{7,6},{8,9},{9,8},{10,11... | collective-permute-start | bytes 1572872 | tf_op jit(solution)/shard_map/ppermute | solution.py:34
  266.9 30.4 %collective-permute-start.29 = (bf16[128,2048]{1,0:T(8,128)(2,1)}, bf16[128,2048]{1,0:T(8,128)(2,1)}, u32[]{:S(2)}, u32[]{:S(2)}) collective-permute-start(bf16[128,2048]{1,0:T(8,128)(2,1)} %pad_maximum_fusion.11), channel_id=1, source_target_pairs={{0,2},{2,0},{4,6},{6,4},{8,10},{10,8},{12,14},{14,12},{1,3},{3,1},... | collective-permute-start | bytes 1572872 | tf_op jit(solution)/shard_map/ppermute | solution.py:39
  269.0 26.0 %collective-permute-start.1 = (bf16[32,2048]{1,0:T(8,128)(2,1)S(1)}, bf16[32,2048]{1,0:T(8,128)(2,1)S(1)}, u32[]{:S(2)}, u32[]{:S(2)}) collective-permute-start(bf16[32,2048]{1,0:T(8,128)(2,1)S(1)} %get-tuple-element.56), channel_id=1, source_target_pairs={{0,4},{2,6},{4,0},{6,2},{8,12},{10,14},{12,8},{14,10},{1,5},{3,7},... | collective-permute-start | bytes 393224 | tf_op jit(solution)/shard_map/ppermute | solution.py:39
  281.5 13.5 %collective-permute-start.2 = (bf16[32,2048]{1,0:T(8,128)(2,1)S(1)}, bf16[32,2048]{1,0:T(8,128)(2,1)S(1)}, u32[]{:S(2)}, u32[]{:S(2)}) collective-permute-start(bf16[32,2048]{1,0:T(8,128)(2,1)S(1)} %get-tuple-element.56), channel_id=1, source_target_pairs={{0,8},{2,10},{4,12},{6,14},{8,0},{10,2},{12,4},{14,6},{1,9},{3,11}... | collective-permute-start | bytes 393224 | tf_op jit(solution)/shard_map/ppermute | solution.py:39
  282.9 12.1 %collective-permute-start.3 = (bf16[32,2048]{1,0:T(8,128)(2,1)S(1)}, bf16[32,2048]{1,0:T(8,128)(2,1)S(1)}, u32[]{:S(2)}, u32[]{:S(2)}) collective-permute-start(bf16[32,2048]{1,0:T(8,128)(2,1)S(1)} %get-tuple-element.56), channel_id=1, source_target_pairs={{0,12},{2,14},{4,8},{6,10},{8,4},{10,6},{12,0},{14,2},{1,13},{3,15... | collective-permute-start | bytes 393224 | tf_op jit(solution)/shard_map/ppermute | solution.py:39
  295.0 29.3 %collective-permute-start.4 = (bf16[128,2048]{1,0:T(8,128)(2,1)S(1)}, bf16[128,2048]{1,0:T(8,128)(2,1)S(1)}, u32[]{:S(2)}, u32[]{:S(2)}) collective-permute-start(bf16[128,2048]{1,0:T(8,128)(2,1)S(1)} %pad_maximum_fusion.9), channel_id=1, source_target_pairs={{0,1},{1,0},{2,3},{3,2},{4,5},{5,4},{6,7},{7,6},{8,9},{9,8},{10,11... | collective-permute-start | bytes 1572872 | tf_op jit(solution)/shard_map/ppermute | solution.py:34
  295.6 30.7 %collective-permute-start.5 = (bf16[128,2048]{1,0:T(8,128)(2,1)S(1)}, bf16[128,2048]{1,0:T(8,128)(2,1)S(1)}, u32[]{:S(2)}, u32[]{:S(2)}) collective-permute-start(bf16[128,2048]{1,0:T(8,128)(2,1)S(1)} %pad_maximum_fusion.9), channel_id=1, source_target_pairs={{0,2},{2,0},{4,6},{6,4},{8,10},{10,8},{12,14},{14,12},{1,3},{3,1},... | collective-permute-start | bytes 1572872 | tf_op jit(solution)/shard_map/ppermute | solution.py:39
  300.9 16.0 %collective-permute-start.31 = (bf16[32,2048]{1,0:T(8,128)(2,1)S(1)}, bf16[32,2048]{1,0:T(8,128)(2,1)S(1)}, u32[]{:S(2)}, u32[]{:S(2)}) collective-permute-start(bf16[32,2048]{1,0:T(8,128)(2,1)S(1)} %get-tuple-element.139), channel_id=1, source_target_pairs={{0,8},{2,10},{4,12},{6,14},{8,0},{10,2},{12,4},{14,6},{1,9},{3,11}... | collective-permute-start | bytes 393224 | tf_op jit(solution)/shard_map/ppermute | solution.py:39
  301.8 15.1 %collective-permute-start.32 = (bf16[32,2048]{1,0:T(8,128)(2,1)S(1)}, bf16[32,2048]{1,0:T(8,128)(2,1)S(1)}, u32[]{:S(2)}, u32[]{:S(2)}) collective-permute-start(bf16[32,2048]{1,0:T(8,128)(2,1)S(1)} %get-tuple-element.138), channel_id=1, source_target_pairs={{0,12},{2,14},{4,8},{6,10},{8,4},{10,6},{12,0},{14,2},{1,13},{3,15... | collective-permute-start | bytes 393224 | tf_op jit(solution)/shard_map/ppermute | solution.py:39
  325.1 57.5 %collective-permute-start.6 = (bf16[64,2048]{1,0:T(8,128)(2,1)}, bf16[64,2048]{1,0:T(8,128)(2,1)}, u32[]{:S(2)}, u32[]{:S(2)}) collective-permute-start(bf16[64,2048]{1,0:T(8,128)(2,1)} %slice.710), channel_id=1, source_target_pairs={{0,2},{2,0},{4,6},{6,4},{8,10},{10,8},{12,14},{14,12},{1,3},{3,1},... | collective-permute-start | bytes 786440 | tf_op jit(solution)/shard_map/ppermute | solution.py:39
  327.8 57.2 %collective-permute-start.7 = (bf16[64,2048]{1,0:T(8,128)(2,1)}, bf16[64,2048]{1,0:T(8,128)(2,1)}, u32[]{:S(2)}, u32[]{:S(2)}) collective-permute-start(bf16[64,2048]{1,0:T(8,128)(2,1)} %slice.711), channel_id=1, source_target_pairs={{0,1},{1,0},{2,3},{3,2},{4,5},{5,4},{6,7},{7,6},{8,9},{9,8},{10,11... | collective-permute-start | bytes 786440 | tf_op jit(solution)/shard_map/ppermute | solution.py:34
  395.1 13.6 %collective-permute-start.38 = (bf16[32,2176]{1,0:T(8,128)(2,1)}, bf16[32,2176]{1,0:T(8,128)(2,1)S(1)}, u32[]{:S(2)}, u32[]{:S(2)}) collective-permute-start(bf16[32,2176]{1,0:T(8,128)(2,1)} %concatenate.219), channel_id=1, source_target_pairs={{0,8},{2,10},{4,12},{6,14},{8,0},{10,2},{12,4},{14,6},{1,9},{3,11}... | collective-permute-start | bytes 417800 | tf_op jit(solution)/shard_map/ppermute | solution.py:39
  397.2 11.6 %collective-permute-start.39 = (bf16[32,2176]{1,0:T(8,128)(2,1)}, bf16[32,2176]{1,0:T(8,128)(2,1)S(1)}, u32[]{:S(2)}, u32[]{:S(2)}) collective-permute-start(bf16[32,2176]{1,0:T(8,128)(2,1)} %concatenate.219), channel_id=1, source_target_pairs={{0,12},{2,14},{4,8},{6,10},{8,4},{10,6},{12,0},{14,2},{1,13},{3,15... | collective-permute-start | bytes 417800 | tf_op jit(solution)/shard_map/ppermute | solution.py:39
  409.7 11.5 %collective-permute-start.40 = (bf16[128,2176]{1,0:T(8,128)(2,1)S(1)}, bf16[128,2176]{1,0:T(8,128)(2,1)S(1)}, u32[]{:S(2)}, u32[]{:S(2)}) collective-permute-start(bf16[128,2176]{1,0:T(8,128)(2,1)S(1)} %pad_maximum_fusion.4), channel_id=1, source_target_pairs={{0,1},{1,0},{2,3},{3,2},{4,5},{5,4},{6,7},{7,6},{8,9},{9,8},{10,11... | collective-permute-start | bytes 1671176 | tf_op jit(solution)/shard_map/ppermute | solution.py:34
  410.4 14.0 %collective-permute-start.41 = (bf16[128,2176]{1,0:T(8,128)(2,1)S(1)}, bf16[128,2176]{1,0:T(8,128)(2,1)S(1)}, u32[]{:S(2)}, u32[]{:S(2)}) collective-permute-start(bf16[128,2176]{1,0:T(8,128)(2,1)S(1)} %pad_maximum_fusion.4), channel_id=1, source_target_pairs={{0,2},{2,0},{4,6},{6,4},{8,10},{10,8},{12,14},{14,12},{1,3},{3,1},... | collective-permute-start | bytes 1671176 | tf_op jit(solution)/shard_map/ppermute | solution.py:39
  495.1 10.2 %collective-permute-start.45 = (bf16[128,2176]{1,0:T(8,128)(2,1)}, bf16[128,2176]{1,0:T(8,128)(2,1)}, u32[]{:S(2)}, u32[]{:S(2)}) collective-permute-start(bf16[128,2176]{1,0:T(8,128)(2,1)} %pad_maximum_fusion.5), channel_id=1, source_target_pairs={{0,1},{1,0},{2,3},{3,2},{4,5},{5,4},{6,7},{7,6},{8,9},{9,8},{10,11... | collective-permute-start | bytes 1671176 | tf_op jit(solution)/shard_map/ppermute | solution.py:34
  495.9 9.8 %collective-permute-start.47 = (bf16[128,2176]{1,0:T(8,128)(2,1)}, bf16[128,2176]{1,0:T(8,128)(2,1)}, u32[]{:S(2)}, u32[]{:S(2)}) collective-permute-start(bf16[128,2176]{1,0:T(8,128)(2,1)} %pad_maximum_fusion.6), channel_id=1, source_target_pairs={{0,2},{2,0},{4,6},{6,4},{8,10},{10,8},{12,14},{14,12},{1,3},{3,1},... | collective-permute-start | bytes 1671176 | tf_op jit(solution)/shard_map/ppermute | solution.py:39
  510.2 13.4 %collective-permute-start.49 = (bf16[32,2176]{1,0:T(8,128)(2,1)S(1)}, bf16[32,2176]{1,0:T(8,128)(2,1)S(1)}, u32[]{:S(2)}, u32[]{:S(2)}) collective-permute-start(bf16[32,2176]{1,0:T(8,128)(2,1)S(1)} %get-tuple-element.131), channel_id=1, source_target_pairs={{0,8},{2,10},{4,12},{6,14},{8,0},{10,2},{12,4},{14,6},{1,9},{3,11}... | collective-permute-start | bytes 417800 | tf_op jit(solution)/shard_map/ppermute | solution.py:39
  511.4 12.3 %collective-permute-start.50 = (bf16[32,2176]{1,0:T(8,128)(2,1)S(1)}, bf16[32,2176]{1,0:T(8,128)(2,1)S(1)}, u32[]{:S(2)}, u32[]{:S(2)}) collective-permute-start(bf16[32,2176]{1,0:T(8,128)(2,1)S(1)} %get-tuple-element.130), channel_id=1, source_target_pairs={{0,12},{2,14},{4,8},{6,10},{8,4},{10,6},{12,0},{14,2},{1,13},{3,15... | collective-permute-start | bytes 417800 | tf_op jit(solution)/shard_map/ppermute | solution.py:39
  527.4 315.6 %all-gather.17.cloned.1.call-start = ((), (), s32[]{:S(2)}) async-start(), calls=%async_computation.6 | async-start | bytes 5898240 | tf_op jit(solution)/shard_map/all_gather | solution.py:80
  535.3 253.7 %collective-permute-start.92 = (bf16[512,768]{1,0:T(8,128)(2,1)}, bf16[512,768]{1,0:T(8,128)(2,1)}, u32[]{:S(2)}, u32[]{:S(2)}) collective-permute-start(bf16[512,768]{1,0:T(8,128)(2,1)} %get-tuple-element.39), channel_id=1, source_target_pairs={{0,16},{16,0},{1,17},{17,1},{2,18},{18,2},{3,19},{19,3},{4,20},{20... | collective-permute-start | bytes 2359304 | tf_op jit(solution)/shard_map/ppermute | solution.py:30
  535.7 172.9 %collective-permute-start.89 = (bf16[512,2048]{1,0:T(8,128)(2,1)}, bf16[512,2048]{1,0:T(8,128)(2,1)}, u32[]{:S(2)}, u32[]{:S(2)}) collective-permute-start(bf16[512,2048]{1,0:T(8,128)(2,1)} %broadcast_select_fusion.7), channel_id=1, source_target_pairs={{0,16},{16,0},{1,17},{17,1},{2,18},{18,2},{3,19},{19,3},{4,20},{20... | collective-permute-start | bytes 6291464 | tf_op jit(solution)/shard_map/ppermute | solution.py:30
  559.5 15.5 %collective-permute-start.75 = (bf16[64,2048]{1,0:T(8,128)(2,1)S(1)}, bf16[64,2048]{1,0:T(8,128)(2,1)S(1)}, u32[]{:S(2)}, u32[]{:S(2)}) collective-permute-start(bf16[64,2048]{1,0:T(8,128)(2,1)S(1)} %get-tuple-element.98), channel_id=1, source_target_pairs={{0,1},{1,0},{2,3},{3,2},{4,5},{5,4},{6,7},{7,6},{8,9},{9,8},{10,11... | collective-permute-start | bytes 786440 | tf_op jit(solution)/shard_map/ppermute | solution.py:34
  564.0 14.0 %collective-permute-start.55 = (bf16[32,2048]{1,0:T(8,128)(2,1)S(1)}, bf16[32,2048]{1,0:T(8,128)(2,1)S(1)}, u32[]{:S(2)}, u32[]{:S(2)}) collective-permute-start(bf16[32,2048]{1,0:T(8,128)(2,1)S(1)} %get-tuple-element.52), channel_id=1, source_target_pairs={{0,4},{2,6},{4,0},{6,2},{8,12},{10,14},{12,8},{14,10},{1,5},{3,7},... | collective-permute-start | bytes 393224 | tf_op jit(solution)/shard_map/ppermute | solution.py:39
  567.4 23.3 %collective-permute-start.56 = (bf16[32,2048]{1,0:T(8,128)(2,1)S(1)}, bf16[32,2048]{1,0:T(8,128)(2,1)S(1)}, u32[]{:S(2)}, u32[]{:S(2)}) collective-permute-start(bf16[32,2048]{1,0:T(8,128)(2,1)S(1)} %get-tuple-element.52), channel_id=1, source_target_pairs={{0,8},{2,10},{4,12},{6,14},{8,0},{10,2},{12,4},{14,6},{1,9},{3,11}... | collective-permute-start | bytes 393224 | tf_op jit(solution)/shard_map/ppermute | solution.py:39
  575.1 15.7 %collective-permute-start.57 = (bf16[32,2048]{1,0:T(8,128)(2,1)S(1)}, bf16[32,2048]{1,0:T(8,128)(2,1)S(1)}, u32[]{:S(2)}, u32[]{:S(2)}) collective-permute-start(bf16[32,2048]{1,0:T(8,128)(2,1)S(1)} %get-tuple-element.52), channel_id=1, source_target_pairs={{0,12},{2,14},{4,8},{6,10},{8,4},{10,6},{12,0},{14,2},{1,13},{3,15... | collective-permute-start | bytes 393224 | tf_op jit(solution)/shard_map/ppermute | solution.py:39
  590.8 12.1 %collective-permute-start.58 = (bf16[128,2048]{1,0:T(8,128)(2,1)S(1)}, bf16[128,2048]{1,0:T(8,128)(2,1)S(1)}, u32[]{:S(2)}, u32[]{:S(2)}) collective-permute-start(bf16[128,2048]{1,0:T(8,128)(2,1)S(1)} %pad_maximum_fusion.12), channel_id=1, source_target_pairs={{0,1},{1,0},{2,3},{3,2},{4,5},{5,4},{6,7},{7,6},{8,9},{9,8},{10,11... | collective-permute-start | bytes 1572872 | tf_op jit(solution)/shard_map/ppermute | solution.py:34
  591.4 12.3 %collective-permute-start.59 = (bf16[128,2048]{1,0:T(8,128)(2,1)S(1)}, bf16[128,2048]{1,0:T(8,128)(2,1)S(1)}, u32[]{:S(2)}, u32[]{:S(2)}) collective-permute-start(bf16[128,2048]{1,0:T(8,128)(2,1)S(1)} %pad_maximum_fusion.12), channel_id=1, source_target_pairs={{0,2},{2,0},{4,6},{6,4},{8,10},{10,8},{12,14},{14,12},{1,3},{3,1},... | collective-permute-start | bytes 1572872 | tf_op jit(solution)/shard_map/ppermute | solution.py:39
  642.7 9.6 %collective-permute-start.62 = (bf16[64,2176]{1,0:T(8,128)(2,1)S(1)}, bf16[64,2176]{1,0:T(8,128)(2,1)S(1)}, u32[]{:S(2)}, u32[]{:S(2)}) collective-permute-start(bf16[64,2176]{1,0:T(8,128)(2,1)S(1)} %get-tuple-element.89), channel_id=1, source_target_pairs={{0,2},{2,0},{4,6},{6,4},{8,10},{10,8},{12,14},{14,12},{1,3},{3,1},... | collective-permute-start | bytes 835592 | tf_op jit(solution)/shard_map/ppermute | solution.py:39
  644.6 18.9 %collective-permute-start.74 = (bf16[128,2048]{1,0:T(8,128)(2,1)S(1)}, bf16[128,2048]{1,0:T(8,128)(2,1)S(1)}, u32[]{:S(2)}, u32[]{:S(2)}) collective-permute-start(bf16[128,2048]{1,0:T(8,128)(2,1)S(1)} %pad_maximum_fusion.13), channel_id=1, source_target_pairs={{0,1},{1,0},{2,3},{3,2},{4,5},{5,4},{6,7},{7,6},{8,9},{9,8},{10,11... | collective-permute-start | bytes 1572872 | tf_op jit(solution)/shard_map/ppermute | solution.py:34
  652.3 12.8 %collective-permute-start.76 = (bf16[128,2048]{1,0:T(8,128)(2,1)S(1)}, bf16[128,2048]{1,0:T(8,128)(2,1)S(1)}, u32[]{:S(2)}, u32[]{:S(2)}) collective-permute-start(bf16[128,2048]{1,0:T(8,128)(2,1)S(1)} %pad_maximum_fusion.14), channel_id=1, source_target_pairs={{0,2},{2,0},{4,6},{6,4},{8,10},{10,8},{12,14},{14,12},{1,3},{3,1},... | collective-permute-start | bytes 1572872 | tf_op jit(solution)/shard_map/ppermute | solution.py:39
  653.8 15.7 %collective-permute-start.63 = (bf16[128,2176]{1,0:T(8,128)(2,1)S(1)}, bf16[128,2176]{1,0:T(8,128)(2,1)S(1)}, u32[]{:S(2)}, u32[]{:S(2)}) collective-permute-start(bf16[128,2176]{1,0:T(8,128)(2,1)S(1)} %pad_maximum_fusion.7), channel_id=1, source_target_pairs={{0,1},{1,0},{2,3},{3,2},{4,5},{5,4},{6,7},{7,6},{8,9},{9,8},{10,11... | collective-permute-start | bytes 1671176 | tf_op jit(solution)/shard_map/ppermute | solution.py:34
  675.0 19.9 %collective-permute-start.66 = (bf16[32,2176]{1,0:T(8,128)(2,1)}, bf16[32,2176]{1,0:T(8,128)(2,1)}, u32[]{:S(2)}, u32[]{:S(2)}) collective-permute-start(bf16[32,2176]{1,0:T(8,128)(2,1)} %get-tuple-element.126), channel_id=1, source_target_pairs={{0,4},{2,6},{4,0},{6,2},{8,12},{10,14},{12,8},{14,10},{1,5},{3,7},... | collective-permute-start | bytes 417800 | tf_op jit(solution)/shard_map/ppermute | solution.py:39
  684.9 11.2 %collective-permute-start.67 = (bf16[32,2176]{1,0:T(8,128)(2,1)}, bf16[32,2176]{1,0:T(8,128)(2,1)}, u32[]{:S(2)}, u32[]{:S(2)}) collective-permute-start(bf16[32,2176]{1,0:T(8,128)(2,1)} %get-tuple-element.128), channel_id=1, source_target_pairs={{0,8},{2,10},{4,12},{6,14},{8,0},{10,2},{12,4},{14,6},{1,9},{3,11}... | collective-permute-start | bytes 417800 | tf_op jit(solution)/shard_map/ppermute | solution.py:39
  684.9 11.2 %collective-permute-start.68 = (bf16[32,2176]{1,0:T(8,128)(2,1)}, bf16[32,2176]{1,0:T(8,128)(2,1)}, u32[]{:S(2)}, u32[]{:S(2)}) collective-permute-start(bf16[32,2176]{1,0:T(8,128)(2,1)} %get-tuple-element.127), channel_id=1, source_target_pairs={{0,12},{2,14},{4,8},{6,10},{8,4},{10,6},{12,0},{14,2},{1,13},{3,15... | collective-permute-start | bytes 417800 | tf_op jit(solution)/shard_map/ppermute | solution.py:39
  694.9 78.8 %collective-permute-start.77 = (bf16[32,2048]{1,0:T(8,128)(2,1)}, bf16[32,2048]{1,0:T(8,128)(2,1)}, u32[]{:S(2)}, u32[]{:S(2)}) collective-permute-start(bf16[32,2048]{1,0:T(8,128)(2,1)} %get-tuple-element.134), channel_id=1, source_target_pairs={{0,4},{2,6},{4,0},{6,2},{8,12},{10,14},{12,8},{14,10},{1,5},{3,7},... | collective-permute-start | bytes 393224 | tf_op jit(solution)/shard_map/ppermute | solution.py:39
  696.1 15.0 %collective-permute-start.91 = (bf16[512,768]{1,0:T(8,128)(2,1)}, bf16[512,768]{1,0:T(8,128)(2,1)S(1)}, u32[]{:S(2)}, u32[]{:S(2)}) collective-permute-start(bf16[512,768]{1,0:T(8,128)(2,1)} %get-tuple-element.71), channel_id=1, source_target_pairs={{0,16},{16,0},{1,17},{17,1},{2,18},{18,2},{3,19},{19,3},{4,20},{20... | collective-permute-start | bytes 2359304 | tf_op jit(solution)/shard_map/ppermute | solution.py:30
  707.7 66.0 %collective-permute-start.78 = (bf16[32,2048]{1,0:T(8,128)(2,1)}, bf16[32,2048]{1,0:T(8,128)(2,1)}, u32[]{:S(2)}, u32[]{:S(2)}) collective-permute-start(bf16[32,2048]{1,0:T(8,128)(2,1)} %get-tuple-element.136), channel_id=1, source_target_pairs={{0,8},{2,10},{4,12},{6,14},{8,0},{10,2},{12,4},{14,6},{1,9},{3,11}... | collective-permute-start | bytes 393224 | tf_op jit(solution)/shard_map/ppermute | solution.py:39
  708.6 65.1 %collective-permute-start.79 = (bf16[32,2048]{1,0:T(8,128)(2,1)}, bf16[32,2048]{1,0:T(8,128)(2,1)}, u32[]{:S(2)}, u32[]{:S(2)}) collective-permute-start(bf16[32,2048]{1,0:T(8,128)(2,1)} %get-tuple-element.135), channel_id=1, source_target_pairs={{0,12},{2,14},{4,8},{6,10},{8,4},{10,6},{12,0},{14,2},{1,13},{3,15... | collective-permute-start | bytes 393224 | tf_op jit(solution)/shard_map/ppermute | solution.py:39
  748.1 18.5 %collective-permute-start.71 = (bf16[64,2048]{1,0:T(8,128)(2,1)}, bf16[64,2048]{1,0:T(8,128)(2,1)S(1)}, u32[]{:S(2)}, u32[]{:S(2)}) collective-permute-start(bf16[64,2048]{1,0:T(8,128)(2,1)} %slice.1074), channel_id=1, source_target_pairs={{0,16},{16,0},{1,17},{17,1},{2,18},{18,2},{3,19},{19,3},{4,20},{20... | collective-permute-start | bytes 786440 | tf_op jit(solution)/shard_map/ppermute | solution.py:30
  769.4 55.7 %all-to-all-start.1 = ((bf16[128,8,256]{2,0,1:T(8,128)(2,1)}), bf16[128,8,256]{2,0,1:T(8,128)(2,1)S(1)}, u32[]{:S(2)}, u32[]{:S(2)}) async-start(bf16[128,8,256]{2,0,1:T(8,128)(2,1)} %maximum_select_fusion.1), calls=%async_computation.1 | async-start | bytes 1048576 | tf_op jit(solution)/shard_map/all_to_all | solution.py:431
  773.4 15.6 %collective-permute-start.93 = (bf16[512,2048]{1,0:T(8,128)(2,1)}, bf16[512,2048]{1,0:T(8,128)(2,1)S(1)}, u32[]{:S(2)}, u32[]{:S(2)}) collective-permute-start(bf16[512,2048]{1,0:T(8,128)(2,1)} %broadcast_select_fusion.6), channel_id=1, source_target_pairs={{0,16},{16,0},{1,17},{17,1},{2,18},{18,2},{3,19},{19,3},{4,20},{20... | collective-permute-start | bytes 6291464 | tf_op jit(solution)/shard_map/ppermute | solution.py:30
  779.6 34.3 %collective-permute-start.81 = (bf16[2,32,2048]{2,1,0:T(8,128)(2,1)S(1)}, bf16[2,32,2048]{2,1,0:T(8,128)(2,1)S(1)}, u32[]{:S(2)}, u32[]{:S(2)}) collective-permute-start(bf16[2,32,2048]{2,1,0:T(8,128)(2,1)S(1)} %pad_maximum_fusion.23), channel_id=1, source_target_pairs={{0,1},{1,0},{2,3},{3,2},{4,5},{5,4},{6,7},{7,6},{8,9},{9,8},{10,11... | collective-permute-start | bytes 786440 | tf_op jit(solution)/shard_map/ppermute | solution.py:34
  786.1 27.7 %collective-permute-start.84 = (f32[4,19,256]{2,1,0:T(8,128)S(1)}, f32[4,19,256]{2,1,0:T(8,128)S(1)}, u32[]{:S(2)}, u32[]{:S(2)}) collective-permute-start(f32[4,19,256]{2,1,0:T(8,128)S(1)} %slice_select_fusion.2), channel_id=1, source_target_pairs={{0,8},{2,10},{4,12},{6,14},{8,0},{10,2},{12,4},{14,6},{1,9},{3,11}... | collective-permute-start | bytes 233480 | tf_op jit(solution)/shard_map/ppermute | solution.py:39
  825.1 17.9 %all-to-all-start = ((bf16[128,8,256]{2,0,1:T(8,128)(2,1)}), bf16[128,8,256]{2,0,1:T(8,128)(2,1)S(1)}, u32[]{:S(2)}, u32[]{:S(2)}) async-start(bf16[128,8,256]{2,0,1:T(8,128)(2,1)} %maximum_select_fusion), calls=%async_computation | async-start | bytes 1048576 | tf_op jit(solution)/shard_map/all_to_all | solution.py:431
  (282 other events, 3236.4 us)
Sparse Core Ops, SparseCore 0:
  12.8 90.0 all-gather.8
  105.5 73.3 all-gather.10
  181.6 112.9 all-gather.12
  297.1 81.3 all-gather.14
  527.5 82.3 all-gather.18
  732.8 97.2 all-gather.16

commit v2 on v1

v2 whole, which is shorter than its diff:
```python
import functools

import jax
import jax.numpy as jnp
import numpy as np
from jax import lax
from jax.experimental import pallas as pl
from jax.experimental.pallas import tpu as pltpu
from jax.sharding import PartitionSpec as P

epsilon = 1e-06
rope_base = 1000000.0
masked_score = -1e30
bf16 = jnp.bfloat16
f32 = jnp.float32
lanes = 128
tile_rows = 512


def dot(left, right):
    return jnp.dot(left, right, preferred_element_type=f32)


def dot_rows(left, right):
    return lax.dot_general(left, right, (((0,), (0,)), ((), ())), preferred_element_type=f32)


def dot_cols(left, right):
    return lax.dot_general(left, right, (((1,), (1,)), ((), ())), preferred_element_type=f32)


def cat(*pieces, axis=0):
    return jnp.concatenate(pieces, axis=axis)


def swap_core(value):
    return lax.ppermute(value, "section", [(0, 1), (1, 0)])


def swap_x(value):
    return lax.ppermute(value, "tensor", [(0, 1), (1, 0)])


def swap_e(value, bits):
    count = lax.axis_size("expert")
    return lax.ppermute(value, "expert", [(i, i ^ bits) for i in range(count)])


def small_grid():
    return lax.axis_size("expert") == 8


def after(value, *others):
    return lax.optimization_barrier((value, *others))[0] if others else value


anywhere = pl.BlockSpec(memory_space=pl.ANY)


def full(one):
    return pl.BlockSpec(one.shape, lambda *_: (0,) * len(one.shape))


def array(shape, kind):
    return jax.ShapeDtypeStruct(shape, kind)


def kernel_params(megabytes):
    return pltpu.CompilerParams(vmem_limit_bytes=megabytes * 2**20)


def cost(flops, moved):
    return pl.CostEstimate(flops=flops, bytes_accessed=moved, transcendentals=0)


def simple(kernel, shapes, *operands):
    return pl.pallas_call(
        kernel,
        in_specs=[full(one) for one in operands],
        out_specs=tuple(full(one) for one in shapes),
        out_shape=tuple(shapes),
        compiler_params=kernel_params(16),
        cost_estimate=cost(1000, 1000),
    )(*operands)


def stack_kernel(*refs):
    start = 0
    for ref in refs[:-1]:
        refs[-1][start : start + ref.shape[0]] = ref[...]
        start += ref.shape[0]


def stack(*pieces):
    rows = sum(one.shape[0] for one in pieces)
    return simple(stack_kernel, [array((rows, pieces[0].shape[1]), pieces[0].dtype)], *pieces)[0]


def near_kernel(to_x, top, to_y, bottom, out_x, out_y):
    half = top.shape[0]
    out_x[:half] = (to_x[:half].astype(f32) + top[...].astype(f32)).astype(bf16)
    out_x[half:] = to_x[half:]
    out_y[:half] = to_y[:half]
    out_y[half:] = (to_y[half:].astype(f32) + bottom[...].astype(f32)).astype(bf16)


def total_kernel(own, from_x, from_y, kept, *blocks):
    total = own[...].astype(f32) + from_x[...].astype(f32) + from_y[...].astype(f32)
    step = kept.shape[0]
    kept[...] = total[:step]
    for number, block in enumerate(blocks):
        block[...] = total[(number + 1) * step : (number + 2) * step].astype(bf16)


class Gather:
    def __init__(self, shard):
        self.shard = shard
        self.small = small_grid()

    def along_z(self, *gate):
        if self.small:
            shard = after(self.shard, *gate)
            self.line = (shard, swap_e(shard, 2), swap_e(shard, 4), swap_e(shard, 6))
            return self.line[1:]
        return ()

    def near(self, *gate):
        if self.small:
            own = after(stack(*self.line), *gate)
            self.near_pieces = (own, swap_x(own), swap_e(own, 1))
            return self.near_pieces[1:]
        return ()

    def far(self, *gate):
        if self.small:
            own, from_x, from_y = self.near_pieces
            half = own.shape[0] // 2
            self.far_pieces = (
                swap_e(after(from_x[:half], *gate), 1),
                swap_x(after(from_y[half:], *gate)),
            )
            return self.far_pieces
        shard = after(self.shard, *gate)
        self.whole = lax.all_gather(shard, ("expert", "tensor"), axis=0, tiled=True)
        return (self.whole,)

    def tiles(self, *gate):
        if self.small:
            top, bottom = self.far_pieces
            return [[*self.near_pieces, top, after(bottom, *gate)]]
        whole = after(self.whole, *gate)
        return [[whole]] * (whole.shape[0] // tile_rows)


class Scatter:
    def __init__(self, tiles):
        self.tiles = tiles
        self.small = small_grid()

    def far(self, *gate):
        if self.small:
            far_top, far_bottom = self.tiles[0][3:]
            self.top = swap_e(after(far_top, *gate), 1)
            self.bottom = swap_x(after(far_bottom, *gate))
            return (self.top, self.bottom)
        return ()

    def near(self, *gate, beside=()):
        if self.small:
            own, to_x, to_y = self.tiles[0][:3]
            shape = array(to_x.shape, bf16)
            to_x, to_y = simple(near_kernel, [shape] * 2, to_x, self.top, to_y, self.bottom)
            from_x, from_y = swap_x(after(to_x, *gate)), swap_e(after(to_y, *gate), 1)
            from_x = after(from_x, *beside)
            rows, columns = own.shape
            shapes = [array((rows // 4, columns), kind) for kind in (f32, bf16, bf16, bf16)]
            self.blocks = simple(total_kernel, shapes, own, from_x, from_y)
            return self.blocks[:1]
        return ()

    def along_z(self, *gate):
        if self.small:
            kept, *blocks = self.blocks
            moved = [swap_e(after(one, *gate), bits) for one, bits in zip(blocks, (2, 4, 6))]
            return [kept, *moved]
        whole = cat(*[one for pieces in self.tiles for one in pieces])
        whole = after(whole, *gate).astype(f32)
        return [lax.psum_scatter(whole, ("expert", "tensor"), scatter_dimension=0, tiled=True)]


cycle = (0, 2, 4, 6, 7, 5, 3, 1)


def owner_at(distance):
    index = lax.axis_index("expert")
    place = jnp.where(index % 2 == 0, index // 2, 7 - index // 2)
    spot = (place + distance) & 7
    return jnp.where(spot < 4, 2 * spot, 15 - 2 * spot)


class Ring:
    def __init__(self, shard):
        self.shard = shard
        self.rows = shard.shape[0]
        self.plus = self.minus = shard
        self.pieces = [shard]
        self.plan = [(0, 0)]
        self.latest = (shard,)
        self.small = small_grid()

    def advance(self, *gate):
        if not self.small:
            if len(self.latest) == 1 and self.latest[0] is self.shard:
                whole = lax.all_gather(after(self.shard, *gate), "expert", axis=0, tiled=True)
                self.pieces, self.plan, self.latest = [whole], [(None, 0)], (whole,)
            return self.latest
        number = len(self.pieces) // 2 + 1
        up = [(a, b) for a, b in zip(cycle, cycle[1:] + cycle[:1])]
        down = [(b, a) for a, b in up]
        plus, minus, middle = self.plus, self.minus, 0
        if number == 4:
            middle = self.rows // 32 * 16
            plus, minus = plus[:middle], minus[middle:]
        self.plus = lax.ppermute(after(plus, *gate), "expert", up)
        self.minus = lax.ppermute(after(minus, *gate), "expert", down)
        self.pieces += [self.plus, self.minus]
        self.plan += [(-number, 0), (number, middle)]
        self.latest = (self.plus, self.minus)
        return self.latest

    def collect(self, part):
        if not self.small:
            return part(self.pieces[0])
        columns = part(self.shard).shape[1]
        whole = jnp.zeros((8 * self.rows, columns), self.shard.dtype)
        for (distance, start), piece in zip(self.plan, self.pieces):
            place = (owner_at(distance) * self.rows + start, 0)
            whole = lax.dynamic_update_slice(whole, part(piece), place)
        return whole


def copy_pieces(pieces, plan, rows, columns, target, sems, first=0):
    copies = []
    for number, ((distance, start), piece) in enumerate(zip(plan, pieces)):
        place = start
        if distance is not None:
            place = pl.multiple_of(owner_at(distance) * rows + start, 16)
        copies.append(
            pltpu.make_async_copy(
                piece.at[:, columns],
                target.at[pl.ds(place, piece.shape[0]), columns],
                sems.at[first + number],
            )
        )
    return copies


def start_all(copies):
    for one in copies:
        one.start()


def wait_all(copies):
    for one in copies:
        one.wait()


def inverse_rms(value):
    return lax.rsqrt(jnp.mean(value * value, axis=-1, keepdims=True) + epsilon)


def rms_norm(value, gain):
    return value * inverse_rms(value) * gain


def layout(lengths_row, row_index):
    ends = jnp.cumsum(lengths_row, dtype=jnp.int32)
    starts = ends - lengths_row
    segment = jnp.sum((row_index[:, None] >= ends[None, :]).astype(jnp.int32), axis=1)
    member = segment[:, None] == jnp.arange(ends.shape[0], dtype=jnp.int32)[None, :]
    return segment, row_index - jnp.sum(jnp.where(member, starts[None, :], 0), axis=1)


def make_tables(length_pair, row_index, head):
    half = head // 2
    inverse = np.power(rope_base, -(np.arange(half) * 2.0) / head).astype(np.float32)
    segments, angles = [], []
    for number, one in enumerate(length_pair):
        segment, position = layout(one, row_index)
        segments.append(segment + number * (one.shape[0] + 1))
        angles.append(position.astype(f32)[:, None] * inverse[None, :])
    segment, angle = cat(*segments), cat(*angles)
    order = cat(row_index, row_index)
    allowed = (segment[:, None] == segment[None, :]) & (order[None, :] <= order[:, None])
    cosine, sine = jnp.cos(angle), jnp.sin(angle)
    return cat(cosine, cosine, axis=1), cat(-sine, sine, axis=1), allowed.astype(f32)


def rope(value, cosine, sine):
    return value * cosine + pltpu.roll(value, value.shape[1] // 2, 1) * sine


def rope_back(value, cosine, sine):
    return value * cosine + pltpu.roll(value * sine, value.shape[1] // 2, 1)


def from_heads(row, split, share):
    wide, head = row.shape[1], split * share
    part = wide // split
    lane = lax.broadcasted_iota(jnp.int32, (wide, head), 0)
    place = lax.broadcasted_iota(jnp.int32, (wide, head), 1)
    found = (lane // part == place // share) & (lane % part == place % share)
    chosen = jnp.where(found, 1.0, 0.0).astype(bf16)
    return dot(jnp.broadcast_to(row, (8, wide)).astype(bf16), chosen)[:1]


def attend_kernel(plan, rows, layer, split, experts, *refs):
    count = len(plan)
    pieces, refs = refs[:count], refs[count:]
    if layer == 0:
        (x_hat, cosine, sine, allowed), refs = refs[:4], refs[4:]
        tiny, normed, *refs = refs
    else:
        normed_pieces, (tiny, cosine, sine, allowed), refs = refs[:4], refs[4:8], refs[8:]
        normed, *refs = refs
    mixed, raw_out, probs_out, out_own, out_other, weights, sems = refs
    head = cosine.shape[1]
    group = probs_out.shape[0]
    near_columns = raw_out.shape[1]
    far_columns = mixed.shape[1]
    breadth = near_columns + far_columns
    near = copy_pieces(pieces, plan, rows, pl.ds(0, near_columns), weights, sems)
    far = copy_pieces(pieces, plan, rows, pl.ds(near_columns, far_columns), weights, sems, count)
    if layer == 0:
        last = pl.ds(breadth, weights.shape[1] - breadth)
        small = copy_pieces(pieces, plan, rows, last, weights, sems, 2 * count)
        start_all(small)
    start_all(near)
    start_all(far)
    share = head // split
    size = experts + 4
    if layer == 0:
        wait_all(small)
        tiny[...] = jnp.transpose(weights[:, breadth:].astype(f32))
        normed[...] = (x_hat[...] * tiny[experts : experts + 1]).astype(bf16)
    else:
        half = normed_pieces[0].shape[0]
        for number, piece in enumerate(normed_pieces):
            normed[number * half : (number + 1) * half] = piece[...]
    start = layer * size + experts
    query_gain = from_heads(tiny[start + 2 : start + 3], split, share)
    key_gain = from_heads(tiny[start + 3 : start + 4], split, share)
    wait_all(near)
    raw = dot(normed[...], weights[:, :near_columns])
    raw_out[...] = raw
    cos, sin, allow = cosine[...], sine[...], allowed[...] > 0.0
    k_raw = raw[:, group * head : (group + 1) * head]
    keys = rope(k_raw * inverse_rms(k_raw) * key_gain, cos, sin).astype(bf16)
    values = raw[:, (group + 1) * head :].astype(bf16)
    for number in range(group):
        q_raw = raw[:, number * head : (number + 1) * head]
        query = rope(q_raw * inverse_rms(q_raw) * query_gain, cos, sin) * head ** (-0.5)
        scores = jnp.where(allow, dot_cols(query.astype(bf16), keys), masked_score)
        unscaled = jnp.exp(scores - jnp.max(scores, axis=-1, keepdims=True))
        probs = unscaled / jnp.sum(unscaled, axis=-1, keepdims=True)
        probs_out[number] = probs
        mixed[:, number * head : (number + 1) * head] = dot(probs.astype(bf16), values).astype(
            bf16
        )
    wait_all(far)
    out = dot_cols(mixed[...], weights[:, near_columns:breadth])
    half = out_own.shape[0]
    out_own[...] = out[:half]
    out_other[...] = out[half:].astype(bf16)


def attend(layer, ring, breadth, split, experts, inputs, tables):
    head = tables[0].shape[1]
    rows = tables[0].shape[0]
    width = inputs[0].shape[1]
    group = (breadth // head - 2) // 2
    near = (group + 2) * head
    columns = breadth if layer else ring.shard.shape[1]
    small = (*inputs, *tables)
    shapes = (
        array((rows, width), bf16),
        array((rows, group * head), bf16),
        array((rows, near), f32),
        array((group, rows, rows), f32),
        array((rows // 2, width), f32),
        array((rows // 2, width), bf16),
    )
    if layer == 0:
        shapes = (array((columns - breadth, width), f32), *shapes)
    count = len(ring.pieces)
    return pl.pallas_call(
        functools.partial(attend_kernel, ring.plan, ring.rows, layer, split, experts),
        in_specs=[anywhere] * count + [full(one) for one in small],
        out_specs=tuple(full(one) for one in shapes),
        out_shape=shapes,
        scratch_shapes=[pltpu.VMEM((width, columns), bf16), pltpu.SemaphoreType.DMA((3 * count,))],
        compiler_params=kernel_params(26),
        cost_estimate=cost(12 * rows * width * breadth, 2 * width * breadth),
    )(*ring.pieces, *small)


def attend_back_kernel(plan, rows, layer, axis, experts, *refs):
    count = len(plan)
    pieces, refs = refs[:count], refs[count:]
    d_pieces, refs = refs[:4], refs[4:]
    raw_in, probs_in, tiny, cosine, sine = refs[:5]
    d_attn, d_qkv, d_own, d_other, g_query_gain, g_key_gain, weights, sems = refs[5:]
    head = cosine.shape[1]
    start = layer * (experts + 4) + experts
    query_gain = from_heads(tiny[start + 2 : start + 3], axis, head // axis)
    key_gain = from_heads(tiny[start + 3 : start + 4], axis, head // axis)
    half = d_pieces[0].shape[0]
    for number, piece in enumerate(d_pieces):
        d_attn[number * half : (number + 1) * half] = piece[...]
    group = probs_in.shape[0]
    split = raw_in.shape[1]
    rest = weights.shape[1] - split
    near = copy_pieces(pieces, plan, rows, pl.ds(split, rest), weights, sems)
    far = copy_pieces(pieces, plan, rows, pl.ds(0, split), weights, sems, count)
    start_all(near)
    start_all(far)
    cos, sin = cosine[...], sine[...]
    wait_all(near)
    d_mixed = dot(d_attn[...], weights[:, split:]).astype(bf16)
    k_raw = raw_in[:, group * head : (group + 1) * head]
    k_inverse = inverse_rms(k_raw)
    k_hat = k_raw * k_inverse
    keys = rope(k_hat * key_gain, cos, sin).astype(bf16)
    values = raw_in[:, (group + 1) * head :].astype(bf16)
    factor = head ** (-0.5)
    d_keys = jnp.zeros_like(k_raw)
    d_values = jnp.zeros_like(k_raw)
    gain_sum = jnp.zeros_like(query_gain)
    for number in range(group):
        span = slice(number * head, (number + 1) * head)
        q_raw = raw_in[:, span]
        q_inverse = inverse_rms(q_raw)
        q_hat = q_raw * q_inverse
        query = (rope(q_hat * query_gain, cos, sin) * factor).astype(bf16)
        probs = probs_in[number]
        d_one = d_mixed[:, span]
        d_probs = dot_cols(d_one, values)
        d_scores = probs * (d_probs - jnp.sum(probs * d_probs, axis=-1, keepdims=True))
        d_scores = d_scores.astype(bf16)
        d_values = d_values + dot_rows(probs.astype(bf16), d_one)
        d_keys = d_keys + dot_rows(d_scores, query)
        d_gained = rope_back(dot(d_scores, keys) * factor, cos, sin)
        gain_sum = gain_sum + jnp.sum(d_gained * q_hat, axis=0, keepdims=True)
        d_hat = d_gained * query_gain
        d_q = q_inverse * (d_hat - q_hat * jnp.mean(d_hat * q_hat, axis=-1, keepdims=True))
        d_qkv[:, span] = d_q.astype(bf16)
    g_query_gain[...] = gain_sum
    d_gained = rope_back(d_keys, cos, sin)
    g_key_gain[...] = jnp.sum(d_gained * k_hat, axis=0, keepdims=True)
    d_hat = d_gained * key_gain
    d_k = k_inverse * (d_hat - k_hat * jnp.mean(d_hat * k_hat, axis=-1, keepdims=True))
    d_qkv[:, group * head : (group + 1) * head] = d_k.astype(bf16)
    d_qkv[:, (group + 1) * head :] = d_values.astype(bf16)
    wait_all(far)
    d_normed = dot_cols(d_qkv[...], weights[:, :split])
    half = d_own.shape[0]
    d_own[...] = d_normed[:half]
    d_other[...] = d_normed[half:].astype(bf16)


def attend_back(layer, ring, breadth, split, experts, pieces, raw, probs, tiny, tables):
    head = tables[0].shape[1]
    width = pieces[0].shape[1]
    rows = raw.shape[0]
    small = (*pieces, raw, probs, tiny, tables[0], tables[1])
    shapes = (
        array((rows, width), bf16),
        array(raw.shape, bf16),
        array((rows // 2, width), f32),
        array((rows // 2, width), bf16),
        array((1, head), f32),
        array((1, head), f32),
    )
    count = len(ring.pieces)
    return pl.pallas_call(
        functools.partial(attend_back_kernel, ring.plan, ring.rows, layer, split, experts),
        in_specs=[anywhere] * count + [full(one) for one in small],
        out_specs=tuple(full(one) for one in shapes),
        out_shape=shapes,
        scratch_shapes=[pltpu.VMEM((width, breadth), bf16), pltpu.SemaphoreType.DMA((2 * count,))],
        compiler_params=kernel_params(26),
        cost_estimate=cost(12 * rows * width * breadth, 2 * width * breadth),
    )(*ring.pieces, *small)


def start_expert_weights(layer, refs, w_both, w_down, sems):
    is_own = lax.axis_index("section") == layer
    units = w_down.shape[0] // refs[0].shape[0]
    waits = []
    for number in range(refs[0].shape[0]):
        gate = pl.ds(2 * number * units, units)
        up = pl.ds((2 * number + 1) * units, units)
        targets = [w_both.at[:, gate], w_both.at[:, up], w_down.at[pl.ds(number * units, units)]]
        makers = [
            lambda ref, target=target, sem=sems.at[3 * number + i]: pltpu.make_async_copy(
                ref.at[number], target, sem
            )
            for i, target in enumerate(targets)
        ]

        @pl.when(is_own)
        def _():
            start_all([make(ref) for make, ref in zip(makers, refs[:3])])

        @pl.when(jnp.logical_not(is_own))
        def _():
            start_all([make(ref) for make, ref in zip(makers, refs[3:])])

        waits.append([make(ref) for make, ref in zip(makers, refs[:3])])
    return waits


def load_pieces(pieces, tile, scratch, sems):
    if len(pieces) == 1:
        pieces = [pieces[0].at[pl.ds(tile * tile_rows, tile_rows)]]
    copies, start = [], 0
    for number, piece in enumerate(pieces):
        rows = piece.shape[0]
        target = scratch.at[pl.ds(start, rows)]
        copies.append(pltpu.make_async_copy(piece, target, sems.at[number]))
        start += rows
    start_all(copies)
    return copies


def store_pieces(value, outs, columns):
    start = 0
    for out in outs:
        rows = out.shape[0]
        out[:, columns] = value[start : start + rows]
        start += rows


def experts_kernel(count, layer, tile, before, *refs):
    pieces, refs = refs[:count], refs[count:]
    weight_refs, ones, refs = refs[:6], refs[6], refs[7 + before :]
    outs, refs = refs[:count], refs[count:]
    act_out, gates_out, rows_store, scaled_store = refs[:4]
    rows_in, scaled, w_both, w_down, sems, weight_sems, store_sems = refs[4:]
    width = w_both.shape[0]
    experts = ones.shape[0]
    units = w_down.shape[0] // experts
    loads = load_pieces(pieces, tile, rows_in, sems)
    waits = start_expert_weights(layer, weight_refs, w_both, w_down, weight_sems)
    place = pl.ds(tile * tile_rows, tile_rows)
    stores = [
        pltpu.make_async_copy(
            rows_in.at[:, pl.ds(0, width)], rows_store.at[place], store_sems.at[0]
        ),
        pltpu.make_async_copy(scaled, scaled_store.at[place], store_sems.at[1]),
    ]
    wait_all(loads)
    stores[0].start()
    extra = rows_in[:, width:].astype(f32)
    gates = extra + pltpu.roll(extra, lanes // 2, 1)
    gates_out[...] = gates
    for number in range(experts):
        wait_all(waits[number])
        span = slice(2 * number * units, 2 * (number + 1) * units)
        act = dot(rows_in[:, :width], w_both[:, span])
        act_out[:, span] = act.astype(act_out.dtype)
        gate_act, up_act = act[:, :units], act[:, units:]
        hidden = (gate_act / (1.0 + jnp.exp(-gate_act)) * up_act).astype(bf16)
        gate = jnp.sum(gates * ones[number : number + 1], axis=1, keepdims=True)
        scaled[:, number * units : (number + 1) * units] = (hidden.astype(f32) * gate).astype(bf16)
    stores[1].start()
    step = width // 4
    for number in range(4):
        span = slice(number * step, (number + 1) * step)
        store_pieces(dot(scaled[...], w_down[:, span]).astype(bf16), outs, span)
    wait_all(stores)


def expert_scratch(wide, width, total_units, kind, count, experts):
    return [
        pltpu.VMEM((tile_rows, wide), bf16),
        kind,
        pltpu.VMEM((width, 2 * total_units), bf16),
        pltpu.VMEM((total_units, width), bf16),
        pltpu.SemaphoreType.DMA((count,)),
        pltpu.SemaphoreType.DMA((3 * experts,)),
        pltpu.SemaphoreType.DMA((2,)),
    ]


def run_experts(pieces, weights, ones, layer, tile, rows, stores):
    count = len(pieces)
    experts, width, units = weights[0].shape
    total_units = experts * units
    stores = stores or ()
    sizes = [min(one.shape[0], tile_rows) for one in pieces]
    shapes = tuple([array((one, width), bf16) for one in sizes]) + (
        array((tile_rows, 2 * total_units), f32 if small_grid() else bf16),
        array((tile_rows, lanes), f32),
        array((rows, width), bf16),
        array((rows, total_units), bf16),
    )
    outs = pl.pallas_call(
        functools.partial(experts_kernel, count, layer, tile, len(stores)),
        in_specs=[anywhere] * (count + 6) + [full(ones)] + [anywhere] * len(stores),
        out_specs=tuple(full(one) for one in shapes[: count + 2]) + (anywhere,) * 2,
        out_shape=shapes,
        scratch_shapes=expert_scratch(
            pieces[0].shape[1],
            width,
            total_units,
            pltpu.VMEM((tile_rows, total_units), bf16),
            count,
            experts,
        ),
        input_output_aliases={count + 7: count + 2, count + 8: count + 3} if stores else {},
        compiler_params=kernel_params(32),
        cost_estimate=cost(12 * tile_rows * width * total_units, 6 * width * total_units),
    )(*pieces, *weights, ones, *stores)
    return list(outs[:count]), outs[count : count + 2], outs[count + 2 :]


def experts_back_kernel(count, layer, tile, before, *refs):
    pieces, refs = refs[:count], refs[count:]
    weight_refs, ones, act, gates_in = refs[:6], refs[6], refs[7], refs[8]
    refs = refs[9 + before :]
    outs, refs = refs[:count], refs[count:]
    d_store, grad_store = refs[:2]
    rows_in, d_act, w_both, w_down, sems, weight_sems, store_sems = refs[2:]
    width = w_both.shape[0]
    experts = ones.shape[0]
    units = w_down.shape[0] // experts
    loads = load_pieces(pieces, tile, rows_in, sems)
    waits = start_expert_weights(layer, weight_refs, w_both, w_down, weight_sems)
    place = pl.ds(tile * tile_rows, tile_rows)
    stores = [
        pltpu.make_async_copy(rows_in, grad_store.at[place], store_sems.at[0]),
        pltpu.make_async_copy(d_act, d_store.at[place], store_sems.at[1]),
    ]
    wait_all(loads)
    stores[0].start()
    gates = gates_in[...]
    placed = jnp.zeros_like(gates)
    for number in range(experts):
        wait_all(waits[number])
        base = 2 * number * units
        plain = dot_cols(rows_in[...], w_down[number * units : (number + 1) * units])
        one = ones[number : number + 1]
        gate = jnp.sum(gates * one, axis=1, keepdims=True)
        gate_act = act[:, base : base + units].astype(f32)
        up_act = act[:, base + units : base + 2 * units].astype(f32)
        sigmoid = 1.0 / (1.0 + jnp.exp(-gate_act))
        silu = gate_act * sigmoid
        hidden = (silu * up_act).astype(bf16).astype(f32)
        placed = placed + jnp.sum(plain * hidden, axis=1, keepdims=True) * one
        d_hidden = plain * gate
        d_act[:, base + units : base + 2 * units] = (d_hidden * silu).astype(bf16)
        d_gate = d_hidden * up_act * (sigmoid + silu * (1.0 - sigmoid))
        d_act[:, base : base + units] = d_gate.astype(bf16)
    stores[1].start()
    step = width // 4
    for number in range(4):
        span = slice(number * step, (number + 1) * step)
        store_pieces(dot_cols(d_act[...], w_both[span]).astype(bf16), outs, span)
    store_pieces(placed.astype(bf16), outs, slice(width, width + lanes))
    wait_all(stores)


def run_experts_back(pieces, weights, ones, kept, layer, tile, rows, stores):
    count = len(pieces)
    experts, width, units = weights[0].shape
    total_units = experts * units
    stores = stores or ()
    act, gates = kept
    sizes = [min(one.shape[0], tile_rows) for one in pieces]
    shapes = tuple([array((one, width + lanes), bf16) for one in sizes]) + (
        array((rows, 2 * total_units), bf16),
        array((rows, width), bf16),
    )
    outs = pl.pallas_call(
        functools.partial(experts_back_kernel, count, layer, tile, len(stores)),
        in_specs=[anywhere] * (count + 6)
        + [full(ones), full(act), full(gates)]
        + [anywhere] * len(stores),
        out_specs=tuple(full(one) for one in shapes[:count]) + (anywhere,) * 2,
        out_shape=shapes,
        scratch_shapes=expert_scratch(
            width,
            width,
            total_units,
            pltpu.VMEM((tile_rows, 2 * total_units), bf16),
            count,
            experts,
        ),
        input_output_aliases={count + 9: count, count + 10: count + 1} if stores else {},
        compiler_params=kernel_params(32),
        cost_estimate=cost(12 * tile_rows * width * total_units, 6 * width * total_units),
    )(*pieces, *weights, ones, act, gates, *stores)
    return list(outs[:count]), outs[count:]


def grads_kernel(column, before, count, *refs):
    sources, refs = refs[:8], refs[8 + before :]
    outs, (left, right, result, sems, out_sems) = refs[:count], refs[count:]
    core = lax.axis_index("section")
    rows = left.shape[0] // 2
    place, step = column
    spans = [pl.ds(0, left.shape[1]), pl.ds(0, right.shape[1])]
    spans[place] = pl.ds(step * 512, 512)

    def copies(layer):
        made = []
        for number, target in enumerate((left, right)):
            for got in range(2):
                source = sources[4 * number + 2 * got + layer]
                made.append(
                    pltpu.make_async_copy(
                        source.at[:, spans[number]],
                        target.at[pl.ds(got * rows, rows)],
                        sems.at[2 * number + got],
                    )
                )
        return made

    for layer in range(2):

        @pl.when(core == layer)
        def _():
            start_all(copies(layer))

    wait_all(copies(0))
    experts = outs[0].shape[0]
    units = result.shape[1 - place] // (experts * count)
    result[...] = dot_rows(left[...], right[...])
    stores = []
    for expert in range(experts):
        for number, out in enumerate(outs):
            start = (expert * len(outs) + number) * units
            if place == 0:
                source = result.at[:, pl.ds(start, units)]
                target = out.at[expert, spans[0]]
            else:
                source = result.at[pl.ds(start, units)]
                target = out.at[expert, :, spans[1]]
            stores.append(pltpu.make_async_copy(source, target, out_sems.at[len(stores)]))
    start_all(stores)
    wait_all(stores)


def run_grads(place, step, left, right, shapes, before):
    before = before or ()
    rows = left[0].shape[0]
    widths = [left[0].shape[1], right[0].shape[1]]
    widths[place] = 512
    experts = shapes[0].shape[0]
    return pl.pallas_call(
        functools.partial(grads_kernel, (place, step), len(before), len(shapes)),
        in_specs=[anywhere] * (8 + len(before)),
        out_specs=(anywhere,) * len(shapes),
        out_shape=shapes,
        scratch_shapes=[
            pltpu.VMEM((2 * rows, widths[0]), bf16),
            pltpu.VMEM((2 * rows, widths[1]), bf16),
            pltpu.VMEM((widths[0], widths[1]), f32),
            pltpu.SemaphoreType.DMA((4,)),
            pltpu.SemaphoreType.DMA((experts * len(shapes),)),
        ],
        input_output_aliases={8 + i: i for i in range(len(before))},
        compiler_params=kernel_params(40),
        cost_estimate=cost(4 * 10**9, 10**7),
    )(*left, *right, *before)


def wide_grads(experts, rows_in, d_act):
    width, units = rows_in[0].shape[1], d_act[0].shape[1] // (2 * experts)
    shapes = (array((experts, width, units), f32),) * 2
    made = []
    for step in range(width // 512):
        made.append(run_grads(0, step, rows_in, d_act, shapes, made[-1] if made else None))
    return made


def down_grads(experts, scaled, grads):
    width, units = grads[0].shape[1], scaled[0].shape[1] // experts
    shapes = (array((experts, units, width), f32),)
    made = []
    for step in range(width // 512):
        made.append(run_grads(1, step, scaled, grads, shapes, made[-1] if made else None))
    return made


def out_grads_kernel(plan, rows, *refs):
    count = len(plan)
    pieces, (d_cols, g_out, mixed, sems) = refs[:count], refs[count:]
    copies = copy_pieces(pieces, plan, rows, pl.ds(0, mixed.shape[1]), mixed, sems)
    start_all(copies)
    wait_all(copies)
    g_out[...] = dot_rows(mixed[...], d_cols[...])


def out_grads(ring, d_cols):
    rows, columns = d_cols.shape
    breadth = ring.shard.shape[1]
    count = len(ring.pieces)
    shape = array((breadth, columns), f32)
    return pl.pallas_call(
        functools.partial(out_grads_kernel, ring.plan, ring.rows),
        in_specs=[anywhere] * count + [full(d_cols)],
        out_specs=full(shape),
        out_shape=shape,
        scratch_shapes=[pltpu.VMEM((rows, breadth), bf16), pltpu.SemaphoreType.DMA((count,))],
        compiler_params=kernel_params(24),
        cost_estimate=cost(2 * rows * columns * breadth, 4 * columns * breadth),
    )(*ring.pieces, d_cols)


def stack_layer_kernel(zero, one, got, out):
    core = lax.axis_index("section")
    columns = zero.shape[1]
    half = zero.shape[0] // 2
    for number, own in ((0, zero), (1, one)):

        @pl.when(core == number)
        def _():
            here = slice(number * columns, (number + 1) * columns)
            there = slice((1 - number) * columns, (2 - number) * columns)
            out[:, here] = own[...]
            out[:half, there] = got[half:]
            out[half:, there] = got[:half]


def stack_layer(core, zero, one, got):
    rows, columns = zero.shape
    return simple(stack_layer_kernel, [array((rows, 2 * columns), zero.dtype)], zero, one, got)[0]


def projection_grads_kernel(plan, rows, *refs):
    count = len(plan)
    pieces, (normed, g_query, g_key, g_value, d_qkv, sems) = refs[:count], refs[count:]
    copies = copy_pieces(pieces, plan, rows, pl.ds(0, d_qkv.shape[1]), d_qkv, sems)
    start_all(copies)
    wait_all(copies)
    wide = g_query.shape[1] // 2
    head = g_key.shape[1] // 2
    both = dot_rows(normed[...], d_qkv[...])
    for side in range(2):
        start = side * (wide + 2 * head)
        g_query[:, side * wide : (side + 1) * wide] = both[:, start : start + wide]
        g_key[:, side * head : (side + 1) * head] = both[:, start + wide : start + wide + head]
        g_value[:, side * head : (side + 1) * head] = both[
            :, start + wide + head : start + wide + 2 * head
        ]


def projection_grads(ring, normed, head):
    rows, part = normed.shape
    breadth = ring.shard.shape[1]
    wide = breadth // 2 - 2 * head
    count = len(ring.pieces)
    shapes = (
        array((part, 2 * wide), f32),
        array((part, 2 * head), f32),
        array((part, 2 * head), f32),
    )
    return pl.pallas_call(
        functools.partial(projection_grads_kernel, ring.plan, ring.rows),
        in_specs=[anywhere] * count + [full(normed)],
        out_specs=tuple(full(one) for one in shapes),
        out_shape=shapes,
        scratch_shapes=[pltpu.VMEM((rows, breadth), bf16), pltpu.SemaphoreType.DMA((count,))],
        compiler_params=kernel_params(24),
        cost_estimate=cost(2 * rows * part * breadth, 4 * rows * breadth),
    )(*ring.pieces, normed)


def both_rows(shard):
    far = swap_x(shard)
    return (shard, far, swap_core(shard), swap_core(far))


def merge_kernel(own, got, kept, given):
    block = own[...] + got[...].astype(f32)
    half = kept.shape[0]
    kept[...] = block[:half]
    given[...] = block[half:].astype(bf16)


def own_rows(own, other):
    rows, width = own.shape
    shapes = [array((rows // 2, width), kind) for kind in (f32, bf16)]
    kept, given = simple(merge_kernel, shapes, own, swap_core(other))
    return kept, swap_x(given)


def route_kernel(layer, x, kept, got, tiny, mask, mid_out, payload, gates_out):
    experts = mask.shape[1]
    width = x.shape[1]
    start = layer * (experts + 4)
    mid = x[...] + kept[...] + got[...].astype(f32)
    mid_out[...] = mid
    gain = tiny[start + experts + 1 : start + experts + 2]
    normed = (mid * inverse_rms(mid) * gain).astype(bf16)
    payload[:, :width] = normed
    logits = dot_cols(normed, tiny[start : start + experts].astype(bf16))
    logits = jnp.where(mask[...] > 0.0, logits, masked_score)
    weights = jnp.exp(logits - jnp.max(logits, axis=-1, keepdims=True))
    gates = weights / jnp.sum(weights, axis=-1, keepdims=True)
    gates_out[...] = gates
    high = gates.astype(bf16)
    low = (gates - high.astype(f32)).astype(bf16)
    payload[:, width:] = jnp.zeros((x.shape[0], lanes), bf16)
    payload[:, width : width + experts] = high
    payload[:, width + lanes // 2 : width + lanes // 2 + experts] = low


def route(layer, x, kept, got, tiny, mask):
    rows, width = x.shape
    shapes = [
        array((rows, width), f32),
        array((rows, width + lanes), bf16),
        array(mask.shape, f32),
    ]
    kernel = functools.partial(route_kernel, layer)
    return simple(kernel, shapes, x, kept, got, tiny, mask)


def sum_parts(parts):
    total = parts[0][...]
    for one in parts[1:]:
        total = total + one[...].astype(f32)
    return total


def enter_kernel(count, experts, mid, *refs):
    parts, (tiny, x_out, normed) = refs[:count], refs[count:]
    x = (mid[...] + sum_parts(parts)).astype(bf16).astype(f32)
    x_out[...] = x
    row = 2 * experts + 4
    normed[...] = (x * inverse_rms(x) * tiny[row : row + 1]).astype(bf16)


def enter(mid, parts, tiny, experts):
    shapes = [array(mid.shape, f32), array(mid.shape, bf16)]
    kernel = functools.partial(enter_kernel, len(parts), experts)
    return simple(kernel, shapes, mid, *parts, tiny)


def finish_kernel(mid, *refs):
    refs[-1][...] = (mid[...] + sum_parts(refs[:-1])).astype(bf16)


def finish(mid, parts):
    return simple(finish_kernel, [array(mid.shape, bf16)], mid, *parts)[0]


def norm_back(value, gain, grad):
    inverse = inverse_rms(value)
    hat = value * inverse
    d_hat = grad * gain
    d_value = inverse * (d_hat - hat * jnp.mean(d_hat * hat, axis=-1, keepdims=True))
    return d_value, jnp.sum(grad * hat, axis=0, keepdims=True)


def unroute_kernel(count, layer, *refs):
    parts, refs = refs[:count], refs[count:]
    grad, mid, tiny, gates_in, payload, d_out, d_low, g_router, g_gain = refs
    width = mid.shape[1]
    experts = gates_in.shape[1]
    start = layer * (experts + 4)
    back = sum_parts(parts)
    gates = gates_in[...]
    gate_grad = back[:, width : width + experts]
    d_logits = gates * (gate_grad - jnp.sum(gates * gate_grad, axis=-1, keepdims=True))
    d_logits = d_logits.astype(bf16)
    d_normed = back[:, :width] + dot(d_logits, tiny[start : start + experts].astype(bf16))
    gain = tiny[start + experts + 1 : start + experts + 2]
    d_mid, gain_sum = norm_back(mid[...], gain, d_normed)
    d_mid = d_mid + grad[...].astype(f32)
    d_out[...] = d_mid
    d_low[...] = d_mid.astype(bf16)
    g_router[...] = dot_rows(d_logits, payload[:, :width])
    g_gain[...] = gain_sum


def unroute(layer, parts, grad, mid, tiny, gates, payload):
    width, experts = mid.shape[1], gates.shape[1]
    shapes = [
        array(mid.shape, f32),
        array(mid.shape, bf16),
        array((experts, width), f32),
        array((1, width), f32),
    ]
    kernel = functools.partial(unroute_kernel, len(parts), layer)
    return simple(kernel, shapes, *parts, grad, mid, tiny, gates, payload)


def leave_kernel(row, kept, got, x, d_mid, tiny, d_out, g_gain):
    d_normed = kept[...] + got[...].astype(f32)
    d_x, gain_sum = norm_back(x[...], tiny[row : row + 1], d_normed)
    d_out[...] = (d_mid[...] + d_x).astype(bf16)
    g_gain[...] = gain_sum


def leave(layer, experts, kept, got, x, d_mid, tiny):
    shapes = [array(x.shape, bf16), array((1, x.shape[1]), f32)]
    kernel = functools.partial(leave_kernel, layer * (experts + 4) + experts)
    return simple(kernel, shapes, kept, got, x, d_mid, tiny)


def count_rows(tiles):
    return max(tile_rows, tiles[0][0].shape[0])


def apply_experts(tiles, weights, ones, layer):
    kept, outs, stores = [], [], None
    for number, pieces in enumerate(tiles):
        out, saved, stores = run_experts(
            pieces, weights, ones, layer, number, count_rows(tiles), stores
        )
        outs.append(out)
        kept.append(saved)
    return outs, kept, stores


def apply_experts_back(tiles, weights, ones, kept, layer):
    backs, stores = [], None
    for number, (pieces, saved) in enumerate(zip(tiles, kept)):
        back, stores = run_experts_back(
            pieces, weights, ones, saved, layer, number, count_rows(tiles), stores
        )
        backs.append(back)
    return backs, stores


def sum_small(own, other):
    value = own + swap_core(other)
    if not small_grid():
        value = lax.psum(value, "tensor")
        return lax.psum_scatter(value, "expert", scatter_dimension=1, tiled=True)
    value = value + swap_x(value)
    index = lax.axis_index("expert")
    for bit in (4, 2, 1):
        middle = value.shape[1] // 2
        lower, upper = value[:, :middle], value[:, middle:]
        high = (index & bit) != 0
        value = jnp.where(high, upper, lower) + swap_e(jnp.where(high, lower, upper), bit)
    return value


def body(
    ends_in,
    attn_gain,
    w_query,
    key_matrix,
    value_matrix,
    query_gain,
    key_gain,
    w_out,
    ffn_gain,
    router,
    w_gate,
    w_up,
    w_down,
    routes,
    lengths,
):
    core = lax.axis_index("section")
    first = core == 0
    side = lax.axis_index("tensor")
    index = lax.axis_index("expert")
    split = lax.axis_size("expert")
    rows, width = ends_in.shape[2:]
    half = rows // 2
    experts = router.shape[2]
    head = query_gain.shape[1] * split

    def pick(zero, one):
        return jnp.where(first, zero, one)

    def mine(pair):
        return pick(pair[0], pair[1])

    def theirs(pair):
        return pick(pair[1], pair[0])

    def by_layer(own):
        got = swap_core(own)
        return pick(own, got), pick(got, own)

    def pick_side(zero, one):
        return jnp.where(side == 0, zero, one)

    def half_rows(block):
        return pick_side(block[:half], block[half:])

    def side_first(block):
        return pick_side(block, cat(block[half:], block[:half]))

    part = w_query.shape[1]
    columns = w_query.shape[2] // 2
    transposed = w_out[0].T
    groups = [
        cat(
            w_query[0][:, g * columns : (g + 1) * columns],
            key_matrix[0][:, g * head : (g + 1) * head],
            value_matrix[0][:, g * head : (g + 1) * head],
            transposed[:, g * columns : (g + 1) * columns],
            axis=1,
        )
        for g in range(2)
    ]
    kept, got = mine(groups), swap_core(theirs(groups))
    breadth = kept.shape[1]

    share = head // split
    gains = cat(query_gain[0][:, None], key_gain[0][:, None], axis=1)
    tiny = cat(
        router[0],
        attn_gain[0][:, None],
        ffn_gain[0][:, None],
        jnp.pad(gains, ((0, part - share), (0, 0))),
        axis=1,
    )
    size = tiny.shape[1]
    tiny = cat(*by_layer(tiny), axis=1)
    tiny = jnp.pad(tiny, ((0, 0), (0, -2 * size % lanes)))
    ring0 = Ring(cat(pick(kept, got), tiny, axis=1))
    ring1 = Ring(pick(got, kept))
    started = ring0.advance()

    ends_in, w_gate, w_up, w_down = lax.optimization_barrier(
        (ends_in, w_gate, w_up, w_down, *started)
    )[:4]
    own_weights = (w_gate[0], w_up[0], w_down[0])
    expert_weights = own_weights + tuple(swap_core(one) for one in own_weights)
    crossed = swap_core(ends_in[0])
    x_all, grad_all = pick(ends_in[0], crossed), pick(crossed, ends_in[0])
    x_own = mine(x_all)
    x_in = half_rows(x_own).astype(f32)
    grad_last = half_rows(mine(grad_all))
    x_both = cat(side_first(x_own), side_first(theirs(x_all))).astype(f32)
    x_hat = x_both * inverse_rms(x_both)

    routes, lengths = lax.optimization_barrier((routes, lengths, *ring0.advance()))[:2]
    routes_crossed = swap_core(pick(routes[0, 1], routes[0, 0]))
    routes_own = [pick(routes[0, 0], routes_crossed), pick(routes_crossed, routes[0, 1])]
    expert_ids = jnp.arange(experts, dtype=jnp.int32)
    masks = [
        jnp.any(half_rows(r)[:, :, None] == expert_ids[None, None, :], axis=1).astype(f32)
        for r in routes_own
    ]
    per_device = w_gate.shape[1]
    lane_ids = jnp.arange(lanes, dtype=jnp.int32)
    local_ids = index * per_device + jnp.arange(per_device, dtype=jnp.int32)
    ones = (lane_ids[None, :] == local_ids[:, None]).astype(f32)
    row_index = (jnp.arange(rows, dtype=jnp.int32) + side * half) % rows
    length_pair = [pick(lengths[0, 0], lengths[1, 0]), pick(lengths[1, 0], lengths[0, 0])]
    tables = make_tables(length_pair, row_index, head)

    ring0.advance()
    ring0.advance()
    ring1.advance(*ring0.latest)

    tiny, normed0, mixed0, raw0, probs0, own, other = attend(
        0, ring0, breadth, split, experts, (x_hat,), tables
    )
    other = after(other, *ring1.latest)
    mid0, payload0, gates0 = route(0, x_in, *own_rows(own, other), tiny, masks[0])
    gather = Gather(payload0)
    gather.along_z()
    gather.near()
    gather.far()
    tiles = gather.tiles()
    ring1.advance(tiles[-1][-1])
    outs0, kept0, stores0 = apply_experts(tiles, expert_weights, ones, 0)
    scatter = Scatter(outs0)
    scatter.far()
    scatter.near(beside=ring1.latest)
    parts = scatter.along_z()
    ring1.advance(*parts)
    ring1.advance()
    x_mid, shard = enter(mid0, parts, tiny, experts)

    normed_pieces = both_rows(shard)
    grad_gather = Gather(grad_last)
    along = grad_gather.along_z(normed_pieces[-1])
    normed1, mixed1, raw1, probs1, own, other = attend(
        1, ring1, breadth, split, experts, (*normed_pieces, tiny), tables
    )
    other = after(other, *along)
    beside = grad_gather.near(own)
    mid1, payload1, gates1 = route(1, x_mid, *own_rows(own, other), tiny, masks[1])
    gather = Gather(after(payload1, *beside))
    gather.along_z()
    gather.near()
    gather.far()
    tiles = gather.tiles()
    beside = grad_gather.far(tiles[-1][-1])
    mixed_got = swap_core(pick(mixed1, mixed0))
    ring_mixed = Ring(stack_layer(core, mixed0, mixed1, mixed_got))
    ring_mixed.advance(tiles[-1][-1])
    outs1, kept1, stores1 = apply_experts(tiles, expert_weights, ones, 1)

    outs1[-1][-1] = after(outs1[-1][-1], *ring_mixed.latest, *beside)
    tiles = grad_gather.tiles(outs1[-1][-1])
    ring_mixed.advance(tiles[-1][-1])
    backs, back_stores1 = apply_experts_back(tiles, expert_weights, ones, kept1, 1)
    scatter = Scatter(backs)
    scatter.far(*ring_mixed.latest)
    reached = scatter.near()
    out_scatter = Scatter(outs1)
    beside = out_scatter.far(*reached)
    parts = scatter.along_z()
    parts[-1] = after(parts[-1], *beside)
    d_mid, d_low, g_router1, g_ffn_gain1 = unroute(
        1, parts, grad_last, mid1, tiny, gates1, payload1
    )
    d_pieces = both_rows(d_low)
    ring_mixed.advance(d_pieces[-1])
    d_attn1, d_qkv1, d_own, d_other, g_query_gain1, g_key_gain1 = attend_back(
        1, ring1, breadth, split, experts, d_pieces, raw1, probs1, tiny, tables
    )
    d_other = after(d_other, *ring_mixed.latest)
    d_one, g_attn_gain1 = leave(1, experts, *own_rows(d_own, d_other), x_mid, d_mid, tiny)

    gather = Gather(d_one)
    gather.along_z()
    beside = out_scatter.near(d_one)
    gather.near(*beside)
    gather.far()
    tiles = gather.tiles()
    backs, back_stores0 = apply_experts_back(tiles, expert_weights, ones, kept0, 0)

    def with_got(zero, one):
        if small_grid():
            to_zero = lax.ppermute(zero, "section", [(1, 0)])
            return zero, one, to_zero, lax.ppermute(one, "section", [(0, 1)])
        got = swap_core(pick(one, zero))
        return zero, one, got, got

    rows_in = with_got(stores0[0], stores1[0])
    scaled = with_got(stores0[1], stores1[1])
    d_act = with_got(back_stores0[0], back_stores1[0])
    grads = with_got(back_stores0[1], back_stores1[1])
    wide = wide_grads(per_device, rows_in, d_act)
    scatter = Scatter(backs)
    scatter.far()
    scatter.near(beside=wide[1])
    parts = scatter.along_z()
    parts[-1] = after(parts[-1], *wide[3])
    d_mid, d_low, g_router0, g_ffn_gain0 = unroute(
        0, parts, d_one, mid0, tiny, gates0, payload0
    )
    d_pieces = both_rows(d_low)
    ring_mixed.advance(d_pieces[-1])
    d_attn0, d_qkv0, d_own, d_other, g_query_gain0, g_key_gain0 = attend_back(
        0, ring0, breadth, split, experts, d_pieces, raw0, probs0, tiny, tables
    )
    d_other = after(d_other, *ring_mixed.latest)

    qkv_got = swap_core(pick(d_qkv1, d_qkv0))
    ring_d = Ring(stack_layer(core, d_qkv0, d_qkv1, qkv_got))
    ring_d.advance()
    out1 = finish(mid1, out_scatter.along_z(qkv_got))
    d_zero, g_attn_gain0 = leave(0, experts, *own_rows(d_own, d_other), x_in, d_mid, tiny)
    down = down_grads(per_device, scaled, (after(grads[0], qkv_got), *grads[1:]))
    down_early, down_late = down[1], down[3]
    ring_d.advance(*down_early)

    def spread(value):
        return lax.all_to_all(value, "expert", split_axis=1, concat_axis=0, tiled=True)

    end_own = pick(d_zero, out1)
    end_got = swap_core(pick(out1, d_zero))
    normed_cols = spread(pick(normed0, normed1))
    g_out = out_grads(ring_mixed, spread(pick(d_attn0, d_attn1)))
    ring_d.advance(*down_late)
    ring_d.advance()
    g_query, g_key, g_value = projection_grads(ring_d, normed_cols, head)
    (g_gate, g_up), (g_down,) = wide[-1], down[-1]

    def stacked(g_router, g_attn_gain, g_ffn_gain, g_query_gain, g_key_gain):
        heads = cat(g_query_gain.reshape(split, share), g_key_gain.reshape(split, share), axis=1)
        heads = jnp.pad(heads, ((0, 0), (0, part - 2 * share))).reshape(1, width)
        return cat(g_router, g_attn_gain, g_ffn_gain, heads)

    small = (
        stacked(g_router0, g_attn_gain0, g_ffn_gain0, g_query_gain0, g_key_gain0),
        stacked(g_router1, g_attn_gain1, g_ffn_gain1, g_query_gain1, g_key_gain1),
    )
    summed = sum_small(mine(small), theirs(small))
    g_router = summed[:experts].T
    g_attn_gain = summed[experts]
    g_ffn_gain = summed[experts + 1]
    g_query_gain = summed[experts + 2, :share]
    g_key_gain = summed[experts + 2, share : 2 * share]

    ends = jnp.stack([pick(end_own, end_got), pick(end_got, end_own)])
    ends_far = swap_x(ends)
    ends_out = cat(pick_side(ends, ends_far), pick_side(ends_far, ends), axis=1)

    outs = (
        ends_out,
        g_attn_gain,
        g_query,
        g_key,
        g_value,
        g_query_gain,
        g_key_gain,
        g_out,
        g_ffn_gain,
        g_router,
        g_gate,
        g_up,
        g_down,
    )
    return tuple(one[None] for one in outs)


def solution(mesh):
    return jax.shard_map(
        body,
        mesh=mesh,
        in_specs=(
            P("section", None, "expert", None),
            P("section", "expert"),
            P("section", "expert", "tensor"),
            P("section", "expert", "tensor"),
            P("section", "expert", "tensor"),
            P("section", "expert"),
            P("section", "expert"),
            P("section", "tensor", "expert"),
            P("section", "expert"),
            P("section", "expert", None),
            P("section", "expert", None, "tensor"),
            P("section", "expert", None, "tensor"),
            P("section", "expert", "tensor", None),
            P("section", None, "expert", None),
            P(None, "expert", None),
        ),
        out_specs=(
            P("section", None, "expert", None),
            P("section", "expert"),
            P("section", "expert", "tensor"),
            P("section", "expert", "tensor"),
            P("section", "expert", "tensor"),
            P("section", "expert"),
            P("section", "expert"),
            P("section", "tensor", "expert"),
            P("section", "expert"),
            P("section", "expert", None),
            P("section", "expert", None, "tensor"),
            P("section", "expert", None, "tensor"),
            P("section", "expert", "tensor", None),
        ),
        check_vma=False,
    )
```

time: 864 us -> 755 us (0.87)
  matrix products: 141 us -> 0 us
  Pallas kernels: 0 us -> 116 us
  other arithmetic: 79.7 us -> 26 us
  starting transfers between devices: 120 us -> 160 us
  blocking collectives: 33 us -> 0 us
  local copies, waits for them, and re-layouts: 110 us -> 87.3 us
  between operations: 18.4 us -> 3.13 us
    ppermute x0 -> x40, waiting for transfers between devices: none -> 155 us  [the longest x16 140 us: advance(): self.plus = lax.ppermute(after(plus, *gate), 'expert', up)]
    dot_general x44 -> x0, matrix products: 137 us -> none  [the longest x12 45.6 us: dot_cols(): lax.dot_general(left, right, (((1,), (1,)), ((), ())), preferred_element_...]
    all_gather x6 -> x0, waiting for transfers between devices: 129 us -> none  [gather_expert(): return lax.all_gather(shard, 'expert', axis=0, tiled=True)]
    pallas_call x0 -> x44, Pallas kernels: none -> 116 us  [the longest x8 30.4 us: run_grads(): pl.pallas_call(functools.partial(grads_kernel, (place, step), len(before)...]
    ppermute x0 -> x40, starting transfers between devices: none -> 57.7 us  [the longest x16 29.3 us: advance(): self.plus = lax.ppermute(after(plus, *gate), 'expert', up)]
    ppermute x43, waiting for transfers between devices: 142 us -> 89.4 us  [swap_e(): return lax.ppermute(value, 'expert', [(i, i ^ bits) for i in range(count)])]
    unnamed x529 -> x341, local copies, waits for them, and re-layouts: 29.9 us -> 68.4 us
    all_gather x1 -> x0, blocking collectives: 33 us -> none  [body(): tiny_all = lax.all_gather(tiny_layers[None], 'expert', axis=0, tiled=True)]
  transfers between devices with their start and end apart: 102 -> 131, of which waited for: 52 -> 64; matrix products, arithmetic and copies ran while one was open for 29% -> 6% of each run, Pallas kernels for 0% -> 15%
where the time goes in v2:
time: 755 us; the launch traced here: 745 us
  waiting for transfers between devices  352 us (47%)
  starting transfers between devices  160 us (21%)
  Pallas kernels  116 us (15%)
  local copies, waits for them, and re-layouts  87.3 us (12%)
  other arithmetic  26 us (3%)
    ppermute x16, waiting for transfers between devices, advance(): self.plus = lax.ppermute(after(plus, *gate), 'expert', up)  140 us
    ppermute x25, waiting for transfers between devices, swap_x(): return lax.ppermute(value, 'tensor', [(0, 1), (1, 0)])  97.8 us
    ppermute x43, waiting for transfers between devices, swap_e(): return lax.ppermute(value, 'expert', [(i, i ^ bits) for i in range(count)])  89.4 us
    unnamed x341, local copies, waits for them, and re-layouts  68.4 us
    ppermute x43, starting transfers between devices, swap_e(): return lax.ppermute(value, 'expert', [(i, i ^ bits) for i in range(count)])  56.4 us
    pallas_call x8, Pallas kernels, run_grads(): pl.pallas_call(functools.partial(grads_kernel, (place, step), len(before)...  30.4 us
    ppermute x16, starting transfers between devices, advance(): self.plus = lax.ppermute(after(plus, *gate), 'expert', up)  29.3 us
    ppermute x25, starting transfers between devices, swap_x(): return lax.ppermute(value, 'tensor', [(0, 1), (1, 0)])  29 us
  transfers between devices with their start and end apart: 131, of which 64 were waited for; matrix products, arithmetic and copies ran while one was open for 6% of the time, Pallas kernels for 15%

profile of v2, /device:TPU:0, one launch (start us, length us, event | category | flops | bytes accessed | tf_op | source)
XLA Modules:
  0.0 744.7 jit_solution(10101640844333020886)
XLA Ops:
  11.7 3.0 collective-permute-start.2
  14.7 27.6 %collective-permute-done.2.refs_1_ = bf16[256,2432]{1,0:T(8,128)(2,1)S(1)} collective-permute-done((bf16[256,2432]{1,0:T(8,128)(2,1)S(1)}, bf16[256,2432]{1,0:T(8,128)(2,1)S(1)}, u32[]{:S(2)}, u32[]{:S(2)}) %collective-permute-start.2) | collective-permute-done | bytes 1245216 | tf_op jit(solution)/shard_map/ppermute | solution.py:224
  50.4 25.1 %collective-permute-done.4.refs_3_ = bf16[256,2432]{1,0:T(8,128)(2,1)} collective-permute-done((bf16[256,2432]{1,0:T(8,128)(2,1)S(1)}, bf16[256,2432]{1,0:T(8,128)(2,1)}, u32[]{:S(2)}, u32[]{:S(2)}) %collective-permute-start.4) | collective-permute-done | bytes 1245216 | tf_op jit(solution)/shard_map/ppermute | solution.py:224
  79.1 25.0 %collective-permute-done.6.refs_5_ = bf16[256,2432]{1,0:T(8,128)(2,1)S(1)} collective-permute-done((bf16[256,2432]{1,0:T(8,128)(2,1)}, bf16[256,2432]{1,0:T(8,128)(2,1)S(1)}, u32[]{:S(2)}, u32[]{:S(2)}) %collective-permute-start.6) | collective-permute-done | bytes 1245216 | tf_op jit(solution)/shard_map/ppermute | solution.py:224
  107.8 10.8 %collective-permute-done.8.refs_7_ = bf16[128,2432]{1,0:T(8,128)(2,1)S(1)} collective-permute-done((bf16[128,2432]{1,0:T(8,128)(2,1)S(1)}, bf16[128,2432]{1,0:T(8,128)(2,1)S(1)}, u32[]{:S(2)}, u32[]{:S(2)}) %collective-permute-start.8) | collective-permute-done | bytes 622624 | tf_op jit(solution)/shard_map/ppermute | solution.py:224
  126.1 7.2 shard_map.264
  134.1 12.2 %collective-permute-done.10.refs_1_ = bf16[256,2304]{1,0:T(8,128)(2,1)S(1)} collective-permute-done((bf16[256,2304]{1,0:T(8,128)(2,1)}, bf16[256,2304]{1,0:T(8,128)(2,1)S(1)}, u32[]{:S(2)}, u32[]{:S(2)}) %collective-permute-start.10) | collective-permute-done | bytes 1179680 | tf_op jit(solution)/shard_map/ppermute | solution.py:224
  151.0 3.8 collective-permute-done.14.got
  159.4 3.6 collective-permute-done.16.refs_1_
  165.2 5.1 collective-permute-done.17.refs_2_
  172.5 9.2 %collective-permute-done.23.refs_1_ = bf16[128,2176]{1,0:T(8,128)(2,1)S(1)} collective-permute-done((bf16[128,2176]{1,0:T(8,128)(2,1)S(1)}, bf16[128,2176]{1,0:T(8,128)(2,1)S(1)}, u32[]{:S(2)}, u32[]{:S(2)}) %collective-permute-start.23) | collective-permute-done | bytes 557088 | tf_op jit(solution)/shard_map/ppermute | solution.py:41
  182.1 3.4 collective-permute-done.19.refs_2_
  186.7 6.4 collective-permute-done.20.refs_4_
  201.2 8.7 %shard_map.268 = (bf16[128,2048]{1,0:T(8,128)(2,1)S(1)}, bf16[128,2048]{1,0:T(8,128)(2,1)S(1)}, bf16[128,2048]{1,0:T(8,128)(2,1)S(1)}, bf16[64,2048]{1,0:T(8,128...) custom-call(bf16[128,2176]{1,0:T(8,128)(2,1)S(1)} %shard_map.267.ref, ...), custom_call_target="tpu_custom_call" | custom-call | flops 9663676416 | bytes 9437184 | tf_op jit(solution)/shard_map/pallas_call | solution.py:608
  213.6 9.8 %collective-permute-done.28.top = bf16[64,2048]{1,0:T(8,128)(2,1)S(1)} collective-permute-done((bf16[64,2048]{1,0:T(8,128)(2,1)S(1)}, bf16[64,2048]{1,0:T(8,128)(2,1)S(1)}, u32[]{:S(2)}, u32[]{:S(2)}) %collective-permute-start.28) | collective-permute-done | bytes 262176 | tf_op jit(solution)/shard_map/ppermute | solution.py:46
  228.3 5.6 collective-permute-done.30.from_x
  236.3 3.4 collective-permute-start.33
  241.3 2.9 collective-permute-done.33.refs_2_
  244.2 3.7 collective-permute-done.34.refs_3_
  251.1 19.4 %collective-permute-done.35.refs_5_ = bf16[256,2304]{1,0:T(8,128)(2,1)S(1)} collective-permute-done((bf16[256,2304]{1,0:T(8,128)(2,1)S(1)}, bf16[256,2304]{1,0:T(8,128)(2,1)S(1)}, u32[]{:S(2)}, u32[]{:S(2)}) %collective-permute-start.35) | collective-permute-done | bytes 1179680 | tf_op jit(solution)/shard_map/ppermute | solution.py:224
  270.6 3.4 collective-permute-start.37
  281.2 3.2 collective-permute-done.37.refs_7_
  284.4 2.9 collective-permute-done.38.refs_8_
  287.3 6.7 shard_map.273
  300.2 12.8 %collective-permute-done.48.got = bf16[32,2048]{1,0:T(8,128)(2,1)S(1)} collective-permute-done((bf16[32,2048]{1,0:T(8,128)(2,1)}, bf16[32,2048]{1,0:T(8,128)(2,1)S(1)}, u32[]{:S(2)}, u32[]{:S(2)}) %collective-permute-start.48) | collective-permute-done | bytes 131104 | tf_op jit(solution)/shard_map/ppermute | solution.py:41
  314.5 7.0 collective-permute-start.49
  326.0 8.4 %collective-permute-done.50.refs_2_ = bf16[32,2176]{1,0:T(8,128)(2,1)S(1)} collective-permute-done((bf16[32,2176]{1,0:T(8,128)(2,1)S(1)}, bf16[32,2176]{1,0:T(8,128)(2,1)S(1)}, u32[]{:S(2)}, u32[]{:S(2)}) %collective-permute-start.50) | collective-permute-done | bytes 139296 | tf_op jit(solution)/shard_map/ppermute | solution.py:46
  335.8 11.4 %collective-permute-done.56.refs_1_ = bf16[128,2176]{1,0:T(8,128)(2,1)S(1)} collective-permute-done((bf16[128,2176]{1,0:T(8,128)(2,1)S(1)}, bf16[128,2176]{1,0:T(8,128)(2,1)S(1)}, u32[]{:S(2)}, u32[]{:S(2)}) %collective-permute-start.56) | collective-permute-done | bytes 557088 | tf_op jit(solution)/shard_map/ppermute | solution.py:41
  362.9 9.3 %shard_map.277 = (bf16[128,2048]{1,0:T(8,128)(2,1)S(1)}, bf16[128,2048]{1,0:T(8,128)(2,1)S(1)}, bf16[128,2048]{1,0:T(8,128)(2,1)S(1)}, bf16[64,2048]{1,0:T(8,128...) custom-call(bf16[128,2176]{1,0:T(8,128)(2,1)S(1)} %shard_map.276.ref, ...), custom_call_target="tpu_custom_call" | custom-call | flops 9663676416 | bytes 9437184 | tf_op jit(solution)/shard_map/pallas_call | solution.py:608
  385.2 11.7 %shard_map.279 = (bf16[128,2176]{1,0:T(8,128)(2,1)S(1)}, bf16[128,2176]{1,0:T(8,128)(2,1)S(1)}, bf16[128,2176]{1,0:T(8,128)(2,1)S(1)}, bf16[64,2176]{1,0:T(8,128...) custom-call(bf16[128,2048]{1,0:T(8,128)(2,1)S(1)} %copy-done.44, ...), custom_call_target="tpu_custom_call" | custom-call | flops 9663676416 | bytes 9437184 | tf_op jit(solution)/shard_map/pallas_call | solution.py:685
  399.0 6.4 collective-permute-done.63.top
  409.3 10.2 %collective-permute-done.65.from_x = bf16[128,2176]{1,0:T(8,128)(2,1)S(1)} collective-permute-done((bf16[128,2176]{1,0:T(8,128)(2,1)S(1)}, bf16[128,2176]{1,0:T(8,128)(2,1)S(1)}, u32[]{:S(2)}, u32[]{:S(2)}) %collective-permute-start.65) | collective-permute-done | bytes 557088 | tf_op jit(solution)/shard_map/ppermute | solution.py:41
  435.1 4.5 collective-permute-done.72.refs_10_
  446.5 6.2 shard_map.283
  457.3 4.9 collective-permute-done.78.got
  472.1 5.5 collective-permute-done.80.refs_2_
  479.5 10.6 %collective-permute-done.84.refs_1_ = bf16[128,2048]{1,0:T(8,128)(2,1)S(1)} collective-permute-done((bf16[128,2048]{1,0:T(8,128)(2,1)S(1)}, bf16[128,2048]{1,0:T(8,128)(2,1)S(1)}, u32[]{:S(2)}, u32[]{:S(2)}) %collective-permute-start.84) | collective-permute-done | bytes 524320 | tf_op jit(solution)/shard_map/ppermute | solution.py:41
  490.3 3.8 collective-permute-start.87
  495.5 4.5 collective-permute-start.92
  504.5 10.0 %shard_map.289 = (bf16[128,2176]{1,0:T(8,128)(2,1)S(1)}, bf16[128,2176]{1,0:T(8,128)(2,1)S(1)}, bf16[128,2176]{1,0:T(8,128)(2,1)S(1)}, bf16[64,2176]{1,0:T(8,128...) custom-call(bf16[128,2048]{1,0:T(8,128)(2,1)S(1)} %shard_map.286.refs_0_, ...), custom_call_target="tpu_custom_call" | custom-call | flops 9663676416 | bytes 9437184 | tf_op jit(solution)/shard_map/pallas_call | solution.py:685
  517.2 9.3 %collective-permute-done.88.top = bf16[64,2176]{1,0:T(8,128)(2,1)S(1)} collective-permute-done((bf16[64,2176]{1,0:T(8,128)(2,1)S(1)}, bf16[64,2176]{1,0:T(8,128)(2,1)S(1)}, u32[]{:S(2)}, u32[]{:S(2)}) %collective-permute-start.88) | collective-permute-done | bytes 278560 | tf_op jit(solution)/shard_map/ppermute | solution.py:46
  526.5 8.6 %collective-permute-done.89.bottom = bf16[64,2176]{1,0:T(8,128)(2,1)S(1)} collective-permute-done((bf16[64,2176]{1,0:T(8,128)(2,1)S(1)}, bf16[64,2176]{1,0:T(8,128)(2,1)S(1)}, u32[]{:S(2)}, u32[]{:S(2)}) %collective-permute-start.89) | collective-permute-done | bytes 278560 | tf_op jit(solution)/shard_map/ppermute | solution.py:41
  535.7 3.9 shard_map.291
  539.6 3.9 shard_map.292
  543.6 5.6 collective-permute-done.90.from_x
  554.2 3.9 shard_map.294
  558.2 4.3 shard_map.295
  568.0 5.3 collective-permute-start.122
  590.6 3.3 collective-permute-start.120
  607.7 7.7 %shard_map.297 = (bf16[128,2048]{1,0:T(8,128)(2,1)S(1)}, bf16[128,1280]{1,0:T(8,128)(2,1)S(1)}, f32[64,2048]{1,0:T(8,128)S(1)}, bf16[64,2048]{1,0:T(8,128)(2,1)S...) custom-call(bf16[256,2432]{1,0:T(8,128)(2,1)S(1)} %copy-done.18, bf16[256,2432]{1,0:T(8,128)(2,1)S(1)} %copy-done.95, ...), custom_call_target="tpu_custom_call" | custom-call | flops 7247757312 | bytes 9437184 | tf_op jit(solution)/shard_map/pallas_call | solution.py:485
  629.0 4.9 collective-permute-done.103.refs_8_
  636.5 4.2 all-to-all-start.1
  652.0 3.6 shard_map.302.refs_8_
  656.5 3.5 shard_map.303.refs_8_
  661.4 3.6 collective-permute-done.108.refs_2_
  670.6 5.8 all-to-all-start
  683.7 5.2 shard_map.307
  689.9 3.0 collective-permute-start.114
  695.0 3.6 shard_map.304.refs_8_
  698.5 3.6 shard_map.305
  704.7 7.0 collective-permute-done.115
  716.6 10.9 %collective-permute-done.125.refs_5_ = bf16[128,2560]{1,0:T(8,128)(2,1)S(1)} collective-permute-done((bf16[128,2560]{1,0:T(8,128)(2,1)S(1)}, bf16[128,2560]{1,0:T(8,128)(2,1)S(1)}, u32[]{:S(2)}, u32[]{:S(2)}) %collective-permute-start.125) | collective-permute-done | bytes 655392 | tf_op jit(solution)/shard_map/ppermute | solution.py:224
  730.9 3.8 collective-permute-done.127.refs_7_
  738.8 5.6 shard_map.306
  (685 shorter events, 277.9 us)
Async XLA Ops:
  11.7 30.6 %collective-permute-start.2 = (bf16[256,2432]{1,0:T(8,128)(2,1)S(1)}, bf16[256,2432]{1,0:T(8,128)(2,1)S(1)}, u32[]{:S(2)}, u32[]{:S(2)}) collective-permute-start(bf16[256,2432]{1,0:T(8,128)(2,1)S(1)} %fusion.1.refs_0_), channel_id=1, source_target_pairs={{0,4},{4,8},{8,12},{12,14},{14,10},{10,6},{6,2},{2,0},{1,5},{5,9},... | collective-permute-start | bytes 3735560 | tf_op jit(solution)/shard_map/ppermute | solution.py:224
  14.7 29.1 %collective-permute-start.3 = (bf16[256,2432]{1,0:T(8,128)(2,1)S(1)}, bf16[256,2432]{1,0:T(8,128)(2,1)S(1)}, u32[]{:S(2)}, u32[]{:S(2)}) collective-permute-start(bf16[256,2432]{1,0:T(8,128)(2,1)S(1)} %fusion.1.refs_0_), channel_id=1, source_target_pairs={{4,0},{8,4},{12,8},{14,12},{10,14},{6,10},{2,6},{0,2},{5,1},{9,5},... | collective-permute-start | bytes 3735560 | tf_op jit(solution)/shard_map/ppermute | solution.py:225
  44.9 150.6 %collective-permute-start.25 = (bf16[2,2048,384]{2,1,0:T(8,128)(2,1)}, bf16[2,2048,384]{2,1,0:T(8,128)(2,1)}, u32[]{:S(2)}, u32[]{:S(2)}) collective-permute-start(bf16[2,2048,384]{2,1,0:T(8,128)(2,1)} %bitcast.92), channel_id=1, source_target_pairs={{0,16},{16,0},{1,17},{17,1},{2,18},{18,2},{3,19},{19,3},{4,20},{20... | collective-permute-start | bytes 9437192 | tf_op jit(solution)/shard_map/ppermute | solution.py:37
  45.4 150.1 %collective-permute-start.26 = (bf16[2,2048,384]{2,1,0:T(8,128)(2,1)}, bf16[2,2048,384]{2,1,0:T(8,128)(2,1)}, u32[]{:S(2)}, u32[]{:S(2)}) collective-permute-start(bf16[2,2048,384]{2,1,0:T(8,128)(2,1)} %bitcast.97), channel_id=1, source_target_pairs={{0,16},{16,0},{1,17},{17,1},{2,18},{18,2},{3,19},{19,3},{4,20},{20... | collective-permute-start | bytes 9437192 | tf_op jit(solution)/shard_map/ppermute | solution.py:37
  45.5 150.0 %collective-permute-start.27 = (bf16[2,384,2048]{2,1,0:T(8,128)(2,1)}, bf16[2,384,2048]{2,1,0:T(8,128)(2,1)}, u32[]{:S(2)}, u32[]{:S(2)}) collective-permute-start(bf16[2,384,2048]{2,1,0:T(8,128)(2,1)} %bitcast.102), channel_id=1, source_target_pairs={{0,16},{16,0},{1,17},{17,1},{2,18},{18,2},{3,19},{19,3},{4,20},{20... | collective-permute-start | bytes 9437192 | tf_op jit(solution)/shard_map/ppermute | solution.py:37
  45.9 29.5 %collective-permute-start.4 = (bf16[256,2432]{1,0:T(8,128)(2,1)S(1)}, bf16[256,2432]{1,0:T(8,128)(2,1)}, u32[]{:S(2)}, u32[]{:S(2)}) collective-permute-start(bf16[256,2432]{1,0:T(8,128)(2,1)S(1)} %collective-permute-done.2.refs_1_), channel_id=1, source_target_pairs={{0,4},{4,8},{8,12},{12,14},{14,10},{10,6},{6,2},{2,0},{1,5},{5,9},... | collective-permute-start | bytes 3735560 | tf_op jit(solution)/shard_map/ppermute | solution.py:224
  47.5 29.5 %collective-permute-start.5 = (bf16[256,2432]{1,0:T(8,128)(2,1)}, bf16[256,2432]{1,0:T(8,128)(2,1)}, u32[]{:S(2)}, u32[]{:S(2)}) collective-permute-start(bf16[256,2432]{1,0:T(8,128)(2,1)} %copy-done.96), channel_id=1, source_target_pairs={{4,0},{8,4},{12,8},{14,12},{10,14},{6,10},{2,6},{0,2},{5,1},{9,5},... | collective-permute-start | bytes 3735560 | tf_op jit(solution)/shard_map/ppermute | solution.py:225
  75.4 28.7 %collective-permute-start.6 = (bf16[256,2432]{1,0:T(8,128)(2,1)}, bf16[256,2432]{1,0:T(8,128)(2,1)S(1)}, u32[]{:S(2)}, u32[]{:S(2)}) collective-permute-start(bf16[256,2432]{1,0:T(8,128)(2,1)} %collective-permute-done.4.refs_3_), channel_id=1, source_target_pairs={{0,4},{4,8},{8,12},{12,14},{14,10},{10,6},{6,2},{2,0},{1,5},{5,9},... | collective-permute-start | bytes 3735560 | tf_op jit(solution)/shard_map/ppermute | solution.py:224
  77.0 28.8 %collective-permute-start.7 = (bf16[256,2432]{1,0:T(8,128)(2,1)}, bf16[256,2432]{1,0:T(8,128)(2,1)}, u32[]{:S(2)}, u32[]{:S(2)}) collective-permute-start(bf16[256,2432]{1,0:T(8,128)(2,1)} %collective-permute-done.5.refs_4_), channel_id=1, source_target_pairs={{4,0},{8,4},{12,8},{14,12},{10,14},{6,10},{2,6},{0,2},{5,1},{9,5},... | collective-permute-start | bytes 3735560 | tf_op jit(solution)/shard_map/ppermute | solution.py:225
  104.2 14.4 %collective-permute-start.8 = (bf16[128,2432]{1,0:T(8,128)(2,1)S(1)}, bf16[128,2432]{1,0:T(8,128)(2,1)S(1)}, u32[]{:S(2)}, u32[]{:S(2)}) collective-permute-start(bf16[128,2432]{1,0:T(8,128)(2,1)S(1)} %slice.246), channel_id=1, source_target_pairs={{0,4},{4,8},{8,12},{12,14},{14,10},{10,6},{6,2},{2,0},{1,5},{5,9},... | collective-permute-start | bytes 1867784 | tf_op jit(solution)/shard_map/ppermute | solution.py:224
  106.9 14.1 %collective-permute-start.9 = (bf16[128,2432]{1,0:T(8,128)(2,1)S(1)}, bf16[128,2432]{1,0:T(8,128)(2,1)S(1)}, u32[]{:S(2)}, u32[]{:S(2)}) collective-permute-start(bf16[128,2432]{1,0:T(8,128)(2,1)S(1)} %slice.247), channel_id=1, source_target_pairs={{4,0},{8,4},{12,8},{14,12},{10,14},{6,10},{2,6},{0,2},{5,1},{9,5},... | collective-permute-start | bytes 1867784 | tf_op jit(solution)/shard_map/ppermute | solution.py:225
  121.1 25.3 %collective-permute-start.10 = (bf16[256,2304]{1,0:T(8,128)(2,1)}, bf16[256,2304]{1,0:T(8,128)(2,1)S(1)}, u32[]{:S(2)}, u32[]{:S(2)}) collective-permute-start(bf16[256,2304]{1,0:T(8,128)(2,1)} %get-tuple-element.181.refs_0_), channel_id=1, source_target_pairs={{0,4},{4,8},{8,12},{12,14},{14,10},{10,6},{6,2},{2,0},{1,5},{5,9},... | collective-permute-start | bytes 3538952 | tf_op jit(solution)/shard_map/ppermute | solution.py:224
  122.6 25.0 %collective-permute-start.11 = (bf16[256,2304]{1,0:T(8,128)(2,1)}, bf16[256,2304]{1,0:T(8,128)(2,1)S(1)}, u32[]{:S(2)}, u32[]{:S(2)}) collective-permute-start(bf16[256,2304]{1,0:T(8,128)(2,1)} %get-tuple-element.181.refs_0_), channel_id=1, source_target_pairs={{4,0},{8,4},{12,8},{14,12},{10,14},{6,10},{2,6},{0,2},{5,1},{9,5},... | collective-permute-start | bytes 3538952 | tf_op jit(solution)/shard_map/ppermute | solution.py:225
  181.8 13.8 %collective-permute-start.24 = (bf16[64,2176]{1,0:T(8,128)(2,1)S(1)}, bf16[64,2176]{1,0:T(8,128)(2,1)S(1)}, u32[]{:S(2)}, u32[]{:S(2)}) collective-permute-start(bf16[64,2176]{1,0:T(8,128)(2,1)S(1)} %slice.255), channel_id=1, source_target_pairs={{0,2},{2,0},{4,6},{6,4},{8,10},{10,8},{12,14},{14,12},{1,3},{3,1},... | collective-permute-start | bytes 835592 | tf_op jit(solution)/shard_map/ppermute | solution.py:46
  193.1 40.8 %collective-permute-start.21 = (bf16[256,2304]{1,0:T(8,128)(2,1)}, bf16[256,2304]{1,0:T(8,128)(2,1)S(1)}, u32[]{:S(2)}, u32[]{:S(2)}) collective-permute-start(bf16[256,2304]{1,0:T(8,128)(2,1)} %copy-done.99), channel_id=1, source_target_pairs={{0,4},{4,8},{8,12},{12,14},{14,10},{10,6},{6,2},{2,0},{1,5},{5,9},... | collective-permute-start | bytes 3538952 | tf_op jit(solution)/shard_map/ppermute | solution.py:224
  195.5 38.3 %collective-permute-start.22 = (bf16[256,2304]{1,0:T(8,128)(2,1)}, bf16[256,2304]{1,0:T(8,128)(2,1)S(1)}, u32[]{:S(2)}, u32[]{:S(2)}) collective-permute-start(bf16[256,2304]{1,0:T(8,128)(2,1)} %copy-done.102), channel_id=1, source_target_pairs={{4,0},{8,4},{12,8},{14,12},{10,14},{6,10},{2,6},{0,2},{5,1},{9,5},... | collective-permute-start | bytes 3538952 | tf_op jit(solution)/shard_map/ppermute | solution.py:225
  248.0 22.6 %collective-permute-start.35 = (bf16[256,2304]{1,0:T(8,128)(2,1)S(1)}, bf16[256,2304]{1,0:T(8,128)(2,1)S(1)}, u32[]{:S(2)}, u32[]{:S(2)}) collective-permute-start(bf16[256,2304]{1,0:T(8,128)(2,1)S(1)} %collective-permute-done.21.refs_3_), channel_id=1, source_target_pairs={{0,4},{4,8},{8,12},{12,14},{14,10},{10,6},{6,2},{2,0},{1,5},{5,9},... | collective-permute-start | bytes 3538952 | tf_op jit(solution)/shard_map/ppermute | solution.py:224
  248.7 25.3 %collective-permute-start.36 = (bf16[256,2304]{1,0:T(8,128)(2,1)S(1)}, bf16[256,2304]{1,0:T(8,128)(2,1)S(1)}, u32[]{:S(2)}, u32[]{:S(2)}) collective-permute-start(bf16[256,2304]{1,0:T(8,128)(2,1)S(1)} %collective-permute-done.22.refs_4_), channel_id=1, source_target_pairs={{4,0},{8,4},{12,8},{14,12},{10,14},{6,10},{2,6},{0,2},{5,1},{9,5},... | collective-permute-start | bytes 3538952 | tf_op jit(solution)/shard_map/ppermute | solution.py:225
  250.3 24.0 %collective-permute-start.39 = (bf16[32,2048]{1,0:T(8,128)(2,1)S(1)}, bf16[32,2048]{1,0:T(8,128)(2,1)S(1)}, u32[]{:S(2)}, u32[]{:S(2)}) collective-permute-start(bf16[32,2048]{1,0:T(8,128)(2,1)S(1)} %get-tuple-element.212.refs_9_), channel_id=1, source_target_pairs={{0,1},{1,0},{2,3},{3,2},{4,5},{5,4},{6,7},{7,6},{8,9},{9,8},{10,11... | collective-permute-start | bytes 393224 | tf_op jit(solution)/shard_map/ppermute | solution.py:41
  270.6 13.8 %collective-permute-start.37 = (bf16[128,2304]{1,0:T(8,128)(2,1)S(1)}, bf16[128,2304]{1,0:T(8,128)(2,1)S(1)}, u32[]{:S(2)}, u32[]{:S(2)}) collective-permute-start(bf16[128,2304]{1,0:T(8,128)(2,1)S(1)} %slice.256), channel_id=1, source_target_pairs={{0,4},{4,8},{8,12},{12,14},{14,10},{10,6},{6,2},{2,0},{1,5},{5,9},... | collective-permute-start | bytes 1769480 | tf_op jit(solution)/shard_map/ppermute | solution.py:224
  275.8 19.1 %collective-permute-start.41 = (bf16[32,2048]{1,0:T(8,128)(2,1)S(1)}, bf16[32,2048]{1,0:T(8,128)(2,1)S(1)}, u32[]{:S(2)}, u32[]{:S(2)}) collective-permute-start(bf16[32,2048]{1,0:T(8,128)(2,1)S(1)} %fusion.4.refs_0_.refs_4_), channel_id=1, source_target_pairs={{0,4},{2,6},{4,0},{6,2},{8,12},{10,14},{12,8},{14,10},{1,5},{3,7},... | collective-permute-start | bytes 393224 | tf_op jit(solution)/shard_map/ppermute | solution.py:46
  278.3 17.5 %collective-permute-start.42 = (bf16[32,2048]{1,0:T(8,128)(2,1)S(1)}, bf16[32,2048]{1,0:T(8,128)(2,1)S(1)}, u32[]{:S(2)}, u32[]{:S(2)}) collective-permute-start(bf16[32,2048]{1,0:T(8,128)(2,1)S(1)} %fusion.4.refs_0_.refs_4_), channel_id=1, source_target_pairs={{0,8},{2,10},{4,12},{6,14},{8,0},{10,2},{12,4},{14,6},{1,9},{3,11}... | collective-permute-start | bytes 393224 | tf_op jit(solution)/shard_map/ppermute | solution.py:46
  279.7 16.0 %collective-permute-start.43 = (bf16[32,2048]{1,0:T(8,128)(2,1)S(1)}, bf16[32,2048]{1,0:T(8,128)(2,1)S(1)}, u32[]{:S(2)}, u32[]{:S(2)}) collective-permute-start(bf16[32,2048]{1,0:T(8,128)(2,1)S(1)} %fusion.4.refs_0_.refs_4_), channel_id=1, source_target_pairs={{0,12},{2,14},{4,8},{6,10},{8,4},{10,6},{12,0},{14,2},{1,13},{3,15... | collective-permute-start | bytes 393224 | tf_op jit(solution)/shard_map/ppermute | solution.py:46
  295.8 18.7 %collective-permute-start.45 = (bf16[128,2048]{1,0:T(8,128)(2,1)S(1)}, bf16[128,2048]{1,0:T(8,128)(2,1)}, u32[]{:S(2)}, u32[]{:S(2)}) collective-permute-start(bf16[128,2048]{1,0:T(8,128)(2,1)S(1)} %shard_map.272.refs_0_), channel_id=1, source_target_pairs={{0,1},{1,0},{2,3},{3,2},{4,5},{5,4},{6,7},{7,6},{8,9},{9,8},{10,11... | collective-permute-start | bytes 1572872 | tf_op jit(solution)/shard_map/ppermute | solution.py:41
  297.2 17.3 %collective-permute-start.46 = (bf16[128,2048]{1,0:T(8,128)(2,1)S(1)}, bf16[128,2048]{1,0:T(8,128)(2,1)}, u32[]{:S(2)}, u32[]{:S(2)}) collective-permute-start(bf16[128,2048]{1,0:T(8,128)(2,1)S(1)} %shard_map.272.refs_0_), channel_id=1, source_target_pairs={{0,2},{2,0},{4,6},{6,4},{8,10},{10,8},{12,14},{14,12},{1,3},{3,1},... | collective-permute-start | bytes 1572872 | tf_op jit(solution)/shard_map/ppermute | solution.py:46
  298.8 14.2 %collective-permute-start.48 = (bf16[32,2048]{1,0:T(8,128)(2,1)}, bf16[32,2048]{1,0:T(8,128)(2,1)S(1)}, u32[]{:S(2)}, u32[]{:S(2)}) collective-permute-start(bf16[32,2048]{1,0:T(8,128)(2,1)} %get-tuple-element.220), channel_id=1, source_target_pairs={{0,1},{1,0},{2,3},{3,2},{4,5},{5,4},{6,7},{7,6},{8,9},{9,8},{10,11... | collective-permute-start | bytes 393224 | tf_op jit(solution)/shard_map/ppermute | solution.py:41
  335.7 13.9 %collective-permute-start.52 = (bf16[128,2176]{1,0:T(8,128)(2,1)S(1)}, bf16[128,2176]{1,0:T(8,128)(2,1)S(1)}, u32[]{:S(2)}, u32[]{:S(2)}) collective-permute-start(bf16[128,2176]{1,0:T(8,128)(2,1)S(1)} %shard_map.276.refs_0_), channel_id=1, source_target_pairs={{0,2},{2,0},{4,6},{6,4},{8,10},{10,8},{12,14},{14,12},{1,3},{3,1},... | collective-permute-start | bytes 1671176 | tf_op jit(solution)/shard_map/ppermute | solution.py:46
  347.2 13.8 %collective-permute-start.57 = (bf16[64,2176]{1,0:T(8,128)(2,1)S(1)}, bf16[64,2176]{1,0:T(8,128)(2,1)S(1)}, u32[]{:S(2)}, u32[]{:S(2)}) collective-permute-start(bf16[64,2176]{1,0:T(8,128)(2,1)S(1)} %slice.265), channel_id=1, source_target_pairs={{0,2},{2,0},{4,6},{6,4},{8,10},{10,8},{12,14},{14,12},{1,3},{3,1},... | collective-permute-start | bytes 835592 | tf_op jit(solution)/shard_map/ppermute | solution.py:46
  356.3 22.1 %collective-permute-start.59 = (bf16[128,2048]{1,0:T(8,128)(2,1)S(1)}, bf16[128,2048]{1,0:T(8,128)(2,1)S(1)}, u32[]{:S(2)}, u32[]{:S(2)}) collective-permute-start(bf16[128,2048]{1,0:T(8,128)(2,1)S(1)} %shard_map.278.refs_0_), channel_id=1, source_target_pairs={{0,4},{4,8},{8,12},{12,14},{14,10},{10,6},{6,2},{2,0},{1,5},{5,9},... | collective-permute-start | bytes 1572872 | tf_op jit(solution)/shard_map/ppermute | solution.py:224
  358.8 19.5 %collective-permute-start.60 = (bf16[128,2048]{1,0:T(8,128)(2,1)S(1)}, bf16[128,2048]{1,0:T(8,128)(2,1)S(1)}, u32[]{:S(2)}, u32[]{:S(2)}) collective-permute-start(bf16[128,2048]{1,0:T(8,128)(2,1)S(1)} %shard_map.278.refs_0_), channel_id=1, source_target_pairs={{4,0},{8,4},{12,8},{14,12},{10,14},{6,10},{2,6},{0,2},{5,1},{9,5},... | collective-permute-start | bytes 1572872 | tf_op jit(solution)/shard_map/ppermute | solution.py:225
  358.8 18.1 %collective-permute-start.54 = (bf16[64,2048]{1,0:T(8,128)(2,1)S(1)}, bf16[64,2048]{1,0:T(8,128)(2,1)S(1)}, u32[]{:S(2)}, u32[]{:S(2)}) collective-permute-start(bf16[64,2048]{1,0:T(8,128)(2,1)S(1)} %slice.262), channel_id=1, source_target_pairs={{0,2},{2,0},{4,6},{6,4},{8,10},{10,8},{12,14},{14,12},{1,3},{3,1},... | collective-permute-start | bytes 786440 | tf_op jit(solution)/shard_map/ppermute | solution.py:46
  359.4 18.2 %collective-permute-start.55 = (bf16[64,2048]{1,0:T(8,128)(2,1)S(1)}, bf16[64,2048]{1,0:T(8,128)(2,1)S(1)}, u32[]{:S(2)}, u32[]{:S(2)}) collective-permute-start(bf16[64,2048]{1,0:T(8,128)(2,1)S(1)} %slice.264), channel_id=1, source_target_pairs={{0,1},{1,0},{2,3},{3,2},{4,5},{5,4},{6,7},{7,6},{8,9},{9,8},{10,11... | collective-permute-start | bytes 786440 | tf_op jit(solution)/shard_map/ppermute | solution.py:41
  378.4 18.6 %collective-permute-start.61 = (bf16[128,2048]{1,0:T(8,128)(2,1)S(1)}, bf16[128,2048]{1,0:T(8,128)(2,1)S(1)}, u32[]{:S(2)}, u32[]{:S(2)}) collective-permute-start(bf16[128,2048]{1,0:T(8,128)(2,1)S(1)} %collective-permute-done.59.refs_1_), channel_id=1, source_target_pairs={{0,4},{4,8},{8,12},{12,14},{14,10},{10,6},{6,2},{2,0},{1,5},{5,9},... | collective-permute-start | bytes 1572872 | tf_op jit(solution)/shard_map/ppermute | solution.py:224
  380.4 16.5 %collective-permute-start.62 = (bf16[128,2048]{1,0:T(8,128)(2,1)S(1)}, bf16[128,2048]{1,0:T(8,128)(2,1)S(1)}, u32[]{:S(2)}, u32[]{:S(2)}) collective-permute-start(bf16[128,2048]{1,0:T(8,128)(2,1)S(1)} %collective-permute-done.60.refs_2_), channel_id=1, source_target_pairs={{4,0},{8,4},{12,8},{14,12},{10,14},{6,10},{2,6},{0,2},{5,1},{9,5},... | collective-permute-start | bytes 1572872 | tf_op jit(solution)/shard_map/ppermute | solution.py:225
  441.0 14.0 %collective-permute-start.75 = (bf16[128,2048]{1,0:T(8,128)(2,1)S(1)}, bf16[128,2048]{1,0:T(8,128)(2,1)S(1)}, u32[]{:S(2)}, u32[]{:S(2)}) collective-permute-start(bf16[128,2048]{1,0:T(8,128)(2,1)S(1)} %collective-permute-done.61.refs_3_), channel_id=1, source_target_pairs={{0,4},{4,8},{8,12},{12,14},{14,10},{10,6},{6,2},{2,0},{1,5},{5,9},... | collective-permute-start | bytes 1572872 | tf_op jit(solution)/shard_map/ppermute | solution.py:224
  441.0 14.0 %collective-permute-start.76 = (bf16[128,2048]{1,0:T(8,128)(2,1)S(1)}, bf16[128,2048]{1,0:T(8,128)(2,1)S(1)}, u32[]{:S(2)}, u32[]{:S(2)}) collective-permute-start(bf16[128,2048]{1,0:T(8,128)(2,1)S(1)} %collective-permute-done.62.refs_4_), channel_id=1, source_target_pairs={{4,0},{8,4},{12,8},{14,12},{10,14},{6,10},{2,6},{0,2},{5,1},{9,5},... | collective-permute-start | bytes 1572872 | tf_op jit(solution)/shard_map/ppermute | solution.py:225
  462.6 15.1 %collective-permute-start.82 = (bf16[128,2048]{1,0:T(8,128)(2,1)S(1)}, bf16[128,2048]{1,0:T(8,128)(2,1)S(1)}, u32[]{:S(2)}, u32[]{:S(2)}) collective-permute-start(bf16[128,2048]{1,0:T(8,128)(2,1)S(1)} %get-tuple-element.270), channel_id=1, source_target_pairs={{0,1},{1,0},{2,3},{3,2},{4,5},{5,4},{6,7},{7,6},{8,9},{9,8},{10,11... | collective-permute-start | bytes 1572872 | tf_op jit(solution)/shard_map/ppermute | solution.py:41
  463.1 14.5 %collective-permute-start.83 = (bf16[128,2048]{1,0:T(8,128)(2,1)S(1)}, bf16[128,2048]{1,0:T(8,128)(2,1)S(1)}, u32[]{:S(2)}, u32[]{:S(2)}) collective-permute-start(bf16[128,2048]{1,0:T(8,128)(2,1)S(1)} %get-tuple-element.272), channel_id=1, source_target_pairs={{0,2},{2,0},{4,6},{6,4},{8,10},{10,8},{12,14},{14,12},{1,3},{3,1},... | collective-permute-start | bytes 1572872 | tf_op jit(solution)/shard_map/ppermute | solution.py:46
  494.0 41.6 %collective-permute-start.91 = (bf16[512,2048]{1,0:T(8,128)(2,1)S(1)}, bf16[512,2048]{1,0:T(8,128)(2,1)S(1)}, u32[]{:S(2)}, u32[]{:S(2)}) collective-permute-start(bf16[512,2048]{1,0:T(8,128)(2,1)S(1)} %copy-done.4), channel_id=1, source_target_pairs={{16,0},{17,1},{18,2},{19,3},{20,4},{21,5},{22,6},{23,7},{24,8},{25... | collective-permute-start | bytes 6291464 | tf_op jit(solution)/shard_map/ppermute | solution.py:1241
  495.5 40.1 %collective-permute-start.92 = (bf16[512,2048]{1,0:T(8,128)(2,1)S(1)}, bf16[512,2048]{1,0:T(8,128)(2,1)}, u32[]{:S(2)}, u32[]{:S(2)}) collective-permute-start(bf16[512,2048]{1,0:T(8,128)(2,1)S(1)} %get-tuple-element.284.refs_1_), channel_id=1, source_target_pairs={{0,16},{1,17},{2,18},{3,19},{4,20},{5,21},{6,22},{7,23},{8,24},{9,... | collective-permute-start | bytes 6291464 | tf_op jit(solution)/shard_map/ppermute | solution.py:1242
  500.0 35.6 %collective-permute-start.94 = (bf16[512,1536]{1,0:T(8,128)(2,1)S(1)}, bf16[512,1536]{1,0:T(8,128)(2,1)}, u32[]{:S(2)}, u32[]{:S(2)}) collective-permute-start(bf16[512,1536]{1,0:T(8,128)(2,1)S(1)} %get-tuple-element.286.refs_5_), channel_id=1, source_target_pairs={{0,16},{1,17},{2,18},{3,19},{4,20},{5,21},{6,22},{7,23},{8,24},{9,... | collective-permute-start | bytes 4718600 | tf_op jit(solution)/shard_map/ppermute | solution.py:1242
  515.8 19.9 %collective-permute-start.93 = (bf16[512,1536]{1,0:T(8,128)(2,1)S(1)}, bf16[512,1536]{1,0:T(8,128)(2,1)S(1)}, u32[]{:S(2)}, u32[]{:S(2)}) collective-permute-start(bf16[512,1536]{1,0:T(8,128)(2,1)S(1)} %get-tuple-element.285.refs_4_), channel_id=1, source_target_pairs={{16,0},{17,1},{18,2},{19,3},{20,4},{21,5},{22,6},{23,7},{24,8},{25... | collective-permute-start | bytes 4718600 | tf_op jit(solution)/shard_map/ppermute | solution.py:1241
  535.3 13.9 %collective-permute-start.90 = (bf16[128,2176]{1,0:T(8,128)(2,1)S(1)}, bf16[128,2176]{1,0:T(8,128)(2,1)S(1)}, u32[]{:S(2)}, u32[]{:S(2)}) collective-permute-start(bf16[128,2176]{1,0:T(8,128)(2,1)S(1)} %get-tuple-element.282), channel_id=1, source_target_pairs={{0,1},{1,0},{2,3},{3,2},{4,5},{5,4},{6,7},{7,6},{8,9},{9,8},{10,11... | collective-permute-start | bytes 1671176 | tf_op jit(solution)/shard_map/ppermute | solution.py:41
  535.6 13.8 %collective-permute-start.95 = (bf16[128,2176]{1,0:T(8,128)(2,1)S(1)}, bf16[128,2176]{1,0:T(8,128)(2,1)S(1)}, u32[]{:S(2)}, u32[]{:S(2)}) collective-permute-start(bf16[128,2176]{1,0:T(8,128)(2,1)S(1)} %get-tuple-element.292), channel_id=1, source_target_pairs={{0,2},{2,0},{4,6},{6,4},{8,10},{10,8},{12,14},{14,12},{1,3},{3,1},... | collective-permute-start | bytes 1671176 | tf_op jit(solution)/shard_map/ppermute | solution.py:46
  566.7 78.4 %collective-permute-start.119 = (bf16[512,768]{1,0:T(8,128)(2,1)}, bf16[512,768]{1,0:T(8,128)(2,1)}, u32[]{:S(2)}, u32[]{:S(2)}) collective-permute-start(bf16[512,768]{1,0:T(8,128)(2,1)} %copy-done.5), channel_id=1, source_target_pairs={{16,0},{17,1},{18,2},{19,3},{20,4},{21,5},{22,6},{23,7},{24,8},{25... | collective-permute-start | bytes 2359304 | tf_op jit(solution)/shard_map/ppermute | solution.py:1241
  568.0 81.2 %collective-permute-start.122 = (bf16[512,2048]{1,0:T(8,128)(2,1)S(1)}, bf16[512,2048]{1,0:T(8,128)(2,1)}, u32[]{:S(2)}, u32[]{:S(2)}) collective-permute-start(bf16[512,2048]{1,0:T(8,128)(2,1)S(1)} %get-tuple-element.337.refs_5_), channel_id=1, source_target_pairs={{0,16},{1,17},{2,18},{3,19},{4,20},{5,21},{6,22},{7,23},{8,24},{9,... | collective-permute-start | bytes 6291464 | tf_op jit(solution)/shard_map/ppermute | solution.py:1242
  573.3 76.2 %collective-permute-start.121 = (bf16[512,2048]{1,0:T(8,128)(2,1)}, bf16[512,2048]{1,0:T(8,128)(2,1)}, u32[]{:S(2)}, u32[]{:S(2)}) collective-permute-start(bf16[512,2048]{1,0:T(8,128)(2,1)} %copy-done), channel_id=1, source_target_pairs={{16,0},{17,1},{18,2},{19,3},{20,4},{21,5},{22,6},{23,7},{24,8},{25... | collective-permute-start | bytes 6291464 | tf_op jit(solution)/shard_map/ppermute | solution.py:1241
  574.6 19.3 %collective-permute-start.100 = (bf16[32,2048]{1,0:T(8,128)(2,1)}, bf16[32,2048]{1,0:T(8,128)(2,1)}, u32[]{:S(2)}, u32[]{:S(2)}) collective-permute-start(bf16[32,2048]{1,0:T(8,128)(2,1)} %get-tuple-element.303.refs_9_), channel_id=1, source_target_pairs={{0,16},{16,0},{1,17},{17,1},{2,18},{18,2},{3,19},{19,3},{4,20},{20... | collective-permute-start | bytes 393224 | tf_op jit(solution)/shard_map/ppermute | solution.py:37
  590.6 56.2 %collective-permute-start.120 = (bf16[512,768]{1,0:T(8,128)(2,1)}, bf16[512,768]{1,0:T(8,128)(2,1)}, u32[]{:S(2)}, u32[]{:S(2)}) collective-permute-start(bf16[512,768]{1,0:T(8,128)(2,1)} %copy-done.8), channel_id=1, source_target_pairs={{0,16},{1,17},{2,18},{3,19},{4,20},{5,21},{6,22},{7,23},{8,24},{9,... | collective-permute-start | bytes 2359304 | tf_op jit(solution)/shard_map/ppermute | solution.py:1242
  593.9 33.3 %collective-permute-start.102 = (bf16[64,2048]{1,0:T(8,128)(2,1)}, bf16[64,2048]{1,0:T(8,128)(2,1)}, u32[]{:S(2)}, u32[]{:S(2)}) collective-permute-start(bf16[64,2048]{1,0:T(8,128)(2,1)} %slice.268), channel_id=1, source_target_pairs={{0,4},{4,8},{8,12},{12,14},{14,10},{10,6},{6,2},{2,0},{1,5},{5,9},... | collective-permute-start | bytes 786440 | tf_op jit(solution)/shard_map/ppermute | solution.py:224
  636.5 34.1 %all-to-all-start.1 = ((bf16[128,8,256]{2,0,1:T(8,128)(2,1)}), bf16[128,8,256]{2,0,1:T(8,128)(2,1)}, u32[]{:S(2)}, u32[]{:S(2)}) async-start(bf16[128,8,256]{2,0,1:T(8,128)(2,1)} %bitcast.112), calls=%async_computation.1 | async-start | bytes 1048576 | tf_op jit(solution)/shard_map/all_to_all | solution.py:1276
  640.7 14.8 %collective-permute-start.104 = (bf16[64,2048]{1,0:T(8,128)(2,1)}, bf16[64,2048]{1,0:T(8,128)(2,1)S(1)}, u32[]{:S(2)}, u32[]{:S(2)}) collective-permute-start(bf16[64,2048]{1,0:T(8,128)(2,1)} %copy-done.121), channel_id=1, source_target_pairs={{0,16},{16,0},{1,17},{17,1},{2,18},{18,2},{3,19},{19,3},{4,20},{20... | collective-permute-start | bytes 786440 | tf_op jit(solution)/shard_map/ppermute | solution.py:37
  645.1 15.0 %collective-permute-start.107 = (bf16[32,2048]{1,0:T(8,128)(2,1)}, bf16[32,2048]{1,0:T(8,128)(2,1)S(1)}, u32[]{:S(2)}, u32[]{:S(2)}) collective-permute-start(bf16[32,2048]{1,0:T(8,128)(2,1)} %copy-done.128), channel_id=1, source_target_pairs={{0,4},{2,6},{4,0},{6,2},{8,12},{10,14},{12,8},{14,10},{1,5},{3,7},... | collective-permute-start | bytes 393224 | tf_op jit(solution)/shard_map/ppermute | solution.py:46
  646.9 18.1 %collective-permute-start.108 = (bf16[32,2048]{1,0:T(8,128)(2,1)}, bf16[32,2048]{1,0:T(8,128)(2,1)S(1)}, u32[]{:S(2)}, u32[]{:S(2)}) collective-permute-start(bf16[32,2048]{1,0:T(8,128)(2,1)} %copy-done.127), channel_id=1, source_target_pairs={{0,8},{2,10},{4,12},{6,14},{8,0},{10,2},{12,4},{14,6},{1,9},{3,11}... | collective-permute-start | bytes 393224 | tf_op jit(solution)/shard_map/ppermute | solution.py:46
  649.3 15.7 %collective-permute-start.109 = (bf16[32,2048]{1,0:T(8,128)(2,1)}, bf16[32,2048]{1,0:T(8,128)(2,1)S(1)}, u32[]{:S(2)}, u32[]{:S(2)}) collective-permute-start(bf16[32,2048]{1,0:T(8,128)(2,1)} %copy-done.126), channel_id=1, source_target_pairs={{0,12},{2,14},{4,8},{6,10},{8,4},{10,6},{12,0},{14,2},{1,13},{3,15... | collective-permute-start | bytes 393224 | tf_op jit(solution)/shard_map/ppermute | solution.py:46
  649.5 43.4 %collective-permute-start.117 = (bf16[128,2560]{1,0:T(8,128)(2,1)}, bf16[128,2560]{1,0:T(8,128)(2,1)}, u32[]{:S(2)}, u32[]{:S(2)}) collective-permute-start(bf16[128,2560]{1,0:T(8,128)(2,1)} %shard_map.301.refs_0_), channel_id=1, source_target_pairs={{0,4},{4,8},{8,12},{12,14},{14,10},{10,6},{6,2},{2,0},{1,5},{5,9},... | collective-permute-start | bytes 1966088 | tf_op jit(solution)/shard_map/ppermute | solution.py:224
  660.2 34.2 %collective-permute-start.118 = (bf16[128,2560]{1,0:T(8,128)(2,1)}, bf16[128,2560]{1,0:T(8,128)(2,1)}, u32[]{:S(2)}, u32[]{:S(2)}) collective-permute-start(bf16[128,2560]{1,0:T(8,128)(2,1)} %shard_map.301.refs_0_), channel_id=1, source_target_pairs={{4,0},{8,4},{12,8},{14,12},{10,14},{6,10},{2,6},{0,2},{5,1},{9,5},... | collective-permute-start | bytes 1966088 | tf_op jit(solution)/shard_map/ppermute | solution.py:225
  667.9 21.0 %collective-permute-start.113 = (f32[19,2048]{1,0:T(8,128)}, f32[19,2048]{1,0:T(8,128)}, u32[]{:S(2)}, u32[]{:S(2)}) collective-permute-start(f32[19,2048]{1,0:T(8,128)} %select_add_fusion), channel_id=1, source_target_pairs={{0,1},{1,0},{2,3},{3,2},{4,5},{5,4},{6,7},{7,6},{8,9},{9,8},{10,11... | collective-permute-start | bytes 466952 | tf_op jit(solution)/shard_map/ppermute | solution.py:41
  669.4 34.3 %collective-permute-start.111 = (bf16[2,32,2048]{2,1,0:T(8,128)(2,1)}, bf16[2,32,2048]{2,1,0:T(8,128)(2,1)}, u32[]{:S(2)}, u32[]{:S(2)}) collective-permute-start(bf16[2,32,2048]{2,1,0:T(8,128)(2,1)} %pad_maximum_fusion.3), channel_id=1, source_target_pairs={{0,1},{1,0},{2,3},{3,2},{4,5},{5,4},{6,7},{7,6},{8,9},{9,8},{10,11... | collective-permute-start | bytes 786440 | tf_op jit(solution)/shard_map/ppermute | solution.py:41
  670.6 60.2 %all-to-all-start = ((bf16[128,8,256]{2,0,1:T(8,128)(2,1)}), bf16[128,8,256]{2,0,1:T(8,128)(2,1)}, u32[]{:S(2)}, u32[]{:S(2)}) async-start(bf16[128,8,256]{2,0,1:T(8,128)(2,1)} %bitcast.91), calls=%async_computation | async-start | bytes 1048576 | tf_op jit(solution)/shard_map/all_to_all | solution.py:1276
  692.9 19.5 %collective-permute-start.123 = (bf16[128,2560]{1,0:T(8,128)(2,1)}, bf16[128,2560]{1,0:T(8,128)(2,1)S(1)}, u32[]{:S(2)}, u32[]{:S(2)}) collective-permute-start(bf16[128,2560]{1,0:T(8,128)(2,1)} %collective-permute-done.117.refs_1_), channel_id=1, source_target_pairs={{0,4},{4,8},{8,12},{12,14},{14,10},{10,6},{6,2},{2,0},{1,5},{5,9},... | collective-permute-start | bytes 1966088 | tf_op jit(solution)/shard_map/ppermute | solution.py:224
  694.4 19.8 %collective-permute-start.124 = (bf16[128,2560]{1,0:T(8,128)(2,1)}, bf16[128,2560]{1,0:T(8,128)(2,1)S(1)}, u32[]{:S(2)}, u32[]{:S(2)}) collective-permute-start(bf16[128,2560]{1,0:T(8,128)(2,1)} %collective-permute-done.118.refs_2_), channel_id=1, source_target_pairs={{4,0},{8,4},{12,8},{14,12},{10,14},{6,10},{2,6},{0,2},{5,1},{9,5},... | collective-permute-start | bytes 1966088 | tf_op jit(solution)/shard_map/ppermute | solution.py:225
  712.4 15.0 %collective-permute-start.125 = (bf16[128,2560]{1,0:T(8,128)(2,1)S(1)}, bf16[128,2560]{1,0:T(8,128)(2,1)S(1)}, u32[]{:S(2)}, u32[]{:S(2)}) collective-permute-start(bf16[128,2560]{1,0:T(8,128)(2,1)S(1)} %collective-permute-done.123.refs_3_), channel_id=1, source_target_pairs={{0,4},{4,8},{8,12},{12,14},{14,10},{10,6},{6,2},{2,0},{1,5},{5,9},... | collective-permute-start | bytes 1966088 | tf_op jit(solution)/shard_map/ppermute | solution.py:224
  714.2 15.2 %collective-permute-start.126 = (bf16[128,2560]{1,0:T(8,128)(2,1)S(1)}, bf16[128,2560]{1,0:T(8,128)(2,1)S(1)}, u32[]{:S(2)}, u32[]{:S(2)}) collective-permute-start(bf16[128,2560]{1,0:T(8,128)(2,1)S(1)} %collective-permute-done.124.refs_4_), channel_id=1, source_target_pairs={{4,0},{8,4},{12,8},{14,12},{10,14},{6,10},{2,6},{0,2},{5,1},{9,5},... | collective-permute-start | bytes 1966088 | tf_op jit(solution)/shard_map/ppermute | solution.py:225
  (236 other events, 3479.0 us)

commit v3 on v2

--- a/solution.py
+++ b/solution.py
@@ -404,13 +404,31 @@
     )(*ring.pieces, *small)
 
 
-def attend_back_kernel(plan, rows, layer, axis, experts, *refs):
+extra_rows = 16
+
+
+def split_rows(out, start, value):
+    size = value.shape[1]
+    out[start:] = jnp.zeros((extra_rows, out.shape[1]), bf16)
+    high = value.astype(bf16)
+    out[start : start + 1, :size] = high
+    out[start + 1 : start + 2, :size] = (value - high.astype(f32)).astype(bf16)
+
+
+def joined_rows(rows, start, size):
+    return rows[start : start + 1, :size].astype(f32) + rows[
+        start + 1 : start + 2, :size
+    ].astype(f32)
+
+
+def attend_back_kernel(plan, block_rows, layer, axis, experts, *refs):
     count = len(plan)
     pieces, refs = refs[:count], refs[count:]
     d_pieces, refs = refs[:4], refs[4:]
     raw_in, probs_in, tiny, cosine, sine = refs[:5]
-    d_attn, d_qkv, d_own, d_other, g_query_gain, g_key_gain, weights, sems = refs[5:]
+    d_attn, d_qkv, d_own, d_other, weights, sems = refs[5:]
     head = cosine.shape[1]
+    rows = raw_in.shape[0]
     start = layer * (experts + 4) + experts
     query_gain = from_heads(tiny[start + 2 : start + 3], axis, head // axis)
     key_gain = from_heads(tiny[start + 3 : start + 4], axis, head // axis)
@@ -420,12 +438,12 @@
     group = probs_in.shape[0]
     split = raw_in.shape[1]
     rest = weights.shape[1] - split
-    near = copy_pieces(pieces, plan, rows, pl.ds(split, rest), weights, sems)
-    far = copy_pieces(pieces, plan, rows, pl.ds(0, split), weights, sems, count)
+    near = copy_pieces(pieces, plan, block_rows, pl.ds(split, rest), weights, sems)
+    far = copy_pieces(pieces, plan, block_rows, pl.ds(0, split), weights, sems, count)
     start_all(near)
-    start_all(far)
     cos, sin = cosine[...], sine[...]
     wait_all(near)
+    start_all(far)
     d_mixed = dot(d_attn[...], weights[:, split:]).astype(bf16)
     k_raw = raw_in[:, group * head : (group + 1) * head]
     k_inverse = inverse_rms(k_raw)
@@ -453,33 +471,30 @@
         gain_sum = gain_sum + jnp.sum(d_gained * q_hat, axis=0, keepdims=True)
         d_hat = d_gained * query_gain
         d_q = q_inverse * (d_hat - q_hat * jnp.mean(d_hat * q_hat, axis=-1, keepdims=True))
-        d_qkv[:, span] = d_q.astype(bf16)
-    g_query_gain[...] = gain_sum
+        d_qkv[:rows, span] = d_q.astype(bf16)
     d_gained = rope_back(d_keys, cos, sin)
-    g_key_gain[...] = jnp.sum(d_gained * k_hat, axis=0, keepdims=True)
+    key_sum = jnp.sum(d_gained * k_hat, axis=0, keepdims=True)
+    split_rows(d_qkv, rows, jnp.concatenate([gain_sum, key_sum], axis=1))
     d_hat = d_gained * key_gain
     d_k = k_inverse * (d_hat - k_hat * jnp.mean(d_hat * k_hat, axis=-1, keepdims=True))
-    d_qkv[:, group * head : (group + 1) * head] = d_k.astype(bf16)
-    d_qkv[:, (group + 1) * head :] = d_values.astype(bf16)
+    d_qkv[:rows, group * head : (group + 1) * head] = d_k.astype(bf16)
+    d_qkv[:rows, (group + 1) * head :] = d_values.astype(bf16)
     wait_all(far)
-    d_normed = dot_cols(d_qkv[...], weights[:, :split])
+    d_normed = dot_cols(d_qkv[:rows], weights[:, :split])
     half = d_own.shape[0]
     d_own[...] = d_normed[:half]
     d_other[...] = d_normed[half:].astype(bf16)
 
 
 def attend_back(layer, ring, breadth, split, experts, pieces, raw, probs, tiny, tables):
-    head = tables[0].shape[1]
     width = pieces[0].shape[1]
     rows = raw.shape[0]
     small = (*pieces, raw, probs, tiny, tables[0], tables[1])
     shapes = (
         array((rows, width), bf16),
-        array(raw.shape, bf16),
+        array((rows + extra_rows, raw.shape[1]), bf16),
         array((rows // 2, width), f32),
         array((rows // 2, width), bf16),
-        array((1, head), f32),
-        array((1, head), f32),
     )
     count = len(ring.pieces)
     return pl.pallas_call(
@@ -488,36 +503,40 @@
         out_specs=tuple(full(one) for one in shapes),
         out_shape=shapes,
         scratch_shapes=[pltpu.VMEM((width, breadth), bf16), pltpu.SemaphoreType.DMA((2 * count,))],
-        compiler_params=kernel_params(26),
+        compiler_params=kernel_params(56),
         cost_estimate=cost(12 * rows * width * breadth, 2 * width * breadth),
     )(*ring.pieces, *small)
 
 
-def start_expert_weights(layer, refs, w_both, w_down, sems):
+def expert_copies(layer, refs, w_both, w_down, sems):
     is_own = lax.axis_index("section") == layer
-    units = w_down.shape[0] // refs[0].shape[0]
-    waits = []
-    for number in range(refs[0].shape[0]):
+    experts = refs[0].shape[0]
+    units = w_down.shape[0] // experts
+    groups = []
+    for number in range(experts):
         gate = pl.ds(2 * number * units, units)
         up = pl.ds((2 * number + 1) * units, units)
         targets = [w_both.at[:, gate], w_both.at[:, up], w_down.at[pl.ds(number * units, units)]]
-        makers = [
-            lambda ref, target=target, sem=sems.at[3 * number + i]: pltpu.make_async_copy(
-                ref.at[number], target, sem
+
+        def make(source, i, number=number, targets=targets):
+            return pltpu.make_async_copy(
+                source.at[number], targets[i], sems.at[3 * number + i]
             )
-            for i, target in enumerate(targets)
-        ]
-
-        @pl.when(is_own)
-        def _():
-            start_all([make(ref) for make, ref in zip(makers, refs[:3])])
-
-        @pl.when(jnp.logical_not(is_own))
-        def _():
-            start_all([make(ref) for make, ref in zip(makers, refs[3:])])
-
-        waits.append([make(ref) for make, ref in zip(makers, refs[:3])])
-    return waits
+
+        def start(which, make=make):
+            @pl.when(is_own)
+            def _():
+                start_all([make(refs[i], i) for i in which])
+
+            @pl.when(jnp.logical_not(is_own))
+            def _():
+                start_all([make(refs[3 + i], i) for i in which])
+
+        def wait(which, make=make):
+            wait_all([make(refs[i], i) for i in which])
+
+        groups.append((start, wait))
+    return groups
 
 
 def load_pieces(pieces, tile, scratch, sems):
@@ -545,19 +564,21 @@
     pieces, refs = refs[:count], refs[count:]
     weight_refs, ones, refs = refs[:6], refs[6], refs[7 + before :]
     outs, refs = refs[:count], refs[count:]
-    act_out, gates_out, rows_store, scaled_store = refs[:4]
-    rows_in, scaled, w_both, w_down, sems, weight_sems, store_sems = refs[4:]
+    act_store, gates_out, rows_store, scaled_store = refs[:4]
+    rows_in, scaled, w_both, w_down, sems, weight_sems, store_sems, act_out = refs[4:]
     width = w_both.shape[0]
     experts = ones.shape[0]
     units = w_down.shape[0] // experts
     loads = load_pieces(pieces, tile, rows_in, sems)
-    waits = start_expert_weights(layer, weight_refs, w_both, w_down, weight_sems)
+    weights = expert_copies(layer, weight_refs, w_both, w_down, weight_sems)
+    weights[0][0]((0, 1))
     place = pl.ds(tile * tile_rows, tile_rows)
     stores = [
         pltpu.make_async_copy(
             rows_in.at[:, pl.ds(0, width)], rows_store.at[place], store_sems.at[0]
         ),
         pltpu.make_async_copy(scaled, scaled_store.at[place], store_sems.at[1]),
+        pltpu.make_async_copy(act_out, act_store, store_sems.at[2]),
     ]
     wait_all(loads)
     stores[0].start()
@@ -565,7 +586,10 @@
     gates = extra + pltpu.roll(extra, lanes // 2, 1)
     gates_out[...] = gates
     for number in range(experts):
-        wait_all(waits[number])
+        weights[number][1]((0, 1))
+        if number + 1 < experts:
+            weights[number + 1][0]((0, 1))
+        weights[number][0]((2,))
         span = slice(2 * number * units, 2 * (number + 1) * units)
         act = dot(rows_in[:, :width], w_both[:, span])
         act_out[:, span] = act.astype(act_out.dtype)
@@ -574,6 +598,9 @@
         gate = jnp.sum(gates * ones[number : number + 1], axis=1, keepdims=True)
         scaled[:, number * units : (number + 1) * units] = (hidden.astype(f32) * gate).astype(bf16)
     stores[1].start()
+    stores[2].start()
+    for number in range(experts):
+        weights[number][1]((2,))
     step = width // 4
     for number in range(4):
         span = slice(number * step, (number + 1) * step)
@@ -589,7 +616,7 @@
         pltpu.VMEM((total_units, width), bf16),
         pltpu.SemaphoreType.DMA((count,)),
         pltpu.SemaphoreType.DMA((3 * experts,)),
-        pltpu.SemaphoreType.DMA((2,)),
+        pltpu.SemaphoreType.DMA((3,)),
     ]
 
 
@@ -608,7 +635,8 @@
     outs = pl.pallas_call(
         functools.partial(experts_kernel, count, layer, tile, len(stores)),
         in_specs=[anywhere] * (count + 6) + [full(ones)] + [anywhere] * len(stores),
-        out_specs=tuple(full(one) for one in shapes[: count + 2]) + (anywhere,) * 2,
+        out_specs=tuple(full(one) for one in shapes[:count])
+        + (anywhere, full(shapes[count + 1]), anywhere, anywhere),
         out_shape=shapes,
         scratch_shapes=expert_scratch(
             pieces[0].shape[1],
@@ -617,9 +645,10 @@
             pltpu.VMEM((tile_rows, total_units), bf16),
             count,
             experts,
-        ),
+        )
+        + [pltpu.VMEM(shapes[count].shape, shapes[count].dtype)],
         input_output_aliases={count + 7: count + 2, count + 8: count + 3} if stores else {},
-        compiler_params=kernel_params(32),
+        compiler_params=kernel_params(56),
         cost_estimate=cost(12 * tile_rows * width * total_units, 6 * width * total_units),
     )(*pieces, *weights, ones, *stores)
     return list(outs[:count]), outs[count : count + 2], outs[count + 2 :]
@@ -627,16 +656,19 @@
 
 def experts_back_kernel(count, layer, tile, before, *refs):
     pieces, refs = refs[:count], refs[count:]
-    weight_refs, ones, act, gates_in = refs[:6], refs[6], refs[7], refs[8]
+    weight_refs, ones, act_in, gates_in = refs[:6], refs[6], refs[7], refs[8]
     refs = refs[9 + before :]
     outs, refs = refs[:count], refs[count:]
     d_store, grad_store = refs[:2]
-    rows_in, d_act, w_both, w_down, sems, weight_sems, store_sems = refs[2:]
+    rows_in, d_act, w_both, w_down, sems, weight_sems, store_sems, act = refs[2:]
     width = w_both.shape[0]
     experts = ones.shape[0]
     units = w_down.shape[0] // experts
     loads = load_pieces(pieces, tile, rows_in, sems)
-    waits = start_expert_weights(layer, weight_refs, w_both, w_down, weight_sems)
+    weights = expert_copies(layer, weight_refs, w_both, w_down, weight_sems)
+    weights[0][0]((2,))
+    act_copy = pltpu.make_async_copy(act_in, act, store_sems.at[2])
+    act_copy.start()
     place = pl.ds(tile * tile_rows, tile_rows)
     stores = [
         pltpu.make_async_copy(rows_in, grad_store.at[place], store_sems.at[0]),
@@ -647,9 +679,14 @@
     gates = gates_in[...]
     placed = jnp.zeros_like(gates)
     for number in range(experts):
-        wait_all(waits[number])
+        weights[number][1]((2,))
+        if number + 1 < experts:
+            weights[number + 1][0]((2,))
+        weights[number][0]((0, 1))
         base = 2 * number * units
         plain = dot_cols(rows_in[...], w_down[number * units : (number + 1) * units])
+        if number == 0:
+            act_copy.wait()
         one = ones[number : number + 1]
         gate = jnp.sum(gates * one, axis=1, keepdims=True)
         gate_act = act[:, base : base + units].astype(f32)
@@ -663,6 +700,8 @@
         d_gate = d_hidden * up_act * (sigmoid + silu * (1.0 - sigmoid))
         d_act[:, base : base + units] = d_gate.astype(bf16)
     stores[1].start()
+    for number in range(experts):
+        weights[number][1]((0, 1))
     step = width // 4
     for number in range(4):
         span = slice(number * step, (number + 1) * step)
@@ -685,7 +724,7 @@
     outs = pl.pallas_call(
         functools.partial(experts_back_kernel, count, layer, tile, len(stores)),
         in_specs=[anywhere] * (count + 6)
-        + [full(ones), full(act), full(gates)]
+        + [full(ones), anywhere, full(gates)]
         + [anywhere] * len(stores),
         out_specs=tuple(full(one) for one in shapes[:count]) + (anywhere,) * 2,
         out_shape=shapes,
@@ -696,9 +735,10 @@
             pltpu.VMEM((tile_rows, 2 * total_units), bf16),
             count,
             experts,
-        ),
+        )
+        + [pltpu.VMEM(act.shape, act.dtype)],
         input_output_aliases={count + 9: count, count + 10: count + 1} if stores else {},
-        compiler_params=kernel_params(32),
+        compiler_params=kernel_params(56),
         cost_estimate=cost(12 * tile_rows * width * total_units, 6 * width * total_units),
     )(*pieces, *weights, ones, act, gates, *stores)
     return list(outs[:count]), outs[count:]
@@ -771,8 +811,8 @@
             pltpu.SemaphoreType.DMA((experts * len(shapes),)),
         ],
         input_output_aliases={8 + i: i for i in range(len(before))},
-        compiler_params=kernel_params(40),
-        cost_estimate=cost(4 * 10**9, 10**7),
+        compiler_params=kernel_params(56),
+        cost_estimate=cost(10**8, 10**5),
     )(*left, *right, *before)
 
 
@@ -796,58 +836,81 @@
 
 def out_grads_kernel(plan, rows, *refs):
     count = len(plan)
-    pieces, (d_cols, g_out, mixed, sems) = refs[:count], refs[count:]
+    pieces, (spread, g_out, mixed, d_cols, sems) = refs[:count], refs[count:]
     copies = copy_pieces(pieces, plan, rows, pl.ds(0, mixed.shape[1]), mixed, sems)
+    copies.append(pltpu.make_async_copy(spread.at[:, pl.ds(0, rows)], d_cols, sems.at[count]))
     start_all(copies)
     wait_all(copies)
-    g_out[...] = dot_rows(mixed[...], d_cols[...])
-
-
-def out_grads(ring, d_cols):
-    rows, columns = d_cols.shape
+    g_out[...] = dot_rows(mixed[...], d_cols[...].reshape(mixed.shape[0], d_cols.shape[2]))
+
+
+def out_grads(ring, spread):
+    blocks, _, columns = spread.shape
     breadth = ring.shard.shape[1]
     count = len(ring.pieces)
     shape = array((breadth, columns), f32)
+    total = blocks * ring.rows
     return pl.pallas_call(
         functools.partial(out_grads_kernel, ring.plan, ring.rows),
-        in_specs=[anywhere] * count + [full(d_cols)],
+        in_specs=[anywhere] * (count + 1),
         out_specs=full(shape),
         out_shape=shape,
-        scratch_shapes=[pltpu.VMEM((rows, breadth), bf16), pltpu.SemaphoreType.DMA((count,))],
-        compiler_params=kernel_params(24),
-        cost_estimate=cost(2 * rows * columns * breadth, 4 * columns * breadth),
-    )(*ring.pieces, d_cols)
-
-
-def stack_layer_kernel(zero, one, got, out):
+        scratch_shapes=[
+            pltpu.VMEM((total, breadth), bf16),
+            pltpu.VMEM((blocks, ring.rows, columns), bf16),
+            pltpu.SemaphoreType.DMA((count + 1,)),
+        ],
+        compiler_params=kernel_params(56),
+        cost_estimate=cost(10**8, 10**5),
+    )(*ring.pieces, spread)
+
+
+def stack_layer_kernel(sums, zero, one, got, out):
     core = lax.axis_index("section")
     columns = zero.shape[1]
-    half = zero.shape[0] // 2
+    rows = zero.shape[0] - (extra_rows if sums else 0)
+    half = rows // 2
     for number, own in ((0, zero), (1, one)):
 
         @pl.when(core == number)
         def _():
             here = slice(number * columns, (number + 1) * columns)
             there = slice((1 - number) * columns, (2 - number) * columns)
-            out[:, here] = own[...]
-            out[:half, there] = got[half:]
-            out[half:, there] = got[:half]
-
-
-def stack_layer(core, zero, one, got):
+            out[:rows, here] = own[:rows]
+            out[:half, there] = got[half:rows]
+            out[half:rows, there] = got[:half]
+            if sums:
+                total = joined_rows(own, rows, sums) + joined_rows(got, rows, sums)
+                split_rows(out, rows, total)
+
+
+def stack_layer(zero, one, got, sums=0):
     rows, columns = zero.shape
-    return simple(stack_layer_kernel, [array((rows, 2 * columns), zero.dtype)], zero, one, got)[0]
+    kernel = functools.partial(stack_layer_kernel, sums)
+    return simple(kernel, [array((rows, 2 * columns), zero.dtype)], zero, one, got)[0]
 
 
 def projection_grads_kernel(plan, rows, *refs):
     count = len(plan)
-    pieces, (normed, g_query, g_key, g_value, d_qkv, sems) = refs[:count], refs[count:]
+    pieces, (spread, late_spread, w_query, w_key, w_value), refs = (
+        refs[:count],
+        refs[count : count + 5],
+        refs[count + 5 :],
+    )
+    g_query, g_key, g_value, late, d_qkv, normed, parts, sems = refs
+    tokens = rows - extra_rows
     copies = copy_pieces(pieces, plan, rows, pl.ds(0, d_qkv.shape[1]), d_qkv, sems)
+    target = normed.at[:, pl.ds(0, tokens)]
+    copies.append(pltpu.make_async_copy(spread, target, sems.at[count]))
+    source = late_spread.at[:, pl.ds(tokens, parts.shape[1])]
+    copies.append(pltpu.make_async_copy(source, parts, sems.at[count + 1]))
     start_all(copies)
+    blocks, _, part = normed.shape
+    normed[:, tokens:] = jnp.zeros((blocks, extra_rows, part), bf16)
     wait_all(copies)
     wide = g_query.shape[1] // 2
     head = g_key.shape[1] // 2
-    both = dot_rows(normed[...], d_qkv[...])
+    both = dot_rows(normed[...].reshape(blocks * rows, part), d_qkv[...])
     for side in range(2):
         start = side * (wide + 2 * head)
         g_query[:, side * wide : (side + 1) * wide] = both[:, start : start + wide]
@@ -855,27 +918,47 @@
         g_value[:, side * head : (side + 1) * head] = both[
             :, start + wide + head : start + wide + 2 * head
         ]
-
-
-def projection_grads(ring, normed, head):
-    rows, part = normed.shape
+    products = (
+        jnp.sum(w_query[...].astype(f32) * g_query[...], axis=1, keepdims=True)
+        + jnp.sum(w_key[...].astype(f32) * g_key[...], axis=1, keepdims=True)
+        + jnp.sum(w_value[...].astype(f32) * g_value[...], axis=1, keepdims=True)
+    )
+    heads = jnp.zeros((1, 2 * head), f32)
+    for block in range(blocks):
+        heads = heads + joined_rows(d_qkv, block * rows + tokens, 2 * head)
+    late[...] = jnp.zeros_like(late)
+    late[8:, :part] = jnp.sum(parts[...].astype(f32), axis=0)
+    late[:1, :part] = jnp.transpose(jnp.broadcast_to(products, (part, lanes)))[:1]
+    late[1:2, : 2 * head] = heads
+
+
+def projection_grads(ring, spread, late_spread, weights, head):
+    blocks, tokens, part = spread.shape
+    size = late_spread.shape[1] - tokens
     breadth = ring.shard.shape[1]
     wide = breadth // 2 - 2 * head
     count = len(ring.pieces)
+    total = blocks * ring.rows
     shapes = (
         array((part, 2 * wide), f32),
         array((part, 2 * head), f32),
         array((part, 2 * head), f32),
+        array((8 + size, max(part, 2 * head)), f32),
     )
     return pl.pallas_call(
         functools.partial(projection_grads_kernel, ring.plan, ring.rows),
-        in_specs=[anywhere] * count + [full(normed)],
+        in_specs=[anywhere] * (count + 2) + [full(one) for one in weights],
         out_specs=tuple(full(one) for one in shapes),
         out_shape=shapes,
-        scratch_shapes=[pltpu.VMEM((rows, breadth), bf16), pltpu.SemaphoreType.DMA((count,))],
-        compiler_params=kernel_params(24),
-        cost_estimate=cost(2 * rows * part * breadth, 4 * rows * breadth),
-    )(*ring.pieces, normed)
+        scratch_shapes=[
+            pltpu.VMEM((total, breadth), bf16),
+            pltpu.VMEM((blocks, ring.rows, part), bf16),
+            pltpu.VMEM((blocks, size, part), bf16),
+            pltpu.SemaphoreType.DMA((count + 2,)),
+        ],
+        compiler_params=kernel_params(56),
+        cost_estimate=cost(20 * total * part * breadth, 4 * total * breadth),
+    )(*ring.pieces, spread, late_spread, *weights)
 
 
 def both_rows(shard):
@@ -999,17 +1082,15 @@
     return simple(kernel, shapes, *parts, grad, mid, tiny, gates, payload)
 
 
-def leave_kernel(row, kept, got, x, d_mid, tiny, d_out, g_gain):
+def leave_kernel(row, kept, got, x, d_mid, tiny, d_out):
     d_normed = kept[...] + got[...].astype(f32)
-    d_x, gain_sum = norm_back(x[...], tiny[row : row + 1], d_normed)
+    d_x, _ = norm_back(x[...], tiny[row : row + 1], d_normed)
     d_out[...] = (d_mid[...] + d_x).astype(bf16)
-    g_gain[...] = gain_sum
 
 
 def leave(layer, experts, kept, got, x, d_mid, tiny):
-    shapes = [array(x.shape, bf16), array((1, x.shape[1]), f32)]
     kernel = functools.partial(leave_kernel, layer * (experts + 4) + experts)
-    return simple(kernel, shapes, kept, got, x, d_mid, tiny)
+    return simple(kernel, [array(x.shape, bf16)], kept, got, x, d_mid, tiny)[0]
 
 
 def count_rows(tiles):
@@ -1037,19 +1118,68 @@
     return backs, stores
 
 
-def sum_small(own, other):
-    value = own + swap_core(other)
-    if not small_grid():
-        value = lax.psum(value, "tensor")
-        return lax.psum_scatter(value, "expert", scatter_dimension=1, tiled=True)
-    value = value + swap_x(value)
-    index = lax.axis_index("expert")
-    for bit in (4, 2, 1):
-        middle = value.shape[1] // 2
-        lower, upper = value[:, :middle], value[:, middle:]
-        high = (index & bit) != 0
-        value = jnp.where(high, upper, lower) + swap_e(jnp.where(high, lower, upper), bit)
-    return value
+def choose_kernel(zero, one, out):
+    core = lax.axis_index("section")
+    for number, own in enumerate((zero, one)):
+
+        @pl.when(core == number)
+        def _():
+            out[: own.shape[0]] = own[...]
+
+
+def small_kernel(router0, gain0, router1, gain1, own, other):
+    core = lax.axis_index("section")
+    layers = ((router0, gain0), (router1, gain1))
+    experts = router0.shape[0]
+    for number in range(2):
+
+        @pl.when(core == number)
+        def _():
+            for out, layer in ((own, number), (other, 1 - number)):
+                router, gain = layers[layer]
+                out[...] = jnp.zeros_like(out)
+                out[:experts] = router[...]
+                out[experts : experts + 1] = gain[...]
+
+
+def late_kernel(zero, one, own, got, out):
+    rows = zero.shape[0]
+    choose_kernel(zero, one, out)
+    out[rows:] = (own[...] + got[...]).astype(bf16)
+
+
+def other_layer_kernel(zero, one, out, sem):
+    core = lax.axis_index("section")
+    for number, source in enumerate((one, zero)):
+
+        @pl.when(core == number)
+        def _():
+            pltpu.make_async_copy(source, out, sem).start()
+
+    pltpu.make_async_copy(zero, out, sem).wait()
+
+
+def exchange(zero, one):
+    sent = pl.pallas_call(
+        other_layer_kernel,
+        in_specs=[anywhere] * 2,
+        out_specs=anywhere,
+        out_shape=array(zero.shape, zero.dtype),
+        scratch_shapes=[pltpu.SemaphoreType.DMA],
+        compiler_params=kernel_params(8),
+        cost_estimate=cost(1000, 1000),
+    )(zero, one)
+    got = swap_core(sent)
+    return zero, one, got, got
+
+
+def by_columns(value, split):
+    columns = value.shape[1] // split
+    return jnp.stack([value[:, i * columns : (i + 1) * columns] for i in range(split)])
+
+
+def to_owners(blocks):
+    return lax.all_to_all(blocks, "expert", split_axis=0, concat_axis=0, tiled=True)
 
 
 def body(
@@ -1202,7 +1332,7 @@
     tiles = gather.tiles()
     beside = grad_gather.far(tiles[-1][-1])
     mixed_got = swap_core(pick(mixed1, mixed0))
-    ring_mixed = Ring(stack_layer(core, mixed0, mixed1, mixed_got))
+    ring_mixed = Ring(stack_layer(mixed0, mixed1, mixed_got))
     ring_mixed.advance(tiles[-1][-1])
     outs1, kept1, stores1 = apply_experts(tiles, expert_weights, ones, 1)
 
@@ -1222,11 +1352,17 @@
     )
     d_pieces = both_rows(d_low)
     ring_mixed.advance(d_pieces[-1])
-    d_attn1, d_qkv1, d_own, d_other, g_query_gain1, g_key_gain1 = attend_back(
+
+    if small_grid():
+        rows_in = exchange(after(stores0[0], d_pieces[-1]), stores1[0])
+        early = (rows_in[2],)
+    else:
+        early = ()
+    d_attn1, d_qkv1, d_own, d_other = attend_back(
         1, ring1, breadth, split, experts, d_pieces, raw1, probs1, tiny, tables
     )
-    d_other = after(d_other, *ring_mixed.latest)
-    d_one, g_attn_gain1 = leave(1, experts, *own_rows(d_own, d_other), x_mid, d_mid, tiny)
+    d_other = after(d_other, *ring_mixed.latest, *early)
+    d_one = leave(1, experts, *own_rows(d_own, d_other), x_mid, d_mid, tiny)
 
     gather = Gather(d_one)
     gather.along_z()
@@ -1236,69 +1372,75 @@
     tiles = gather.tiles()
     backs, back_stores0 = apply_experts_back(tiles, expert_weights, ones, kept0, 0)
 
-    def with_got(zero, one):
-        if small_grid():
-            to_zero = lax.ppermute(zero, "section", [(1, 0)])
-            return zero, one, to_zero, lax.ppermute(one, "section", [(0, 1)])
-        got = swap_core(pick(one, zero))
-        return zero, one, got, got
-
-    rows_in = with_got(stores0[0], stores1[0])
-    scaled = with_got(stores0[1], stores1[1])
-    d_act = with_got(back_stores0[0], back_stores1[0])
-    grads = with_got(back_stores0[1], back_stores1[1])
+    if not small_grid():
+        rows_in = exchange(after(stores0[0], back_stores0[0]), stores1[0])
+    d_act = exchange(after(back_stores0[0], rows_in[2]), back_stores1[0])
     wide = wide_grads(per_device, rows_in, d_act)
     scatter = Scatter(backs)
-    scatter.far()
-    scatter.near(beside=wide[1])
+    normed_own = simple(
+        choose_kernel, [array(normed0.shape, bf16)], normed0, after(normed1, *scatter.far())
+    )[0]
+    normed_blocks = by_columns(normed_own, split)
+    scatter.near(beside=(*wide[1], normed_blocks))
     parts = scatter.along_z()
     parts[-1] = after(parts[-1], *wide[3])
     d_mid, d_low, g_router0, g_ffn_gain0 = unroute(
         0, parts, d_one, mid0, tiny, gates0, payload0
     )
     d_pieces = both_rows(d_low)
-    ring_mixed.advance(d_pieces[-1])
-    d_attn0, d_qkv0, d_own, d_other, g_query_gain0, g_key_gain0 = attend_back(
+    normed_spread = to_owners(after(normed_blocks, d_pieces[-1]))
+    out_parts = out_scatter.along_z(d_pieces[-1])
+    d_attn0, d_qkv0, d_own, d_other = attend_back(
         0, ring0, breadth, split, experts, d_pieces, raw0, probs0, tiny, tables
     )
-    d_other = after(d_other, *ring_mixed.latest)
-
-    qkv_got = swap_core(pick(d_qkv1, d_qkv0))
-    ring_d = Ring(stack_layer(core, d_qkv0, d_qkv1, qkv_got))
+
+    qkv_got = swap_core(pick(d_qkv1, after(d_qkv0, normed_spread, *out_parts)))
+    ring_d = Ring(stack_layer(d_qkv0, d_qkv1, qkv_got, 2 * head))
+    one_round = ring_d.advance()
+    d_other = after(d_other, ring_d.shard)
+    d_zero = leave(0, experts, *own_rows(d_own, d_other), x_in, d_mid, tiny)
+    scaled = exchange(after(stores0[1], ring_d.shard), stores1[1])
+    gate = ring_d.shard if small_grid() else scaled[2]
+    late = (scaled, exchange(after(back_stores0[1], gate), back_stores1[1]))
+    down = down_grads(per_device, *late)
     ring_d.advance()
-    out1 = finish(mid1, out_scatter.along_z(qkv_got))
-    d_zero, g_attn_gain0 = leave(0, experts, *own_rows(d_own, d_other), x_in, d_mid, tiny)
-    down = down_grads(per_device, scaled, (after(grads[0], qkv_got), *grads[1:]))
-    down_early, down_late = down[1], down[3]
-    ring_d.advance(*down_early)
-
-    def spread(value):
-        return lax.all_to_all(value, "expert", split_axis=1, concat_axis=0, tiled=True)
-
+    rows_small = -(-(experts + 1) // 16) * 16
+    small_own, small_other = simple(
+        small_kernel,
+        [array((rows_small, width), f32)] * 2,
+        after(g_router0, *one_round),
+        g_ffn_gain0,
+        g_router1,
+        g_ffn_gain1,
+    )
+    late_rows = simple(
+        late_kernel,
+        [array((2 * rows + rows_small, width), bf16)],
+        d_attn0,
+        d_attn1,
+        small_own,
+        swap_core(small_other),
+    )[0]
+    late_spread = to_owners(by_columns(late_rows, split))
+    three_rounds = ring_d.advance(*down[1])
+    ring_d.advance(*down[3])
+    ring_mixed.advance(*three_rounds)
+    g_out = out_grads(ring_mixed, late_spread)
+    out1 = finish(mid1, out_parts)
     end_own = pick(d_zero, out1)
     end_got = swap_core(pick(out1, d_zero))
-    normed_cols = spread(pick(normed0, normed1))
-    g_out = out_grads(ring_mixed, spread(pick(d_attn0, d_attn1)))
-    ring_d.advance(*down_late)
-    ring_d.advance()
-    g_query, g_key, g_value = projection_grads(ring_d, normed_cols, head)
+    projections = (w_query[0], key_matrix[0], value_matrix[0])
+    g_query, g_key, g_value, late = projection_grads(
+        ring_d, normed_spread, after(late_spread, *ring_mixed.latest), projections, head
+    )
     (g_gate, g_up), (g_down,) = wide[-1], down[-1]
 
-    def stacked(g_router, g_attn_gain, g_ffn_gain, g_query_gain, g_key_gain):
-        heads = cat(g_query_gain.reshape(split, share), g_key_gain.reshape(split, share), axis=1)
-        heads = jnp.pad(heads, ((0, 0), (0, part - 2 * share))).reshape(1, width)
-        return cat(g_router, g_attn_gain, g_ffn_gain, heads)
-
-    small = (
-        stacked(g_router0, g_attn_gain0, g_ffn_gain0, g_query_gain0, g_key_gain0),
-        stacked(g_router1, g_attn_gain1, g_ffn_gain1, g_query_gain1, g_key_gain1),
-    )
-    summed = sum_small(mine(small), theirs(small))
-    g_router = summed[:experts].T
-    g_attn_gain = summed[experts]
-    g_ffn_gain = summed[experts + 1]
-    g_query_gain = summed[experts + 2, :share]
-    g_key_gain = summed[experts + 2, share : 2 * share]
+    small = late + swap_x(late)
+    g_attn_gain = small[0, :part] / attn_gain[0].astype(f32)
+    g_query_gain = lax.dynamic_slice(small[1], (index * share,), (share,))
+    g_key_gain = lax.dynamic_slice(small[1], (head + index * share,), (share,))
+    g_router = small[8 : 8 + experts, :part].T
+    g_ffn_gain = small[8 + experts, :part]
 
     ends = jnp.stack([pick(end_own, end_got), pick(end_got, end_own)])
     ends_far = swap_x(ends)

time: 755 us -> 713 us (0.944)
  local copies, waits for them, and re-layouts: 87.3 us -> 50.6 us
  Pallas kernels: 116 us -> 145 us
  other arithmetic: 26 us -> 9.77 us
  starting transfers between devices: 160 us -> 146 us
    ppermute x16, waiting for transfers between devices: 15.2 us -> 122 us  [advance(): self.minus = lax.ppermute(after(minus, *gate), 'expert', down)]
    ppermute x16, waiting for transfers between devices: 140 us -> 45.1 us  [advance(): self.plus = lax.ppermute(after(plus, *gate), 'expert', up)]
    unnamed x341 -> x291, local copies, waits for them, and re-layouts: 68.4 us -> 38.1 us
    ppermute x8 -> x0, starting transfers between devices: 20.9 us -> none  [the longest x4 15.6 us: with_got(): return (zero, one, to_zero, lax.ppermute(one, 'section', [(0, 1)]))]
    ppermute x25, waiting for transfers between devices: 97.8 us -> 81.7 us  [swap_x(): return lax.ppermute(value, 'tensor', [(0, 1), (1, 0)])]
    ppermute x16, starting transfers between devices: 7.5 us -> 20.1 us  [advance(): self.minus = lax.ppermute(after(minus, *gate), 'expert', down)]
    pallas_call x8, Pallas kernels: 30.4 us -> 38.7 us  [run_grads(): pl.pallas_call(functools.partial(grads_kernel, (place, step), len(before)...]
    ppermute x16, starting transfers between devices: 29.3 us -> 21.5 us  [advance(): self.plus = lax.ppermute(after(plus, *gate), 'expert', up)]
  transfers between devices with their start and end apart: 131 -> 124, of which waited for: 64 -> 68; matrix products, arithmetic and copies ran while one was open for 6% -> 3% of each run, Pallas kernels for 15% -> 17%
where the time goes in v3:
time: 713 us; the launch traced here: 705 us
  waiting for transfers between devices  351 us (49%)
  starting transfers between devices  146 us (20%)
  Pallas kernels  145 us (20%)
  local copies, waits for them, and re-layouts  50.6 us (7%)
  other arithmetic  9.77 us (1%)
    ppermute x16, waiting for transfers between devices, advance(): self.minus = lax.ppermute(after(minus, *gate), 'expert', down)  122 us
    ppermute x40, waiting for transfers between devices, swap_e(): return lax.ppermute(value, 'expert', [(i, i ^ bits) for i in range(count)])  87.7 us
    ppermute x25, waiting for transfers between devices, swap_x(): return lax.ppermute(value, 'tensor', [(0, 1), (1, 0)])  81.7 us
    ppermute x40, starting transfers between devices, swap_e(): return lax.ppermute(value, 'expert', [(i, i ^ bits) for i in range(count)])  61.1 us
    ppermute x16, waiting for transfers between devices, advance(): self.plus = lax.ppermute(after(plus, *gate), 'expert', up)  45.1 us
    pallas_call x8, Pallas kernels, run_grads(): pl.pallas_call(functools.partial(grads_kernel, (place, step), len(before)...  38.7 us
    unnamed x291, local copies, waits for them, and re-layouts  38.1 us
    ppermute x25, starting transfers between devices, swap_x(): return lax.ppermute(value, 'tensor', [(0, 1), (1, 0)])  29.7 us
  transfers between devices with their start and end apart: 124, of which 68 were waited for; matrix products, arithmetic and copies ran while one was open for 3% of the time, Pallas kernels for 17%

profile of v3, /device:TPU:0, one launch (start us, length us, event | category | flops | bytes accessed | tf_op | source)
XLA Modules:
  0.0 705.1 jit_solution(17149371200543704318)
XLA Ops:
  15.0 27.7 %collective-permute-done.3.refs_2_ = bf16[256,2432]{1,0:T(8,128)(2,1)S(1)} collective-permute-done((bf16[256,2432]{1,0:T(8,128)(2,1)S(1)}, bf16[256,2432]{1,0:T(8,128)(2,1)S(1)}, u32[]{:S(2)}, u32[]{:S(2)}) %collective-permute-start.3) | collective-permute-done | bytes 1245216 | tf_op jit(solution)/shard_map/ppermute | solution.py:225
  48.7 26.1 %collective-permute-done.5.refs_4_ = bf16[256,2432]{1,0:T(8,128)(2,1)} collective-permute-done((bf16[256,2432]{1,0:T(8,128)(2,1)S(1)}, bf16[256,2432]{1,0:T(8,128)(2,1)}, u32[]{:S(2)}, u32[]{:S(2)}) %collective-permute-start.5) | collective-permute-done | bytes 1245216 | tf_op jit(solution)/shard_map/ppermute | solution.py:225
  78.6 24.9 %collective-permute-done.7.refs_6_ = bf16[256,2432]{1,0:T(8,128)(2,1)S(1)} collective-permute-done((bf16[256,2432]{1,0:T(8,128)(2,1)}, bf16[256,2432]{1,0:T(8,128)(2,1)S(1)}, u32[]{:S(2)}, u32[]{:S(2)}) %collective-permute-start.7) | collective-permute-done | bytes 1245216 | tf_op jit(solution)/shard_map/ppermute | solution.py:225
  107.2 10.8 %collective-permute-done.9.refs_8_ = bf16[128,2432]{1,0:T(8,128)(2,1)S(1)} collective-permute-done((bf16[128,2432]{1,0:T(8,128)(2,1)S(1)}, bf16[128,2432]{1,0:T(8,128)(2,1)S(1)}, u32[]{:S(2)}, u32[]{:S(2)}) %collective-permute-start.9) | collective-permute-done | bytes 622624 | tf_op jit(solution)/shard_map/ppermute | solution.py:225
  124.2 7.4 %shard_map.264 = (f32[128,2048]{1,0:T(8,128)S(1)}, bf16[128,2048]{1,0:T(8,128)(2,1)S(1)}, bf16[128,1024]{1,0:T(8,128)(2,1)S(1)}, f32[128,1280]{1,0:T(8,128)S(1)}...) custom-call(bf16[256,2432]{1,0:T(8,128)(2,1)S(1)} %fusion.1.refs_0_, ...), custom_call_target="tpu_custom_call" | custom-call | flops 7247757312 | bytes 9437184 | tf_op jit(solution)/shard_map/pallas_call | solution.py:396
  134.1 11.8 %collective-permute-done.11.refs_2_ = bf16[256,2304]{1,0:T(8,128)(2,1)} collective-permute-done((bf16[256,2304]{1,0:T(8,128)(2,1)}, bf16[256,2304]{1,0:T(8,128)(2,1)}, u32[]{:S(2)}, u32[]{:S(2)}) %collective-permute-start.11) | collective-permute-done | bytes 1179680 | tf_op jit(solution)/shard_map/ppermute | solution.py:225
  150.5 3.9 collective-permute-done.14.got
  156.8 6.5 collective-permute-done.18.refs_3_
  163.3 4.2 collective-permute-start.16
  172.2 3.7 collective-permute-start.19
  175.9 6.6 collective-permute-done.23.refs_1_
  182.5 6.4 collective-permute-start.24
  192.1 5.3 collective-permute-done.20.refs_4_
  200.3 11.6 %shard_map.268 = (bf16[128,2048]{1,0:T(8,128)(2,1)}, bf16[128,2048]{1,0:T(8,128)(2,1)}, bf16[128,2048]{1,0:T(8,128)(2,1)}, bf16[64,2048]{1,0:T(8,128)(2,1)}, bf1...) custom-call(bf16[128,2176]{1,0:T(8,128)(2,1)} %copy-done.22, ...), custom_call_target="tpu_custom_call" | custom-call | flops 9663676416 | bytes 9437184 | tf_op jit(solution)/shard_map/pallas_call | solution.py:635
  214.5 14.5 %collective-permute-done.28.top = bf16[64,2048]{1,0:T(8,128)(2,1)S(1)} collective-permute-done((bf16[64,2048]{1,0:T(8,128)(2,1)}, bf16[64,2048]{1,0:T(8,128)(2,1)S(1)}, u32[]{:S(2)}, u32[]{:S(2)}) %collective-permute-start.28) | collective-permute-done | bytes 262176 | tf_op jit(solution)/shard_map/ppermute | solution.py:46
  234.7 7.4 %collective-permute-done.30.from_x = bf16[128,2048]{1,0:T(8,128)(2,1)S(1)} collective-permute-done((bf16[128,2048]{1,0:T(8,128)(2,1)S(1)}, bf16[128,2048]{1,0:T(8,128)(2,1)S(1)}, u32[]{:S(2)}, u32[]{:S(2)}) %collective-permute-start.30) | collective-permute-done | bytes 524320 | tf_op jit(solution)/shard_map/ppermute | solution.py:41
  250.1 3.8 collective-permute-done.33.refs_2_
  254.4 3.2 collective-permute-start.35
  258.9 20.2 %collective-permute-done.35.refs_5_ = bf16[256,2304]{1,0:T(8,128)(2,1)S(1)} collective-permute-done((bf16[256,2304]{1,0:T(8,128)(2,1)S(1)}, bf16[256,2304]{1,0:T(8,128)(2,1)S(1)}, u32[]{:S(2)}, u32[]{:S(2)}) %collective-permute-start.35) | collective-permute-done | bytes 1179680 | tf_op jit(solution)/shard_map/ppermute | solution.py:224
  283.4 3.0 collective-permute-start.43
  287.8 4.0 collective-permute-done.37.refs_7_
  291.9 3.5 collective-permute-done.38.refs_8_
  295.4 7.1 %shard_map.273 = (bf16[128,2048]{1,0:T(8,128)(2,1)S(1)}, bf16[128,1024]{1,0:T(8,128)(2,1)S(1)}, f32[128,1280]{1,0:T(8,128)S(1)}, f32[8,128,128]{2,1,0:T(8,128)S(...) custom-call(bf16[256,2304]{1,0:T(8,128)(2,1)} %get-tuple-element.184.refs_0_, ...), custom_call_target="tpu_custom_call" | custom-call | flops 7247757312 | bytes 9437184 | tf_op jit(solution)/shard_map/pallas_call | solution.py:396
  310.3 13.4 %collective-permute-done.48.got = bf16[32,2048]{1,0:T(8,128)(2,1)S(1)} collective-permute-done((bf16[32,2048]{1,0:T(8,128)(2,1)}, bf16[32,2048]{1,0:T(8,128)(2,1)S(1)}, u32[]{:S(2)}, u32[]{:S(2)}) %collective-permute-start.48) | collective-permute-done | bytes 131104 | tf_op jit(solution)/shard_map/ppermute | solution.py:41
  329.4 4.2 collective-permute-start.50
  333.7 8.9 %collective-permute-done.50.refs_2_ = bf16[32,2176]{1,0:T(8,128)(2,1)S(1)} collective-permute-done((bf16[32,2176]{1,0:T(8,128)(2,1)S(1)}, bf16[32,2176]{1,0:T(8,128)(2,1)S(1)}, u32[]{:S(2)}, u32[]{:S(2)}) %collective-permute-start.50) | collective-permute-done | bytes 139296 | tf_op jit(solution)/shard_map/ppermute | solution.py:46
  344.4 11.2 %collective-permute-done.56.refs_1_ = bf16[128,2176]{1,0:T(8,128)(2,1)S(1)} collective-permute-done((bf16[128,2176]{1,0:T(8,128)(2,1)S(1)}, bf16[128,2176]{1,0:T(8,128)(2,1)S(1)}, u32[]{:S(2)}, u32[]{:S(2)}) %collective-permute-start.56) | collective-permute-done | bytes 557088 | tf_op jit(solution)/shard_map/ppermute | solution.py:41
  368.8 11.3 %shard_map.277 = (bf16[128,2048]{1,0:T(8,128)(2,1)}, bf16[128,2048]{1,0:T(8,128)(2,1)}, bf16[128,2048]{1,0:T(8,128)(2,1)}, bf16[64,2048]{1,0:T(8,128)(2,1)}, bf1...) custom-call(bf16[128,2176]{1,0:T(8,128)(2,1)} %copy-done.23, ...), custom_call_target="tpu_custom_call" | custom-call | flops 9663676416 | bytes 9437184 | tf_op jit(solution)/shard_map/pallas_call | solution.py:635
  384.9 13.6 %shard_map.279 = (bf16[128,2176]{1,0:T(8,128)(2,1)}, bf16[128,2176]{1,0:T(8,128)(2,1)}, bf16[128,2176]{1,0:T(8,128)(2,1)}, bf16[64,2176]{1,0:T(8,128)(2,1)}, bf1...) custom-call(bf16[128,2048]{1,0:T(8,128)(2,1)} %shard_map.272.refs_0_, ...), custom_call_target="tpu_custom_call" | custom-call | flops 9663676416 | bytes 9437184 | tf_op jit(solution)/shard_map/pallas_call | solution.py:724
  399.6 5.8 collective-permute-done.64.bottom
  409.7 8.5 %collective-permute-done.65.from_x = bf16[128,2176]{1,0:T(8,128)(2,1)S(1)} collective-permute-done((bf16[128,2176]{1,0:T(8,128)(2,1)S(1)}, bf16[128,2176]{1,0:T(8,128)(2,1)S(1)}, u32[]{:S(2)}, u32[]{:S(2)}) %collective-permute-start.65) | collective-permute-done | bytes 557088 | tf_op jit(solution)/shard_map/ppermute | solution.py:41
  418.2 2.8 collective-permute-done.66.from_y
  423.1 4.5 collective-permute-start.69
  430.7 3.5 collective-permute-done.67.refs_1_
  436.1 3.6 collective-permute-done.72.refs_10_
  446.5 10.0 %shard_map.283 = (bf16[128,2048]{1,0:T(8,128)(2,1)}, bf16[144,1280]{1,0:T(8,128)(2,1)}, f32[64,2048]{1,0:T(8,128)}, bf16[64,2048]{1,0:T(8,128)(2,1)}) custom-call(bf16[256,2304]{1,0:T(8,128)(2,1)} %get-tuple-element.184.refs_0_, bf16[256,2304]{1,0:T(8,128)(2,1)} %collective-permute-done.10.refs_1_, bf16[256,2304]{1,0:T(8,128)(2,1)} %collective-permute-done.11.refs_2_, ...), custom_call_target="tpu_custom_call" | custom-call | flops 7247757312 | bytes 9437184 | tf_op jit(solution)/shard_map/pallas_call | solution.py:500
  462.2 4.0 collective-permute-done.79.got
  472.9 3.8 collective-permute-done.82.refs_3_
  476.7 5.0 collective-permute-done.81.refs_2_
  484.4 10.5 %collective-permute-done.86.refs_2_ = bf16[128,2048]{1,0:T(8,128)(2,1)S(1)} collective-permute-done((bf16[128,2048]{1,0:T(8,128)(2,1)S(1)}, bf16[128,2048]{1,0:T(8,128)(2,1)S(1)}, u32[]{:S(2)}, u32[]{:S(2)}) %collective-permute-start.86) | collective-permute-done | bytes 524320 | tf_op jit(solution)/shard_map/ppermute | solution.py:46
  497.5 4.5 collective-permute-done.88.refs_4_
  504.1 13.6 %shard_map.290 = (bf16[128,2176]{1,0:T(8,128)(2,1)}, bf16[128,2176]{1,0:T(8,128)(2,1)}, bf16[128,2176]{1,0:T(8,128)(2,1)}, bf16[64,2176]{1,0:T(8,128)(2,1)}, bf1...) custom-call(bf16[128,2048]{1,0:T(8,128)(2,1)} %copy-done.43, ...), custom_call_target="tpu_custom_call" | custom-call | flops 9663676416 | bytes 9437184 | tf_op jit(solution)/shard_map/pallas_call | solution.py:724
  521.3 3.3 collective-permute-done.89.top
  532.9 5.8 shard_map.293
  538.6 5.8 shard_map.294
  549.2 5.8 shard_map.297
  554.9 5.8 shard_map.298
  564.0 3.5 collective-permute-done.97.refs_10_
  568.8 4.4 all-to-all-start
  578.3 9.8 %shard_map.300 = (bf16[128,2048]{1,0:T(8,128)(2,1)}, bf16[144,1280]{1,0:T(8,128)(2,1)}, f32[64,2048]{1,0:T(8,128)}, bf16[64,2048]{1,0:T(8,128)(2,1)}) custom-call(bf16[256,2432]{1,0:T(8,128)(2,1)} %copy-done.14, bf16[256,2432]{1,0:T(8,128)(2,1)} %collective-permute-done.2.refs_1_, bf16[256,2432]{1,0:T(8,128)(2,1)} %copy-done.78, ...), custom_call_target="tpu_custom_call" | custom-call | flops 7247757312 | bytes 9437184 | tf_op jit(solution)/shard_map/pallas_call | solution.py:500
  588.2 9.3 %collective-permute-done.101.refs_2_ = bf16[32,2048]{1,0:T(8,128)(2,1)S(1)} collective-permute-done((bf16[32,2048]{1,0:T(8,128)(2,1)S(1)}, bf16[32,2048]{1,0:T(8,128)(2,1)S(1)}, u32[]{:S(2)}, u32[]{:S(2)}) %collective-permute-start.101) | collective-permute-done | bytes 131104 | tf_op jit(solution)/shard_map/ppermute | solution.py:46
  612.9 6.9 collective-permute-done.109.refs_2_
  629.0 4.6 all-to-all-start.1
  635.0 3.9 shard_map.307.refs_8_
  638.9 4.0 shard_map.308.refs_8_
  647.5 3.9 shard_map.309.refs_8_
  651.4 3.9 shard_map.310
  655.3 10.9 %collective-permute-done.114.refs_5_ = bf16[144,2560]{1,0:T(8,128)(2,1)} collective-permute-done((bf16[144,2560]{1,0:T(8,128)(2,1)}, bf16[144,2560]{1,0:T(8,128)(2,1)}, u32[]{:S(2)}, u32[]{:S(2)}) %collective-permute-start.114) | collective-permute-done | bytes 737312 | tf_op jit(solution)/shard_map/ppermute | solution.py:224
  666.9 4.3 collective-permute-start.119
  677.5 3.5 collective-permute-done.120.refs_8_
  681.0 2.7 collective-permute-done.116.refs_7_
  683.7 4.3 collective-permute-done.117.refs_8_
  688.1 7.6 %shard_map.313 = (f32[256,2048]{1,0:T(8,128)}, f32[256,256]{1,0:T(8,128)}, f32[256,256]{1,0:T(8,128)}, f32[40,256]{1,0:T(8,128)}) custom-call(bf16[144,2560]{1,0:T(8,128)(2,1)} %copy-done.20, bf16[144,2560]{1,0:T(8,128)(2,1)} %collective-permute-done.108.refs_1_, bf16[144,2560]{1,0:T(8,128)(2,1)} %collective-permute-done.109.refs_2_, ...), custom_call_target="tpu_custom_call" | custom-call | flops 15099494400 | bytes 11796480 | tf_op jit(solution)/shard_map/pallas_call | solution.py:948
  697.7 5.1 shard_map.314
  (607 shorter events, 216.7 us)
Async XLA Ops:
  12.2 30.5 %collective-permute-start.3 = (bf16[256,2432]{1,0:T(8,128)(2,1)S(1)}, bf16[256,2432]{1,0:T(8,128)(2,1)S(1)}, u32[]{:S(2)}, u32[]{:S(2)}) collective-permute-start(bf16[256,2432]{1,0:T(8,128)(2,1)S(1)} %fusion.1.refs_0_), channel_id=1, source_target_pairs={{4,0},{8,4},{12,8},{14,12},{10,14},{6,10},{2,6},{0,2},{5,1},{9,5},... | collective-permute-start | bytes 3735560 | tf_op jit(solution)/shard_map/ppermute | solution.py:225
  14.9 29.3 %collective-permute-start.2 = (bf16[256,2432]{1,0:T(8,128)(2,1)S(1)}, bf16[256,2432]{1,0:T(8,128)(2,1)}, u32[]{:S(2)}, u32[]{:S(2)}) collective-permute-start(bf16[256,2432]{1,0:T(8,128)(2,1)S(1)} %fusion.1.refs_0_), channel_id=1, source_target_pairs={{0,4},{4,8},{8,12},{12,14},{14,10},{10,6},{6,2},{2,0},{1,5},{5,9},... | collective-permute-start | bytes 3735560 | tf_op jit(solution)/shard_map/ppermute | solution.py:224
  44.3 153.0 %collective-permute-start.26 = (bf16[2,2048,384]{2,1,0:T(8,128)(2,1)}, bf16[2,2048,384]{2,1,0:T(8,128)(2,1)}, u32[]{:S(2)}, u32[]{:S(2)}) collective-permute-start(bf16[2,2048,384]{2,1,0:T(8,128)(2,1)} %bitcast.161), channel_id=1, source_target_pairs={{0,16},{16,0},{1,17},{17,1},{2,18},{18,2},{3,19},{19,3},{4,20},{20... | collective-permute-start | bytes 9437192 | tf_op jit(solution)/shard_map/ppermute | solution.py:37
  44.9 154.7 %collective-permute-start.25 = (bf16[2,2048,384]{2,1,0:T(8,128)(2,1)}, bf16[2,2048,384]{2,1,0:T(8,128)(2,1)}, u32[]{:S(2)}, u32[]{:S(2)}) collective-permute-start(bf16[2,2048,384]{2,1,0:T(8,128)(2,1)} %bitcast.156), channel_id=1, source_target_pairs={{0,16},{16,0},{1,17},{17,1},{2,18},{18,2},{3,19},{19,3},{4,20},{20... | collective-permute-start | bytes 9437192 | tf_op jit(solution)/shard_map/ppermute | solution.py:37
  44.9 154.7 %collective-permute-start.27 = (bf16[2,384,2048]{2,1,0:T(8,128)(2,1)}, bf16[2,384,2048]{2,1,0:T(8,128)(2,1)}, u32[]{:S(2)}, u32[]{:S(2)}) collective-permute-start(bf16[2,384,2048]{2,1,0:T(8,128)(2,1)} %bitcast.166), channel_id=1, source_target_pairs={{0,16},{16,0},{1,17},{17,1},{2,18},{18,2},{3,19},{19,3},{4,20},{20... | collective-permute-start | bytes 9437192 | tf_op jit(solution)/shard_map/ppermute | solution.py:37
  45.4 29.5 %collective-permute-start.5 = (bf16[256,2432]{1,0:T(8,128)(2,1)S(1)}, bf16[256,2432]{1,0:T(8,128)(2,1)}, u32[]{:S(2)}, u32[]{:S(2)}) collective-permute-start(bf16[256,2432]{1,0:T(8,128)(2,1)S(1)} %collective-permute-done.3.refs_2_), channel_id=1, source_target_pairs={{4,0},{8,4},{12,8},{14,12},{10,14},{6,10},{2,6},{0,2},{5,1},{9,5},... | collective-permute-start | bytes 3735560 | tf_op jit(solution)/shard_map/ppermute | solution.py:225
  46.9 29.5 %collective-permute-start.4 = (bf16[256,2432]{1,0:T(8,128)(2,1)}, bf16[256,2432]{1,0:T(8,128)(2,1)}, u32[]{:S(2)}, u32[]{:S(2)}) collective-permute-start(bf16[256,2432]{1,0:T(8,128)(2,1)} %collective-permute-done.2.refs_1_), channel_id=1, source_target_pairs={{0,4},{4,8},{8,12},{12,14},{14,10},{10,6},{6,2},{2,0},{1,5},{5,9},... | collective-permute-start | bytes 3735560 | tf_op jit(solution)/shard_map/ppermute | solution.py:224
  74.8 28.7 %collective-permute-start.7 = (bf16[256,2432]{1,0:T(8,128)(2,1)}, bf16[256,2432]{1,0:T(8,128)(2,1)S(1)}, u32[]{:S(2)}, u32[]{:S(2)}) collective-permute-start(bf16[256,2432]{1,0:T(8,128)(2,1)} %collective-permute-done.5.refs_4_), channel_id=1, source_target_pairs={{4,0},{8,4},{12,8},{14,12},{10,14},{6,10},{2,6},{0,2},{5,1},{9,5},... | collective-permute-start | bytes 3735560 | tf_op jit(solution)/shard_map/ppermute | solution.py:225
  76.4 28.8 %collective-permute-start.6 = (bf16[256,2432]{1,0:T(8,128)(2,1)}, bf16[256,2432]{1,0:T(8,128)(2,1)}, u32[]{:S(2)}, u32[]{:S(2)}) collective-permute-start(bf16[256,2432]{1,0:T(8,128)(2,1)} %collective-permute-done.4.refs_3_), channel_id=1, source_target_pairs={{0,4},{4,8},{8,12},{12,14},{14,10},{10,6},{6,2},{2,0},{1,5},{5,9},... | collective-permute-start | bytes 3735560 | tf_op jit(solution)/shard_map/ppermute | solution.py:224
  103.6 14.4 %collective-permute-start.9 = (bf16[128,2432]{1,0:T(8,128)(2,1)S(1)}, bf16[128,2432]{1,0:T(8,128)(2,1)S(1)}, u32[]{:S(2)}, u32[]{:S(2)}) collective-permute-start(bf16[128,2432]{1,0:T(8,128)(2,1)S(1)} %slice.284), channel_id=1, source_target_pairs={{4,0},{8,4},{12,8},{14,12},{10,14},{6,10},{2,6},{0,2},{5,1},{9,5},... | collective-permute-start | bytes 1867784 | tf_op jit(solution)/shard_map/ppermute | solution.py:225
  106.4 14.1 %collective-permute-start.8 = (bf16[128,2432]{1,0:T(8,128)(2,1)S(1)}, bf16[128,2432]{1,0:T(8,128)(2,1)S(1)}, u32[]{:S(2)}, u32[]{:S(2)}) collective-permute-start(bf16[128,2432]{1,0:T(8,128)(2,1)S(1)} %slice.283), channel_id=1, source_target_pairs={{0,4},{4,8},{8,12},{12,14},{14,10},{10,6},{6,2},{2,0},{1,5},{5,9},... | collective-permute-start | bytes 1867784 | tf_op jit(solution)/shard_map/ppermute | solution.py:224
  120.5 25.4 %collective-permute-start.11 = (bf16[256,2304]{1,0:T(8,128)(2,1)}, bf16[256,2304]{1,0:T(8,128)(2,1)}, u32[]{:S(2)}, u32[]{:S(2)}) collective-permute-start(bf16[256,2304]{1,0:T(8,128)(2,1)} %get-tuple-element.184.refs_0_), channel_id=1, source_target_pairs={{4,0},{8,4},{12,8},{14,12},{10,14},{6,10},{2,6},{0,2},{5,1},{9,5},... | collective-permute-start | bytes 3538952 | tf_op jit(solution)/shard_map/ppermute | solution.py:225
  122.1 25.1 %collective-permute-start.10 = (bf16[256,2304]{1,0:T(8,128)(2,1)}, bf16[256,2304]{1,0:T(8,128)(2,1)}, u32[]{:S(2)}, u32[]{:S(2)}) collective-permute-start(bf16[256,2304]{1,0:T(8,128)(2,1)} %get-tuple-element.184.refs_0_), channel_id=1, source_target_pairs={{0,4},{4,8},{8,12},{12,14},{14,10},{10,6},{6,2},{2,0},{1,5},{5,9},... | collective-permute-start | bytes 3538952 | tf_op jit(solution)/shard_map/ppermute | solution.py:224
  172.2 16.7 %collective-permute-start.19 = (bf16[128,2176]{1,0:T(8,128)(2,1)S(1)}, bf16[128,2176]{1,0:T(8,128)(2,1)}, u32[]{:S(2)}, u32[]{:S(2)}) collective-permute-start(bf16[128,2176]{1,0:T(8,128)(2,1)S(1)} %shard_map.267.refs_0_), channel_id=1, source_target_pairs={{0,2},{2,0},{4,6},{6,4},{8,10},{10,8},{12,14},{14,12},{1,3},{3,1},... | collective-permute-start | bytes 1671176 | tf_op jit(solution)/shard_map/ppermute | solution.py:46
  182.5 17.1 %collective-permute-start.24 = (bf16[64,2176]{1,0:T(8,128)(2,1)S(1)}, bf16[64,2176]{1,0:T(8,128)(2,1)S(1)}, u32[]{:S(2)}, u32[]{:S(2)}) collective-permute-start(bf16[64,2176]{1,0:T(8,128)(2,1)S(1)} %slice.292), channel_id=1, source_target_pairs={{0,2},{2,0},{4,6},{6,4},{8,10},{10,8},{12,14},{14,12},{1,3},{3,1},... | collective-permute-start | bytes 835592 | tf_op jit(solution)/shard_map/ppermute | solution.py:46
  197.4 44.7 %collective-permute-start.21 = (bf16[256,2304]{1,0:T(8,128)(2,1)}, bf16[256,2304]{1,0:T(8,128)(2,1)S(1)}, u32[]{:S(2)}, u32[]{:S(2)}) collective-permute-start(bf16[256,2304]{1,0:T(8,128)(2,1)} %collective-permute-done.10.refs_1_), channel_id=1, source_target_pairs={{0,4},{4,8},{8,12},{12,14},{14,10},{10,6},{6,2},{2,0},{1,5},{5,9},... | collective-permute-start | bytes 3538952 | tf_op jit(solution)/shard_map/ppermute | solution.py:224
  197.4 44.7 %collective-permute-start.22 = (bf16[256,2304]{1,0:T(8,128)(2,1)}, bf16[256,2304]{1,0:T(8,128)(2,1)S(1)}, u32[]{:S(2)}, u32[]{:S(2)}) collective-permute-start(bf16[256,2304]{1,0:T(8,128)(2,1)} %collective-permute-done.11.refs_2_), channel_id=1, source_target_pairs={{4,0},{8,4},{12,8},{14,12},{10,14},{6,10},{2,6},{0,2},{5,1},{9,5},... | collective-permute-start | bytes 3538952 | tf_op jit(solution)/shard_map/ppermute | solution.py:225
  211.9 17.0 %collective-permute-start.28 = (bf16[64,2048]{1,0:T(8,128)(2,1)}, bf16[64,2048]{1,0:T(8,128)(2,1)S(1)}, u32[]{:S(2)}, u32[]{:S(2)}) collective-permute-start(bf16[64,2048]{1,0:T(8,128)(2,1)} %get-tuple-element.202), channel_id=1, source_target_pairs={{0,2},{2,0},{4,6},{6,4},{8,10},{10,8},{12,14},{14,12},{1,3},{3,1},... | collective-permute-start | bytes 786440 | tf_op jit(solution)/shard_map/ppermute | solution.py:46
  213.1 15.9 %collective-permute-start.29 = (bf16[64,2048]{1,0:T(8,128)(2,1)}, bf16[64,2048]{1,0:T(8,128)(2,1)S(1)}, u32[]{:S(2)}, u32[]{:S(2)}) collective-permute-start(bf16[64,2048]{1,0:T(8,128)(2,1)} %get-tuple-element.204), channel_id=1, source_target_pairs={{0,1},{1,0},{2,3},{3,2},{4,5},{5,4},{6,7},{7,6},{8,9},{9,8},{10,11... | collective-permute-start | bytes 786440 | tf_op jit(solution)/shard_map/ppermute | solution.py:41
  254.4 24.7 %collective-permute-start.35 = (bf16[256,2304]{1,0:T(8,128)(2,1)S(1)}, bf16[256,2304]{1,0:T(8,128)(2,1)S(1)}, u32[]{:S(2)}, u32[]{:S(2)}) collective-permute-start(bf16[256,2304]{1,0:T(8,128)(2,1)S(1)} %collective-permute-done.21.refs_3_), channel_id=1, source_target_pairs={{0,4},{4,8},{8,12},{12,14},{14,10},{10,6},{6,2},{2,0},{1,5},{5,9},... | collective-permute-start | bytes 3538952 | tf_op jit(solution)/shard_map/ppermute | solution.py:224
  257.5 24.1 %collective-permute-start.36 = (bf16[256,2304]{1,0:T(8,128)(2,1)S(1)}, bf16[256,2304]{1,0:T(8,128)(2,1)S(1)}, u32[]{:S(2)}, u32[]{:S(2)}) collective-permute-start(bf16[256,2304]{1,0:T(8,128)(2,1)S(1)} %collective-permute-done.22.refs_4_), channel_id=1, source_target_pairs={{4,0},{8,4},{12,8},{14,12},{10,14},{6,10},{2,6},{0,2},{5,1},{9,5},... | collective-permute-start | bytes 3538952 | tf_op jit(solution)/shard_map/ppermute | solution.py:225
  257.8 24.1 %collective-permute-start.39 = (bf16[32,2048]{1,0:T(8,128)(2,1)S(1)}, bf16[32,2048]{1,0:T(8,128)(2,1)S(1)}, u32[]{:S(2)}, u32[]{:S(2)}) collective-permute-start(bf16[32,2048]{1,0:T(8,128)(2,1)S(1)} %get-tuple-element.215.refs_9_), channel_id=1, source_target_pairs={{0,1},{1,0},{2,3},{3,2},{4,5},{5,4},{6,7},{7,6},{8,9},{9,8},{10,11... | collective-permute-start | bytes 393224 | tf_op jit(solution)/shard_map/ppermute | solution.py:41
  281.7 13.7 %collective-permute-start.38 = (bf16[128,2304]{1,0:T(8,128)(2,1)S(1)}, bf16[128,2304]{1,0:T(8,128)(2,1)S(1)}, u32[]{:S(2)}, u32[]{:S(2)}) collective-permute-start(bf16[128,2304]{1,0:T(8,128)(2,1)S(1)} %slice.294), channel_id=1, source_target_pairs={{4,0},{8,4},{12,8},{14,12},{10,14},{6,10},{2,6},{0,2},{5,1},{9,5},... | collective-permute-start | bytes 1769480 | tf_op jit(solution)/shard_map/ppermute | solution.py:225
  283.4 19.2 %collective-permute-start.43 = (bf16[32,2048]{1,0:T(8,128)(2,1)S(1)}, bf16[32,2048]{1,0:T(8,128)(2,1)S(1)}, u32[]{:S(2)}, u32[]{:S(2)}) collective-permute-start(bf16[32,2048]{1,0:T(8,128)(2,1)S(1)} %fusion.3.refs_0_.refs_4_), channel_id=1, source_target_pairs={{0,12},{2,14},{4,8},{6,10},{8,4},{10,6},{12,0},{14,2},{1,13},{3,15... | collective-permute-start | bytes 393224 | tf_op jit(solution)/shard_map/ppermute | solution.py:46
  286.4 18.0 %collective-permute-start.42 = (bf16[32,2048]{1,0:T(8,128)(2,1)S(1)}, bf16[32,2048]{1,0:T(8,128)(2,1)S(1)}, u32[]{:S(2)}, u32[]{:S(2)}) collective-permute-start(bf16[32,2048]{1,0:T(8,128)(2,1)S(1)} %fusion.3.refs_0_.refs_4_), channel_id=1, source_target_pairs={{0,8},{2,10},{4,12},{6,14},{8,0},{10,2},{12,4},{14,6},{1,9},{3,11}... | collective-permute-start | bytes 393224 | tf_op jit(solution)/shard_map/ppermute | solution.py:46
  287.0 17.4 %collective-permute-start.41 = (bf16[32,2048]{1,0:T(8,128)(2,1)S(1)}, bf16[32,2048]{1,0:T(8,128)(2,1)S(1)}, u32[]{:S(2)}, u32[]{:S(2)}) collective-permute-start(bf16[32,2048]{1,0:T(8,128)(2,1)S(1)} %fusion.3.refs_0_.refs_4_), channel_id=1, source_target_pairs={{0,4},{2,6},{4,0},{6,2},{8,12},{10,14},{12,8},{14,10},{1,5},{3,7},... | collective-permute-start | bytes 393224 | tf_op jit(solution)/shard_map/ppermute | solution.py:46
  305.3 21.5 %collective-permute-start.46 = (bf16[128,2048]{1,0:T(8,128)(2,1)}, bf16[128,2048]{1,0:T(8,128)(2,1)}, u32[]{:S(2)}, u32[]{:S(2)}) collective-permute-start(bf16[128,2048]{1,0:T(8,128)(2,1)} %shard_map.272.refs_0_), channel_id=1, source_target_pairs={{0,2},{2,0},{4,6},{6,4},{8,10},{10,8},{12,14},{14,12},{1,3},{3,1},... | collective-permute-start | bytes 1572872 | tf_op jit(solution)/shard_map/ppermute | solution.py:46
  306.6 20.1 %collective-permute-start.45 = (bf16[128,2048]{1,0:T(8,128)(2,1)}, bf16[128,2048]{1,0:T(8,128)(2,1)}, u32[]{:S(2)}, u32[]{:S(2)}) collective-permute-start(bf16[128,2048]{1,0:T(8,128)(2,1)} %shard_map.272.refs_0_), channel_id=1, source_target_pairs={{0,1},{1,0},{2,3},{3,2},{4,5},{5,4},{6,7},{7,6},{8,9},{9,8},{10,11... | collective-permute-start | bytes 1572872 | tf_op jit(solution)/shard_map/ppermute | solution.py:41
  309.0 14.7 %collective-permute-start.48 = (bf16[32,2048]{1,0:T(8,128)(2,1)}, bf16[32,2048]{1,0:T(8,128)(2,1)S(1)}, u32[]{:S(2)}, u32[]{:S(2)}) collective-permute-start(bf16[32,2048]{1,0:T(8,128)(2,1)} %get-tuple-element.223), channel_id=1, source_target_pairs={{0,1},{1,0},{2,3},{3,2},{4,5},{5,4},{6,7},{7,6},{8,9},{9,8},{10,11... | collective-permute-start | bytes 393224 | tf_op jit(solution)/shard_map/ppermute | solution.py:41
  329.4 13.2 %collective-permute-start.50 = (bf16[32,2176]{1,0:T(8,128)(2,1)S(1)}, bf16[32,2176]{1,0:T(8,128)(2,1)S(1)}, u32[]{:S(2)}, u32[]{:S(2)}) collective-permute-start(bf16[32,2176]{1,0:T(8,128)(2,1)S(1)} %get-tuple-element.225.refs_0_.refs_8_), channel_id=1, source_target_pairs={{0,8},{2,10},{4,12},{6,14},{8,0},{10,2},{12,4},{14,6},{1,9},{3,11}... | collective-permute-start | bytes 417800 | tf_op jit(solution)/shard_map/ppermute | solution.py:46
  343.8 13.7 %collective-permute-start.52 = (bf16[128,2176]{1,0:T(8,128)(2,1)S(1)}, bf16[128,2176]{1,0:T(8,128)(2,1)S(1)}, u32[]{:S(2)}, u32[]{:S(2)}) collective-permute-start(bf16[128,2176]{1,0:T(8,128)(2,1)S(1)} %shard_map.276.refs_0_), channel_id=1, source_target_pairs={{0,2},{2,0},{4,6},{6,4},{8,10},{10,8},{12,14},{14,12},{1,3},{3,1},... | collective-permute-start | bytes 1671176 | tf_op jit(solution)/shard_map/ppermute | solution.py:46
  364.1 18.6 %collective-permute-start.60 = (bf16[128,2048]{1,0:T(8,128)(2,1)S(1)}, bf16[128,2048]{1,0:T(8,128)(2,1)S(1)}, u32[]{:S(2)}, u32[]{:S(2)}) collective-permute-start(bf16[128,2048]{1,0:T(8,128)(2,1)S(1)} %shard_map.278.refs_0_), channel_id=1, source_target_pairs={{4,0},{8,4},{12,8},{14,12},{10,14},{6,10},{2,6},{0,2},{5,1},{9,5},... | collective-permute-start | bytes 1572872 | tf_op jit(solution)/shard_map/ppermute | solution.py:225
  364.4 18.4 %collective-permute-start.59 = (bf16[128,2048]{1,0:T(8,128)(2,1)S(1)}, bf16[128,2048]{1,0:T(8,128)(2,1)S(1)}, u32[]{:S(2)}, u32[]{:S(2)}) collective-permute-start(bf16[128,2048]{1,0:T(8,128)(2,1)S(1)} %shard_map.278.refs_0_), channel_id=1, source_target_pairs={{0,4},{4,8},{8,12},{12,14},{14,10},{10,6},{6,2},{2,0},{1,5},{5,9},... | collective-permute-start | bytes 1572872 | tf_op jit(solution)/shard_map/ppermute | solution.py:224
  366.6 16.2 %collective-permute-start.54 = (bf16[64,2048]{1,0:T(8,128)(2,1)S(1)}, bf16[64,2048]{1,0:T(8,128)(2,1)S(1)}, u32[]{:S(2)}, u32[]{:S(2)}) collective-permute-start(bf16[64,2048]{1,0:T(8,128)(2,1)S(1)} %slice.299), channel_id=1, source_target_pairs={{0,2},{2,0},{4,6},{6,4},{8,10},{10,8},{12,14},{14,12},{1,3},{3,1},... | collective-permute-start | bytes 786440 | tf_op jit(solution)/shard_map/ppermute | solution.py:46
  366.8 15.9 %collective-permute-start.55 = (bf16[64,2048]{1,0:T(8,128)(2,1)S(1)}, bf16[64,2048]{1,0:T(8,128)(2,1)S(1)}, u32[]{:S(2)}, u32[]{:S(2)}) collective-permute-start(bf16[64,2048]{1,0:T(8,128)(2,1)S(1)} %slice.301), channel_id=1, source_target_pairs={{0,1},{1,0},{2,3},{3,2},{4,5},{5,4},{6,7},{7,6},{8,9},{9,8},{10,11... | collective-permute-start | bytes 786440 | tf_op jit(solution)/shard_map/ppermute | solution.py:41
  382.8 15.7 %collective-permute-start.61 = (bf16[128,2048]{1,0:T(8,128)(2,1)S(1)}, bf16[128,2048]{1,0:T(8,128)(2,1)}, u32[]{:S(2)}, u32[]{:S(2)}) collective-permute-start(bf16[128,2048]{1,0:T(8,128)(2,1)S(1)} %collective-permute-done.59.refs_1_), channel_id=1, source_target_pairs={{0,4},{4,8},{8,12},{12,14},{14,10},{10,6},{6,2},{2,0},{1,5},{5,9},... | collective-permute-start | bytes 1572872 | tf_op jit(solution)/shard_map/ppermute | solution.py:224
  382.8 15.7 %collective-permute-start.62 = (bf16[128,2048]{1,0:T(8,128)(2,1)S(1)}, bf16[128,2048]{1,0:T(8,128)(2,1)}, u32[]{:S(2)}, u32[]{:S(2)}) collective-permute-start(bf16[128,2048]{1,0:T(8,128)(2,1)S(1)} %collective-permute-done.60.refs_2_), channel_id=1, source_target_pairs={{4,0},{8,4},{12,8},{14,12},{10,14},{6,10},{2,6},{0,2},{5,1},{9,5},... | collective-permute-start | bytes 1572872 | tf_op jit(solution)/shard_map/ppermute | solution.py:225
  441.7 16.1 %collective-permute-start.77 = (bf16[512,2048]{1,0:T(8,128)(2,1)S(1)}, bf16[512,2048]{1,0:T(8,128)(2,1)}, u32[]{:S(2)}, u32[]{:S(2)}) collective-permute-start(bf16[512,2048]{1,0:T(8,128)(2,1)S(1)} %shard_map.284), channel_id=1, source_target_pairs={{0,16},{16,0},{1,17},{17,1},{2,18},{18,2},{3,19},{19,3},{4,20},{20... | collective-permute-start | bytes 6291464 | tf_op jit(solution)/shard_map/ppermute | solution.py:37
  442.2 14.3 %collective-permute-start.75 = (bf16[128,2048]{1,0:T(8,128)(2,1)}, bf16[128,2048]{1,0:T(8,128)(2,1)S(1)}, u32[]{:S(2)}, u32[]{:S(2)}) collective-permute-start(bf16[128,2048]{1,0:T(8,128)(2,1)} %collective-permute-done.61.refs_3_), channel_id=1, source_target_pairs={{0,4},{4,8},{8,12},{12,14},{14,10},{10,6},{6,2},{2,0},{1,5},{5,9},... | collective-permute-start | bytes 1572872 | tf_op jit(solution)/shard_map/ppermute | solution.py:224
  443.7 14.1 %collective-permute-start.76 = (bf16[128,2048]{1,0:T(8,128)(2,1)}, bf16[128,2048]{1,0:T(8,128)(2,1)S(1)}, u32[]{:S(2)}, u32[]{:S(2)}) collective-permute-start(bf16[128,2048]{1,0:T(8,128)(2,1)} %collective-permute-done.62.refs_4_), channel_id=1, source_target_pairs={{4,0},{8,4},{12,8},{14,12},{10,14},{6,10},{2,6},{0,2},{5,1},{9,5},... | collective-permute-start | bytes 1572872 | tf_op jit(solution)/shard_map/ppermute | solution.py:225
  466.5 15.2 %collective-permute-start.83 = (bf16[128,2048]{1,0:T(8,128)(2,1)S(1)}, bf16[128,2048]{1,0:T(8,128)(2,1)S(1)}, u32[]{:S(2)}, u32[]{:S(2)}) collective-permute-start(bf16[128,2048]{1,0:T(8,128)(2,1)S(1)} %get-tuple-element.275), channel_id=1, source_target_pairs={{0,1},{1,0},{2,3},{3,2},{4,5},{5,4},{6,7},{7,6},{8,9},{9,8},{10,11... | collective-permute-start | bytes 1572872 | tf_op jit(solution)/shard_map/ppermute | solution.py:41
  467.9 13.8 %collective-permute-start.84 = (bf16[128,2048]{1,0:T(8,128)(2,1)S(1)}, bf16[128,2048]{1,0:T(8,128)(2,1)S(1)}, u32[]{:S(2)}, u32[]{:S(2)}) collective-permute-start(bf16[128,2048]{1,0:T(8,128)(2,1)S(1)} %get-tuple-element.277), channel_id=1, source_target_pairs={{0,2},{2,0},{4,6},{6,4},{8,10},{10,8},{12,14},{14,12},{1,3},{3,1},... | collective-permute-start | bytes 1572872 | tf_op jit(solution)/shard_map/ppermute | solution.py:46
  482.0 12.9 %collective-permute-start.86 = (bf16[128,2048]{1,0:T(8,128)(2,1)S(1)}, bf16[128,2048]{1,0:T(8,128)(2,1)S(1)}, u32[]{:S(2)}, u32[]{:S(2)}) collective-permute-start(bf16[128,2048]{1,0:T(8,128)(2,1)S(1)} %shard_map.287.refs_0_), channel_id=1, source_target_pairs={{0,2},{2,0},{4,6},{6,4},{8,10},{10,8},{12,14},{14,12},{1,3},{3,1},... | collective-permute-start | bytes 1572872 | tf_op jit(solution)/shard_map/ppermute | solution.py:46
  483.8 13.2 %collective-permute-start.85 = (bf16[128,2048]{1,0:T(8,128)(2,1)S(1)}, bf16[128,2048]{1,0:T(8,128)(2,1)S(1)}, u32[]{:S(2)}, u32[]{:S(2)}) collective-permute-start(bf16[128,2048]{1,0:T(8,128)(2,1)S(1)} %shard_map.287.refs_0_), channel_id=1, source_target_pairs={{0,1},{1,0},{2,3},{3,2},{4,5},{5,4},{6,7},{7,6},{8,9},{9,8},{10,11... | collective-permute-start | bytes 1572872 | tf_op jit(solution)/shard_map/ppermute | solution.py:41
  526.1 18.4 %collective-permute-start.91 = (bf16[128,2176]{1,0:T(8,128)(2,1)S(1)}, bf16[128,2176]{1,0:T(8,128)(2,1)S(1)}, u32[]{:S(2)}, u32[]{:S(2)}) collective-permute-start(bf16[128,2176]{1,0:T(8,128)(2,1)S(1)} %get-tuple-element.287), channel_id=1, source_target_pairs={{0,1},{1,0},{2,3},{3,2},{4,5},{5,4},{6,7},{7,6},{8,9},{9,8},{10,11... | collective-permute-start | bytes 1671176 | tf_op jit(solution)/shard_map/ppermute | solution.py:41
  527.6 16.8 %collective-permute-start.93 = (bf16[128,2176]{1,0:T(8,128)(2,1)S(1)}, bf16[128,2176]{1,0:T(8,128)(2,1)S(1)}, u32[]{:S(2)}, u32[]{:S(2)}) collective-permute-start(bf16[128,2176]{1,0:T(8,128)(2,1)S(1)} %get-tuple-element.299), channel_id=1, source_target_pairs={{0,2},{2,0},{4,6},{6,4},{8,10},{10,8},{12,14},{14,12},{1,3},{3,1},... | collective-permute-start | bytes 1671176 | tf_op jit(solution)/shard_map/ppermute | solution.py:46
  544.7 16.0 %collective-permute-start.96 = (bf16[32,2176]{1,0:T(8,128)(2,1)S(1)}, bf16[32,2176]{1,0:T(8,128)(2,1)S(1)}, u32[]{:S(2)}, u32[]{:S(2)}) collective-permute-start(bf16[32,2176]{1,0:T(8,128)(2,1)S(1)} %get-tuple-element.303), channel_id=1, source_target_pairs={{0,12},{2,14},{4,8},{6,10},{8,4},{10,6},{12,0},{14,2},{1,13},{3,15... | collective-permute-start | bytes 417800 | tf_op jit(solution)/shard_map/ppermute | solution.py:46
  546.7 14.0 %collective-permute-start.94 = (bf16[32,2176]{1,0:T(8,128)(2,1)S(1)}, bf16[32,2176]{1,0:T(8,128)(2,1)S(1)}, u32[]{:S(2)}, u32[]{:S(2)}) collective-permute-start(bf16[32,2176]{1,0:T(8,128)(2,1)S(1)} %get-tuple-element.301), channel_id=1, source_target_pairs={{0,4},{2,6},{4,0},{6,2},{8,12},{10,14},{12,8},{14,10},{1,5},{3,7},... | collective-permute-start | bytes 417800 | tf_op jit(solution)/shard_map/ppermute | solution.py:46
  546.7 14.0 %collective-permute-start.95 = (bf16[32,2176]{1,0:T(8,128)(2,1)S(1)}, bf16[32,2176]{1,0:T(8,128)(2,1)S(1)}, u32[]{:S(2)}, u32[]{:S(2)}) collective-permute-start(bf16[32,2176]{1,0:T(8,128)(2,1)S(1)} %get-tuple-element.302), channel_id=1, source_target_pairs={{0,8},{2,10},{4,12},{6,14},{8,0},{10,2},{12,4},{14,6},{1,9},{3,11}... | collective-permute-start | bytes 417800 | tf_op jit(solution)/shard_map/ppermute | solution.py:46
  568.8 28.7 %all-to-all-start = ((bf16[8,128,256]{2,1,0:T(8,128)(2,1)}), bf16[8,128,256]{2,1,0:T(8,128)(2,1)S(1)}, u32[]{:S(2)}, u32[]{:S(2)}) async-start(bf16[8,128,256]{2,1,0:T(8,128)(2,1)} %fusion.12), calls=%async_computation | async-start | bytes 1048576 | tf_op jit(solution)/shard_map/all_to_all | solution.py:1182
  573.2 15.0 %collective-permute-start.100 = (bf16[32,2048]{1,0:T(8,128)(2,1)S(1)}, bf16[32,2048]{1,0:T(8,128)(2,1)S(1)}, u32[]{:S(2)}, u32[]{:S(2)}) collective-permute-start(bf16[32,2048]{1,0:T(8,128)(2,1)S(1)} %get-tuple-element.319), channel_id=1, source_target_pairs={{0,4},{2,6},{4,0},{6,2},{8,12},{10,14},{12,8},{14,10},{1,5},{3,7},... | collective-permute-start | bytes 393224 | tf_op jit(solution)/shard_map/ppermute | solution.py:46
  575.2 22.3 %collective-permute-start.101 = (bf16[32,2048]{1,0:T(8,128)(2,1)S(1)}, bf16[32,2048]{1,0:T(8,128)(2,1)S(1)}, u32[]{:S(2)}, u32[]{:S(2)}) collective-permute-start(bf16[32,2048]{1,0:T(8,128)(2,1)S(1)} %get-tuple-element.321), channel_id=1, source_target_pairs={{0,8},{2,10},{4,12},{6,14},{8,0},{10,2},{12,4},{14,6},{1,9},{3,11}... | collective-permute-start | bytes 393224 | tf_op jit(solution)/shard_map/ppermute | solution.py:46
  577.6 19.9 %collective-permute-start.102 = (bf16[32,2048]{1,0:T(8,128)(2,1)S(1)}, bf16[32,2048]{1,0:T(8,128)(2,1)S(1)}, u32[]{:S(2)}, u32[]{:S(2)}) collective-permute-start(bf16[32,2048]{1,0:T(8,128)(2,1)S(1)} %get-tuple-element.323), channel_id=1, source_target_pairs={{0,12},{2,14},{4,8},{6,10},{8,4},{10,6},{12,0},{14,2},{1,13},{3,15... | collective-permute-start | bytes 393224 | tf_op jit(solution)/shard_map/ppermute | solution.py:46
  600.5 19.3 %collective-permute-start.109 = (bf16[144,2560]{1,0:T(8,128)(2,1)S(1)}, bf16[144,2560]{1,0:T(8,128)(2,1)}, u32[]{:S(2)}, u32[]{:S(2)}) collective-permute-start(bf16[144,2560]{1,0:T(8,128)(2,1)S(1)} %shard_map.301.refs_0_), channel_id=1, source_target_pairs={{4,0},{8,4},{12,8},{14,12},{10,14},{6,10},{2,6},{0,2},{5,1},{9,5},... | collective-permute-start | bytes 2211848 | tf_op jit(solution)/shard_map/ppermute | solution.py:225
  601.9 19.1 %collective-permute-start.108 = (bf16[144,2560]{1,0:T(8,128)(2,1)S(1)}, bf16[144,2560]{1,0:T(8,128)(2,1)}, u32[]{:S(2)}, u32[]{:S(2)}) collective-permute-start(bf16[144,2560]{1,0:T(8,128)(2,1)S(1)} %shard_map.301.refs_0_), channel_id=1, source_target_pairs={{0,4},{4,8},{8,12},{12,14},{14,10},{10,6},{6,2},{2,0},{1,5},{5,9},... | collective-permute-start | bytes 2211848 | tf_op jit(solution)/shard_map/ppermute | solution.py:224
  610.4 23.2 %collective-permute-start.112 = (bf16[512,768]{1,0:T(8,128)(2,1)}, bf16[512,768]{1,0:T(8,128)(2,1)}, u32[]{:S(2)}, u32[]{:S(2)}) collective-permute-start(bf16[512,768]{1,0:T(8,128)(2,1)} %shard_map.305), channel_id=1, source_target_pairs={{0,16},{16,0},{1,17},{17,1},{2,18},{18,2},{3,19},{19,3},{4,20},{20... | collective-permute-start | bytes 2359304 | tf_op jit(solution)/shard_map/ppermute | solution.py:37
  612.0 21.6 %collective-permute-start.113 = (bf16[512,2048]{1,0:T(8,128)(2,1)}, bf16[512,2048]{1,0:T(8,128)(2,1)S(1)}, u32[]{:S(2)}, u32[]{:S(2)}) collective-permute-start(bf16[512,2048]{1,0:T(8,128)(2,1)} %shard_map.306), channel_id=1, source_target_pairs={{0,16},{16,0},{1,17},{17,1},{2,18},{18,2},{3,19},{19,3},{4,20},{20... | collective-permute-start | bytes 6291464 | tf_op jit(solution)/shard_map/ppermute | solution.py:37
  621.2 25.3 %collective-permute-start.106 = (bf16[32,2048]{1,0:T(8,128)(2,1)S(1)}, bf16[32,2048]{1,0:T(8,128)(2,1)S(1)}, u32[]{:S(2)}, u32[]{:S(2)}) collective-permute-start(bf16[32,2048]{1,0:T(8,128)(2,1)S(1)} %broadcast_select_fusion.12), channel_id=1, source_target_pairs={{0,16},{16,0},{1,17},{17,1},{2,18},{18,2},{3,19},{19,3},{4,20},{20... | collective-permute-start | bytes 393224 | tf_op jit(solution)/shard_map/ppermute | solution.py:37
  621.8 21.1 %collective-permute-start.111 = (bf16[144,2560]{1,0:T(8,128)(2,1)}, bf16[144,2560]{1,0:T(8,128)(2,1)}, u32[]{:S(2)}, u32[]{:S(2)}) collective-permute-start(bf16[144,2560]{1,0:T(8,128)(2,1)} %collective-permute-done.109.refs_2_), channel_id=1, source_target_pairs={{4,0},{8,4},{12,8},{14,12},{10,14},{6,10},{2,6},{0,2},{5,1},{9,5},... | collective-permute-start | bytes 2211848 | tf_op jit(solution)/shard_map/ppermute | solution.py:225
  623.5 19.4 %collective-permute-start.110 = (bf16[144,2560]{1,0:T(8,128)(2,1)}, bf16[144,2560]{1,0:T(8,128)(2,1)}, u32[]{:S(2)}, u32[]{:S(2)}) collective-permute-start(bf16[144,2560]{1,0:T(8,128)(2,1)} %collective-permute-done.108.refs_1_), channel_id=1, source_target_pairs={{0,4},{4,8},{8,12},{12,14},{14,10},{10,6},{6,2},{2,0},{1,5},{5,9},... | collective-permute-start | bytes 2211848 | tf_op jit(solution)/shard_map/ppermute | solution.py:224
  629.0 47.8 %all-to-all-start.1 = ((bf16[8,160,256]{2,1,0:T(8,128)(2,1)}), bf16[8,160,256]{2,1,0:T(8,128)(2,1)S(1)}, u32[]{:S(2)}, u32[]{:S(2)}) async-start(bf16[8,160,256]{2,1,0:T(8,128)(2,1)} %fusion.4), calls=%async_computation.1 | async-start | bytes 1310720 | tf_op jit(solution)/shard_map/all_to_all | solution.py:1182
  642.9 23.3 %collective-permute-start.114 = (bf16[144,2560]{1,0:T(8,128)(2,1)}, bf16[144,2560]{1,0:T(8,128)(2,1)}, u32[]{:S(2)}, u32[]{:S(2)}) collective-permute-start(bf16[144,2560]{1,0:T(8,128)(2,1)} %collective-permute-done.110.refs_3_), channel_id=1, source_target_pairs={{0,4},{4,8},{8,12},{12,14},{14,10},{10,6},{6,2},{2,0},{1,5},{5,9},... | collective-permute-start | bytes 2211848 | tf_op jit(solution)/shard_map/ppermute | solution.py:224
  644.9 21.9 %collective-permute-start.115 = (bf16[144,2560]{1,0:T(8,128)(2,1)}, bf16[144,2560]{1,0:T(8,128)(2,1)}, u32[]{:S(2)}, u32[]{:S(2)}) collective-permute-start(bf16[144,2560]{1,0:T(8,128)(2,1)} %collective-permute-done.111.refs_4_), channel_id=1, source_target_pairs={{4,0},{8,4},{12,8},{14,12},{10,14},{6,10},{2,6},{0,2},{5,1},{9,5},... | collective-permute-start | bytes 2211848 | tf_op jit(solution)/shard_map/ppermute | solution.py:225
  646.6 30.2 %collective-permute-start.107 = (bf16[2,32,2048]{2,1,0:T(8,128)(2,1)S(1)}, bf16[2,32,2048]{2,1,0:T(8,128)(2,1)S(1)}, u32[]{:S(2)}, u32[]{:S(2)}) collective-permute-start(bf16[2,32,2048]{2,1,0:T(8,128)(2,1)S(1)} %pad_maximum_fusion.3), channel_id=1, source_target_pairs={{0,1},{1,0},{2,3},{3,2},{4,5},{5,4},{6,7},{7,6},{8,9},{9,8},{10,11... | collective-permute-start | bytes 786440 | tf_op jit(solution)/shard_map/ppermute | solution.py:41
  (198 other events, 2589.7 us)

commit v4 on v3

--- a/solution.py
+++ b/solution.py
@@ -15,6 +15,7 @@
 f32 = jnp.float32
 lanes = 128
 tile_rows = 512
+grad_columns = 1024
 
 
 def dot(left, right):
@@ -508,34 +509,68 @@
     )(*ring.pieces, *small)
 
 
-def expert_copies(layer, refs, w_both, w_down, sems):
+def choose_weights_kernel(layer, *refs):
+    refs, (w_both, w_down, sems) = refs[:6], refs[6:]
     is_own = lax.axis_index("section") == layer
     experts = refs[0].shape[0]
     units = w_down.shape[0] // experts
+
+    def copies(sources):
+        made = []
+        for number in range(experts):
+            gate = pl.ds(2 * number * units, units)
+            up = pl.ds((2 * number + 1) * units, units)
+            targets = (
+                w_both.at[:, gate],
+                w_both.at[:, up],
+                w_down.at[pl.ds(number * units, units)],
+            )
+            for i, target in enumerate(targets):
+                sem = sems.at[3 * number + i]
+                made.append(pltpu.make_async_copy(sources[i].at[number], target, sem))
+        return made
+
+    @pl.when(is_own)
+    def _():
+        start_all(copies(refs[:3]))
+
+    @pl.when(jnp.logical_not(is_own))
+    def _():
+        start_all(copies(refs[3:]))
+
+    wait_all(copies(refs[:3]))
+
+
+def choose_weights(layer, weights):
+    experts, width, units = weights[0].shape
+    total = experts * units
+    return pl.pallas_call(
+        functools.partial(choose_weights_kernel, layer),
+        in_specs=[anywhere] * 6,
+        out_specs=(anywhere,) * 2,
+        out_shape=(array((width, 2 * total), bf16), array((total, width), bf16)),
+        scratch_shapes=[pltpu.SemaphoreType.DMA((3 * experts,))],
+        compiler_params=kernel_params(8),
+        cost_estimate=cost(1000, 1000),
+    )(*weights)
+
+
+def expert_copies(experts, sources, w_both, w_down, sems):
+    units = w_down.shape[0] // experts
     groups = []
     for number in range(experts):
-        gate = pl.ds(2 * number * units, units)
-        up = pl.ds((2 * number + 1) * units, units)
-        targets = [w_both.at[:, gate], w_both.at[:, up], w_down.at[pl.ds(number * units, units)]]
-
-        def make(source, i, number=number, targets=targets):
-            return pltpu.make_async_copy(
-                source.at[number], targets[i], sems.at[3 * number + i]
+        wide = pl.ds(2 * number * units, 2 * units)
+        narrow = pl.ds(number * units, units)
+        groups.append(
+            (
+                pltpu.make_async_copy(
+                    sources[0].at[:, wide], w_both.at[:, wide], sems.at[2 * number]
+                ),
+                pltpu.make_async_copy(
+                    sources[1].at[narrow], w_down.at[narrow], sems.at[2 * number + 1]
+                ),
             )
-
-        def start(which, make=make):
-            @pl.when(is_own)
-            def _():
-                start_all([make(refs[i], i) for i in which])
-
-            @pl.when(jnp.logical_not(is_own))
-            def _():
-                start_all([make(refs[3 + i], i) for i in which])
-
-        def wait(which, make=make):
-            wait_all([make(refs[i], i) for i in which])
-
-        groups.append((start, wait))
+        )
     return groups
 
 
@@ -562,7 +597,7 @@
 
 def experts_kernel(count, layer, tile, before, *refs):
     pieces, refs = refs[:count], refs[count:]
-    weight_refs, ones, refs = refs[:6], refs[6], refs[7 + before :]
+    weight_refs, ones, refs = refs[:2], refs[2], refs[3 + before :]
     outs, refs = refs[:count], refs[count:]
     act_store, gates_out, rows_store, scaled_store = refs[:4]
     rows_in, scaled, w_both, w_down, sems, weight_sems, store_sems, act_out = refs[4:]
@@ -570,8 +605,8 @@
     experts = ones.shape[0]
     units = w_down.shape[0] // experts
     loads = load_pieces(pieces, tile, rows_in, sems)
-    weights = expert_copies(layer, weight_refs, w_both, w_down, weight_sems)
-    weights[0][0]((0, 1))
+    weights = expert_copies(experts, weight_refs, w_both, w_down, weight_sems)
+    weights[0][0].start()
     place = pl.ds(tile * tile_rows, tile_rows)
     stores = [
         pltpu.make_async_copy(
@@ -586,10 +621,10 @@
     gates = extra + pltpu.roll(extra, lanes // 2, 1)
     gates_out[...] = gates
     for number in range(experts):
-        weights[number][1]((0, 1))
+        weights[number][0].wait()
         if number + 1 < experts:
-            weights[number + 1][0]((0, 1))
-        weights[number][0]((2,))
+            weights[number + 1][0].start()
+        weights[number][1].start()
         span = slice(2 * number * units, 2 * (number + 1) * units)
         act = dot(rows_in[:, :width], w_both[:, span])
         act_out[:, span] = act.astype(act_out.dtype)
@@ -600,7 +635,7 @@
     stores[1].start()
     stores[2].start()
     for number in range(experts):
-        weights[number][1]((2,))
+        weights[number][1].wait()
     step = width // 4
     for number in range(4):
         span = slice(number * step, (number + 1) * step)
@@ -615,15 +650,14 @@
         pltpu.VMEM((width, 2 * total_units), bf16),
         pltpu.VMEM((total_units, width), bf16),
         pltpu.SemaphoreType.DMA((count,)),
-        pltpu.SemaphoreType.DMA((3 * experts,)),
+        pltpu.SemaphoreType.DMA((2 * experts,)),
         pltpu.SemaphoreType.DMA((3,)),
     ]
 
 
 def run_experts(pieces, weights, ones, layer, tile, rows, stores):
     count = len(pieces)
-    experts, width, units = weights[0].shape
-    total_units = experts * units
+    experts, total_units, width = ones.shape[0], *weights[1].shape
     stores = stores or ()
     sizes = [min(one.shape[0], tile_rows) for one in pieces]
     shapes = tuple([array((one, width), bf16) for one in sizes]) + (
@@ -634,7 +668,7 @@
     )
     outs = pl.pallas_call(
         functools.partial(experts_kernel, count, layer, tile, len(stores)),
-        in_specs=[anywhere] * (count + 6) + [full(ones)] + [anywhere] * len(stores),
+        in_specs=[anywhere] * (count + 2) + [full(ones)] + [anywhere] * len(stores),
         out_specs=tuple(full(one) for one in shapes[:count])
         + (anywhere, full(shapes[count + 1]), anywhere, anywhere),
         out_shape=shapes,
@@ -647,8 +681,8 @@
             experts,
         )
         + [pltpu.VMEM(shapes[count].shape, shapes[count].dtype)],
-        input_output_aliases={count + 7: count + 2, count + 8: count + 3} if stores else {},
-        compiler_params=kernel_params(56),
+        input_output_aliases={count + 3: count + 2, count + 4: count + 3} if stores else {},
+        compiler_params=kernel_params(32),
         cost_estimate=cost(12 * tile_rows * width * total_units, 6 * width * total_units),
     )(*pieces, *weights, ones, *stores)
     return list(outs[:count]), outs[count : count + 2], outs[count + 2 :]
@@ -656,8 +690,8 @@
 
 def experts_back_kernel(count, layer, tile, before, *refs):
     pieces, refs = refs[:count], refs[count:]
-    weight_refs, ones, act_in, gates_in = refs[:6], refs[6], refs[7], refs[8]
-    refs = refs[9 + before :]
+    weight_refs, ones, act_in, gates_in = refs[:2], refs[2], refs[3], refs[4]
+    refs = refs[5 + before :]
     outs, refs = refs[:count], refs[count:]
     d_store, grad_store = refs[:2]
     rows_in, d_act, w_both, w_down, sems, weight_sems, store_sems, act = refs[2:]
@@ -665,8 +699,8 @@
     experts = ones.shape[0]
     units = w_down.shape[0] // experts
     loads = load_pieces(pieces, tile, rows_in, sems)
-    weights = expert_copies(layer, weight_refs, w_both, w_down, weight_sems)
-    weights[0][0]((2,))
+    weights = expert_copies(experts, weight_refs, w_both, w_down, weight_sems)
+    weights[0][1].start()
     act_copy = pltpu.make_async_copy(act_in, act, store_sems.at[2])
     act_copy.start()
     place = pl.ds(tile * tile_rows, tile_rows)
@@ -679,10 +713,10 @@
     gates = gates_in[...]
     placed = jnp.zeros_like(gates)
     for number in range(experts):
-        weights[number][1]((2,))
+        weights[number][1].wait()
         if number + 1 < experts:
-            weights[number + 1][0]((2,))
-        weights[number][0]((0, 1))
+            weights[number + 1][1].start()
+        weights[number][0].start()
         base = 2 * number * units
         plain = dot_cols(rows_in[...], w_down[number * units : (number + 1) * units])
         if number == 0:
@@ -701,7 +735,7 @@
         d_act[:, base : base + units] = d_gate.astype(bf16)
     stores[1].start()
     for number in range(experts):
-        weights[number][1]((0, 1))
+        weights[number][0].wait()
     step = width // 4
     for number in range(4):
         span = slice(number * step, (number + 1) * step)
@@ -712,8 +746,7 @@
 
 def run_experts_back(pieces, weights, ones, kept, layer, tile, rows, stores):
     count = len(pieces)
-    experts, width, units = weights[0].shape
-    total_units = experts * units
+    experts, total_units, width = ones.shape[0], *weights[1].shape
     stores = stores or ()
     act, gates = kept
     sizes = [min(one.shape[0], tile_rows) for one in pieces]
@@ -723,7 +756,7 @@
     )
     outs = pl.pallas_call(
         functools.partial(experts_back_kernel, count, layer, tile, len(stores)),
-        in_specs=[anywhere] * (count + 6)
+        in_specs=[anywhere] * (count + 2)
         + [full(ones), anywhere, full(gates)]
         + [anywhere] * len(stores),
         out_specs=tuple(full(one) for one in shapes[:count]) + (anywhere,) * 2,
@@ -737,8 +770,8 @@
             experts,
         )
         + [pltpu.VMEM(act.shape, act.dtype)],
-        input_output_aliases={count + 9: count, count + 10: count + 1} if stores else {},
-        compiler_params=kernel_params(56),
+        input_output_aliases={count + 5: count, count + 6: count + 1} if stores else {},
+        compiler_params=kernel_params(32),
         cost_estimate=cost(12 * tile_rows * width * total_units, 6 * width * total_units),
     )(*pieces, *weights, ones, act, gates, *stores)
     return list(outs[:count]), outs[count:]
@@ -751,7 +784,7 @@
     rows = left.shape[0] // 2
     place, step = column
     spans = [pl.ds(0, left.shape[1]), pl.ds(0, right.shape[1])]
-    spans[place] = pl.ds(step * 512, 512)
+    spans[place] = pl.ds(step * grad_columns, grad_columns)
 
     def copies(layer):
         made = []
@@ -796,7 +829,7 @@
     before = before or ()
     rows = left[0].shape[0]
     widths = [left[0].shape[1], right[0].shape[1]]
-    widths[place] = 512
+    widths[place] = grad_columns
     experts = shapes[0].shape[0]
     return pl.pallas_call(
         functools.partial(grads_kernel, (place, step), len(before), len(shapes)),
@@ -820,7 +853,7 @@
     width, units = rows_in[0].shape[1], d_act[0].shape[1] // (2 * experts)
     shapes = (array((experts, width, units), f32),) * 2
     made = []
-    for step in range(width // 512):
+    for step in range(width // grad_columns):
         made.append(run_grads(0, step, rows_in, d_act, shapes, made[-1] if made else None))
     return made
 
@@ -829,7 +862,7 @@
     width, units = grads[0].shape[1], scaled[0].shape[1] // experts
     shapes = (array((experts, units, width), f32),)
     made = []
-    for step in range(width // 512):
+    for step in range(width // grad_columns):
         made.append(run_grads(1, step, scaled, grads, shapes, made[-1] if made else None))
     return made
 
@@ -1303,11 +1336,12 @@
     mid0, payload0, gates0 = route(0, x_in, *own_rows(own, other), tiny, masks[0])
     gather = Gather(payload0)
     gather.along_z()
-    gather.near()
+    weights0 = choose_weights(0, (after(expert_weights[0], payload0), *expert_weights[1:]))
+    gather.near(*weights0)
     gather.far()
     tiles = gather.tiles()
     ring1.advance(tiles[-1][-1])
-    outs0, kept0, stores0 = apply_experts(tiles, expert_weights, ones, 0)
+    outs0, kept0, stores0 = apply_experts(tiles, weights0, ones, 0)
     scatter = Scatter(outs0)
     scatter.far()
     scatter.near(beside=ring1.latest)
@@ -1327,19 +1361,20 @@
     mid1, payload1, gates1 = route(1, x_mid, *own_rows(own, other), tiny, masks[1])
     gather = Gather(after(payload1, *beside))
     gather.along_z()
-    gather.near()
+    weights1 = choose_weights(1, (after(expert_weights[0], payload1), *expert_weights[1:]))
+    gather.near(*weights1)
     gather.far()
     tiles = gather.tiles()
     beside = grad_gather.far(tiles[-1][-1])
     mixed_got = swap_core(pick(mixed1, mixed0))
     ring_mixed = Ring(stack_layer(mixed0, mixed1, mixed_got))
     ring_mixed.advance(tiles[-1][-1])
-    outs1, kept1, stores1 = apply_experts(tiles, expert_weights, ones, 1)
+    outs1, kept1, stores1 = apply_experts(tiles, weights1, ones, 1)
 
     outs1[-1][-1] = after(outs1[-1][-1], *ring_mixed.latest, *beside)
     tiles = grad_gather.tiles(outs1[-1][-1])
     ring_mixed.advance(tiles[-1][-1])
-    backs, back_stores1 = apply_experts_back(tiles, expert_weights, ones, kept1, 1)
+    backs, back_stores1 = apply_experts_back(tiles, weights1, ones, kept1, 1)
     scatter = Scatter(backs)
     scatter.far(*ring_mixed.latest)
     reached = scatter.near()
@@ -1367,10 +1402,11 @@
     gather = Gather(d_one)
     gather.along_z()
     beside = out_scatter.near(d_one)
-    gather.near(*beside)
+    weights0 = choose_weights(0, (after(expert_weights[0], d_one), *expert_weights[1:]))
+    gather.near(*beside, *weights0)
     gather.far()
     tiles = gather.tiles()
-    backs, back_stores0 = apply_experts_back(tiles, expert_weights, ones, kept0, 0)
+    backs, back_stores0 = apply_experts_back(tiles, weights0, ones, kept0, 0)
 
     if not small_grid():
         rows_in = exchange(after(stores0[0], back_stores0[0]), stores1[0])
@@ -1381,9 +1417,9 @@
         choose_kernel, [array(normed0.shape, bf16)], normed0, after(normed1, *scatter.far())
     )[0]
     normed_blocks = by_columns(normed_own, split)
-    scatter.near(beside=(*wide[1], normed_blocks))
+    scatter.near(beside=(*wide[0], normed_blocks))
     parts = scatter.along_z()
-    parts[-1] = after(parts[-1], *wide[3])
+    parts[-1] = after(parts[-1], *wide[1])
     d_mid, d_low, g_router0, g_ffn_gain0 = unroute(
         0, parts, d_one, mid0, tiny, gates0, payload0
     )
@@ -1422,8 +1458,8 @@
         swap_core(small_other),
     )[0]
     late_spread = to_owners(by_columns(late_rows, split))
-    three_rounds = ring_d.advance(*down[1])
-    ring_d.advance(*down[3])
+    three_rounds = ring_d.advance(*down[0])
+    ring_d.advance(*down[1])
     ring_mixed.advance(*three_rounds)
     g_out = out_grads(ring_mixed, late_spread)
     out1 = finish(mid1, out_parts)

time: 713 us -> 689 us (0.966)
  Pallas kernels: 145 us -> 130 us
  starting transfers between devices: 146 us -> 138 us
    ppermute x16, waiting for transfers between devices: 45.1 us -> 156 us  [advance(): self.plus = lax.ppermute(after(plus, *gate), 'expert', up)]
    ppermute x16, waiting for transfers between devices: 122 us -> 16.7 us  [advance(): self.minus = lax.ppermute(after(minus, *gate), 'expert', down)]
    ppermute x40, waiting for transfers between devices: 87.7 us -> 62.6 us  [swap_e(): return lax.ppermute(value, 'expert', [(i, i ^ bits) for i in range(count)])]
    ppermute x25, waiting for transfers between devices: 81.7 us -> 94.6 us  [swap_x(): return lax.ppermute(value, 'tensor', [(0, 1), (1, 0)])]
    pallas_call x0 -> x3, Pallas kernels: none -> 11.4 us  [choose_weights(): pl.pallas_call(functools.partial(choose_weights_kernel, layer), in_specs=...]
    pallas_call x8 -> x4, Pallas kernels: 38.7 us -> 28.6 us  [run_grads(): pl.pallas_call(functools.partial(grads_kernel, (place, step), len(before)...]
    pallas_call x2, Pallas kernels: 27.2 us -> 17.2 us  [run_experts_back(): pl.pallas_call(functools.partial(experts_back_kernel, count, layer, tile,...]
    ppermute x16, starting transfers between devices: 20.1 us -> 10.7 us  [advance(): self.minus = lax.ppermute(after(minus, *gate), 'expert', down)]
  transfers between devices with their start and end apart: 124 -> 124, of which waited for: 68 -> 64; matrix products, arithmetic and copies ran while one was open for 3% -> 3% of each run, Pallas kernels for 17% -> 16%
where the time goes in v4:
time: 689 us; the launch traced here: 681 us
  waiting for transfers between devices  345 us (50%)
  starting transfers between devices  138 us (20%)
  Pallas kernels  130 us (19%)
  local copies, waits for them, and re-layouts  53.4 us (8%)
  other arithmetic  11 us (2%)
    ppermute x16, waiting for transfers between devices, advance(): self.plus = lax.ppermute(after(plus, *gate), 'expert', up)  156 us
    ppermute x25, waiting for transfers between devices, swap_x(): return lax.ppermute(value, 'tensor', [(0, 1), (1, 0)])  94.6 us
    ppermute x40, waiting for transfers between devices, swap_e(): return lax.ppermute(value, 'expert', [(i, i ^ bits) for i in range(count)])  62.6 us
    ppermute x40, starting transfers between devices, swap_e(): return lax.ppermute(value, 'expert', [(i, i ^ bits) for i in range(count)])  56.2 us
    unnamed x309, local copies, waits for them, and re-layouts  43.9 us
    ppermute x16, starting transfers between devices, advance(): self.plus = lax.ppermute(after(plus, *gate), 'expert', up)  29.8 us
    pallas_call x4, Pallas kernels, run_grads(): pl.pallas_call(functools.partial(grads_kernel, (place, step), len(before)...  28.6 us
    ppermute x25, starting transfers between devices, swap_x(): return lax.ppermute(value, 'tensor', [(0, 1), (1, 0)])  28 us
  transfers between devices with their start and end apart: 124, of which 64 were waited for; matrix products, arithmetic and copies ran while one was open for 3% of the time, Pallas kernels for 16%

profile of v4, /device:TPU:0, one launch (start us, length us, event | category | flops | bytes accessed | tf_op | source)
XLA Modules:
  0.0 680.8 jit_solution(14826903153262056752)
XLA Ops:
  9.4 3.0 collective-permute-start.2
  12.4 27.7 %collective-permute-done.2.refs_1_ = bf16[256,2432]{1,0:T(8,128)(2,1)} collective-permute-done((bf16[256,2432]{1,0:T(8,128)(2,1)S(1)}, bf16[256,2432]{1,0:T(8,128)(2,1)}, u32[]{:S(2)}, u32[]{:S(2)}) %collective-permute-start.2) | collective-permute-done | bytes 1245216 | tf_op jit(solution)/shard_map/ppermute | solution.py:225
  46.2 26.3 %collective-permute-done.4.refs_3_ = bf16[256,2432]{1,0:T(8,128)(2,1)} collective-permute-done((bf16[256,2432]{1,0:T(8,128)(2,1)}, bf16[256,2432]{1,0:T(8,128)(2,1)}, u32[]{:S(2)}, u32[]{:S(2)}) %collective-permute-start.4) | collective-permute-done | bytes 1245216 | tf_op jit(solution)/shard_map/ppermute | solution.py:225
  76.2 25.0 %collective-permute-done.6.refs_5_ = bf16[256,2432]{1,0:T(8,128)(2,1)} collective-permute-done((bf16[256,2432]{1,0:T(8,128)(2,1)}, bf16[256,2432]{1,0:T(8,128)(2,1)}, u32[]{:S(2)}, u32[]{:S(2)}) %collective-permute-start.6) | collective-permute-done | bytes 1245216 | tf_op jit(solution)/shard_map/ppermute | solution.py:225
  106.2 10.5 %collective-permute-done.8.refs_7_ = bf16[128,2432]{1,0:T(8,128)(2,1)S(1)} collective-permute-done((bf16[128,2432]{1,0:T(8,128)(2,1)S(1)}, bf16[128,2432]{1,0:T(8,128)(2,1)S(1)}, u32[]{:S(2)}, u32[]{:S(2)}) %collective-permute-start.8) | collective-permute-done | bytes 622624 | tf_op jit(solution)/shard_map/ppermute | solution.py:225
  121.5 7.8 %shard_map.264 = (f32[128,2048]{1,0:T(8,128)S(1)}, bf16[128,2048]{1,0:T(8,128)(2,1)S(1)}, bf16[128,1024]{1,0:T(8,128)(2,1)S(1)}, f32[128,1280]{1,0:T(8,128)S(1)}...) custom-call(bf16[256,2432]{1,0:T(8,128)(2,1)S(1)} %fusion.1.refs_0_, ...), custom_call_target="tpu_custom_call" | custom-call | flops 7247757312 | bytes 9437184 | tf_op jit(solution)/shard_map/pallas_call | solution.py:397
  132.5 11.8 %collective-permute-done.10.refs_1_ = bf16[256,2304]{1,0:T(8,128)(2,1)} collective-permute-done((bf16[256,2304]{1,0:T(8,128)(2,1)S(1)}, bf16[256,2304]{1,0:T(8,128)(2,1)}, u32[]{:S(2)}, u32[]{:S(2)}) %collective-permute-start.10) | collective-permute-done | bytes 1179680 | tf_op jit(solution)/shard_map/ppermute | solution.py:225
  148.9 3.9 collective-permute-done.14.got
  157.7 3.8 shard_map.268
  161.5 2.7 copy-done.81
  169.2 10.2 %collective-permute-done.26.refs_1_ = bf16[128,2176]{1,0:T(8,128)(2,1)S(1)} collective-permute-done((bf16[128,2176]{1,0:T(8,128)(2,1)S(1)}, bf16[128,2176]{1,0:T(8,128)(2,1)S(1)}, u32[]{:S(2)}, u32[]{:S(2)}) %collective-permute-start.26) | collective-permute-done | bytes 557088 | tf_op jit(solution)/shard_map/ppermute | solution.py:42
  179.6 3.2 collective-permute-done.22.refs_2_
  183.0 6.4 collective-permute-done.23.refs_4_
  192.0 2.8 copy-done.82
  196.6 8.2 %shard_map.269 = (bf16[128,2048]{1,0:T(8,128)(2,1)S(1)}, bf16[128,2048]{1,0:T(8,128)(2,1)S(1)}, bf16[128,2048]{1,0:T(8,128)(2,1)S(1)}, bf16[64,2048]{1,0:T(8,128...) custom-call(bf16[128,2176]{1,0:T(8,128)(2,1)S(1)} %shard_map.267.ref, ...), custom_call_target="tpu_custom_call" | custom-call | flops 9663676416 | bytes 9437184 | tf_op jit(solution)/shard_map/pallas_call | solution.py:669
  208.4 11.8 %collective-permute-done.28.top = bf16[64,2048]{1,0:T(8,128)(2,1)S(1)} collective-permute-done((bf16[64,2048]{1,0:T(8,128)(2,1)S(1)}, bf16[64,2048]{1,0:T(8,128)(2,1)S(1)}, u32[]{:S(2)}, u32[]{:S(2)}) %collective-permute-start.28) | collective-permute-done | bytes 262176 | tf_op jit(solution)/shard_map/ppermute | solution.py:47
  223.5 6.1 collective-permute-done.30.from_x
  231.0 4.1 collective-permute-start.33
  236.0 3.8 collective-permute-done.33.refs_2_
  239.8 3.6 collective-permute-done.34.refs_3_
  246.4 19.4 %collective-permute-done.35.refs_5_ = bf16[256,2304]{1,0:T(8,128)(2,1)S(1)} collective-permute-done((bf16[256,2304]{1,0:T(8,128)(2,1)S(1)}, bf16[256,2304]{1,0:T(8,128)(2,1)S(1)}, u32[]{:S(2)}, u32[]{:S(2)}) %collective-permute-start.35) | collective-permute-done | bytes 1179680 | tf_op jit(solution)/shard_map/ppermute | solution.py:225
  265.9 3.8 collective-permute-start.37
  276.9 2.9 collective-permute-done.37.refs_7_
  279.8 3.2 collective-permute-done.38.refs_8_
  283.0 6.9 %shard_map.274 = (bf16[128,2048]{1,0:T(8,128)(2,1)S(1)}, bf16[128,1024]{1,0:T(8,128)(2,1)S(1)}, f32[128,1280]{1,0:T(8,128)S(1)}, f32[8,128,128]{2,1,0:T(8,128)S(...) custom-call(bf16[256,2304]{1,0:T(8,128)(2,1)S(1)} %copy-done.22, ...), custom_call_target="tpu_custom_call" | custom-call | flops 7247757312 | bytes 9437184 | tf_op jit(solution)/shard_map/pallas_call | solution.py:397
  294.5 14.2 %collective-permute-done.48.got = bf16[32,2048]{1,0:T(8,128)(2,1)S(1)} collective-permute-done((bf16[32,2048]{1,0:T(8,128)(2,1)}, bf16[32,2048]{1,0:T(8,128)(2,1)S(1)}, u32[]{:S(2)}, u32[]{:S(2)}) %collective-permute-start.48) | collective-permute-done | bytes 131104 | tf_op jit(solution)/shard_map/ppermute | solution.py:42
  309.3 7.1 %collective-permute-start.49 = (bf16[32,2176]{1,0:T(8,128)(2,1)S(1)}, bf16[32,2176]{1,0:T(8,128)(2,1)S(1)}, u32[]{:S(2)}, u32[]{:S(2)}) collective-permute-start(bf16[32,2176]{1,0:T(8,128)(2,1)S(1)} %get-tuple-element.236.refs_0_.refs_8_), channel_id=1, source_target_pairs={{0,4},{2,6},{4,0},{6,2},{8,12},{10,14},{12,8},{14,10},{1,5},{3,7},... | collective-permute-start | bytes 417800 | tf_op jit(solution)/shard_map/ppermute | solution.py:47
  318.9 3.8 shard_map.278
  322.7 6.3 collective-permute-done.50.refs_2_
  330.7 11.4 %collective-permute-done.56.refs_1_ = bf16[128,2176]{1,0:T(8,128)(2,1)S(1)} collective-permute-done((bf16[128,2176]{1,0:T(8,128)(2,1)S(1)}, bf16[128,2176]{1,0:T(8,128)(2,1)S(1)}, u32[]{:S(2)}, u32[]{:S(2)}) %collective-permute-start.56) | collective-permute-done | bytes 557088 | tf_op jit(solution)/shard_map/ppermute | solution.py:42
  342.3 3.3 collective-permute-start.53
  350.1 2.7 collective-permute-start.59
  355.3 8.2 %shard_map.279 = (bf16[128,2048]{1,0:T(8,128)(2,1)S(1)}, bf16[128,2048]{1,0:T(8,128)(2,1)S(1)}, bf16[128,2048]{1,0:T(8,128)(2,1)S(1)}, bf16[64,2048]{1,0:T(8,128...) custom-call(bf16[128,2176]{1,0:T(8,128)(2,1)S(1)} %shard_map.277.ref, ...), custom_call_target="tpu_custom_call" | custom-call | flops 9663676416 | bytes 9437184 | tf_op jit(solution)/shard_map/pallas_call | solution.py:669
  371.1 8.9 %shard_map.281 = (bf16[128,2176]{1,0:T(8,128)(2,1)S(1)}, bf16[128,2176]{1,0:T(8,128)(2,1)S(1)}, bf16[128,2176]{1,0:T(8,128)(2,1)S(1)}, bf16[64,2176]{1,0:T(8,128...) custom-call(bf16[128,2048]{1,0:T(8,128)(2,1)S(1)} %copy-done.52, ...), custom_call_target="tpu_custom_call" | custom-call | flops 9663676416 | bytes 9437184 | tf_op jit(solution)/shard_map/pallas_call | solution.py:757
  384.7 4.2 collective-permute-done.63.top
  388.9 3.7 collective-permute-done.64.bottom
  394.4 10.7 %collective-permute-done.65.from_x = bf16[128,2176]{1,0:T(8,128)(2,1)S(1)} collective-permute-done((bf16[128,2176]{1,0:T(8,128)(2,1)S(1)}, bf16[128,2176]{1,0:T(8,128)(2,1)S(1)}, u32[]{:S(2)}, u32[]{:S(2)}) %collective-permute-start.65) | collective-permute-done | bytes 557088 | tf_op jit(solution)/shard_map/ppermute | solution.py:42
  414.5 2.8 collective-permute-done.67.refs_1_
  419.4 3.4 collective-permute-done.72.refs_10_
  430.4 9.9 %shard_map.285 = (bf16[128,2048]{1,0:T(8,128)(2,1)}, bf16[144,1280]{1,0:T(8,128)(2,1)}, f32[64,2048]{1,0:T(8,128)}, bf16[64,2048]{1,0:T(8,128)(2,1)}) custom-call(bf16[256,2304]{1,0:T(8,128)(2,1)} %copy-done.21, bf16[256,2304]{1,0:T(8,128)(2,1)} %collective-permute-done.10.refs_1_, bf16[256,2304]{1,0:T(8,128)(2,1)} %collective-permute-done.11.refs_2_, ...), custom_call_target="tpu_custom_call" | custom-call | flops 7247757312 | bytes 9437184 | tf_op jit(solution)/shard_map/pallas_call | solution.py:501
  445.6 3.7 collective-permute-done.79.got
  457.0 3.8 shard_map.292
  460.8 2.7 copy-done.83
  467.5 9.5 %collective-permute-done.85.refs_1_ = bf16[128,2048]{1,0:T(8,128)(2,1)S(1)} collective-permute-done((bf16[128,2048]{1,0:T(8,128)(2,1)S(1)}, bf16[128,2048]{1,0:T(8,128)(2,1)S(1)}, u32[]{:S(2)}, u32[]{:S(2)}) %collective-permute-start.85) | collective-permute-done | bytes 524320 | tf_op jit(solution)/shard_map/ppermute | solution.py:42
  485.6 2.8 copy-done.84
  488.3 8.3 %shard_map.293 = (bf16[128,2176]{1,0:T(8,128)(2,1)S(1)}, bf16[128,2176]{1,0:T(8,128)(2,1)S(1)}, bf16[128,2176]{1,0:T(8,128)(2,1)S(1)}, bf16[64,2176]{1,0:T(8,128...) custom-call(bf16[128,2048]{1,0:T(8,128)(2,1)S(1)} %shard_map.289.refs_0_, ...), custom_call_target="tpu_custom_call" | custom-call | flops 9663676416 | bytes 9437184 | tf_op jit(solution)/shard_map/pallas_call | solution.py:757
  499.8 3.5 collective-permute-done.89.top
  511.4 8.8 %shard_map.296 = (f32[2,2048,384]{2,1,0:T(8,128)}, f32[2,2048,384]{2,1,0:T(8,128)}) custom-call(bf16[512,2048]{1,0:T(8,128)(2,1)} %copy-done.6, bf16[512,2048]{1,0:T(8,128)(2,1)} %copy-done.8, bf16[512,2048]{1,0:T(8,128)(2,1)} %copy-done.109, bf16[512,2048]{1,0:T(8,128)(2,1)} %copy-done.109, bf16[512,1536]{1,0:T(8,128)(2,1)} %copy-done.11, ...), custom_call_target="tpu_custom_call" | custom-call | flops 100000000 | bytes 100000 | tf_op jit(solution)/shard_map/pallas_call | solution.py:834
  520.4 2.8 collective-permute-start.96
  524.9 8.7 %shard_map.299 = (f32[2,2048,384]{2,1,0:T(8,128)}, f32[2,2048,384]{2,1,0:T(8,128)}) custom-call(bf16[512,2048]{1,0:T(8,128)(2,1)} %copy-done.6, bf16[512,2048]{1,0:T(8,128)(2,1)} %copy-done.8, bf16[512,2048]{1,0:T(8,128)(2,1)} %copy-done.109, bf16[512,2048]{1,0:T(8,128)(2,1)} %copy-done.109, ...), custom_call_target="tpu_custom_call", output_to_operand_aliasing={{0}: (8, {}), {1}: (9, {})} | custom-call | flops 100000000 | bytes 100000 | tf_op jit(solution)/shard_map/pallas_call | solution.py:834
  536.7 4.9 collective-permute-done.97.refs_10_
  543.0 4.2 all-to-all-start
  552.4 9.9 %shard_map.301 = (bf16[128,2048]{1,0:T(8,128)(2,1)}, bf16[144,1280]{1,0:T(8,128)(2,1)}, f32[64,2048]{1,0:T(8,128)}, bf16[64,2048]{1,0:T(8,128)(2,1)}) custom-call(bf16[256,2432]{1,0:T(8,128)(2,1)} %copy-done.20, bf16[256,2432]{1,0:T(8,128)(2,1)} %collective-permute-done.2.refs_1_, bf16[256,2432]{1,0:T(8,128)(2,1)} %collective-permute-done.3.refs_2_, ...), custom_call_target="tpu_custom_call" | custom-call | flops 7247757312 | bytes 9437184 | tf_op jit(solution)/shard_map/pallas_call | solution.py:501
  562.3 9.0 %collective-permute-done.101.refs_2_ = bf16[32,2048]{1,0:T(8,128)(2,1)S(1)} collective-permute-done((bf16[32,2048]{1,0:T(8,128)(2,1)}, bf16[32,2048]{1,0:T(8,128)(2,1)S(1)}, u32[]{:S(2)}, u32[]{:S(2)}) %collective-permute-start.101) | collective-permute-done | bytes 131104 | tf_op jit(solution)/shard_map/ppermute | solution.py:47
  586.1 9.1 %collective-permute-done.108.refs_1_ = bf16[144,2560]{1,0:T(8,128)(2,1)} collective-permute-done((bf16[144,2560]{1,0:T(8,128)(2,1)S(1)}, bf16[144,2560]{1,0:T(8,128)(2,1)}, u32[]{:S(2)}, u32[]{:S(2)}) %collective-permute-start.108) | collective-permute-done | bytes 737312 | tf_op jit(solution)/shard_map/ppermute | solution.py:225
  605.7 4.6 all-to-all-start.1
  611.7 5.5 shard_map.308.refs_8_
  623.4 5.6 shard_map.309
  629.0 13.1 %collective-permute-done.114.refs_5_ = bf16[144,2560]{1,0:T(8,128)(2,1)} collective-permute-done((bf16[144,2560]{1,0:T(8,128)(2,1)}, bf16[144,2560]{1,0:T(8,128)(2,1)}, u32[]{:S(2)}, u32[]{:S(2)}) %collective-permute-start.114) | collective-permute-done | bytes 737312 | tf_op jit(solution)/shard_map/ppermute | solution.py:225
  643.1 3.9 collective-permute-start.116
  652.0 6.9 %collective-permute-done.119.refs_7_ = bf16[64,2048]{1,0:T(8,128)(2,1)S(1)} collective-permute-done((bf16[64,2048]{1,0:T(8,128)(2,1)S(1)}, bf16[64,2048]{1,0:T(8,128)(2,1)S(1)}, u32[]{:S(2)}, u32[]{:S(2)}) %collective-permute-start.119) | collective-permute-done | bytes 262176 | tf_op jit(solution)/shard_map/ppermute | solution.py:225
  658.9 5.8 collective-permute-done.120.refs_8_
  664.7 7.7 %shard_map.312 = (f32[256,2048]{1,0:T(8,128)}, f32[256,256]{1,0:T(8,128)}, f32[256,256]{1,0:T(8,128)}, f32[40,256]{1,0:T(8,128)}) custom-call(bf16[144,2560]{1,0:T(8,128)(2,1)} %copy-done.32, bf16[144,2560]{1,0:T(8,128)(2,1)} %collective-permute-done.108.refs_1_, bf16[144,2560]{1,0:T(8,128)(2,1)} %collective-permute-done.109.refs_2_, ...), custom_call_target="tpu_custom_call" | custom-call | flops 15099494400 | bytes 11796480 | tf_op jit(solution)/shard_map/pallas_call | solution.py:981
  673.4 5.1 shard_map.313
  (624 shorter events, 208.1 us)
Async XLA Ops:
  9.4 30.7 %collective-permute-start.2 = (bf16[256,2432]{1,0:T(8,128)(2,1)S(1)}, bf16[256,2432]{1,0:T(8,128)(2,1)}, u32[]{:S(2)}, u32[]{:S(2)}) collective-permute-start(bf16[256,2432]{1,0:T(8,128)(2,1)S(1)} %fusion.1.refs_0_), channel_id=1, source_target_pairs={{0,4},{4,8},{8,12},{12,14},{14,10},{10,6},{6,2},{2,0},{1,5},{5,9},... | collective-permute-start | bytes 3735560 | tf_op jit(solution)/shard_map/ppermute | solution.py:225
  12.4 29.2 %collective-permute-start.3 = (bf16[256,2432]{1,0:T(8,128)(2,1)S(1)}, bf16[256,2432]{1,0:T(8,128)(2,1)}, u32[]{:S(2)}, u32[]{:S(2)}) collective-permute-start(bf16[256,2432]{1,0:T(8,128)(2,1)S(1)} %fusion.1.refs_0_), channel_id=1, source_target_pairs={{4,0},{8,4},{12,8},{14,12},{10,14},{6,10},{2,6},{0,2},{5,1},{9,5},... | collective-permute-start | bytes 3735560 | tf_op jit(solution)/shard_map/ppermute | solution.py:226
  41.8 113.6 %collective-permute-start.19 = (bf16[2,2048,384]{2,1,0:T(8,128)(2,1)}, bf16[2,2048,384]{2,1,0:T(8,128)(2,1)}, u32[]{:S(2)}, u32[]{:S(2)}) collective-permute-start(bf16[2,2048,384]{2,1,0:T(8,128)(2,1)} %bitcast.26.refs_0_), channel_id=1, source_target_pairs={{0,16},{16,0},{1,17},{17,1},{2,18},{18,2},{3,19},{19,3},{4,20},{20... | collective-permute-start | bytes 9437192 | tf_op jit(solution)/shard_map/ppermute | solution.py:38
  42.3 115.5 %collective-permute-start.20 = (bf16[2,2048,384]{2,1,0:T(8,128)(2,1)}, bf16[2,2048,384]{2,1,0:T(8,128)(2,1)}, u32[]{:S(2)}, u32[]{:S(2)}) collective-permute-start(bf16[2,2048,384]{2,1,0:T(8,128)(2,1)} %bitcast.27.refs_1_), channel_id=1, source_target_pairs={{0,16},{16,0},{1,17},{17,1},{2,18},{18,2},{3,19},{19,3},{4,20},{20... | collective-permute-start | bytes 9437192 | tf_op jit(solution)/shard_map/ppermute | solution.py:38
  42.4 115.4 %collective-permute-start.21 = (bf16[2,384,2048]{2,1,0:T(8,128)(2,1)}, bf16[2,384,2048]{2,1,0:T(8,128)(2,1)}, u32[]{:S(2)}, u32[]{:S(2)}) collective-permute-start(bf16[2,384,2048]{2,1,0:T(8,128)(2,1)} %bitcast.28.refs_2_), channel_id=1, source_target_pairs={{0,16},{16,0},{1,17},{17,1},{2,18},{18,2},{3,19},{19,3},{4,20},{20... | collective-permute-start | bytes 9437192 | tf_op jit(solution)/shard_map/ppermute | solution.py:38
  42.8 29.7 %collective-permute-start.4 = (bf16[256,2432]{1,0:T(8,128)(2,1)}, bf16[256,2432]{1,0:T(8,128)(2,1)}, u32[]{:S(2)}, u32[]{:S(2)}) collective-permute-start(bf16[256,2432]{1,0:T(8,128)(2,1)} %collective-permute-done.2.refs_1_), channel_id=1, source_target_pairs={{0,4},{4,8},{8,12},{12,14},{14,10},{10,6},{6,2},{2,0},{1,5},{5,9},... | collective-permute-start | bytes 3735560 | tf_op jit(solution)/shard_map/ppermute | solution.py:225
  44.4 29.7 %collective-permute-start.5 = (bf16[256,2432]{1,0:T(8,128)(2,1)}, bf16[256,2432]{1,0:T(8,128)(2,1)}, u32[]{:S(2)}, u32[]{:S(2)}) collective-permute-start(bf16[256,2432]{1,0:T(8,128)(2,1)} %collective-permute-done.3.refs_2_), channel_id=1, source_target_pairs={{4,0},{8,4},{12,8},{14,12},{10,14},{6,10},{2,6},{0,2},{5,1},{9,5},... | collective-permute-start | bytes 3735560 | tf_op jit(solution)/shard_map/ppermute | solution.py:226
  72.5 28.8 %collective-permute-start.6 = (bf16[256,2432]{1,0:T(8,128)(2,1)}, bf16[256,2432]{1,0:T(8,128)(2,1)}, u32[]{:S(2)}, u32[]{:S(2)}) collective-permute-start(bf16[256,2432]{1,0:T(8,128)(2,1)} %collective-permute-done.4.refs_3_), channel_id=1, source_target_pairs={{0,4},{4,8},{8,12},{12,14},{14,10},{10,6},{6,2},{2,0},{1,5},{5,9},... | collective-permute-start | bytes 3735560 | tf_op jit(solution)/shard_map/ppermute | solution.py:225
  74.0 30.0 %collective-permute-start.7 = (bf16[256,2432]{1,0:T(8,128)(2,1)}, bf16[256,2432]{1,0:T(8,128)(2,1)}, u32[]{:S(2)}, u32[]{:S(2)}) collective-permute-start(bf16[256,2432]{1,0:T(8,128)(2,1)} %collective-permute-done.5.refs_4_), channel_id=1, source_target_pairs={{4,0},{8,4},{12,8},{14,12},{10,14},{6,10},{2,6},{0,2},{5,1},{9,5},... | collective-permute-start | bytes 3735560 | tf_op jit(solution)/shard_map/ppermute | solution.py:226
  102.4 14.3 %collective-permute-start.8 = (bf16[128,2432]{1,0:T(8,128)(2,1)S(1)}, bf16[128,2432]{1,0:T(8,128)(2,1)S(1)}, u32[]{:S(2)}, u32[]{:S(2)}) collective-permute-start(bf16[128,2432]{1,0:T(8,128)(2,1)S(1)} %slice.283), channel_id=1, source_target_pairs={{0,4},{4,8},{8,12},{12,14},{14,10},{10,6},{6,2},{2,0},{1,5},{5,9},... | collective-permute-start | bytes 1867784 | tf_op jit(solution)/shard_map/ppermute | solution.py:225
  105.2 14.0 %collective-permute-start.9 = (bf16[128,2432]{1,0:T(8,128)(2,1)S(1)}, bf16[128,2432]{1,0:T(8,128)(2,1)S(1)}, u32[]{:S(2)}, u32[]{:S(2)}) collective-permute-start(bf16[128,2432]{1,0:T(8,128)(2,1)S(1)} %slice.284), channel_id=1, source_target_pairs={{4,0},{8,4},{12,8},{14,12},{10,14},{6,10},{2,6},{0,2},{5,1},{9,5},... | collective-permute-start | bytes 1867784 | tf_op jit(solution)/shard_map/ppermute | solution.py:226
  119.2 25.1 %collective-permute-start.10 = (bf16[256,2304]{1,0:T(8,128)(2,1)S(1)}, bf16[256,2304]{1,0:T(8,128)(2,1)}, u32[]{:S(2)}, u32[]{:S(2)}) collective-permute-start(bf16[256,2304]{1,0:T(8,128)(2,1)S(1)} %get-tuple-element.191.refs_0_), channel_id=1, source_target_pairs={{0,4},{4,8},{8,12},{12,14},{14,10},{10,6},{6,2},{2,0},{1,5},{5,9},... | collective-permute-start | bytes 3538952 | tf_op jit(solution)/shard_map/ppermute | solution.py:225
  120.8 24.8 %collective-permute-start.11 = (bf16[256,2304]{1,0:T(8,128)(2,1)S(1)}, bf16[256,2304]{1,0:T(8,128)(2,1)}, u32[]{:S(2)}, u32[]{:S(2)}) collective-permute-start(bf16[256,2304]{1,0:T(8,128)(2,1)S(1)} %get-tuple-element.191.refs_0_), channel_id=1, source_target_pairs={{4,0},{8,4},{12,8},{14,12},{10,14},{6,10},{2,6},{0,2},{5,1},{9,5},... | collective-permute-start | bytes 3538952 | tf_op jit(solution)/shard_map/ppermute | solution.py:226
  154.9 12.7 %collective-permute-start.17 = (bf16[32,2176]{1,0:T(8,128)(2,1)S(1)}, bf16[32,2176]{1,0:T(8,128)(2,1)S(1)}, u32[]{:S(2)}, u32[]{:S(2)}) collective-permute-start(bf16[32,2176]{1,0:T(8,128)(2,1)S(1)} %get-tuple-element.201.refs_0_.refs_8_), channel_id=1, source_target_pairs={{0,8},{2,10},{4,12},{6,14},{8,0},{10,2},{12,4},{14,6},{1,9},{3,11}... | collective-permute-start | bytes 417800 | tf_op jit(solution)/shard_map/ppermute | solution.py:47
  169.2 13.6 %collective-permute-start.22 = (bf16[128,2176]{1,0:T(8,128)(2,1)S(1)}, bf16[128,2176]{1,0:T(8,128)(2,1)S(1)}, u32[]{:S(2)}, u32[]{:S(2)}) collective-permute-start(bf16[128,2176]{1,0:T(8,128)(2,1)S(1)} %shard_map.267.refs_0_), channel_id=1, source_target_pairs={{0,2},{2,0},{4,6},{6,4},{8,10},{10,8},{12,14},{14,12},{1,3},{3,1},... | collective-permute-start | bytes 1671176 | tf_op jit(solution)/shard_map/ppermute | solution.py:47
  179.3 12.6 %collective-permute-start.27 = (bf16[64,2176]{1,0:T(8,128)(2,1)S(1)}, bf16[64,2176]{1,0:T(8,128)(2,1)S(1)}, u32[]{:S(2)}, u32[]{:S(2)}) collective-permute-start(bf16[64,2176]{1,0:T(8,128)(2,1)S(1)} %slice.292), channel_id=1, source_target_pairs={{0,2},{2,0},{4,6},{6,4},{8,10},{10,8},{12,14},{14,12},{1,3},{3,1},... | collective-permute-start | bytes 835592 | tf_op jit(solution)/shard_map/ppermute | solution.py:47
  189.4 40.2 %collective-permute-start.24 = (bf16[256,2304]{1,0:T(8,128)(2,1)}, bf16[256,2304]{1,0:T(8,128)(2,1)S(1)}, u32[]{:S(2)}, u32[]{:S(2)}) collective-permute-start(bf16[256,2304]{1,0:T(8,128)(2,1)} %collective-permute-done.10.refs_1_), channel_id=1, source_target_pairs={{0,4},{4,8},{8,12},{12,14},{14,10},{10,6},{6,2},{2,0},{1,5},{5,9},... | collective-permute-start | bytes 3538952 | tf_op jit(solution)/shard_map/ppermute | solution.py:225
  191.8 37.8 %collective-permute-start.25 = (bf16[256,2304]{1,0:T(8,128)(2,1)}, bf16[256,2304]{1,0:T(8,128)(2,1)S(1)}, u32[]{:S(2)}, u32[]{:S(2)}) collective-permute-start(bf16[256,2304]{1,0:T(8,128)(2,1)} %collective-permute-done.11.refs_2_), channel_id=1, source_target_pairs={{4,0},{8,4},{12,8},{14,12},{10,14},{6,10},{2,6},{0,2},{5,1},{9,5},... | collective-permute-start | bytes 3538952 | tf_op jit(solution)/shard_map/ppermute | solution.py:226
  206.5 13.7 %collective-permute-start.28 = (bf16[64,2048]{1,0:T(8,128)(2,1)S(1)}, bf16[64,2048]{1,0:T(8,128)(2,1)S(1)}, u32[]{:S(2)}, u32[]{:S(2)}) collective-permute-start(bf16[64,2048]{1,0:T(8,128)(2,1)S(1)} %get-tuple-element.213), channel_id=1, source_target_pairs={{0,2},{2,0},{4,6},{6,4},{8,10},{10,8},{12,14},{14,12},{1,3},{3,1},... | collective-permute-start | bytes 786440 | tf_op jit(solution)/shard_map/ppermute | solution.py:47
  206.9 13.3 %collective-permute-start.29 = (bf16[64,2048]{1,0:T(8,128)(2,1)S(1)}, bf16[64,2048]{1,0:T(8,128)(2,1)S(1)}, u32[]{:S(2)}, u32[]{:S(2)}) collective-permute-start(bf16[64,2048]{1,0:T(8,128)(2,1)S(1)} %get-tuple-element.215), channel_id=1, source_target_pairs={{0,1},{1,0},{2,3},{3,2},{4,5},{5,4},{6,7},{7,6},{8,9},{9,8},{10,11... | collective-permute-start | bytes 786440 | tf_op jit(solution)/shard_map/ppermute | solution.py:42
  243.4 22.5 %collective-permute-start.35 = (bf16[256,2304]{1,0:T(8,128)(2,1)S(1)}, bf16[256,2304]{1,0:T(8,128)(2,1)S(1)}, u32[]{:S(2)}, u32[]{:S(2)}) collective-permute-start(bf16[256,2304]{1,0:T(8,128)(2,1)S(1)} %collective-permute-done.24.refs_3_), channel_id=1, source_target_pairs={{0,4},{4,8},{8,12},{12,14},{14,10},{10,6},{6,2},{2,0},{1,5},{5,9},... | collective-permute-start | bytes 3538952 | tf_op jit(solution)/shard_map/ppermute | solution.py:225
  244.6 25.2 %collective-permute-start.36 = (bf16[256,2304]{1,0:T(8,128)(2,1)S(1)}, bf16[256,2304]{1,0:T(8,128)(2,1)S(1)}, u32[]{:S(2)}, u32[]{:S(2)}) collective-permute-start(bf16[256,2304]{1,0:T(8,128)(2,1)S(1)} %collective-permute-done.25.refs_4_), channel_id=1, source_target_pairs={{4,0},{8,4},{12,8},{14,12},{10,14},{6,10},{2,6},{0,2},{5,1},{9,5},... | collective-permute-start | bytes 3538952 | tf_op jit(solution)/shard_map/ppermute | solution.py:226
  245.7 24.3 %collective-permute-start.39 = (bf16[32,2048]{1,0:T(8,128)(2,1)S(1)}, bf16[32,2048]{1,0:T(8,128)(2,1)S(1)}, u32[]{:S(2)}, u32[]{:S(2)}) collective-permute-start(bf16[32,2048]{1,0:T(8,128)(2,1)S(1)} %get-tuple-element.226.refs_9_), channel_id=1, source_target_pairs={{0,1},{1,0},{2,3},{3,2},{4,5},{5,4},{6,7},{7,6},{8,9},{9,8},{10,11... | collective-permute-start | bytes 393224 | tf_op jit(solution)/shard_map/ppermute | solution.py:42
  265.9 13.9 %collective-permute-start.37 = (bf16[128,2304]{1,0:T(8,128)(2,1)S(1)}, bf16[128,2304]{1,0:T(8,128)(2,1)S(1)}, u32[]{:S(2)}, u32[]{:S(2)}) collective-permute-start(bf16[128,2304]{1,0:T(8,128)(2,1)S(1)} %slice.293), channel_id=1, source_target_pairs={{0,4},{4,8},{8,12},{12,14},{14,10},{10,6},{6,2},{2,0},{1,5},{5,9},... | collective-permute-start | bytes 1769480 | tf_op jit(solution)/shard_map/ppermute | solution.py:225
  269.8 13.2 %collective-permute-start.38 = (bf16[128,2304]{1,0:T(8,128)(2,1)S(1)}, bf16[128,2304]{1,0:T(8,128)(2,1)S(1)}, u32[]{:S(2)}, u32[]{:S(2)}) collective-permute-start(bf16[128,2304]{1,0:T(8,128)(2,1)S(1)} %slice.294), channel_id=1, source_target_pairs={{4,0},{8,4},{12,8},{14,12},{10,14},{6,10},{2,6},{0,2},{5,1},{9,5},... | collective-permute-start | bytes 1769480 | tf_op jit(solution)/shard_map/ppermute | solution.py:226
  271.5 19.3 %collective-permute-start.41 = (bf16[32,2048]{1,0:T(8,128)(2,1)S(1)}, bf16[32,2048]{1,0:T(8,128)(2,1)S(1)}, u32[]{:S(2)}, u32[]{:S(2)}) collective-permute-start(bf16[32,2048]{1,0:T(8,128)(2,1)S(1)} %fusion.3.refs_0_.refs_4_), channel_id=1, source_target_pairs={{0,4},{2,6},{4,0},{6,2},{8,12},{10,14},{12,8},{14,10},{1,5},{3,7},... | collective-permute-start | bytes 393224 | tf_op jit(solution)/shard_map/ppermute | solution.py:47
  274.0 17.5 %collective-permute-start.42 = (bf16[32,2048]{1,0:T(8,128)(2,1)S(1)}, bf16[32,2048]{1,0:T(8,128)(2,1)S(1)}, u32[]{:S(2)}, u32[]{:S(2)}) collective-permute-start(bf16[32,2048]{1,0:T(8,128)(2,1)S(1)} %fusion.3.refs_0_.refs_4_), channel_id=1, source_target_pairs={{0,8},{2,10},{4,12},{6,14},{8,0},{10,2},{12,4},{14,6},{1,9},{3,11}... | collective-permute-start | bytes 393224 | tf_op jit(solution)/shard_map/ppermute | solution.py:47
  275.5 16.0 %collective-permute-start.43 = (bf16[32,2048]{1,0:T(8,128)(2,1)S(1)}, bf16[32,2048]{1,0:T(8,128)(2,1)S(1)}, u32[]{:S(2)}, u32[]{:S(2)}) collective-permute-start(bf16[32,2048]{1,0:T(8,128)(2,1)S(1)} %fusion.3.refs_0_.refs_4_), channel_id=1, source_target_pairs={{0,12},{2,14},{4,8},{6,10},{8,4},{10,6},{12,0},{14,2},{1,13},{3,15... | collective-permute-start | bytes 393224 | tf_op jit(solution)/shard_map/ppermute | solution.py:47
  291.5 17.8 %collective-permute-start.45 = (bf16[128,2048]{1,0:T(8,128)(2,1)S(1)}, bf16[128,2048]{1,0:T(8,128)(2,1)S(1)}, u32[]{:S(2)}, u32[]{:S(2)}) collective-permute-start(bf16[128,2048]{1,0:T(8,128)(2,1)S(1)} %shard_map.273.refs_0_), channel_id=1, source_target_pairs={{0,1},{1,0},{2,3},{3,2},{4,5},{5,4},{6,7},{7,6},{8,9},{9,8},{10,11... | collective-permute-start | bytes 1572872 | tf_op jit(solution)/shard_map/ppermute | solution.py:42
  292.0 17.3 %collective-permute-start.46 = (bf16[128,2048]{1,0:T(8,128)(2,1)S(1)}, bf16[128,2048]{1,0:T(8,128)(2,1)}, u32[]{:S(2)}, u32[]{:S(2)}) collective-permute-start(bf16[128,2048]{1,0:T(8,128)(2,1)S(1)} %shard_map.273.refs_0_), channel_id=1, source_target_pairs={{0,2},{2,0},{4,6},{6,4},{8,10},{10,8},{12,14},{14,12},{1,3},{3,1},... | collective-permute-start | bytes 1572872 | tf_op jit(solution)/shard_map/ppermute | solution.py:47
  293.7 15.0 %collective-permute-start.48 = (bf16[32,2048]{1,0:T(8,128)(2,1)}, bf16[32,2048]{1,0:T(8,128)(2,1)S(1)}, u32[]{:S(2)}, u32[]{:S(2)}) collective-permute-start(bf16[32,2048]{1,0:T(8,128)(2,1)} %get-tuple-element.234), channel_id=1, source_target_pairs={{0,1},{1,0},{2,3},{3,2},{4,5},{5,4},{6,7},{7,6},{8,9},{9,8},{10,11... | collective-permute-start | bytes 393224 | tf_op jit(solution)/shard_map/ppermute | solution.py:42
  309.3 13.4 %collective-permute-start.49 = (bf16[32,2176]{1,0:T(8,128)(2,1)S(1)}, bf16[32,2176]{1,0:T(8,128)(2,1)S(1)}, u32[]{:S(2)}, u32[]{:S(2)}) collective-permute-start(bf16[32,2176]{1,0:T(8,128)(2,1)S(1)} %get-tuple-element.236.refs_0_.refs_8_), channel_id=1, source_target_pairs={{0,4},{2,6},{4,0},{6,2},{8,12},{10,14},{12,8},{14,10},{1,5},{3,7},... | collective-permute-start | bytes 417800 | tf_op jit(solution)/shard_map/ppermute | solution.py:47
  329.1 13.0 %collective-permute-start.56 = (bf16[128,2176]{1,0:T(8,128)(2,1)S(1)}, bf16[128,2176]{1,0:T(8,128)(2,1)S(1)}, u32[]{:S(2)}, u32[]{:S(2)}) collective-permute-start(bf16[128,2176]{1,0:T(8,128)(2,1)S(1)} %shard_map.277.refs_0_), channel_id=1, source_target_pairs={{0,1},{1,0},{2,3},{3,2},{4,5},{5,4},{6,7},{7,6},{8,9},{9,8},{10,11... | collective-permute-start | bytes 1671176 | tf_op jit(solution)/shard_map/ppermute | solution.py:42
  342.1 13.1 %collective-permute-start.57 = (bf16[64,2176]{1,0:T(8,128)(2,1)S(1)}, bf16[64,2176]{1,0:T(8,128)(2,1)S(1)}, u32[]{:S(2)}, u32[]{:S(2)}) collective-permute-start(bf16[64,2176]{1,0:T(8,128)(2,1)S(1)} %slice.302), channel_id=1, source_target_pairs={{0,2},{2,0},{4,6},{6,4},{8,10},{10,8},{12,14},{14,12},{1,3},{3,1},... | collective-permute-start | bytes 835592 | tf_op jit(solution)/shard_map/ppermute | solution.py:47
  350.1 18.4 %collective-permute-start.59 = (bf16[128,2048]{1,0:T(8,128)(2,1)S(1)}, bf16[128,2048]{1,0:T(8,128)(2,1)S(1)}, u32[]{:S(2)}, u32[]{:S(2)}) collective-permute-start(bf16[128,2048]{1,0:T(8,128)(2,1)S(1)} %shard_map.280.refs_0_), channel_id=1, source_target_pairs={{0,4},{4,8},{8,12},{12,14},{14,10},{10,6},{6,2},{2,0},{1,5},{5,9},... | collective-permute-start | bytes 1572872 | tf_op jit(solution)/shard_map/ppermute | solution.py:225
  352.8 15.7 %collective-permute-start.60 = (bf16[128,2048]{1,0:T(8,128)(2,1)S(1)}, bf16[128,2048]{1,0:T(8,128)(2,1)S(1)}, u32[]{:S(2)}, u32[]{:S(2)}) collective-permute-start(bf16[128,2048]{1,0:T(8,128)(2,1)S(1)} %shard_map.280.refs_0_), channel_id=1, source_target_pairs={{4,0},{8,4},{12,8},{14,12},{10,14},{6,10},{2,6},{0,2},{5,1},{9,5},... | collective-permute-start | bytes 1572872 | tf_op jit(solution)/shard_map/ppermute | solution.py:226
  353.2 15.3 %collective-permute-start.54 = (bf16[64,2048]{1,0:T(8,128)(2,1)S(1)}, bf16[64,2048]{1,0:T(8,128)(2,1)S(1)}, u32[]{:S(2)}, u32[]{:S(2)}) collective-permute-start(bf16[64,2048]{1,0:T(8,128)(2,1)S(1)} %slice.299), channel_id=1, source_target_pairs={{0,2},{2,0},{4,6},{6,4},{8,10},{10,8},{12,14},{14,12},{1,3},{3,1},... | collective-permute-start | bytes 786440 | tf_op jit(solution)/shard_map/ppermute | solution.py:47
  354.9 13.6 %collective-permute-start.55 = (bf16[64,2048]{1,0:T(8,128)(2,1)S(1)}, bf16[64,2048]{1,0:T(8,128)(2,1)S(1)}, u32[]{:S(2)}, u32[]{:S(2)}) collective-permute-start(bf16[64,2048]{1,0:T(8,128)(2,1)S(1)} %slice.301), channel_id=1, source_target_pairs={{0,1},{1,0},{2,3},{3,2},{4,5},{5,4},{6,7},{7,6},{8,9},{9,8},{10,11... | collective-permute-start | bytes 786440 | tf_op jit(solution)/shard_map/ppermute | solution.py:42
  368.5 12.6 %collective-permute-start.61 = (bf16[128,2048]{1,0:T(8,128)(2,1)S(1)}, bf16[128,2048]{1,0:T(8,128)(2,1)}, u32[]{:S(2)}, u32[]{:S(2)}) collective-permute-start(bf16[128,2048]{1,0:T(8,128)(2,1)S(1)} %collective-permute-done.59.refs_1_), channel_id=1, source_target_pairs={{0,4},{4,8},{8,12},{12,14},{14,10},{10,6},{6,2},{2,0},{1,5},{5,9},... | collective-permute-start | bytes 1572872 | tf_op jit(solution)/shard_map/ppermute | solution.py:225
  425.6 15.3 %collective-permute-start.77 = (bf16[512,2048]{1,0:T(8,128)(2,1)}, bf16[512,2048]{1,0:T(8,128)(2,1)S(1)}, u32[]{:S(2)}, u32[]{:S(2)}) collective-permute-start(bf16[512,2048]{1,0:T(8,128)(2,1)} %shard_map.286), channel_id=1, source_target_pairs={{0,16},{16,0},{1,17},{17,1},{2,18},{18,2},{3,19},{19,3},{4,20},{20... | collective-permute-start | bytes 6291464 | tf_op jit(solution)/shard_map/ppermute | solution.py:38
  426.2 14.2 %collective-permute-start.75 = (bf16[128,2048]{1,0:T(8,128)(2,1)}, bf16[128,2048]{1,0:T(8,128)(2,1)S(1)}, u32[]{:S(2)}, u32[]{:S(2)}) collective-permute-start(bf16[128,2048]{1,0:T(8,128)(2,1)} %collective-permute-done.61.refs_3_), channel_id=1, source_target_pairs={{0,4},{4,8},{8,12},{12,14},{14,10},{10,6},{6,2},{2,0},{1,5},{5,9},... | collective-permute-start | bytes 1572872 | tf_op jit(solution)/shard_map/ppermute | solution.py:225
  426.8 14.2 %collective-permute-start.76 = (bf16[128,2048]{1,0:T(8,128)(2,1)}, bf16[128,2048]{1,0:T(8,128)(2,1)}, u32[]{:S(2)}, u32[]{:S(2)}) collective-permute-start(bf16[128,2048]{1,0:T(8,128)(2,1)} %collective-permute-done.62.refs_4_), channel_id=1, source_target_pairs={{4,0},{8,4},{12,8},{14,12},{10,14},{6,10},{2,6},{0,2},{5,1},{9,5},... | collective-permute-start | bytes 1572872 | tf_op jit(solution)/shard_map/ppermute | solution.py:226
  449.6 16.0 %collective-permute-start.83 = (bf16[128,2048]{1,0:T(8,128)(2,1)S(1)}, bf16[128,2048]{1,0:T(8,128)(2,1)S(1)}, u32[]{:S(2)}, u32[]{:S(2)}) collective-permute-start(bf16[128,2048]{1,0:T(8,128)(2,1)S(1)} %get-tuple-element.290), channel_id=1, source_target_pairs={{0,1},{1,0},{2,3},{3,2},{4,5},{5,4},{6,7},{7,6},{8,9},{9,8},{10,11... | collective-permute-start | bytes 1572872 | tf_op jit(solution)/shard_map/ppermute | solution.py:42
  451.4 14.2 %collective-permute-start.84 = (bf16[128,2048]{1,0:T(8,128)(2,1)S(1)}, bf16[128,2048]{1,0:T(8,128)(2,1)S(1)}, u32[]{:S(2)}, u32[]{:S(2)}) collective-permute-start(bf16[128,2048]{1,0:T(8,128)(2,1)S(1)} %get-tuple-element.292), channel_id=1, source_target_pairs={{0,2},{2,0},{4,6},{6,4},{8,10},{10,8},{12,14},{14,12},{1,3},{3,1},... | collective-permute-start | bytes 1572872 | tf_op jit(solution)/shard_map/ppermute | solution.py:47
  505.8 14.3 %collective-permute-start.91 = (bf16[128,2176]{1,0:T(8,128)(2,1)S(1)}, bf16[128,2176]{1,0:T(8,128)(2,1)S(1)}, u32[]{:S(2)}, u32[]{:S(2)}) collective-permute-start(bf16[128,2176]{1,0:T(8,128)(2,1)S(1)} %get-tuple-element.305), channel_id=1, source_target_pairs={{0,1},{1,0},{2,3},{3,2},{4,5},{5,4},{6,7},{7,6},{8,9},{9,8},{10,11... | collective-permute-start | bytes 1671176 | tf_op jit(solution)/shard_map/ppermute | solution.py:42
  520.4 13.2 %collective-permute-start.96 = (bf16[32,2176]{1,0:T(8,128)(2,1)S(1)}, bf16[32,2176]{1,0:T(8,128)(2,1)S(1)}, u32[]{:S(2)}, u32[]{:S(2)}) collective-permute-start(bf16[32,2176]{1,0:T(8,128)(2,1)S(1)} %get-tuple-element.319), channel_id=1, source_target_pairs={{0,12},{2,14},{4,8},{6,10},{8,4},{10,6},{12,0},{14,2},{1,13},{3,15... | collective-permute-start | bytes 417800 | tf_op jit(solution)/shard_map/ppermute | solution.py:47
  543.0 29.7 %all-to-all-start = ((bf16[8,128,256]{2,1,0:T(8,128)(2,1)}), bf16[8,128,256]{2,1,0:T(8,128)(2,1)}, u32[]{:S(2)}, u32[]{:S(2)}) async-start(bf16[8,128,256]{2,1,0:T(8,128)(2,1)} %copy-done.117), calls=%async_computation | async-start | bytes 1048576 | tf_op jit(solution)/shard_map/all_to_all | solution.py:1215
  547.4 14.9 %collective-permute-start.100 = (bf16[32,2048]{1,0:T(8,128)(2,1)}, bf16[32,2048]{1,0:T(8,128)(2,1)S(1)}, u32[]{:S(2)}, u32[]{:S(2)}) collective-permute-start(bf16[32,2048]{1,0:T(8,128)(2,1)} %copy-done.95), channel_id=1, source_target_pairs={{0,4},{2,6},{4,0},{6,2},{8,12},{10,14},{12,8},{14,10},{1,5},{3,7},... | collective-permute-start | bytes 393224 | tf_op jit(solution)/shard_map/ppermute | solution.py:47
  549.1 22.3 %collective-permute-start.101 = (bf16[32,2048]{1,0:T(8,128)(2,1)}, bf16[32,2048]{1,0:T(8,128)(2,1)S(1)}, u32[]{:S(2)}, u32[]{:S(2)}) collective-permute-start(bf16[32,2048]{1,0:T(8,128)(2,1)} %copy-done.94), channel_id=1, source_target_pairs={{0,8},{2,10},{4,12},{6,14},{8,0},{10,2},{12,4},{14,6},{1,9},{3,11}... | collective-permute-start | bytes 393224 | tf_op jit(solution)/shard_map/ppermute | solution.py:47
  551.5 20.6 %collective-permute-start.102 = (bf16[32,2048]{1,0:T(8,128)(2,1)}, bf16[32,2048]{1,0:T(8,128)(2,1)S(1)}, u32[]{:S(2)}, u32[]{:S(2)}) collective-permute-start(bf16[32,2048]{1,0:T(8,128)(2,1)} %copy-done.93), channel_id=1, source_target_pairs={{0,12},{2,14},{4,8},{6,10},{8,4},{10,6},{12,0},{14,2},{1,13},{3,15... | collective-permute-start | bytes 393224 | tf_op jit(solution)/shard_map/ppermute | solution.py:47
  576.6 18.7 %collective-permute-start.108 = (bf16[144,2560]{1,0:T(8,128)(2,1)S(1)}, bf16[144,2560]{1,0:T(8,128)(2,1)}, u32[]{:S(2)}, u32[]{:S(2)}) collective-permute-start(bf16[144,2560]{1,0:T(8,128)(2,1)S(1)} %shard_map.302.refs_0_), channel_id=1, source_target_pairs={{0,4},{4,8},{8,12},{12,14},{14,10},{10,6},{6,2},{2,0},{1,5},{5,9},... | collective-permute-start | bytes 2211848 | tf_op jit(solution)/shard_map/ppermute | solution.py:225
  578.6 18.6 %collective-permute-start.109 = (bf16[144,2560]{1,0:T(8,128)(2,1)S(1)}, bf16[144,2560]{1,0:T(8,128)(2,1)}, u32[]{:S(2)}, u32[]{:S(2)}) collective-permute-start(bf16[144,2560]{1,0:T(8,128)(2,1)S(1)} %shard_map.302.refs_0_), channel_id=1, source_target_pairs={{4,0},{8,4},{12,8},{14,12},{10,14},{6,10},{2,6},{0,2},{5,1},{9,5},... | collective-permute-start | bytes 2211848 | tf_op jit(solution)/shard_map/ppermute | solution.py:226
  583.4 27.0 %collective-permute-start.112 = (bf16[512,768]{1,0:T(8,128)(2,1)}, bf16[512,768]{1,0:T(8,128)(2,1)}, u32[]{:S(2)}, u32[]{:S(2)}) collective-permute-start(bf16[512,768]{1,0:T(8,128)(2,1)} %shard_map.306), channel_id=1, source_target_pairs={{0,16},{16,0},{1,17},{17,1},{2,18},{18,2},{3,19},{19,3},{4,20},{20... | collective-permute-start | bytes 2359304 | tf_op jit(solution)/shard_map/ppermute | solution.py:38
  585.0 25.4 %collective-permute-start.113 = (bf16[512,2048]{1,0:T(8,128)(2,1)}, bf16[512,2048]{1,0:T(8,128)(2,1)S(1)}, u32[]{:S(2)}, u32[]{:S(2)}) collective-permute-start(bf16[512,2048]{1,0:T(8,128)(2,1)} %shard_map.307), channel_id=1, source_target_pairs={{0,16},{16,0},{1,17},{17,1},{2,18},{18,2},{3,19},{19,3},{4,20},{20... | collective-permute-start | bytes 6291464 | tf_op jit(solution)/shard_map/ppermute | solution.py:38
  598.0 23.3 %collective-permute-start.106 = (bf16[32,2048]{1,0:T(8,128)(2,1)}, bf16[32,2048]{1,0:T(8,128)(2,1)}, u32[]{:S(2)}, u32[]{:S(2)}) collective-permute-start(bf16[32,2048]{1,0:T(8,128)(2,1)} %broadcast_select_fusion.12), channel_id=1, source_target_pairs={{0,16},{16,0},{1,17},{17,1},{2,18},{18,2},{3,19},{19,3},{4,20},{20... | collective-permute-start | bytes 393224 | tf_op jit(solution)/shard_map/ppermute | solution.py:38
  598.5 20.8 %collective-permute-start.110 = (bf16[144,2560]{1,0:T(8,128)(2,1)}, bf16[144,2560]{1,0:T(8,128)(2,1)}, u32[]{:S(2)}, u32[]{:S(2)}) collective-permute-start(bf16[144,2560]{1,0:T(8,128)(2,1)} %collective-permute-done.108.refs_1_), channel_id=1, source_target_pairs={{0,4},{4,8},{8,12},{12,14},{14,10},{10,6},{6,2},{2,0},{1,5},{5,9},... | collective-permute-start | bytes 2211848 | tf_op jit(solution)/shard_map/ppermute | solution.py:225
  599.5 19.8 %collective-permute-start.111 = (bf16[144,2560]{1,0:T(8,128)(2,1)}, bf16[144,2560]{1,0:T(8,128)(2,1)}, u32[]{:S(2)}, u32[]{:S(2)}) collective-permute-start(bf16[144,2560]{1,0:T(8,128)(2,1)} %collective-permute-done.109.refs_2_), channel_id=1, source_target_pairs={{4,0},{8,4},{12,8},{14,12},{10,14},{6,10},{2,6},{0,2},{5,1},{9,5},... | collective-permute-start | bytes 2211848 | tf_op jit(solution)/shard_map/ppermute | solution.py:226
  605.7 46.3 %all-to-all-start.1 = ((bf16[8,160,256]{2,1,0:T(8,128)(2,1)}), bf16[8,160,256]{2,1,0:T(8,128)(2,1)S(1)}, u32[]{:S(2)}, u32[]{:S(2)}) async-start(bf16[8,160,256]{2,1,0:T(8,128)(2,1)} %fusion.4), calls=%async_computation.1 | async-start | bytes 1310720 | tf_op jit(solution)/shard_map/all_to_all | solution.py:1215
  619.3 22.8 %collective-permute-start.114 = (bf16[144,2560]{1,0:T(8,128)(2,1)}, bf16[144,2560]{1,0:T(8,128)(2,1)}, u32[]{:S(2)}, u32[]{:S(2)}) collective-permute-start(bf16[144,2560]{1,0:T(8,128)(2,1)} %collective-permute-done.110.refs_3_), channel_id=1, source_target_pairs={{0,4},{4,8},{8,12},{12,14},{14,10},{10,6},{6,2},{2,0},{1,5},{5,9},... | collective-permute-start | bytes 2211848 | tf_op jit(solution)/shard_map/ppermute | solution.py:225
  619.3 27.7 %collective-permute-start.115 = (bf16[144,2560]{1,0:T(8,128)(2,1)}, bf16[144,2560]{1,0:T(8,128)(2,1)}, u32[]{:S(2)}, u32[]{:S(2)}) collective-permute-start(bf16[144,2560]{1,0:T(8,128)(2,1)} %collective-permute-done.111.refs_4_), channel_id=1, source_target_pairs={{4,0},{8,4},{12,8},{14,12},{10,14},{6,10},{2,6},{0,2},{5,1},{9,5},... | collective-permute-start | bytes 2211848 | tf_op jit(solution)/shard_map/ppermute | solution.py:226
  622.3 28.7 %collective-permute-start.107 = (bf16[2,32,2048]{2,1,0:T(8,128)(2,1)S(1)}, bf16[2,32,2048]{2,1,0:T(8,128)(2,1)}, u32[]{:S(2)}, u32[]{:S(2)}) collective-permute-start(bf16[2,32,2048]{2,1,0:T(8,128)(2,1)S(1)} %pad_maximum_fusion.3), channel_id=1, source_target_pairs={{0,1},{1,0},{2,3},{3,2},{4,5},{5,4},{6,7},{7,6},{8,9},{9,8},{10,11... | collective-permute-start | bytes 786440 | tf_op jit(solution)/shard_map/ppermute | solution.py:42
  643.1 21.6 %collective-permute-start.116 = (bf16[64,2560]{1,0:T(8,128)(2,1)S(1)}, bf16[64,2560]{1,0:T(8,128)(2,1)}, u32[]{:S(2)}, u32[]{:S(2)}) collective-permute-start(bf16[64,2560]{1,0:T(8,128)(2,1)S(1)} %slice.313), channel_id=1, source_target_pairs={{0,4},{4,8},{8,12},{12,14},{14,10},{10,6},{6,2},{2,0},{1,5},{5,9},... | collective-permute-start | bytes 983048 | tf_op jit(solution)/shard_map/ppermute | solution.py:225
  648.0 16.7 %collective-permute-start.117 = (bf16[80,2560]{1,0:T(8,128)(2,1)S(1)}, bf16[80,2560]{1,0:T(8,128)(2,1)}, u32[]{:S(2)}, u32[]{:S(2)}) collective-permute-start(bf16[80,2560]{1,0:T(8,128)(2,1)S(1)} %slice.314), channel_id=1, source_target_pairs={{4,0},{8,4},{12,8},{14,12},{10,14},{6,10},{2,6},{0,2},{5,1},{9,5},... | collective-permute-start | bytes 1228808 | tf_op jit(solution)/shard_map/ppermute | solution.py:226
  650.6 14.1 %collective-permute-start.120 = (bf16[64,2048]{1,0:T(8,128)(2,1)S(1)}, bf16[64,2048]{1,0:T(8,128)(2,1)S(1)}, u32[]{:S(2)}, u32[]{:S(2)}) collective-permute-start(bf16[64,2048]{1,0:T(8,128)(2,1)S(1)} %slice.324), channel_id=1, source_target_pairs={{4,0},{8,4},{12,8},{14,12},{10,14},{6,10},{2,6},{0,2},{5,1},{9,5},... | collective-permute-start | bytes 786440 | tf_op jit(solution)/shard_map/ppermute | solution.py:226
  (207 other events, 3225.3 us)

commit v5 on v4

--- a/solution.py
+++ b/solution.py
@@ -682,7 +682,7 @@
         )
         + [pltpu.VMEM(shapes[count].shape, shapes[count].dtype)],
         input_output_aliases={count + 3: count + 2, count + 4: count + 3} if stores else {},
-        compiler_params=kernel_params(32),
+        compiler_params=kernel_params(26),
         cost_estimate=cost(12 * tile_rows * width * total_units, 6 * width * total_units),
     )(*pieces, *weights, ones, *stores)
     return list(outs[:count]), outs[count : count + 2], outs[count + 2 :]
@@ -771,7 +771,7 @@
         )
         + [pltpu.VMEM(act.shape, act.dtype)],
         input_output_aliases={count + 5: count, count + 6: count + 1} if stores else {},
-        compiler_params=kernel_params(32),
+        compiler_params=kernel_params(26),
         cost_estimate=cost(12 * tile_rows * width * total_units, 6 * width * total_units),
     )(*pieces, *weights, ones, act, gates, *stores)
     return list(outs[:count]), outs[count:]
@@ -1357,12 +1357,12 @@
         1, ring1, breadth, split, experts, (*normed_pieces, tiny), tables
     )
     other = after(other, *along)
-    beside = grad_gather.near(own)
     mid1, payload1, gates1 = route(1, x_mid, *own_rows(own, other), tiny, masks[1])
-    gather = Gather(after(payload1, *beside))
+    beside = grad_gather.near(payload1)
+    gather = Gather(payload1)
     gather.along_z()
     weights1 = choose_weights(1, (after(expert_weights[0], payload1), *expert_weights[1:]))
-    gather.near(*weights1)
+    gather.near(*weights1, *beside)
     gather.far()
     tiles = gather.tiles()
     beside = grad_gather.far(tiles[-1][-1])
@@ -1397,8 +1397,10 @@
         1, ring1, breadth, split, experts, d_pieces, raw1, probs1, tiny, tables
     )
     d_other = after(d_other, *ring_mixed.latest, *early)
+    ring_mixed.advance(d_qkv1)
     d_one = leave(1, experts, *own_rows(d_own, d_other), x_mid, d_mid, tiny)
 
+    d_one = after(d_one, *ring_mixed.latest)
     gather = Gather(d_one)
     gather.along_z()
     beside = out_scatter.near(d_one)
@@ -1460,7 +1462,6 @@
     late_spread = to_owners(by_columns(late_rows, split))
     three_rounds = ring_d.advance(*down[0])
     ring_d.advance(*down[1])
-    ring_mixed.advance(*three_rounds)
     g_out = out_grads(ring_mixed, late_spread)
     out1 = finish(mid1, out_parts)
     end_own = pick(d_zero, out1)

time: 689 us -> 671 us (0.974)
  waiting for transfers between devices: 345 us -> 335 us
    ppermute x25, waiting for transfers between devices: 94.6 us -> 81.8 us  [swap_x(): return lax.ppermute(value, 'tensor', [(0, 1), (1, 0)])]
    unnamed x309 -> x307, local copies, waits for them, and re-layouts: 43.9 us -> 40.3 us
  transfers between devices with their start and end apart: 124 -> 124, of which waited for: 64 -> 65; matrix products, arithmetic and copies ran while one was open for 3% -> 3% of each run, Pallas kernels for 16% -> 16%
where the time goes in v5:
time: 671 us; the launch traced here: 663 us
  waiting for transfers between devices  335 us (50%)
  starting transfers between devices  140 us (21%)
  Pallas kernels  129 us (19%)
  local copies, waits for them, and re-layouts  46.8 us (7%)
  other arithmetic  10.1 us (2%)
    ppermute x16, waiting for transfers between devices, advance(): self.plus = lax.ppermute(after(plus, *gate), 'expert', up)  155 us
    ppermute x25, waiting for transfers between devices, swap_x(): return lax.ppermute(value, 'tensor', [(0, 1), (1, 0)])  81.8 us
    ppermute x40, waiting for transfers between devices, swap_e(): return lax.ppermute(value, 'expert', [(i, i ^ bits) for i in range(count)])  65.6 us
    ppermute x40, starting transfers between devices, swap_e(): return lax.ppermute(value, 'expert', [(i, i ^ bits) for i in range(count)])  60.9 us
    unnamed x307, local copies, waits for them, and re-layouts  40.3 us
    ppermute x16, starting transfers between devices, advance(): self.plus = lax.ppermute(after(plus, *gate), 'expert', up)  29 us
    pallas_call x4, Pallas kernels, run_grads(): pl.pallas_call(functools.partial(grads_kernel, (place, step), len(before)...  28.6 us
    ppermute x25, starting transfers between devices, swap_x(): return lax.ppermute(value, 'tensor', [(0, 1), (1, 0)])  24.7 us
  transfers between devices with their start and end apart: 124, of which 65 were waited for; matrix products, arithmetic and copies ran while one was open for 3% of the time, Pallas kernels for 16%

profile of v5, /device:TPU:0, one launch (start us, length us, event | category | flops | bytes accessed | tf_op | source)
XLA Modules:
  0.0 663.0 jit_solution(15345694302720448124)
XLA Ops:
  9.4 3.0 collective-permute-start.2
  12.4 27.7 %collective-permute-done.2.refs_1_ = bf16[256,2432]{1,0:T(8,128)(2,1)} collective-permute-done((bf16[256,2432]{1,0:T(8,128)(2,1)S(1)}, bf16[256,2432]{1,0:T(8,128)(2,1)}, u32[]{:S(2)}, u32[]{:S(2)}) %collective-permute-start.2) | collective-permute-done | bytes 1245216 | tf_op jit(solution)/shard_map/ppermute | solution.py:225
  46.2 26.3 %collective-permute-done.4.refs_3_ = bf16[256,2432]{1,0:T(8,128)(2,1)} collective-permute-done((bf16[256,2432]{1,0:T(8,128)(2,1)}, bf16[256,2432]{1,0:T(8,128)(2,1)}, u32[]{:S(2)}, u32[]{:S(2)}) %collective-permute-start.4) | collective-permute-done | bytes 1245216 | tf_op jit(solution)/shard_map/ppermute | solution.py:225
  76.2 25.0 %collective-permute-done.6.refs_5_ = bf16[256,2432]{1,0:T(8,128)(2,1)} collective-permute-done((bf16[256,2432]{1,0:T(8,128)(2,1)}, bf16[256,2432]{1,0:T(8,128)(2,1)}, u32[]{:S(2)}, u32[]{:S(2)}) %collective-permute-start.6) | collective-permute-done | bytes 1245216 | tf_op jit(solution)/shard_map/ppermute | solution.py:225
  106.2 10.5 %collective-permute-done.8.refs_7_ = bf16[128,2432]{1,0:T(8,128)(2,1)S(1)} collective-permute-done((bf16[128,2432]{1,0:T(8,128)(2,1)S(1)}, bf16[128,2432]{1,0:T(8,128)(2,1)S(1)}, u32[]{:S(2)}, u32[]{:S(2)}) %collective-permute-start.8) | collective-permute-done | bytes 622624 | tf_op jit(solution)/shard_map/ppermute | solution.py:225
  121.5 7.8 %shard_map.264 = (f32[128,2048]{1,0:T(8,128)S(1)}, bf16[128,2048]{1,0:T(8,128)(2,1)S(1)}, bf16[128,1024]{1,0:T(8,128)(2,1)S(1)}, f32[128,1280]{1,0:T(8,128)S(1)}...) custom-call(bf16[256,2432]{1,0:T(8,128)(2,1)S(1)} %fusion.1.refs_0_, ...), custom_call_target="tpu_custom_call" | custom-call | flops 7247757312 | bytes 9437184 | tf_op jit(solution)/shard_map/pallas_call | solution.py:397
  132.5 11.8 %collective-permute-done.10.refs_1_ = bf16[256,2304]{1,0:T(8,128)(2,1)} collective-permute-done((bf16[256,2304]{1,0:T(8,128)(2,1)S(1)}, bf16[256,2304]{1,0:T(8,128)(2,1)}, u32[]{:S(2)}, u32[]{:S(2)}) %collective-permute-start.10) | collective-permute-done | bytes 1179680 | tf_op jit(solution)/shard_map/ppermute | solution.py:225
  148.9 3.9 collective-permute-done.14.got
  157.7 3.8 shard_map.268
  161.5 2.7 copy-done.81
  169.2 10.2 %collective-permute-done.26.refs_1_ = bf16[128,2176]{1,0:T(8,128)(2,1)S(1)} collective-permute-done((bf16[128,2176]{1,0:T(8,128)(2,1)S(1)}, bf16[128,2176]{1,0:T(8,128)(2,1)S(1)}, u32[]{:S(2)}, u32[]{:S(2)}) %collective-permute-start.26) | collective-permute-done | bytes 557088 | tf_op jit(solution)/shard_map/ppermute | solution.py:42
  179.6 3.2 collective-permute-done.22.refs_2_
  183.0 6.4 collective-permute-done.23.refs_4_
  192.0 2.8 copy-done.82
  196.6 8.2 %shard_map.269 = (bf16[128,2048]{1,0:T(8,128)(2,1)S(1)}, bf16[128,2048]{1,0:T(8,128)(2,1)S(1)}, bf16[128,2048]{1,0:T(8,128)(2,1)S(1)}, bf16[64,2048]{1,0:T(8,128...) custom-call(bf16[128,2176]{1,0:T(8,128)(2,1)S(1)} %shard_map.267.ref, ...), custom_call_target="tpu_custom_call" | custom-call | flops 9663676416 | bytes 9437184 | tf_op jit(solution)/shard_map/pallas_call | solution.py:669
  208.4 11.8 %collective-permute-done.28.top = bf16[64,2048]{1,0:T(8,128)(2,1)S(1)} collective-permute-done((bf16[64,2048]{1,0:T(8,128)(2,1)S(1)}, bf16[64,2048]{1,0:T(8,128)(2,1)S(1)}, u32[]{:S(2)}, u32[]{:S(2)}) %collective-permute-start.28) | collective-permute-done | bytes 262176 | tf_op jit(solution)/shard_map/ppermute | solution.py:47
  223.5 6.1 collective-permute-done.30.from_x
  231.0 4.1 collective-permute-start.33
  236.0 3.8 collective-permute-done.33.refs_2_
  239.8 3.6 collective-permute-done.34.refs_3_
  246.4 19.4 %collective-permute-done.35.refs_5_ = bf16[256,2304]{1,0:T(8,128)(2,1)S(1)} collective-permute-done((bf16[256,2304]{1,0:T(8,128)(2,1)S(1)}, bf16[256,2304]{1,0:T(8,128)(2,1)S(1)}, u32[]{:S(2)}, u32[]{:S(2)}) %collective-permute-start.35) | collective-permute-done | bytes 1179680 | tf_op jit(solution)/shard_map/ppermute | solution.py:225
  265.9 3.8 collective-permute-start.37
  276.9 2.9 collective-permute-done.37.refs_7_
  279.8 3.2 collective-permute-done.38.refs_8_
  283.0 6.9 %shard_map.274 = (bf16[128,2048]{1,0:T(8,128)(2,1)S(1)}, bf16[128,1024]{1,0:T(8,128)(2,1)S(1)}, f32[128,1280]{1,0:T(8,128)S(1)}, f32[8,128,128]{2,1,0:T(8,128)S(...) custom-call(bf16[256,2304]{1,0:T(8,128)(2,1)S(1)} %copy-done.22, ...), custom_call_target="tpu_custom_call" | custom-call | flops 7247757312 | bytes 9437184 | tf_op jit(solution)/shard_map/pallas_call | solution.py:397
  295.9 3.1 collective-permute-done.46.got
  300.1 7.8 %collective-permute-start.49 = (bf16[32,2176]{1,0:T(8,128)(2,1)S(1)}, bf16[32,2176]{1,0:T(8,128)(2,1)S(1)}, u32[]{:S(2)}, u32[]{:S(2)}) collective-permute-start(bf16[32,2176]{1,0:T(8,128)(2,1)S(1)} %get-tuple-element.234.refs_0_.refs_8_), channel_id=1, source_target_pairs={{0,4},{2,6},{4,0},{6,2},{8,12},{10,14},{12,8},{14,10},{1,5},{3,7},... | collective-permute-start | bytes 417800 | tf_op jit(solution)/shard_map/ppermute | solution.py:47
  310.5 3.8 shard_map.278
  314.3 6.1 collective-permute-done.50.refs_2_
  323.3 7.6 %collective-permute-done.56.refs_1_ = bf16[128,2176]{1,0:T(8,128)(2,1)S(1)} collective-permute-done((bf16[128,2176]{1,0:T(8,128)(2,1)S(1)}, bf16[128,2176]{1,0:T(8,128)(2,1)S(1)}, u32[]{:S(2)}, u32[]{:S(2)}) %collective-permute-start.56) | collective-permute-done | bytes 557088 | tf_op jit(solution)/shard_map/ppermute | solution.py:42
  331.0 3.4 collective-permute-start.57
  337.3 3.7 collective-permute-done.53.refs_4_
  341.0 3.5 collective-permute-start.59
  346.7 8.2 %shard_map.279 = (bf16[128,2048]{1,0:T(8,128)(2,1)S(1)}, bf16[128,2048]{1,0:T(8,128)(2,1)S(1)}, bf16[128,2048]{1,0:T(8,128)(2,1)S(1)}, bf16[64,2048]{1,0:T(8,128...) custom-call(bf16[128,2176]{1,0:T(8,128)(2,1)S(1)} %shard_map.277.ref, ...), custom_call_target="tpu_custom_call" | custom-call | flops 9663676416 | bytes 9437184 | tf_op jit(solution)/shard_map/pallas_call | solution.py:669
  362.6 8.3 %shard_map.281 = (bf16[128,2176]{1,0:T(8,128)(2,1)S(1)}, bf16[128,2176]{1,0:T(8,128)(2,1)S(1)}, bf16[128,2176]{1,0:T(8,128)(2,1)S(1)}, bf16[64,2176]{1,0:T(8,128...) custom-call(bf16[128,2048]{1,0:T(8,128)(2,1)S(1)} %shard_map.273.refs_0_, ...), custom_call_target="tpu_custom_call" | custom-call | flops 9663676416 | bytes 9437184 | tf_op jit(solution)/shard_map/pallas_call | solution.py:757
  375.9 5.5 collective-permute-done.63.top
  381.3 3.0 collective-permute-done.64.bottom
  385.7 11.2 %collective-permute-done.65.from_x = bf16[128,2176]{1,0:T(8,128)(2,1)S(1)} collective-permute-done((bf16[128,2176]{1,0:T(8,128)(2,1)S(1)}, bf16[128,2176]{1,0:T(8,128)(2,1)S(1)}, u32[]{:S(2)}, u32[]{:S(2)}) %collective-permute-start.65) | collective-permute-done | bytes 557088 | tf_op jit(solution)/shard_map/ppermute | solution.py:42
  403.6 2.6 collective-permute-done.69.refs_3_
  406.2 2.8 collective-permute-done.67.refs_1_
  410.7 3.8 collective-permute-done.72.refs_10_
  422.1 9.9 %shard_map.285 = (bf16[128,2048]{1,0:T(8,128)(2,1)}, bf16[144,1280]{1,0:T(8,128)(2,1)}, f32[64,2048]{1,0:T(8,128)}, bf16[64,2048]{1,0:T(8,128)(2,1)}) custom-call(bf16[256,2304]{1,0:T(8,128)(2,1)} %copy-done.21, bf16[256,2304]{1,0:T(8,128)(2,1)} %collective-permute-done.10.refs_1_, bf16[256,2304]{1,0:T(8,128)(2,1)} %collective-permute-done.11.refs_2_, ...), custom_call_target="tpu_custom_call" | custom-call | flops 7247757312 | bytes 9437184 | tf_op jit(solution)/shard_map/pallas_call | solution.py:501
  437.2 4.0 collective-permute-done.79.got
  448.8 3.8 shard_map.292
  452.6 4.8 collective-permute-done.83.refs_2_
  459.7 9.2 %collective-permute-done.87.refs_1_ = bf16[128,2048]{1,0:T(8,128)(2,1)S(1)} collective-permute-done((bf16[128,2048]{1,0:T(8,128)(2,1)S(1)}, bf16[128,2048]{1,0:T(8,128)(2,1)S(1)}, u32[]{:S(2)}, u32[]{:S(2)}) %collective-permute-start.87) | collective-permute-done | bytes 524320 | tf_op jit(solution)/shard_map/ppermute | solution.py:42
  477.3 8.3 %shard_map.293 = (bf16[128,2176]{1,0:T(8,128)(2,1)S(1)}, bf16[128,2176]{1,0:T(8,128)(2,1)S(1)}, bf16[128,2176]{1,0:T(8,128)(2,1)S(1)}, bf16[64,2176]{1,0:T(8,128...) custom-call(bf16[128,2048]{1,0:T(8,128)(2,1)S(1)} %shard_map.289.refs_0_, ...), custom_call_target="tpu_custom_call" | custom-call | flops 9663676416 | bytes 9437184 | tf_op jit(solution)/shard_map/pallas_call | solution.py:757
  488.6 3.6 collective-permute-done.91.top
  500.2 8.8 %shard_map.296 = (f32[2,2048,384]{2,1,0:T(8,128)}, f32[2,2048,384]{2,1,0:T(8,128)}) custom-call(bf16[512,2048]{1,0:T(8,128)(2,1)} %copy-done.6, bf16[512,2048]{1,0:T(8,128)(2,1)} %copy-done.8, bf16[512,2048]{1,0:T(8,128)(2,1)} %copy-done.107, bf16[512,2048]{1,0:T(8,128)(2,1)} %copy-done.107, bf16[512,1536]{1,0:T(8,128)(2,1)} %copy-done.11, ...), custom_call_target="tpu_custom_call" | custom-call | flops 100000000 | bytes 100000 | tf_op jit(solution)/shard_map/pallas_call | solution.py:834
  513.7 8.7 %shard_map.299 = (f32[2,2048,384]{2,1,0:T(8,128)}, f32[2,2048,384]{2,1,0:T(8,128)}) custom-call(bf16[512,2048]{1,0:T(8,128)(2,1)} %copy-done.6, bf16[512,2048]{1,0:T(8,128)(2,1)} %copy-done.8, bf16[512,2048]{1,0:T(8,128)(2,1)} %copy-done.107, bf16[512,2048]{1,0:T(8,128)(2,1)} %copy-done.107, ...), custom_call_target="tpu_custom_call", output_to_operand_aliasing={{0}: (8, {}), {1}: (9, {})} | custom-call | flops 100000000 | bytes 100000 | tf_op jit(solution)/shard_map/pallas_call | solution.py:834
  525.6 4.9 collective-permute-done.99.refs_10_
  531.9 4.2 all-to-all-start
  541.3 9.9 %shard_map.301 = (bf16[128,2048]{1,0:T(8,128)(2,1)}, bf16[144,1280]{1,0:T(8,128)(2,1)}, f32[64,2048]{1,0:T(8,128)}, bf16[64,2048]{1,0:T(8,128)(2,1)}) custom-call(bf16[256,2432]{1,0:T(8,128)(2,1)} %copy-done.20, bf16[256,2432]{1,0:T(8,128)(2,1)} %collective-permute-done.2.refs_1_, bf16[256,2432]{1,0:T(8,128)(2,1)} %collective-permute-done.3.refs_2_, ...), custom_call_target="tpu_custom_call" | custom-call | flops 7247757312 | bytes 9437184 | tf_op jit(solution)/shard_map/pallas_call | solution.py:501
  551.2 9.0 %collective-permute-done.103.refs_2_ = bf16[32,2048]{1,0:T(8,128)(2,1)S(1)} collective-permute-done((bf16[32,2048]{1,0:T(8,128)(2,1)}, bf16[32,2048]{1,0:T(8,128)(2,1)S(1)}, u32[]{:S(2)}, u32[]{:S(2)}) %collective-permute-start.103) | collective-permute-done | bytes 131104 | tf_op jit(solution)/shard_map/ppermute | solution.py:47
  575.0 9.1 %collective-permute-done.110.refs_1_ = bf16[144,2560]{1,0:T(8,128)(2,1)} collective-permute-done((bf16[144,2560]{1,0:T(8,128)(2,1)S(1)}, bf16[144,2560]{1,0:T(8,128)(2,1)}, u32[]{:S(2)}, u32[]{:S(2)}) %collective-permute-start.110) | collective-permute-done | bytes 737312 | tf_op jit(solution)/shard_map/ppermute | solution.py:225
  594.6 4.6 all-to-all-start.1
  600.5 5.5 shard_map.308.refs_8_
  611.2 5.6 shard_map.309
  616.8 14.1 %collective-permute-done.116.refs_5_ = bf16[144,2560]{1,0:T(8,128)(2,1)} collective-permute-done((bf16[144,2560]{1,0:T(8,128)(2,1)}, bf16[144,2560]{1,0:T(8,128)(2,1)}, u32[]{:S(2)}, u32[]{:S(2)}) %collective-permute-start.116) | collective-permute-done | bytes 737312 | tf_op jit(solution)/shard_map/ppermute | solution.py:225
  631.9 3.9 collective-permute-start.118
  636.0 6.1 collective-permute-done.118.refs_7_
  642.1 4.9 collective-permute-done.119.refs_8_
  647.0 7.6 %shard_map.312 = (f32[256,2048]{1,0:T(8,128)}, f32[256,256]{1,0:T(8,128)}, f32[256,256]{1,0:T(8,128)}, f32[40,256]{1,0:T(8,128)}) custom-call(bf16[144,2560]{1,0:T(8,128)(2,1)} %copy-done.32, bf16[144,2560]{1,0:T(8,128)(2,1)} %collective-permute-done.110.refs_1_, bf16[144,2560]{1,0:T(8,128)(2,1)} %collective-permute-done.111.refs_2_, ...), custom_call_target="tpu_custom_call" | custom-call | flops 15099494400 | bytes 11796480 | tf_op jit(solution)/shard_map/pallas_call | solution.py:981
  655.6 5.1 shard_map.313
  (622 shorter events, 200.7 us)
Async XLA Ops:
  9.4 30.7 %collective-permute-start.2 = (bf16[256,2432]{1,0:T(8,128)(2,1)S(1)}, bf16[256,2432]{1,0:T(8,128)(2,1)}, u32[]{:S(2)}, u32[]{:S(2)}) collective-permute-start(bf16[256,2432]{1,0:T(8,128)(2,1)S(1)} %fusion.1.refs_0_), channel_id=1, source_target_pairs={{0,4},{4,8},{8,12},{12,14},{14,10},{10,6},{6,2},{2,0},{1,5},{5,9},... | collective-permute-start | bytes 3735560 | tf_op jit(solution)/shard_map/ppermute | solution.py:225
  12.4 29.2 %collective-permute-start.3 = (bf16[256,2432]{1,0:T(8,128)(2,1)S(1)}, bf16[256,2432]{1,0:T(8,128)(2,1)}, u32[]{:S(2)}, u32[]{:S(2)}) collective-permute-start(bf16[256,2432]{1,0:T(8,128)(2,1)S(1)} %fusion.1.refs_0_), channel_id=1, source_target_pairs={{4,0},{8,4},{12,8},{14,12},{10,14},{6,10},{2,6},{0,2},{5,1},{9,5},... | collective-permute-start | bytes 3735560 | tf_op jit(solution)/shard_map/ppermute | solution.py:226
  41.8 113.6 %collective-permute-start.19 = (bf16[2,2048,384]{2,1,0:T(8,128)(2,1)}, bf16[2,2048,384]{2,1,0:T(8,128)(2,1)}, u32[]{:S(2)}, u32[]{:S(2)}) collective-permute-start(bf16[2,2048,384]{2,1,0:T(8,128)(2,1)} %bitcast.26.refs_0_), channel_id=1, source_target_pairs={{0,16},{16,0},{1,17},{17,1},{2,18},{18,2},{3,19},{19,3},{4,20},{20... | collective-permute-start | bytes 9437192 | tf_op jit(solution)/shard_map/ppermute | solution.py:38
  42.3 115.5 %collective-permute-start.20 = (bf16[2,2048,384]{2,1,0:T(8,128)(2,1)}, bf16[2,2048,384]{2,1,0:T(8,128)(2,1)}, u32[]{:S(2)}, u32[]{:S(2)}) collective-permute-start(bf16[2,2048,384]{2,1,0:T(8,128)(2,1)} %bitcast.27.refs_1_), channel_id=1, source_target_pairs={{0,16},{16,0},{1,17},{17,1},{2,18},{18,2},{3,19},{19,3},{4,20},{20... | collective-permute-start | bytes 9437192 | tf_op jit(solution)/shard_map/ppermute | solution.py:38
  42.4 115.4 %collective-permute-start.21 = (bf16[2,384,2048]{2,1,0:T(8,128)(2,1)}, bf16[2,384,2048]{2,1,0:T(8,128)(2,1)}, u32[]{:S(2)}, u32[]{:S(2)}) collective-permute-start(bf16[2,384,2048]{2,1,0:T(8,128)(2,1)} %bitcast.28.refs_2_), channel_id=1, source_target_pairs={{0,16},{16,0},{1,17},{17,1},{2,18},{18,2},{3,19},{19,3},{4,20},{20... | collective-permute-start | bytes 9437192 | tf_op jit(solution)/shard_map/ppermute | solution.py:38
  42.8 29.7 %collective-permute-start.4 = (bf16[256,2432]{1,0:T(8,128)(2,1)}, bf16[256,2432]{1,0:T(8,128)(2,1)}, u32[]{:S(2)}, u32[]{:S(2)}) collective-permute-start(bf16[256,2432]{1,0:T(8,128)(2,1)} %collective-permute-done.2.refs_1_), channel_id=1, source_target_pairs={{0,4},{4,8},{8,12},{12,14},{14,10},{10,6},{6,2},{2,0},{1,5},{5,9},... | collective-permute-start | bytes 3735560 | tf_op jit(solution)/shard_map/ppermute | solution.py:225
  44.4 29.7 %collective-permute-start.5 = (bf16[256,2432]{1,0:T(8,128)(2,1)}, bf16[256,2432]{1,0:T(8,128)(2,1)}, u32[]{:S(2)}, u32[]{:S(2)}) collective-permute-start(bf16[256,2432]{1,0:T(8,128)(2,1)} %collective-permute-done.3.refs_2_), channel_id=1, source_target_pairs={{4,0},{8,4},{12,8},{14,12},{10,14},{6,10},{2,6},{0,2},{5,1},{9,5},... | collective-permute-start | bytes 3735560 | tf_op jit(solution)/shard_map/ppermute | solution.py:226
  72.5 28.8 %collective-permute-start.6 = (bf16[256,2432]{1,0:T(8,128)(2,1)}, bf16[256,2432]{1,0:T(8,128)(2,1)}, u32[]{:S(2)}, u32[]{:S(2)}) collective-permute-start(bf16[256,2432]{1,0:T(8,128)(2,1)} %collective-permute-done.4.refs_3_), channel_id=1, source_target_pairs={{0,4},{4,8},{8,12},{12,14},{14,10},{10,6},{6,2},{2,0},{1,5},{5,9},... | collective-permute-start | bytes 3735560 | tf_op jit(solution)/shard_map/ppermute | solution.py:225
  74.0 30.0 %collective-permute-start.7 = (bf16[256,2432]{1,0:T(8,128)(2,1)}, bf16[256,2432]{1,0:T(8,128)(2,1)}, u32[]{:S(2)}, u32[]{:S(2)}) collective-permute-start(bf16[256,2432]{1,0:T(8,128)(2,1)} %collective-permute-done.5.refs_4_), channel_id=1, source_target_pairs={{4,0},{8,4},{12,8},{14,12},{10,14},{6,10},{2,6},{0,2},{5,1},{9,5},... | collective-permute-start | bytes 3735560 | tf_op jit(solution)/shard_map/ppermute | solution.py:226
  102.4 14.3 %collective-permute-start.8 = (bf16[128,2432]{1,0:T(8,128)(2,1)S(1)}, bf16[128,2432]{1,0:T(8,128)(2,1)S(1)}, u32[]{:S(2)}, u32[]{:S(2)}) collective-permute-start(bf16[128,2432]{1,0:T(8,128)(2,1)S(1)} %slice.283), channel_id=1, source_target_pairs={{0,4},{4,8},{8,12},{12,14},{14,10},{10,6},{6,2},{2,0},{1,5},{5,9},... | collective-permute-start | bytes 1867784 | tf_op jit(solution)/shard_map/ppermute | solution.py:225
  105.2 14.0 %collective-permute-start.9 = (bf16[128,2432]{1,0:T(8,128)(2,1)S(1)}, bf16[128,2432]{1,0:T(8,128)(2,1)S(1)}, u32[]{:S(2)}, u32[]{:S(2)}) collective-permute-start(bf16[128,2432]{1,0:T(8,128)(2,1)S(1)} %slice.284), channel_id=1, source_target_pairs={{4,0},{8,4},{12,8},{14,12},{10,14},{6,10},{2,6},{0,2},{5,1},{9,5},... | collective-permute-start | bytes 1867784 | tf_op jit(solution)/shard_map/ppermute | solution.py:226
  119.2 25.1 %collective-permute-start.10 = (bf16[256,2304]{1,0:T(8,128)(2,1)S(1)}, bf16[256,2304]{1,0:T(8,128)(2,1)}, u32[]{:S(2)}, u32[]{:S(2)}) collective-permute-start(bf16[256,2304]{1,0:T(8,128)(2,1)S(1)} %get-tuple-element.191.refs_0_), channel_id=1, source_target_pairs={{0,4},{4,8},{8,12},{12,14},{14,10},{10,6},{6,2},{2,0},{1,5},{5,9},... | collective-permute-start | bytes 3538952 | tf_op jit(solution)/shard_map/ppermute | solution.py:225
  120.8 24.8 %collective-permute-start.11 = (bf16[256,2304]{1,0:T(8,128)(2,1)S(1)}, bf16[256,2304]{1,0:T(8,128)(2,1)}, u32[]{:S(2)}, u32[]{:S(2)}) collective-permute-start(bf16[256,2304]{1,0:T(8,128)(2,1)S(1)} %get-tuple-element.191.refs_0_), channel_id=1, source_target_pairs={{4,0},{8,4},{12,8},{14,12},{10,14},{6,10},{2,6},{0,2},{5,1},{9,5},... | collective-permute-start | bytes 3538952 | tf_op jit(solution)/shard_map/ppermute | solution.py:226
  153.3 12.6 %collective-permute-start.16 = (bf16[32,2176]{1,0:T(8,128)(2,1)S(1)}, bf16[32,2176]{1,0:T(8,128)(2,1)S(1)}, u32[]{:S(2)}, u32[]{:S(2)}) collective-permute-start(bf16[32,2176]{1,0:T(8,128)(2,1)S(1)} %get-tuple-element.201.refs_0_.refs_8_), channel_id=1, source_target_pairs={{0,4},{2,6},{4,0},{6,2},{8,12},{10,14},{12,8},{14,10},{1,5},{3,7},... | collective-permute-start | bytes 417800 | tf_op jit(solution)/shard_map/ppermute | solution.py:47
  154.9 12.7 %collective-permute-start.17 = (bf16[32,2176]{1,0:T(8,128)(2,1)S(1)}, bf16[32,2176]{1,0:T(8,128)(2,1)S(1)}, u32[]{:S(2)}, u32[]{:S(2)}) collective-permute-start(bf16[32,2176]{1,0:T(8,128)(2,1)S(1)} %get-tuple-element.201.refs_0_.refs_8_), channel_id=1, source_target_pairs={{0,8},{2,10},{4,12},{6,14},{8,0},{10,2},{12,4},{14,6},{1,9},{3,11}... | collective-permute-start | bytes 417800 | tf_op jit(solution)/shard_map/ppermute | solution.py:47
  155.4 12.1 %collective-permute-start.18 = (bf16[32,2176]{1,0:T(8,128)(2,1)S(1)}, bf16[32,2176]{1,0:T(8,128)(2,1)S(1)}, u32[]{:S(2)}, u32[]{:S(2)}) collective-permute-start(bf16[32,2176]{1,0:T(8,128)(2,1)S(1)} %get-tuple-element.201.refs_0_.refs_8_), channel_id=1, source_target_pairs={{0,12},{2,14},{4,8},{6,10},{8,4},{10,6},{12,0},{14,2},{1,13},{3,15... | collective-permute-start | bytes 417800 | tf_op jit(solution)/shard_map/ppermute | solution.py:47
  169.2 13.6 %collective-permute-start.22 = (bf16[128,2176]{1,0:T(8,128)(2,1)S(1)}, bf16[128,2176]{1,0:T(8,128)(2,1)S(1)}, u32[]{:S(2)}, u32[]{:S(2)}) collective-permute-start(bf16[128,2176]{1,0:T(8,128)(2,1)S(1)} %shard_map.267.refs_0_), channel_id=1, source_target_pairs={{0,2},{2,0},{4,6},{6,4},{8,10},{10,8},{12,14},{14,12},{1,3},{3,1},... | collective-permute-start | bytes 1671176 | tf_op jit(solution)/shard_map/ppermute | solution.py:47
  179.3 12.6 %collective-permute-start.27 = (bf16[64,2176]{1,0:T(8,128)(2,1)S(1)}, bf16[64,2176]{1,0:T(8,128)(2,1)S(1)}, u32[]{:S(2)}, u32[]{:S(2)}) collective-permute-start(bf16[64,2176]{1,0:T(8,128)(2,1)S(1)} %slice.292), channel_id=1, source_target_pairs={{0,2},{2,0},{4,6},{6,4},{8,10},{10,8},{12,14},{14,12},{1,3},{3,1},... | collective-permute-start | bytes 835592 | tf_op jit(solution)/shard_map/ppermute | solution.py:47
  189.4 40.2 %collective-permute-start.24 = (bf16[256,2304]{1,0:T(8,128)(2,1)}, bf16[256,2304]{1,0:T(8,128)(2,1)S(1)}, u32[]{:S(2)}, u32[]{:S(2)}) collective-permute-start(bf16[256,2304]{1,0:T(8,128)(2,1)} %collective-permute-done.10.refs_1_), channel_id=1, source_target_pairs={{0,4},{4,8},{8,12},{12,14},{14,10},{10,6},{6,2},{2,0},{1,5},{5,9},... | collective-permute-start | bytes 3538952 | tf_op jit(solution)/shard_map/ppermute | solution.py:225
  191.8 37.8 %collective-permute-start.25 = (bf16[256,2304]{1,0:T(8,128)(2,1)}, bf16[256,2304]{1,0:T(8,128)(2,1)S(1)}, u32[]{:S(2)}, u32[]{:S(2)}) collective-permute-start(bf16[256,2304]{1,0:T(8,128)(2,1)} %collective-permute-done.11.refs_2_), channel_id=1, source_target_pairs={{4,0},{8,4},{12,8},{14,12},{10,14},{6,10},{2,6},{0,2},{5,1},{9,5},... | collective-permute-start | bytes 3538952 | tf_op jit(solution)/shard_map/ppermute | solution.py:226
  206.5 13.7 %collective-permute-start.28 = (bf16[64,2048]{1,0:T(8,128)(2,1)S(1)}, bf16[64,2048]{1,0:T(8,128)(2,1)S(1)}, u32[]{:S(2)}, u32[]{:S(2)}) collective-permute-start(bf16[64,2048]{1,0:T(8,128)(2,1)S(1)} %get-tuple-element.213), channel_id=1, source_target_pairs={{0,2},{2,0},{4,6},{6,4},{8,10},{10,8},{12,14},{14,12},{1,3},{3,1},... | collective-permute-start | bytes 786440 | tf_op jit(solution)/shard_map/ppermute | solution.py:47
  206.9 13.3 %collective-permute-start.29 = (bf16[64,2048]{1,0:T(8,128)(2,1)S(1)}, bf16[64,2048]{1,0:T(8,128)(2,1)S(1)}, u32[]{:S(2)}, u32[]{:S(2)}) collective-permute-start(bf16[64,2048]{1,0:T(8,128)(2,1)S(1)} %get-tuple-element.215), channel_id=1, source_target_pairs={{0,1},{1,0},{2,3},{3,2},{4,5},{5,4},{6,7},{7,6},{8,9},{9,8},{10,11... | collective-permute-start | bytes 786440 | tf_op jit(solution)/shard_map/ppermute | solution.py:42
  243.4 22.5 %collective-permute-start.35 = (bf16[256,2304]{1,0:T(8,128)(2,1)S(1)}, bf16[256,2304]{1,0:T(8,128)(2,1)S(1)}, u32[]{:S(2)}, u32[]{:S(2)}) collective-permute-start(bf16[256,2304]{1,0:T(8,128)(2,1)S(1)} %collective-permute-done.24.refs_3_), channel_id=1, source_target_pairs={{0,4},{4,8},{8,12},{12,14},{14,10},{10,6},{6,2},{2,0},{1,5},{5,9},... | collective-permute-start | bytes 3538952 | tf_op jit(solution)/shard_map/ppermute | solution.py:225
  244.6 25.2 %collective-permute-start.36 = (bf16[256,2304]{1,0:T(8,128)(2,1)S(1)}, bf16[256,2304]{1,0:T(8,128)(2,1)S(1)}, u32[]{:S(2)}, u32[]{:S(2)}) collective-permute-start(bf16[256,2304]{1,0:T(8,128)(2,1)S(1)} %collective-permute-done.25.refs_4_), channel_id=1, source_target_pairs={{4,0},{8,4},{12,8},{14,12},{10,14},{6,10},{2,6},{0,2},{5,1},{9,5},... | collective-permute-start | bytes 3538952 | tf_op jit(solution)/shard_map/ppermute | solution.py:226
  245.7 24.3 %collective-permute-start.39 = (bf16[32,2048]{1,0:T(8,128)(2,1)S(1)}, bf16[32,2048]{1,0:T(8,128)(2,1)S(1)}, u32[]{:S(2)}, u32[]{:S(2)}) collective-permute-start(bf16[32,2048]{1,0:T(8,128)(2,1)S(1)} %get-tuple-element.226.refs_9_), channel_id=1, source_target_pairs={{0,1},{1,0},{2,3},{3,2},{4,5},{5,4},{6,7},{7,6},{8,9},{9,8},{10,11... | collective-permute-start | bytes 393224 | tf_op jit(solution)/shard_map/ppermute | solution.py:42
  265.9 13.9 %collective-permute-start.37 = (bf16[128,2304]{1,0:T(8,128)(2,1)S(1)}, bf16[128,2304]{1,0:T(8,128)(2,1)S(1)}, u32[]{:S(2)}, u32[]{:S(2)}) collective-permute-start(bf16[128,2304]{1,0:T(8,128)(2,1)S(1)} %slice.293), channel_id=1, source_target_pairs={{0,4},{4,8},{8,12},{12,14},{14,10},{10,6},{6,2},{2,0},{1,5},{5,9},... | collective-permute-start | bytes 1769480 | tf_op jit(solution)/shard_map/ppermute | solution.py:225
  269.8 13.2 %collective-permute-start.38 = (bf16[128,2304]{1,0:T(8,128)(2,1)S(1)}, bf16[128,2304]{1,0:T(8,128)(2,1)S(1)}, u32[]{:S(2)}, u32[]{:S(2)}) collective-permute-start(bf16[128,2304]{1,0:T(8,128)(2,1)S(1)} %slice.294), channel_id=1, source_target_pairs={{4,0},{8,4},{12,8},{14,12},{10,14},{6,10},{2,6},{0,2},{5,1},{9,5},... | collective-permute-start | bytes 1769480 | tf_op jit(solution)/shard_map/ppermute | solution.py:226
  271.5 20.2 %collective-permute-start.41 = (bf16[32,2048]{1,0:T(8,128)(2,1)S(1)}, bf16[32,2048]{1,0:T(8,128)(2,1)S(1)}, u32[]{:S(2)}, u32[]{:S(2)}) collective-permute-start(bf16[32,2048]{1,0:T(8,128)(2,1)S(1)} %fusion.3.refs_0_.refs_4_), channel_id=1, source_target_pairs={{0,4},{2,6},{4,0},{6,2},{8,12},{10,14},{12,8},{14,10},{1,5},{3,7},... | collective-permute-start | bytes 393224 | tf_op jit(solution)/shard_map/ppermute | solution.py:47
  274.0 17.7 %collective-permute-start.42 = (bf16[32,2048]{1,0:T(8,128)(2,1)S(1)}, bf16[32,2048]{1,0:T(8,128)(2,1)S(1)}, u32[]{:S(2)}, u32[]{:S(2)}) collective-permute-start(bf16[32,2048]{1,0:T(8,128)(2,1)S(1)} %fusion.3.refs_0_.refs_4_), channel_id=1, source_target_pairs={{0,8},{2,10},{4,12},{6,14},{8,0},{10,2},{12,4},{14,6},{1,9},{3,11}... | collective-permute-start | bytes 393224 | tf_op jit(solution)/shard_map/ppermute | solution.py:47
  275.5 16.3 %collective-permute-start.43 = (bf16[32,2048]{1,0:T(8,128)(2,1)S(1)}, bf16[32,2048]{1,0:T(8,128)(2,1)S(1)}, u32[]{:S(2)}, u32[]{:S(2)}) collective-permute-start(bf16[32,2048]{1,0:T(8,128)(2,1)S(1)} %fusion.3.refs_0_.refs_4_), channel_id=1, source_target_pairs={{0,12},{2,14},{4,8},{6,10},{8,4},{10,6},{12,0},{14,2},{1,13},{3,15... | collective-permute-start | bytes 393224 | tf_op jit(solution)/shard_map/ppermute | solution.py:47
  299.5 20.9 %collective-permute-start.47 = (bf16[128,2048]{1,0:T(8,128)(2,1)S(1)}, bf16[128,2048]{1,0:T(8,128)(2,1)S(1)}, u32[]{:S(2)}, u32[]{:S(2)}) collective-permute-start(bf16[128,2048]{1,0:T(8,128)(2,1)S(1)} %shard_map.273.refs_0_), channel_id=1, source_target_pairs={{0,1},{1,0},{2,3},{3,2},{4,5},{5,4},{6,7},{7,6},{8,9},{9,8},{10,11... | collective-permute-start | bytes 1572872 | tf_op jit(solution)/shard_map/ppermute | solution.py:42
  299.9 20.5 %collective-permute-start.48 = (bf16[128,2048]{1,0:T(8,128)(2,1)S(1)}, bf16[128,2048]{1,0:T(8,128)(2,1)S(1)}, u32[]{:S(2)}, u32[]{:S(2)}) collective-permute-start(bf16[128,2048]{1,0:T(8,128)(2,1)S(1)} %shard_map.273.refs_0_), channel_id=1, source_target_pairs={{0,2},{2,0},{4,6},{6,4},{8,10},{10,8},{12,14},{14,12},{1,3},{3,1},... | collective-permute-start | bytes 1572872 | tf_op jit(solution)/shard_map/ppermute | solution.py:47
  300.1 14.1 %collective-permute-start.49 = (bf16[32,2176]{1,0:T(8,128)(2,1)S(1)}, bf16[32,2176]{1,0:T(8,128)(2,1)S(1)}, u32[]{:S(2)}, u32[]{:S(2)}) collective-permute-start(bf16[32,2176]{1,0:T(8,128)(2,1)S(1)} %get-tuple-element.234.refs_0_.refs_8_), channel_id=1, source_target_pairs={{0,4},{2,6},{4,0},{6,2},{8,12},{10,14},{12,8},{14,10},{1,5},{3,7},... | collective-permute-start | bytes 417800 | tf_op jit(solution)/shard_map/ppermute | solution.py:47
  307.9 12.5 %collective-permute-start.50 = (bf16[32,2176]{1,0:T(8,128)(2,1)S(1)}, bf16[32,2176]{1,0:T(8,128)(2,1)S(1)}, u32[]{:S(2)}, u32[]{:S(2)}) collective-permute-start(bf16[32,2176]{1,0:T(8,128)(2,1)S(1)} %get-tuple-element.234.refs_0_.refs_8_), channel_id=1, source_target_pairs={{0,8},{2,10},{4,12},{6,14},{8,0},{10,2},{12,4},{14,6},{1,9},{3,11}... | collective-permute-start | bytes 417800 | tf_op jit(solution)/shard_map/ppermute | solution.py:47
  321.8 12.6 %collective-permute-start.52 = (bf16[128,2176]{1,0:T(8,128)(2,1)S(1)}, bf16[128,2176]{1,0:T(8,128)(2,1)S(1)}, u32[]{:S(2)}, u32[]{:S(2)}) collective-permute-start(bf16[128,2176]{1,0:T(8,128)(2,1)S(1)} %shard_map.277.refs_0_), channel_id=1, source_target_pairs={{0,2},{2,0},{4,6},{6,4},{8,10},{10,8},{12,14},{14,12},{1,3},{3,1},... | collective-permute-start | bytes 1671176 | tf_op jit(solution)/shard_map/ppermute | solution.py:47
  331.0 15.7 %collective-permute-start.57 = (bf16[64,2176]{1,0:T(8,128)(2,1)S(1)}, bf16[64,2176]{1,0:T(8,128)(2,1)S(1)}, u32[]{:S(2)}, u32[]{:S(2)}) collective-permute-start(bf16[64,2176]{1,0:T(8,128)(2,1)S(1)} %slice.302), channel_id=1, source_target_pairs={{0,2},{2,0},{4,6},{6,4},{8,10},{10,8},{12,14},{14,12},{1,3},{3,1},... | collective-permute-start | bytes 835592 | tf_op jit(solution)/shard_map/ppermute | solution.py:47
  341.0 19.0 %collective-permute-start.59 = (bf16[128,2048]{1,0:T(8,128)(2,1)S(1)}, bf16[128,2048]{1,0:T(8,128)(2,1)S(1)}, u32[]{:S(2)}, u32[]{:S(2)}) collective-permute-start(bf16[128,2048]{1,0:T(8,128)(2,1)S(1)} %shard_map.280.refs_0_), channel_id=1, source_target_pairs={{0,4},{4,8},{8,12},{12,14},{14,10},{10,6},{6,2},{2,0},{1,5},{5,9},... | collective-permute-start | bytes 1572872 | tf_op jit(solution)/shard_map/ppermute | solution.py:225
  344.5 15.5 %collective-permute-start.60 = (bf16[128,2048]{1,0:T(8,128)(2,1)S(1)}, bf16[128,2048]{1,0:T(8,128)(2,1)S(1)}, u32[]{:S(2)}, u32[]{:S(2)}) collective-permute-start(bf16[128,2048]{1,0:T(8,128)(2,1)S(1)} %shard_map.280.refs_0_), channel_id=1, source_target_pairs={{4,0},{8,4},{12,8},{14,12},{10,14},{6,10},{2,6},{0,2},{5,1},{9,5},... | collective-permute-start | bytes 1572872 | tf_op jit(solution)/shard_map/ppermute | solution.py:226
  344.9 15.1 %collective-permute-start.54 = (bf16[64,2048]{1,0:T(8,128)(2,1)S(1)}, bf16[64,2048]{1,0:T(8,128)(2,1)S(1)}, u32[]{:S(2)}, u32[]{:S(2)}) collective-permute-start(bf16[64,2048]{1,0:T(8,128)(2,1)S(1)} %slice.299), channel_id=1, source_target_pairs={{0,2},{2,0},{4,6},{6,4},{8,10},{10,8},{12,14},{14,12},{1,3},{3,1},... | collective-permute-start | bytes 786440 | tf_op jit(solution)/shard_map/ppermute | solution.py:47
  345.7 14.3 %collective-permute-start.55 = (bf16[64,2048]{1,0:T(8,128)(2,1)S(1)}, bf16[64,2048]{1,0:T(8,128)(2,1)S(1)}, u32[]{:S(2)}, u32[]{:S(2)}) collective-permute-start(bf16[64,2048]{1,0:T(8,128)(2,1)S(1)} %slice.301), channel_id=1, source_target_pairs={{0,1},{1,0},{2,3},{3,2},{4,5},{5,4},{6,7},{7,6},{8,9},{9,8},{10,11... | collective-permute-start | bytes 786440 | tf_op jit(solution)/shard_map/ppermute | solution.py:42
  384.5 12.4 %collective-permute-start.65 = (bf16[128,2176]{1,0:T(8,128)(2,1)S(1)}, bf16[128,2176]{1,0:T(8,128)(2,1)S(1)}, u32[]{:S(2)}, u32[]{:S(2)}) collective-permute-start(bf16[128,2176]{1,0:T(8,128)(2,1)S(1)} %get-tuple-element.259), channel_id=1, source_target_pairs={{0,1},{1,0},{2,3},{3,2},{4,5},{5,4},{6,7},{7,6},{8,9},{9,8},{10,11... | collective-permute-start | bytes 1671176 | tf_op jit(solution)/shard_map/ppermute | solution.py:42
  417.3 15.2 %collective-permute-start.77 = (bf16[512,2048]{1,0:T(8,128)(2,1)}, bf16[512,2048]{1,0:T(8,128)(2,1)S(1)}, u32[]{:S(2)}, u32[]{:S(2)}) collective-permute-start(bf16[512,2048]{1,0:T(8,128)(2,1)} %shard_map.286), channel_id=1, source_target_pairs={{0,16},{16,0},{1,17},{17,1},{2,18},{18,2},{3,19},{19,3},{4,20},{20... | collective-permute-start | bytes 6291464 | tf_op jit(solution)/shard_map/ppermute | solution.py:38
  417.9 14.2 %collective-permute-start.75 = (bf16[128,2048]{1,0:T(8,128)(2,1)}, bf16[128,2048]{1,0:T(8,128)(2,1)S(1)}, u32[]{:S(2)}, u32[]{:S(2)}) collective-permute-start(bf16[128,2048]{1,0:T(8,128)(2,1)} %collective-permute-done.61.refs_3_), channel_id=1, source_target_pairs={{0,4},{4,8},{8,12},{12,14},{14,10},{10,6},{6,2},{2,0},{1,5},{5,9},... | collective-permute-start | bytes 1572872 | tf_op jit(solution)/shard_map/ppermute | solution.py:225
  418.5 14.0 %collective-permute-start.76 = (bf16[128,2048]{1,0:T(8,128)(2,1)}, bf16[128,2048]{1,0:T(8,128)(2,1)S(1)}, u32[]{:S(2)}, u32[]{:S(2)}) collective-permute-start(bf16[128,2048]{1,0:T(8,128)(2,1)} %collective-permute-done.62.refs_4_), channel_id=1, source_target_pairs={{4,0},{8,4},{12,8},{14,12},{10,14},{6,10},{2,6},{0,2},{5,1},{9,5},... | collective-permute-start | bytes 1572872 | tf_op jit(solution)/shard_map/ppermute | solution.py:226
  442.1 15.3 %collective-permute-start.85 = (bf16[128,2048]{1,0:T(8,128)(2,1)S(1)}, bf16[128,2048]{1,0:T(8,128)(2,1)S(1)}, u32[]{:S(2)}, u32[]{:S(2)}) collective-permute-start(bf16[128,2048]{1,0:T(8,128)(2,1)S(1)} %get-tuple-element.293), channel_id=1, source_target_pairs={{0,1},{1,0},{2,3},{3,2},{4,5},{5,4},{6,7},{7,6},{8,9},{9,8},{10,11... | collective-permute-start | bytes 1572872 | tf_op jit(solution)/shard_map/ppermute | solution.py:42
  443.4 14.1 %collective-permute-start.86 = (bf16[128,2048]{1,0:T(8,128)(2,1)S(1)}, bf16[128,2048]{1,0:T(8,128)(2,1)S(1)}, u32[]{:S(2)}, u32[]{:S(2)}) collective-permute-start(bf16[128,2048]{1,0:T(8,128)(2,1)S(1)} %get-tuple-element.295), channel_id=1, source_target_pairs={{0,2},{2,0},{4,6},{6,4},{8,10},{10,8},{12,14},{14,12},{1,3},{3,1},... | collective-permute-start | bytes 1572872 | tf_op jit(solution)/shard_map/ppermute | solution.py:47
  494.8 14.2 %collective-permute-start.93 = (bf16[128,2176]{1,0:T(8,128)(2,1)S(1)}, bf16[128,2176]{1,0:T(8,128)(2,1)S(1)}, u32[]{:S(2)}, u32[]{:S(2)}) collective-permute-start(bf16[128,2176]{1,0:T(8,128)(2,1)S(1)} %get-tuple-element.308), channel_id=1, source_target_pairs={{0,1},{1,0},{2,3},{3,2},{4,5},{5,4},{6,7},{7,6},{8,9},{9,8},{10,11... | collective-permute-start | bytes 1671176 | tf_op jit(solution)/shard_map/ppermute | solution.py:42
  509.3 13.2 %collective-permute-start.98 = (bf16[32,2176]{1,0:T(8,128)(2,1)S(1)}, bf16[32,2176]{1,0:T(8,128)(2,1)S(1)}, u32[]{:S(2)}, u32[]{:S(2)}) collective-permute-start(bf16[32,2176]{1,0:T(8,128)(2,1)S(1)} %get-tuple-element.322), channel_id=1, source_target_pairs={{0,12},{2,14},{4,8},{6,10},{8,4},{10,6},{12,0},{14,2},{1,13},{3,15... | collective-permute-start | bytes 417800 | tf_op jit(solution)/shard_map/ppermute | solution.py:47
  510.2 12.3 %collective-permute-start.96 = (bf16[32,2176]{1,0:T(8,128)(2,1)S(1)}, bf16[32,2176]{1,0:T(8,128)(2,1)S(1)}, u32[]{:S(2)}, u32[]{:S(2)}) collective-permute-start(bf16[32,2176]{1,0:T(8,128)(2,1)S(1)} %get-tuple-element.320), channel_id=1, source_target_pairs={{0,4},{2,6},{4,0},{6,2},{8,12},{10,14},{12,8},{14,10},{1,5},{3,7},... | collective-permute-start | bytes 417800 | tf_op jit(solution)/shard_map/ppermute | solution.py:47
  531.9 29.7 %all-to-all-start = ((bf16[8,128,256]{2,1,0:T(8,128)(2,1)}), bf16[8,128,256]{2,1,0:T(8,128)(2,1)}, u32[]{:S(2)}, u32[]{:S(2)}) async-start(bf16[8,128,256]{2,1,0:T(8,128)(2,1)} %copy-done.115), calls=%async_computation | async-start | bytes 1048576 | tf_op jit(solution)/shard_map/all_to_all | solution.py:1215
  536.2 14.9 %collective-permute-start.102 = (bf16[32,2048]{1,0:T(8,128)(2,1)}, bf16[32,2048]{1,0:T(8,128)(2,1)S(1)}, u32[]{:S(2)}, u32[]{:S(2)}) collective-permute-start(bf16[32,2048]{1,0:T(8,128)(2,1)} %copy-done.93), channel_id=1, source_target_pairs={{0,4},{2,6},{4,0},{6,2},{8,12},{10,14},{12,8},{14,10},{1,5},{3,7},... | collective-permute-start | bytes 393224 | tf_op jit(solution)/shard_map/ppermute | solution.py:47
  537.9 22.3 %collective-permute-start.103 = (bf16[32,2048]{1,0:T(8,128)(2,1)}, bf16[32,2048]{1,0:T(8,128)(2,1)S(1)}, u32[]{:S(2)}, u32[]{:S(2)}) collective-permute-start(bf16[32,2048]{1,0:T(8,128)(2,1)} %copy-done.92), channel_id=1, source_target_pairs={{0,8},{2,10},{4,12},{6,14},{8,0},{10,2},{12,4},{14,6},{1,9},{3,11}... | collective-permute-start | bytes 393224 | tf_op jit(solution)/shard_map/ppermute | solution.py:47
  540.3 20.6 %collective-permute-start.104 = (bf16[32,2048]{1,0:T(8,128)(2,1)}, bf16[32,2048]{1,0:T(8,128)(2,1)S(1)}, u32[]{:S(2)}, u32[]{:S(2)}) collective-permute-start(bf16[32,2048]{1,0:T(8,128)(2,1)} %copy-done.91), channel_id=1, source_target_pairs={{0,12},{2,14},{4,8},{6,10},{8,4},{10,6},{12,0},{14,2},{1,13},{3,15... | collective-permute-start | bytes 393224 | tf_op jit(solution)/shard_map/ppermute | solution.py:47
  565.4 18.7 %collective-permute-start.110 = (bf16[144,2560]{1,0:T(8,128)(2,1)S(1)}, bf16[144,2560]{1,0:T(8,128)(2,1)}, u32[]{:S(2)}, u32[]{:S(2)}) collective-permute-start(bf16[144,2560]{1,0:T(8,128)(2,1)S(1)} %shard_map.302.refs_0_), channel_id=1, source_target_pairs={{0,4},{4,8},{8,12},{12,14},{14,10},{10,6},{6,2},{2,0},{1,5},{5,9},... | collective-permute-start | bytes 2211848 | tf_op jit(solution)/shard_map/ppermute | solution.py:225
  567.4 18.6 %collective-permute-start.111 = (bf16[144,2560]{1,0:T(8,128)(2,1)S(1)}, bf16[144,2560]{1,0:T(8,128)(2,1)}, u32[]{:S(2)}, u32[]{:S(2)}) collective-permute-start(bf16[144,2560]{1,0:T(8,128)(2,1)S(1)} %shard_map.302.refs_0_), channel_id=1, source_target_pairs={{4,0},{8,4},{12,8},{14,12},{10,14},{6,10},{2,6},{0,2},{5,1},{9,5},... | collective-permute-start | bytes 2211848 | tf_op jit(solution)/shard_map/ppermute | solution.py:226
  572.3 26.9 %collective-permute-start.114 = (bf16[512,768]{1,0:T(8,128)(2,1)}, bf16[512,768]{1,0:T(8,128)(2,1)}, u32[]{:S(2)}, u32[]{:S(2)}) collective-permute-start(bf16[512,768]{1,0:T(8,128)(2,1)} %shard_map.306), channel_id=1, source_target_pairs={{0,16},{16,0},{1,17},{17,1},{2,18},{18,2},{3,19},{19,3},{4,20},{20... | collective-permute-start | bytes 2359304 | tf_op jit(solution)/shard_map/ppermute | solution.py:38
  573.9 25.3 %collective-permute-start.115 = (bf16[512,2048]{1,0:T(8,128)(2,1)}, bf16[512,2048]{1,0:T(8,128)(2,1)S(1)}, u32[]{:S(2)}, u32[]{:S(2)}) collective-permute-start(bf16[512,2048]{1,0:T(8,128)(2,1)} %shard_map.307), channel_id=1, source_target_pairs={{0,16},{16,0},{1,17},{17,1},{2,18},{18,2},{3,19},{19,3},{4,20},{20... | collective-permute-start | bytes 6291464 | tf_op jit(solution)/shard_map/ppermute | solution.py:38
  586.8 23.3 %collective-permute-start.108 = (bf16[32,2048]{1,0:T(8,128)(2,1)}, bf16[32,2048]{1,0:T(8,128)(2,1)}, u32[]{:S(2)}, u32[]{:S(2)}) collective-permute-start(bf16[32,2048]{1,0:T(8,128)(2,1)} %broadcast_select_fusion.12), channel_id=1, source_target_pairs={{0,16},{16,0},{1,17},{17,1},{2,18},{18,2},{3,19},{19,3},{4,20},{20... | collective-permute-start | bytes 393224 | tf_op jit(solution)/shard_map/ppermute | solution.py:38
  587.3 20.8 %collective-permute-start.112 = (bf16[144,2560]{1,0:T(8,128)(2,1)}, bf16[144,2560]{1,0:T(8,128)(2,1)}, u32[]{:S(2)}, u32[]{:S(2)}) collective-permute-start(bf16[144,2560]{1,0:T(8,128)(2,1)} %collective-permute-done.110.refs_1_), channel_id=1, source_target_pairs={{0,4},{4,8},{8,12},{12,14},{14,10},{10,6},{6,2},{2,0},{1,5},{5,9},... | collective-permute-start | bytes 2211848 | tf_op jit(solution)/shard_map/ppermute | solution.py:225
  588.4 19.8 %collective-permute-start.113 = (bf16[144,2560]{1,0:T(8,128)(2,1)}, bf16[144,2560]{1,0:T(8,128)(2,1)}, u32[]{:S(2)}, u32[]{:S(2)}) collective-permute-start(bf16[144,2560]{1,0:T(8,128)(2,1)} %collective-permute-done.111.refs_2_), channel_id=1, source_target_pairs={{4,0},{8,4},{12,8},{14,12},{10,14},{6,10},{2,6},{0,2},{5,1},{9,5},... | collective-permute-start | bytes 2211848 | tf_op jit(solution)/shard_map/ppermute | solution.py:226
  594.6 41.4 %all-to-all-start.1 = ((bf16[8,160,256]{2,1,0:T(8,128)(2,1)}), bf16[8,160,256]{2,1,0:T(8,128)(2,1)S(1)}, u32[]{:S(2)}, u32[]{:S(2)}) async-start(bf16[8,160,256]{2,1,0:T(8,128)(2,1)} %fusion.4), calls=%async_computation.1 | async-start | bytes 1310720 | tf_op jit(solution)/shard_map/all_to_all | solution.py:1215
  608.1 22.8 %collective-permute-start.116 = (bf16[144,2560]{1,0:T(8,128)(2,1)}, bf16[144,2560]{1,0:T(8,128)(2,1)}, u32[]{:S(2)}, u32[]{:S(2)}) collective-permute-start(bf16[144,2560]{1,0:T(8,128)(2,1)} %collective-permute-done.112.refs_3_), channel_id=1, source_target_pairs={{0,4},{4,8},{8,12},{12,14},{14,10},{10,6},{6,2},{2,0},{1,5},{5,9},... | collective-permute-start | bytes 2211848 | tf_op jit(solution)/shard_map/ppermute | solution.py:225
  608.2 27.7 %collective-permute-start.117 = (bf16[144,2560]{1,0:T(8,128)(2,1)}, bf16[144,2560]{1,0:T(8,128)(2,1)S(1)}, u32[]{:S(2)}, u32[]{:S(2)}) collective-permute-start(bf16[144,2560]{1,0:T(8,128)(2,1)} %collective-permute-done.113.refs_4_), channel_id=1, source_target_pairs={{4,0},{8,4},{12,8},{14,12},{10,14},{6,10},{2,6},{0,2},{5,1},{9,5},... | collective-permute-start | bytes 2211848 | tf_op jit(solution)/shard_map/ppermute | solution.py:226
  611.1 24.8 %collective-permute-start.109 = (bf16[2,32,2048]{2,1,0:T(8,128)(2,1)S(1)}, bf16[2,32,2048]{2,1,0:T(8,128)(2,1)S(1)}, u32[]{:S(2)}, u32[]{:S(2)}) collective-permute-start(bf16[2,32,2048]{2,1,0:T(8,128)(2,1)S(1)} %pad_maximum_fusion.3), channel_id=1, source_target_pairs={{0,1},{1,0},{2,3},{3,2},{4,5},{5,4},{6,7},{7,6},{8,9},{9,8},{10,11... | collective-permute-start | bytes 786440 | tf_op jit(solution)/shard_map/ppermute | solution.py:42
  (206 other events, 3094.1 us)

commit v6 on v5

--- a/solution.py
+++ b/solution.py
@@ -1337,8 +1337,8 @@
     gather = Gather(payload0)
     gather.along_z()
     weights0 = choose_weights(0, (after(expert_weights[0], payload0), *expert_weights[1:]))
-    gather.near(*weights0)
-    gather.far()
+    gather.near()
+    gather.far(*weights0)
     tiles = gather.tiles()
     ring1.advance(tiles[-1][-1])
     outs0, kept0, stores0 = apply_experts(tiles, weights0, ones, 0)
@@ -1405,8 +1405,8 @@
     gather.along_z()
     beside = out_scatter.near(d_one)
     weights0 = choose_weights(0, (after(expert_weights[0], d_one), *expert_weights[1:]))
-    gather.near(*beside, *weights0)
-    gather.far()
+    gather.near(*beside)
+    gather.far(*weights0)
     tiles = gather.tiles()
     backs, back_stores0 = apply_experts_back(tiles, weights0, ones, kept0, 0)
 

time: 671 us -> 673 us (level)
    ppermute x40, waiting for transfers between devices: 65.6 us -> 83.9 us  [swap_e(): return lax.ppermute(value, 'expert', [(i, i ^ bits) for i in range(count)])]
    ppermute x25, waiting for transfers between devices: 81.8 us -> 71.1 us  [swap_x(): return lax.ppermute(value, 'tensor', [(0, 1), (1, 0)])]
  transfers between devices with their start and end apart: 124 -> 124, of which waited for: 65 -> 66; matrix products, arithmetic and copies ran while one was open for 3% -> 3% of each run, Pallas kernels for 16% -> 16%
where the time goes in v6:
time: 673 us; the launch traced here: 665 us
  waiting for transfers between devices  337 us (50%)
  starting transfers between devices  145 us (22%)
  Pallas kernels  128 us (19%)
  local copies, waits for them, and re-layouts  40.8 us (6%)
  other arithmetic  10.1 us (2%)
    ppermute x16, waiting for transfers between devices, advance(): self.plus = lax.ppermute(after(plus, *gate), 'expert', up)  151 us
    ppermute x40, waiting for transfers between devices, swap_e(): return lax.ppermute(value, 'expert', [(i, i ^ bits) for i in range(count)])  83.9 us
    ppermute x25, waiting for transfers between devices, swap_x(): return lax.ppermute(value, 'tensor', [(0, 1), (1, 0)])  71.1 us
    ppermute x40, starting transfers between devices, swap_e(): return lax.ppermute(value, 'expert', [(i, i ^ bits) for i in range(count)])  59.9 us
    unnamed x307, local copies, waits for them, and re-layouts  34.3 us
    ppermute x25, starting transfers between devices, swap_x(): return lax.ppermute(value, 'tensor', [(0, 1), (1, 0)])  30.7 us
    ppermute x16, starting transfers between devices, advance(): self.plus = lax.ppermute(after(plus, *gate), 'expert', up)  29.5 us
    pallas_call x4, Pallas kernels, run_grads(): pl.pallas_call(functools.partial(grads_kernel, (place, step), len(before)...  28.6 us
  transfers between devices with their start and end apart: 124, of which 66 were waited for; matrix products, arithmetic and copies ran while one was open for 3% of the time, Pallas kernels for 16%

profile of v6, /device:TPU:0, one launch (start us, length us, event | category | flops | bytes accessed | tf_op | source)
XLA Modules:
  0.0 665.2 jit_solution(13947525853523605106)
XLA Ops:
  9.4 3.0 collective-permute-start.2
  12.4 27.7 %collective-permute-done.2.refs_1_ = bf16[256,2432]{1,0:T(8,128)(2,1)} collective-permute-done((bf16[256,2432]{1,0:T(8,128)(2,1)S(1)}, bf16[256,2432]{1,0:T(8,128)(2,1)}, u32[]{:S(2)}, u32[]{:S(2)}) %collective-permute-start.2) | collective-permute-done | bytes 1245216 | tf_op jit(solution)/shard_map/ppermute | solution.py:225
  46.2 26.3 %collective-permute-done.4.refs_3_ = bf16[256,2432]{1,0:T(8,128)(2,1)} collective-permute-done((bf16[256,2432]{1,0:T(8,128)(2,1)}, bf16[256,2432]{1,0:T(8,128)(2,1)}, u32[]{:S(2)}, u32[]{:S(2)}) %collective-permute-start.4) | collective-permute-done | bytes 1245216 | tf_op jit(solution)/shard_map/ppermute | solution.py:225
  76.2 25.0 %collective-permute-done.6.refs_5_ = bf16[256,2432]{1,0:T(8,128)(2,1)} collective-permute-done((bf16[256,2432]{1,0:T(8,128)(2,1)}, bf16[256,2432]{1,0:T(8,128)(2,1)}, u32[]{:S(2)}, u32[]{:S(2)}) %collective-permute-start.6) | collective-permute-done | bytes 1245216 | tf_op jit(solution)/shard_map/ppermute | solution.py:225
  106.2 10.5 %collective-permute-done.8.refs_7_ = bf16[128,2432]{1,0:T(8,128)(2,1)S(1)} collective-permute-done((bf16[128,2432]{1,0:T(8,128)(2,1)S(1)}, bf16[128,2432]{1,0:T(8,128)(2,1)S(1)}, u32[]{:S(2)}, u32[]{:S(2)}) %collective-permute-start.8) | collective-permute-done | bytes 622624 | tf_op jit(solution)/shard_map/ppermute | solution.py:225
  121.5 7.8 %shard_map.264 = (f32[128,2048]{1,0:T(8,128)S(1)}, bf16[128,2048]{1,0:T(8,128)(2,1)S(1)}, bf16[128,1024]{1,0:T(8,128)(2,1)S(1)}, f32[128,1280]{1,0:T(8,128)S(1)}...) custom-call(bf16[256,2432]{1,0:T(8,128)(2,1)S(1)} %fusion.1.refs_0_, ...), custom_call_target="tpu_custom_call" | custom-call | flops 7247757312 | bytes 9437184 | tf_op jit(solution)/shard_map/pallas_call | solution.py:397
  132.5 11.7 %collective-permute-done.10.refs_1_ = bf16[256,2304]{1,0:T(8,128)(2,1)S(1)} collective-permute-done((bf16[256,2304]{1,0:T(8,128)(2,1)S(1)}, bf16[256,2304]{1,0:T(8,128)(2,1)S(1)}, u32[]{:S(2)}, u32[]{:S(2)}) %collective-permute-start.10) | collective-permute-done | bytes 1179680 | tf_op jit(solution)/shard_map/ppermute | solution.py:225
  148.8 3.8 collective-permute-done.14.got
  155.3 4.4 collective-permute-done.16.refs_1_
  161.3 6.1 collective-permute-done.17.refs_2_
  169.7 3.9 shard_map.268
  173.6 5.1 collective-permute-done.26.refs_1_
  182.8 6.4 collective-permute-done.23.refs_4_
  189.2 3.0 collective-permute-start.24
  192.4 8.2 %shard_map.269 = (bf16[128,2048]{1,0:T(8,128)(2,1)S(1)}, bf16[128,2048]{1,0:T(8,128)(2,1)S(1)}, bf16[128,2048]{1,0:T(8,128)(2,1)S(1)}, bf16[64,2048]{1,0:T(8,128...) custom-call(bf16[128,2176]{1,0:T(8,128)(2,1)S(1)} %shard_map.267.ref, ...), custom_call_target="tpu_custom_call" | custom-call | flops 9663676416 | bytes 9437184 | tf_op jit(solution)/shard_map/pallas_call | solution.py:669
  204.3 16.2 %collective-permute-done.28.top = bf16[64,2048]{1,0:T(8,128)(2,1)S(1)} collective-permute-done((bf16[64,2048]{1,0:T(8,128)(2,1)S(1)}, bf16[64,2048]{1,0:T(8,128)(2,1)S(1)}, u32[]{:S(2)}, u32[]{:S(2)}) %collective-permute-start.28) | collective-permute-done | bytes 262176 | tf_op jit(solution)/shard_map/ppermute | solution.py:47
  223.8 6.1 collective-permute-done.30.from_x
  231.3 4.2 collective-permute-start.33
  236.2 3.8 collective-permute-done.33.refs_2_
  240.0 3.6 collective-permute-done.34.refs_3_
  246.8 19.2 %collective-permute-done.35.refs_5_ = bf16[256,2304]{1,0:T(8,128)(2,1)S(1)} collective-permute-done((bf16[256,2304]{1,0:T(8,128)(2,1)S(1)}, bf16[256,2304]{1,0:T(8,128)(2,1)S(1)}, u32[]{:S(2)}, u32[]{:S(2)}) %collective-permute-start.35) | collective-permute-done | bytes 1179680 | tf_op jit(solution)/shard_map/ppermute | solution.py:225
  266.1 3.9 collective-permute-start.37
  277.1 2.9 collective-permute-done.37.refs_7_
  280.0 3.2 collective-permute-done.38.refs_8_
  283.3 6.4 shard_map.274
  296.0 3.0 collective-permute-done.46.got
  300.4 7.1 %collective-permute-start.49 = (bf16[32,2176]{1,0:T(8,128)(2,1)S(1)}, bf16[32,2176]{1,0:T(8,128)(2,1)S(1)}, u32[]{:S(2)}, u32[]{:S(2)}) collective-permute-start(bf16[32,2176]{1,0:T(8,128)(2,1)S(1)} %get-tuple-element.238.refs_0_.refs_8_), channel_id=1, source_target_pairs={{0,4},{2,6},{4,0},{6,2},{8,12},{10,14},{12,8},{14,10},{1,5},{3,7},... | collective-permute-start | bytes 417800 | tf_op jit(solution)/shard_map/ppermute | solution.py:47
  310.2 3.8 shard_map.278
  314.0 6.1 collective-permute-done.50.refs_2_
  323.0 7.6 %collective-permute-done.56.refs_1_ = bf16[128,2176]{1,0:T(8,128)(2,1)S(1)} collective-permute-done((bf16[128,2176]{1,0:T(8,128)(2,1)S(1)}, bf16[128,2176]{1,0:T(8,128)(2,1)S(1)}, u32[]{:S(2)}, u32[]{:S(2)}) %collective-permute-start.56) | collective-permute-done | bytes 557088 | tf_op jit(solution)/shard_map/ppermute | solution.py:42
  330.7 3.6 collective-permute-start.57
  337.4 3.5 collective-permute-done.53.refs_4_
  340.9 3.5 collective-permute-start.59
  346.6 8.2 %shard_map.279 = (bf16[128,2048]{1,0:T(8,128)(2,1)S(1)}, bf16[128,2048]{1,0:T(8,128)(2,1)S(1)}, bf16[128,2048]{1,0:T(8,128)(2,1)S(1)}, bf16[64,2048]{1,0:T(8,128...) custom-call(bf16[128,2176]{1,0:T(8,128)(2,1)S(1)} %shard_map.277.ref, ...), custom_call_target="tpu_custom_call" | custom-call | flops 9663676416 | bytes 9437184 | tf_op jit(solution)/shard_map/pallas_call | solution.py:669
  362.6 8.3 %shard_map.281 = (bf16[128,2176]{1,0:T(8,128)(2,1)S(1)}, bf16[128,2176]{1,0:T(8,128)(2,1)S(1)}, bf16[128,2176]{1,0:T(8,128)(2,1)S(1)}, bf16[64,2176]{1,0:T(8,128...) custom-call(bf16[128,2048]{1,0:T(8,128)(2,1)S(1)} %shard_map.273.refs_0_, ...), custom_call_target="tpu_custom_call" | custom-call | flops 9663676416 | bytes 9437184 | tf_op jit(solution)/shard_map/pallas_call | solution.py:757
  375.6 5.9 collective-permute-done.63.top
  381.5 2.7 collective-permute-done.64.bottom
  385.4 11.4 %collective-permute-done.65.from_x = bf16[128,2176]{1,0:T(8,128)(2,1)S(1)} collective-permute-done((bf16[128,2176]{1,0:T(8,128)(2,1)S(1)}, bf16[128,2176]{1,0:T(8,128)(2,1)S(1)}, u32[]{:S(2)}, u32[]{:S(2)}) %collective-permute-start.65) | collective-permute-done | bytes 557088 | tf_op jit(solution)/shard_map/ppermute | solution.py:42
  400.7 2.8 collective-permute-start.68
  410.4 3.9 collective-permute-done.72.refs_10_
  421.9 9.9 %shard_map.285 = (bf16[128,2048]{1,0:T(8,128)(2,1)}, bf16[144,1280]{1,0:T(8,128)(2,1)}, f32[64,2048]{1,0:T(8,128)}, bf16[64,2048]{1,0:T(8,128)(2,1)}) custom-call(bf16[256,2304]{1,0:T(8,128)(2,1)} %copy-done.21, bf16[256,2304]{1,0:T(8,128)(2,1)} %copy-done.81, bf16[256,2304]{1,0:T(8,128)(2,1)} %copy-done.83, bf16[256,2304]{1,0:T(8,128)(2,1)} %copy-done.85, ...), custom_call_target="tpu_custom_call" | custom-call | flops 7247757312 | bytes 9437184 | tf_op jit(solution)/shard_map/pallas_call | solution.py:501
  437.0 4.2 collective-permute-done.79.got
  451.1 6.9 %collective-permute-done.83.refs_2_ = bf16[32,2048]{1,0:T(8,128)(2,1)S(1)} collective-permute-done((bf16[32,2048]{1,0:T(8,128)(2,1)S(1)}, bf16[32,2048]{1,0:T(8,128)(2,1)S(1)}, u32[]{:S(2)}, u32[]{:S(2)}) %collective-permute-start.83) | collective-permute-done | bytes 131104 | tf_op jit(solution)/shard_map/ppermute | solution.py:47
  461.6 3.8 shard_map.292
  465.4 5.3 collective-permute-done.87.refs_1_
  474.0 3.1 collective-permute-done.89.refs_3_
  479.7 8.3 %shard_map.293 = (bf16[128,2176]{1,0:T(8,128)(2,1)S(1)}, bf16[128,2176]{1,0:T(8,128)(2,1)S(1)}, bf16[128,2176]{1,0:T(8,128)(2,1)S(1)}, bf16[64,2176]{1,0:T(8,128...) custom-call(bf16[128,2048]{1,0:T(8,128)(2,1)S(1)} %shard_map.289.refs_0_, ...), custom_call_target="tpu_custom_call" | custom-call | flops 9663676416 | bytes 9437184 | tf_op jit(solution)/shard_map/pallas_call | solution.py:757
  490.4 4.4 collective-permute-done.91.top
  500.5 8.8 %shard_map.296 = (f32[2,2048,384]{2,1,0:T(8,128)}, f32[2,2048,384]{2,1,0:T(8,128)}) custom-call(bf16[512,2048]{1,0:T(8,128)(2,1)} %copy-done.6, bf16[512,2048]{1,0:T(8,128)(2,1)} %copy-done.8, bf16[512,2048]{1,0:T(8,128)(2,1)} %copy-done.107, bf16[512,2048]{1,0:T(8,128)(2,1)} %copy-done.107, bf16[512,1536]{1,0:T(8,128)(2,1)} %copy-done.11, ...), custom_call_target="tpu_custom_call" | custom-call | flops 100000000 | bytes 100000 | tf_op jit(solution)/shard_map/pallas_call | solution.py:834
  514.0 8.7 %shard_map.299 = (f32[2,2048,384]{2,1,0:T(8,128)}, f32[2,2048,384]{2,1,0:T(8,128)}) custom-call(bf16[512,2048]{1,0:T(8,128)(2,1)} %copy-done.6, bf16[512,2048]{1,0:T(8,128)(2,1)} %copy-done.8, bf16[512,2048]{1,0:T(8,128)(2,1)} %copy-done.107, bf16[512,2048]{1,0:T(8,128)(2,1)} %copy-done.107, ...), custom_call_target="tpu_custom_call", output_to_operand_aliasing={{0}: (8, {}), {1}: (9, {})} | custom-call | flops 100000000 | bytes 100000 | tf_op jit(solution)/shard_map/pallas_call | solution.py:834
  527.8 3.0 collective-permute-done.99.refs_10_
  532.1 4.4 all-to-all-start
  541.6 9.9 %shard_map.301 = (bf16[128,2048]{1,0:T(8,128)(2,1)}, bf16[144,1280]{1,0:T(8,128)(2,1)}, f32[64,2048]{1,0:T(8,128)}, bf16[64,2048]{1,0:T(8,128)(2,1)}) custom-call(bf16[256,2432]{1,0:T(8,128)(2,1)} %copy-done.20, bf16[256,2432]{1,0:T(8,128)(2,1)} %collective-permute-done.2.refs_1_, bf16[256,2432]{1,0:T(8,128)(2,1)} %collective-permute-done.3.refs_2_, ...), custom_call_target="tpu_custom_call" | custom-call | flops 7247757312 | bytes 9437184 | tf_op jit(solution)/shard_map/pallas_call | solution.py:501
  551.5 9.3 %collective-permute-done.103.refs_2_ = bf16[32,2048]{1,0:T(8,128)(2,1)S(1)} collective-permute-done((bf16[32,2048]{1,0:T(8,128)(2,1)}, bf16[32,2048]{1,0:T(8,128)(2,1)S(1)}, u32[]{:S(2)}, u32[]{:S(2)}) %collective-permute-start.103) | collective-permute-done | bytes 131104 | tf_op jit(solution)/shard_map/ppermute | solution.py:47
  576.7 8.0 %collective-permute-done.110.refs_1_ = bf16[144,2560]{1,0:T(8,128)(2,1)} collective-permute-done((bf16[144,2560]{1,0:T(8,128)(2,1)S(1)}, bf16[144,2560]{1,0:T(8,128)(2,1)}, u32[]{:S(2)}, u32[]{:S(2)}) %collective-permute-start.110) | collective-permute-done | bytes 737312 | tf_op jit(solution)/shard_map/ppermute | solution.py:225
  594.6 4.8 all-to-all-start.1
  600.8 5.5 shard_map.308.refs_8_
  613.5 5.5 shard_map.309
  619.0 11.9 %collective-permute-done.116.refs_5_ = bf16[144,2560]{1,0:T(8,128)(2,1)} collective-permute-done((bf16[144,2560]{1,0:T(8,128)(2,1)}, bf16[144,2560]{1,0:T(8,128)(2,1)}, u32[]{:S(2)}, u32[]{:S(2)}) %collective-permute-start.116) | collective-permute-done | bytes 737312 | tf_op jit(solution)/shard_map/ppermute | solution.py:225
  631.9 3.9 collective-permute-start.118
  636.0 6.1 collective-permute-done.118.refs_7_
  642.1 4.9 collective-permute-done.119.refs_8_
  647.0 7.6 %shard_map.312 = (f32[256,2048]{1,0:T(8,128)}, f32[256,256]{1,0:T(8,128)}, f32[256,256]{1,0:T(8,128)}, f32[40,256]{1,0:T(8,128)}) custom-call(bf16[144,2560]{1,0:T(8,128)(2,1)} %copy-done.32, bf16[144,2560]{1,0:T(8,128)(2,1)} %collective-permute-done.110.refs_1_, bf16[144,2560]{1,0:T(8,128)(2,1)} %collective-permute-done.111.refs_2_, ...), custom_call_target="tpu_custom_call" | custom-call | flops 15099494400 | bytes 11796480 | tf_op jit(solution)/shard_map/pallas_call | solution.py:981
  657.9 5.1 shard_map.313
  (622 shorter events, 204.7 us)
Async XLA Ops:
  9.4 30.7 %collective-permute-start.2 = (bf16[256,2432]{1,0:T(8,128)(2,1)S(1)}, bf16[256,2432]{1,0:T(8,128)(2,1)}, u32[]{:S(2)}, u32[]{:S(2)}) collective-permute-start(bf16[256,2432]{1,0:T(8,128)(2,1)S(1)} %fusion.1.refs_0_), channel_id=1, source_target_pairs={{0,4},{4,8},{8,12},{12,14},{14,10},{10,6},{6,2},{2,0},{1,5},{5,9},... | collective-permute-start | bytes 3735560 | tf_op jit(solution)/shard_map/ppermute | solution.py:225
  12.4 29.2 %collective-permute-start.3 = (bf16[256,2432]{1,0:T(8,128)(2,1)S(1)}, bf16[256,2432]{1,0:T(8,128)(2,1)}, u32[]{:S(2)}, u32[]{:S(2)}) collective-permute-start(bf16[256,2432]{1,0:T(8,128)(2,1)S(1)} %fusion.1.refs_0_), channel_id=1, source_target_pairs={{4,0},{8,4},{12,8},{14,12},{10,14},{6,10},{2,6},{0,2},{5,1},{9,5},... | collective-permute-start | bytes 3735560 | tf_op jit(solution)/shard_map/ppermute | solution.py:226
  41.8 127.9 %collective-permute-start.20 = (bf16[2,2048,384]{2,1,0:T(8,128)(2,1)}, bf16[2,2048,384]{2,1,0:T(8,128)(2,1)}, u32[]{:S(2)}, u32[]{:S(2)}) collective-permute-start(bf16[2,2048,384]{2,1,0:T(8,128)(2,1)} %bitcast.26.refs_0_), channel_id=1, source_target_pairs={{0,16},{16,0},{1,17},{17,1},{2,18},{18,2},{3,19},{19,3},{4,20},{20... | collective-permute-start | bytes 9437192 | tf_op jit(solution)/shard_map/ppermute | solution.py:38
  42.3 127.4 %collective-permute-start.21 = (bf16[2,2048,384]{2,1,0:T(8,128)(2,1)}, bf16[2,2048,384]{2,1,0:T(8,128)(2,1)}, u32[]{:S(2)}, u32[]{:S(2)}) collective-permute-start(bf16[2,2048,384]{2,1,0:T(8,128)(2,1)} %bitcast.27.refs_1_), channel_id=1, source_target_pairs={{0,16},{16,0},{1,17},{17,1},{2,18},{18,2},{3,19},{19,3},{4,20},{20... | collective-permute-start | bytes 9437192 | tf_op jit(solution)/shard_map/ppermute | solution.py:38
  42.4 127.3 %collective-permute-start.22 = (bf16[2,384,2048]{2,1,0:T(8,128)(2,1)}, bf16[2,384,2048]{2,1,0:T(8,128)(2,1)}, u32[]{:S(2)}, u32[]{:S(2)}) collective-permute-start(bf16[2,384,2048]{2,1,0:T(8,128)(2,1)} %bitcast.28.refs_2_), channel_id=1, source_target_pairs={{0,16},{16,0},{1,17},{17,1},{2,18},{18,2},{3,19},{19,3},{4,20},{20... | collective-permute-start | bytes 9437192 | tf_op jit(solution)/shard_map/ppermute | solution.py:38
  42.8 29.7 %collective-permute-start.4 = (bf16[256,2432]{1,0:T(8,128)(2,1)}, bf16[256,2432]{1,0:T(8,128)(2,1)}, u32[]{:S(2)}, u32[]{:S(2)}) collective-permute-start(bf16[256,2432]{1,0:T(8,128)(2,1)} %collective-permute-done.2.refs_1_), channel_id=1, source_target_pairs={{0,4},{4,8},{8,12},{12,14},{14,10},{10,6},{6,2},{2,0},{1,5},{5,9},... | collective-permute-start | bytes 3735560 | tf_op jit(solution)/shard_map/ppermute | solution.py:225
  44.4 29.7 %collective-permute-start.5 = (bf16[256,2432]{1,0:T(8,128)(2,1)}, bf16[256,2432]{1,0:T(8,128)(2,1)}, u32[]{:S(2)}, u32[]{:S(2)}) collective-permute-start(bf16[256,2432]{1,0:T(8,128)(2,1)} %collective-permute-done.3.refs_2_), channel_id=1, source_target_pairs={{4,0},{8,4},{12,8},{14,12},{10,14},{6,10},{2,6},{0,2},{5,1},{9,5},... | collective-permute-start | bytes 3735560 | tf_op jit(solution)/shard_map/ppermute | solution.py:226
  72.5 28.8 %collective-permute-start.6 = (bf16[256,2432]{1,0:T(8,128)(2,1)}, bf16[256,2432]{1,0:T(8,128)(2,1)}, u32[]{:S(2)}, u32[]{:S(2)}) collective-permute-start(bf16[256,2432]{1,0:T(8,128)(2,1)} %collective-permute-done.4.refs_3_), channel_id=1, source_target_pairs={{0,4},{4,8},{8,12},{12,14},{14,10},{10,6},{6,2},{2,0},{1,5},{5,9},... | collective-permute-start | bytes 3735560 | tf_op jit(solution)/shard_map/ppermute | solution.py:225
  74.0 30.0 %collective-permute-start.7 = (bf16[256,2432]{1,0:T(8,128)(2,1)}, bf16[256,2432]{1,0:T(8,128)(2,1)}, u32[]{:S(2)}, u32[]{:S(2)}) collective-permute-start(bf16[256,2432]{1,0:T(8,128)(2,1)} %collective-permute-done.5.refs_4_), channel_id=1, source_target_pairs={{4,0},{8,4},{12,8},{14,12},{10,14},{6,10},{2,6},{0,2},{5,1},{9,5},... | collective-permute-start | bytes 3735560 | tf_op jit(solution)/shard_map/ppermute | solution.py:226
  102.4 14.3 %collective-permute-start.8 = (bf16[128,2432]{1,0:T(8,128)(2,1)S(1)}, bf16[128,2432]{1,0:T(8,128)(2,1)S(1)}, u32[]{:S(2)}, u32[]{:S(2)}) collective-permute-start(bf16[128,2432]{1,0:T(8,128)(2,1)S(1)} %slice.283), channel_id=1, source_target_pairs={{0,4},{4,8},{8,12},{12,14},{14,10},{10,6},{6,2},{2,0},{1,5},{5,9},... | collective-permute-start | bytes 1867784 | tf_op jit(solution)/shard_map/ppermute | solution.py:225
  105.2 14.0 %collective-permute-start.9 = (bf16[128,2432]{1,0:T(8,128)(2,1)S(1)}, bf16[128,2432]{1,0:T(8,128)(2,1)S(1)}, u32[]{:S(2)}, u32[]{:S(2)}) collective-permute-start(bf16[128,2432]{1,0:T(8,128)(2,1)S(1)} %slice.284), channel_id=1, source_target_pairs={{4,0},{8,4},{12,8},{14,12},{10,14},{6,10},{2,6},{0,2},{5,1},{9,5},... | collective-permute-start | bytes 1867784 | tf_op jit(solution)/shard_map/ppermute | solution.py:226
  119.2 25.0 %collective-permute-start.10 = (bf16[256,2304]{1,0:T(8,128)(2,1)S(1)}, bf16[256,2304]{1,0:T(8,128)(2,1)S(1)}, u32[]{:S(2)}, u32[]{:S(2)}) collective-permute-start(bf16[256,2304]{1,0:T(8,128)(2,1)S(1)} %get-tuple-element.194.refs_0_), channel_id=1, source_target_pairs={{0,4},{4,8},{8,12},{12,14},{14,10},{10,6},{6,2},{2,0},{1,5},{5,9},... | collective-permute-start | bytes 3538952 | tf_op jit(solution)/shard_map/ppermute | solution.py:225
  120.8 24.7 %collective-permute-start.11 = (bf16[256,2304]{1,0:T(8,128)(2,1)S(1)}, bf16[256,2304]{1,0:T(8,128)(2,1)S(1)}, u32[]{:S(2)}, u32[]{:S(2)}) collective-permute-start(bf16[256,2304]{1,0:T(8,128)(2,1)S(1)} %get-tuple-element.194.refs_0_), channel_id=1, source_target_pairs={{4,0},{8,4},{12,8},{14,12},{10,14},{6,10},{2,6},{0,2},{5,1},{9,5},... | collective-permute-start | bytes 3538952 | tf_op jit(solution)/shard_map/ppermute | solution.py:226
  154.7 12.7 %collective-permute-start.17 = (bf16[32,2176]{1,0:T(8,128)(2,1)S(1)}, bf16[32,2176]{1,0:T(8,128)(2,1)S(1)}, u32[]{:S(2)}, u32[]{:S(2)}) collective-permute-start(bf16[32,2176]{1,0:T(8,128)(2,1)S(1)} %get-tuple-element.204.refs_0_.refs_8_), channel_id=1, source_target_pairs={{0,8},{2,10},{4,12},{6,14},{8,0},{10,2},{12,4},{14,6},{1,9},{3,11}... | collective-permute-start | bytes 417800 | tf_op jit(solution)/shard_map/ppermute | solution.py:47
  169.6 13.0 %collective-permute-start.19 = (bf16[128,2176]{1,0:T(8,128)(2,1)S(1)}, bf16[128,2176]{1,0:T(8,128)(2,1)S(1)}, u32[]{:S(2)}, u32[]{:S(2)}) collective-permute-start(bf16[128,2176]{1,0:T(8,128)(2,1)S(1)} %shard_map.267.refs_0_), channel_id=1, source_target_pairs={{0,2},{2,0},{4,6},{6,4},{8,10},{10,8},{12,14},{14,12},{1,3},{3,1},... | collective-permute-start | bytes 1671176 | tf_op jit(solution)/shard_map/ppermute | solution.py:47
  178.8 13.6 %collective-permute-start.27 = (bf16[64,2176]{1,0:T(8,128)(2,1)S(1)}, bf16[64,2176]{1,0:T(8,128)(2,1)S(1)}, u32[]{:S(2)}, u32[]{:S(2)}) collective-permute-start(bf16[64,2176]{1,0:T(8,128)(2,1)S(1)} %slice.292), channel_id=1, source_target_pairs={{0,2},{2,0},{4,6},{6,4},{8,10},{10,8},{12,14},{14,12},{1,3},{3,1},... | collective-permute-start | bytes 835592 | tf_op jit(solution)/shard_map/ppermute | solution.py:47
  189.2 40.6 %collective-permute-start.24 = (bf16[256,2304]{1,0:T(8,128)(2,1)S(1)}, bf16[256,2304]{1,0:T(8,128)(2,1)S(1)}, u32[]{:S(2)}, u32[]{:S(2)}) collective-permute-start(bf16[256,2304]{1,0:T(8,128)(2,1)S(1)} %copy-done.82), channel_id=1, source_target_pairs={{0,4},{4,8},{8,12},{12,14},{14,10},{10,6},{6,2},{2,0},{1,5},{5,9},... | collective-permute-start | bytes 3538952 | tf_op jit(solution)/shard_map/ppermute | solution.py:225
  192.2 37.6 %collective-permute-start.25 = (bf16[256,2304]{1,0:T(8,128)(2,1)S(1)}, bf16[256,2304]{1,0:T(8,128)(2,1)S(1)}, u32[]{:S(2)}, u32[]{:S(2)}) collective-permute-start(bf16[256,2304]{1,0:T(8,128)(2,1)S(1)} %copy-done.84), channel_id=1, source_target_pairs={{4,0},{8,4},{12,8},{14,12},{10,14},{6,10},{2,6},{0,2},{5,1},{9,5},... | collective-permute-start | bytes 3538952 | tf_op jit(solution)/shard_map/ppermute | solution.py:226
  202.3 18.1 %collective-permute-start.28 = (bf16[64,2048]{1,0:T(8,128)(2,1)S(1)}, bf16[64,2048]{1,0:T(8,128)(2,1)S(1)}, u32[]{:S(2)}, u32[]{:S(2)}) collective-permute-start(bf16[64,2048]{1,0:T(8,128)(2,1)S(1)} %get-tuple-element.217), channel_id=1, source_target_pairs={{0,2},{2,0},{4,6},{6,4},{8,10},{10,8},{12,14},{14,12},{1,3},{3,1},... | collective-permute-start | bytes 786440 | tf_op jit(solution)/shard_map/ppermute | solution.py:47
  202.8 17.7 %collective-permute-start.29 = (bf16[64,2048]{1,0:T(8,128)(2,1)S(1)}, bf16[64,2048]{1,0:T(8,128)(2,1)S(1)}, u32[]{:S(2)}, u32[]{:S(2)}) collective-permute-start(bf16[64,2048]{1,0:T(8,128)(2,1)S(1)} %get-tuple-element.219), channel_id=1, source_target_pairs={{0,1},{1,0},{2,3},{3,2},{4,5},{5,4},{6,7},{7,6},{8,9},{9,8},{10,11... | collective-permute-start | bytes 786440 | tf_op jit(solution)/shard_map/ppermute | solution.py:42
  243.7 22.4 %collective-permute-start.35 = (bf16[256,2304]{1,0:T(8,128)(2,1)S(1)}, bf16[256,2304]{1,0:T(8,128)(2,1)S(1)}, u32[]{:S(2)}, u32[]{:S(2)}) collective-permute-start(bf16[256,2304]{1,0:T(8,128)(2,1)S(1)} %collective-permute-done.24.refs_3_), channel_id=1, source_target_pairs={{0,4},{4,8},{8,12},{12,14},{14,10},{10,6},{6,2},{2,0},{1,5},{5,9},... | collective-permute-start | bytes 3538952 | tf_op jit(solution)/shard_map/ppermute | solution.py:225
  244.8 25.2 %collective-permute-start.36 = (bf16[256,2304]{1,0:T(8,128)(2,1)S(1)}, bf16[256,2304]{1,0:T(8,128)(2,1)S(1)}, u32[]{:S(2)}, u32[]{:S(2)}) collective-permute-start(bf16[256,2304]{1,0:T(8,128)(2,1)S(1)} %collective-permute-done.25.refs_4_), channel_id=1, source_target_pairs={{4,0},{8,4},{12,8},{14,12},{10,14},{6,10},{2,6},{0,2},{5,1},{9,5},... | collective-permute-start | bytes 3538952 | tf_op jit(solution)/shard_map/ppermute | solution.py:226
  246.0 24.2 %collective-permute-start.39 = (bf16[32,2048]{1,0:T(8,128)(2,1)S(1)}, bf16[32,2048]{1,0:T(8,128)(2,1)S(1)}, u32[]{:S(2)}, u32[]{:S(2)}) collective-permute-start(bf16[32,2048]{1,0:T(8,128)(2,1)S(1)} %get-tuple-element.230.refs_9_), channel_id=1, source_target_pairs={{0,1},{1,0},{2,3},{3,2},{4,5},{5,4},{6,7},{7,6},{8,9},{9,8},{10,11... | collective-permute-start | bytes 393224 | tf_op jit(solution)/shard_map/ppermute | solution.py:42
  266.1 13.9 %collective-permute-start.37 = (bf16[128,2304]{1,0:T(8,128)(2,1)S(1)}, bf16[128,2304]{1,0:T(8,128)(2,1)S(1)}, u32[]{:S(2)}, u32[]{:S(2)}) collective-permute-start(bf16[128,2304]{1,0:T(8,128)(2,1)S(1)} %slice.293), channel_id=1, source_target_pairs={{0,4},{4,8},{8,12},{12,14},{14,10},{10,6},{6,2},{2,0},{1,5},{5,9},... | collective-permute-start | bytes 1769480 | tf_op jit(solution)/shard_map/ppermute | solution.py:225
  270.0 13.2 %collective-permute-start.38 = (bf16[128,2304]{1,0:T(8,128)(2,1)S(1)}, bf16[128,2304]{1,0:T(8,128)(2,1)S(1)}, u32[]{:S(2)}, u32[]{:S(2)}) collective-permute-start(bf16[128,2304]{1,0:T(8,128)(2,1)S(1)} %slice.294), channel_id=1, source_target_pairs={{4,0},{8,4},{12,8},{14,12},{10,14},{6,10},{2,6},{0,2},{5,1},{9,5},... | collective-permute-start | bytes 1769480 | tf_op jit(solution)/shard_map/ppermute | solution.py:226
  271.7 19.6 %collective-permute-start.41 = (bf16[32,2048]{1,0:T(8,128)(2,1)S(1)}, bf16[32,2048]{1,0:T(8,128)(2,1)S(1)}, u32[]{:S(2)}, u32[]{:S(2)}) collective-permute-start(bf16[32,2048]{1,0:T(8,128)(2,1)S(1)} %fusion.3.refs_0_.refs_4_), channel_id=1, source_target_pairs={{0,4},{2,6},{4,0},{6,2},{8,12},{10,14},{12,8},{14,10},{1,5},{3,7},... | collective-permute-start | bytes 393224 | tf_op jit(solution)/shard_map/ppermute | solution.py:47
  274.2 17.5 %collective-permute-start.42 = (bf16[32,2048]{1,0:T(8,128)(2,1)S(1)}, bf16[32,2048]{1,0:T(8,128)(2,1)S(1)}, u32[]{:S(2)}, u32[]{:S(2)}) collective-permute-start(bf16[32,2048]{1,0:T(8,128)(2,1)S(1)} %fusion.3.refs_0_.refs_4_), channel_id=1, source_target_pairs={{0,8},{2,10},{4,12},{6,14},{8,0},{10,2},{12,4},{14,6},{1,9},{3,11}... | collective-permute-start | bytes 393224 | tf_op jit(solution)/shard_map/ppermute | solution.py:47
  275.7 16.0 %collective-permute-start.43 = (bf16[32,2048]{1,0:T(8,128)(2,1)S(1)}, bf16[32,2048]{1,0:T(8,128)(2,1)S(1)}, u32[]{:S(2)}, u32[]{:S(2)}) collective-permute-start(bf16[32,2048]{1,0:T(8,128)(2,1)S(1)} %fusion.3.refs_0_.refs_4_), channel_id=1, source_target_pairs={{0,12},{2,14},{4,8},{6,10},{8,4},{10,6},{12,0},{14,2},{1,13},{3,15... | collective-permute-start | bytes 393224 | tf_op jit(solution)/shard_map/ppermute | solution.py:47
  299.5 20.6 %collective-permute-start.47 = (bf16[128,2048]{1,0:T(8,128)(2,1)S(1)}, bf16[128,2048]{1,0:T(8,128)(2,1)S(1)}, u32[]{:S(2)}, u32[]{:S(2)}) collective-permute-start(bf16[128,2048]{1,0:T(8,128)(2,1)S(1)} %shard_map.273.refs_0_), channel_id=1, source_target_pairs={{0,1},{1,0},{2,3},{3,2},{4,5},{5,4},{6,7},{7,6},{8,9},{9,8},{10,11... | collective-permute-start | bytes 1572872 | tf_op jit(solution)/shard_map/ppermute | solution.py:42
  300.1 20.1 %collective-permute-start.48 = (bf16[128,2048]{1,0:T(8,128)(2,1)S(1)}, bf16[128,2048]{1,0:T(8,128)(2,1)S(1)}, u32[]{:S(2)}, u32[]{:S(2)}) collective-permute-start(bf16[128,2048]{1,0:T(8,128)(2,1)S(1)} %shard_map.273.refs_0_), channel_id=1, source_target_pairs={{0,2},{2,0},{4,6},{6,4},{8,10},{10,8},{12,14},{14,12},{1,3},{3,1},... | collective-permute-start | bytes 1572872 | tf_op jit(solution)/shard_map/ppermute | solution.py:47
  300.4 13.6 %collective-permute-start.49 = (bf16[32,2176]{1,0:T(8,128)(2,1)S(1)}, bf16[32,2176]{1,0:T(8,128)(2,1)S(1)}, u32[]{:S(2)}, u32[]{:S(2)}) collective-permute-start(bf16[32,2176]{1,0:T(8,128)(2,1)S(1)} %get-tuple-element.238.refs_0_.refs_8_), channel_id=1, source_target_pairs={{0,4},{2,6},{4,0},{6,2},{8,12},{10,14},{12,8},{14,10},{1,5},{3,7},... | collective-permute-start | bytes 417800 | tf_op jit(solution)/shard_map/ppermute | solution.py:47
  307.5 12.6 %collective-permute-start.50 = (bf16[32,2176]{1,0:T(8,128)(2,1)S(1)}, bf16[32,2176]{1,0:T(8,128)(2,1)S(1)}, u32[]{:S(2)}, u32[]{:S(2)}) collective-permute-start(bf16[32,2176]{1,0:T(8,128)(2,1)S(1)} %get-tuple-element.238.refs_0_.refs_8_), channel_id=1, source_target_pairs={{0,8},{2,10},{4,12},{6,14},{8,0},{10,2},{12,4},{14,6},{1,9},{3,11}... | collective-permute-start | bytes 417800 | tf_op jit(solution)/shard_map/ppermute | solution.py:47
  321.5 12.7 %collective-permute-start.52 = (bf16[128,2176]{1,0:T(8,128)(2,1)S(1)}, bf16[128,2176]{1,0:T(8,128)(2,1)S(1)}, u32[]{:S(2)}, u32[]{:S(2)}) collective-permute-start(bf16[128,2176]{1,0:T(8,128)(2,1)S(1)} %shard_map.277.refs_0_), channel_id=1, source_target_pairs={{0,2},{2,0},{4,6},{6,4},{8,10},{10,8},{12,14},{14,12},{1,3},{3,1},... | collective-permute-start | bytes 1671176 | tf_op jit(solution)/shard_map/ppermute | solution.py:47
  330.7 16.0 %collective-permute-start.57 = (bf16[64,2176]{1,0:T(8,128)(2,1)S(1)}, bf16[64,2176]{1,0:T(8,128)(2,1)S(1)}, u32[]{:S(2)}, u32[]{:S(2)}) collective-permute-start(bf16[64,2176]{1,0:T(8,128)(2,1)S(1)} %slice.302), channel_id=1, source_target_pairs={{0,2},{2,0},{4,6},{6,4},{8,10},{10,8},{12,14},{14,12},{1,3},{3,1},... | collective-permute-start | bytes 835592 | tf_op jit(solution)/shard_map/ppermute | solution.py:47
  340.9 19.1 %collective-permute-start.59 = (bf16[128,2048]{1,0:T(8,128)(2,1)S(1)}, bf16[128,2048]{1,0:T(8,128)(2,1)S(1)}, u32[]{:S(2)}, u32[]{:S(2)}) collective-permute-start(bf16[128,2048]{1,0:T(8,128)(2,1)S(1)} %shard_map.280.refs_0_), channel_id=1, source_target_pairs={{0,4},{4,8},{8,12},{12,14},{14,10},{10,6},{6,2},{2,0},{1,5},{5,9},... | collective-permute-start | bytes 1572872 | tf_op jit(solution)/shard_map/ppermute | solution.py:225
  344.4 15.5 %collective-permute-start.60 = (bf16[128,2048]{1,0:T(8,128)(2,1)S(1)}, bf16[128,2048]{1,0:T(8,128)(2,1)S(1)}, u32[]{:S(2)}, u32[]{:S(2)}) collective-permute-start(bf16[128,2048]{1,0:T(8,128)(2,1)S(1)} %shard_map.280.refs_0_), channel_id=1, source_target_pairs={{4,0},{8,4},{12,8},{14,12},{10,14},{6,10},{2,6},{0,2},{5,1},{9,5},... | collective-permute-start | bytes 1572872 | tf_op jit(solution)/shard_map/ppermute | solution.py:226
  344.9 15.1 %collective-permute-start.54 = (bf16[64,2048]{1,0:T(8,128)(2,1)S(1)}, bf16[64,2048]{1,0:T(8,128)(2,1)S(1)}, u32[]{:S(2)}, u32[]{:S(2)}) collective-permute-start(bf16[64,2048]{1,0:T(8,128)(2,1)S(1)} %slice.299), channel_id=1, source_target_pairs={{0,2},{2,0},{4,6},{6,4},{8,10},{10,8},{12,14},{14,12},{1,3},{3,1},... | collective-permute-start | bytes 786440 | tf_op jit(solution)/shard_map/ppermute | solution.py:47
  345.4 14.5 %collective-permute-start.55 = (bf16[64,2048]{1,0:T(8,128)(2,1)S(1)}, bf16[64,2048]{1,0:T(8,128)(2,1)S(1)}, u32[]{:S(2)}, u32[]{:S(2)}) collective-permute-start(bf16[64,2048]{1,0:T(8,128)(2,1)S(1)} %slice.301), channel_id=1, source_target_pairs={{0,1},{1,0},{2,3},{3,2},{4,5},{5,4},{6,7},{7,6},{8,9},{9,8},{10,11... | collective-permute-start | bytes 786440 | tf_op jit(solution)/shard_map/ppermute | solution.py:42
  360.2 11.9 %collective-permute-start.62 = (bf16[128,2048]{1,0:T(8,128)(2,1)S(1)}, bf16[128,2048]{1,0:T(8,128)(2,1)}, u32[]{:S(2)}, u32[]{:S(2)}) collective-permute-start(bf16[128,2048]{1,0:T(8,128)(2,1)S(1)} %collective-permute-done.60.refs_2_), channel_id=1, source_target_pairs={{4,0},{8,4},{12,8},{14,12},{10,14},{6,10},{2,6},{0,2},{5,1},{9,5},... | collective-permute-start | bytes 1572872 | tf_op jit(solution)/shard_map/ppermute | solution.py:226
  384.4 12.4 %collective-permute-start.65 = (bf16[128,2176]{1,0:T(8,128)(2,1)S(1)}, bf16[128,2176]{1,0:T(8,128)(2,1)S(1)}, u32[]{:S(2)}, u32[]{:S(2)}) collective-permute-start(bf16[128,2176]{1,0:T(8,128)(2,1)S(1)} %get-tuple-element.263), channel_id=1, source_target_pairs={{0,1},{1,0},{2,3},{3,2},{4,5},{5,4},{6,7},{7,6},{8,9},{9,8},{10,11... | collective-permute-start | bytes 1671176 | tf_op jit(solution)/shard_map/ppermute | solution.py:42
  417.1 15.4 %collective-permute-start.77 = (bf16[512,2048]{1,0:T(8,128)(2,1)}, bf16[512,2048]{1,0:T(8,128)(2,1)S(1)}, u32[]{:S(2)}, u32[]{:S(2)}) collective-permute-start(bf16[512,2048]{1,0:T(8,128)(2,1)} %shard_map.286), channel_id=1, source_target_pairs={{0,16},{16,0},{1,17},{17,1},{2,18},{18,2},{3,19},{19,3},{4,20},{20... | collective-permute-start | bytes 6291464 | tf_op jit(solution)/shard_map/ppermute | solution.py:38
  417.6 14.2 %collective-permute-start.75 = (bf16[128,2048]{1,0:T(8,128)(2,1)}, bf16[128,2048]{1,0:T(8,128)(2,1)S(1)}, u32[]{:S(2)}, u32[]{:S(2)}) collective-permute-start(bf16[128,2048]{1,0:T(8,128)(2,1)} %collective-permute-done.61.refs_3_), channel_id=1, source_target_pairs={{0,4},{4,8},{8,12},{12,14},{14,10},{10,6},{6,2},{2,0},{1,5},{5,9},... | collective-permute-start | bytes 1572872 | tf_op jit(solution)/shard_map/ppermute | solution.py:225
  418.4 14.0 %collective-permute-start.76 = (bf16[128,2048]{1,0:T(8,128)(2,1)}, bf16[128,2048]{1,0:T(8,128)(2,1)S(1)}, u32[]{:S(2)}, u32[]{:S(2)}) collective-permute-start(bf16[128,2048]{1,0:T(8,128)(2,1)} %collective-permute-done.62.refs_4_), channel_id=1, source_target_pairs={{4,0},{8,4},{12,8},{14,12},{10,14},{6,10},{2,6},{0,2},{5,1},{9,5},... | collective-permute-start | bytes 1572872 | tf_op jit(solution)/shard_map/ppermute | solution.py:226
  442.9 15.1 %collective-permute-start.85 = (bf16[128,2048]{1,0:T(8,128)(2,1)S(1)}, bf16[128,2048]{1,0:T(8,128)(2,1)S(1)}, u32[]{:S(2)}, u32[]{:S(2)}) collective-permute-start(bf16[128,2048]{1,0:T(8,128)(2,1)S(1)} %get-tuple-element.297), channel_id=1, source_target_pairs={{0,1},{1,0},{2,3},{3,2},{4,5},{5,4},{6,7},{7,6},{8,9},{9,8},{10,11... | collective-permute-start | bytes 1572872 | tf_op jit(solution)/shard_map/ppermute | solution.py:42
  443.9 14.1 %collective-permute-start.86 = (bf16[128,2048]{1,0:T(8,128)(2,1)S(1)}, bf16[128,2048]{1,0:T(8,128)(2,1)S(1)}, u32[]{:S(2)}, u32[]{:S(2)}) collective-permute-start(bf16[128,2048]{1,0:T(8,128)(2,1)S(1)} %get-tuple-element.299), channel_id=1, source_target_pairs={{0,2},{2,0},{4,6},{6,4},{8,10},{10,8},{12,14},{14,12},{1,3},{3,1},... | collective-permute-start | bytes 1572872 | tf_op jit(solution)/shard_map/ppermute | solution.py:47
  446.2 11.7 %collective-permute-start.83 = (bf16[32,2048]{1,0:T(8,128)(2,1)S(1)}, bf16[32,2048]{1,0:T(8,128)(2,1)S(1)}, u32[]{:S(2)}, u32[]{:S(2)}) collective-permute-start(bf16[32,2048]{1,0:T(8,128)(2,1)S(1)} %shard_map.288.refs_0_.refs_4_), channel_id=1, source_target_pairs={{0,8},{2,10},{4,12},{6,14},{8,0},{10,2},{12,4},{14,6},{1,9},{3,11}... | collective-permute-start | bytes 393224 | tf_op jit(solution)/shard_map/ppermute | solution.py:47
  460.6 12.7 %collective-permute-start.88 = (bf16[128,2048]{1,0:T(8,128)(2,1)S(1)}, bf16[128,2048]{1,0:T(8,128)(2,1)S(1)}, u32[]{:S(2)}, u32[]{:S(2)}) collective-permute-start(bf16[128,2048]{1,0:T(8,128)(2,1)S(1)} %shard_map.289.refs_0_), channel_id=1, source_target_pairs={{0,2},{2,0},{4,6},{6,4},{8,10},{10,8},{12,14},{14,12},{1,3},{3,1},... | collective-permute-start | bytes 1572872 | tf_op jit(solution)/shard_map/ppermute | solution.py:47
  497.3 12.1 %collective-permute-start.93 = (bf16[128,2176]{1,0:T(8,128)(2,1)S(1)}, bf16[128,2176]{1,0:T(8,128)(2,1)S(1)}, u32[]{:S(2)}, u32[]{:S(2)}) collective-permute-start(bf16[128,2176]{1,0:T(8,128)(2,1)S(1)} %get-tuple-element.314), channel_id=1, source_target_pairs={{0,1},{1,0},{2,3},{3,2},{4,5},{5,4},{6,7},{7,6},{8,9},{9,8},{10,11... | collective-permute-start | bytes 1671176 | tf_op jit(solution)/shard_map/ppermute | solution.py:42
  509.6 13.2 %collective-permute-start.98 = (bf16[32,2176]{1,0:T(8,128)(2,1)S(1)}, bf16[32,2176]{1,0:T(8,128)(2,1)S(1)}, u32[]{:S(2)}, u32[]{:S(2)}) collective-permute-start(bf16[32,2176]{1,0:T(8,128)(2,1)S(1)} %get-tuple-element.328), channel_id=1, source_target_pairs={{0,12},{2,14},{4,8},{6,10},{8,4},{10,6},{12,0},{14,2},{1,13},{3,15... | collective-permute-start | bytes 417800 | tf_op jit(solution)/shard_map/ppermute | solution.py:47
  532.1 30.0 %all-to-all-start = ((bf16[8,128,256]{2,1,0:T(8,128)(2,1)}), bf16[8,128,256]{2,1,0:T(8,128)(2,1)}, u32[]{:S(2)}, u32[]{:S(2)}) async-start(bf16[8,128,256]{2,1,0:T(8,128)(2,1)} %copy-done.115), calls=%async_computation | async-start | bytes 1048576 | tf_op jit(solution)/shard_map/all_to_all | solution.py:1215
  536.5 15.0 %collective-permute-start.102 = (bf16[32,2048]{1,0:T(8,128)(2,1)}, bf16[32,2048]{1,0:T(8,128)(2,1)S(1)}, u32[]{:S(2)}, u32[]{:S(2)}) collective-permute-start(bf16[32,2048]{1,0:T(8,128)(2,1)} %copy-done.93), channel_id=1, source_target_pairs={{0,4},{2,6},{4,0},{6,2},{8,12},{10,14},{12,8},{14,10},{1,5},{3,7},... | collective-permute-start | bytes 393224 | tf_op jit(solution)/shard_map/ppermute | solution.py:47
  538.5 22.3 %collective-permute-start.103 = (bf16[32,2048]{1,0:T(8,128)(2,1)}, bf16[32,2048]{1,0:T(8,128)(2,1)S(1)}, u32[]{:S(2)}, u32[]{:S(2)}) collective-permute-start(bf16[32,2048]{1,0:T(8,128)(2,1)} %copy-done.92), channel_id=1, source_target_pairs={{0,8},{2,10},{4,12},{6,14},{8,0},{10,2},{12,4},{14,6},{1,9},{3,11}... | collective-permute-start | bytes 393224 | tf_op jit(solution)/shard_map/ppermute | solution.py:47
  540.9 20.6 %collective-permute-start.104 = (bf16[32,2048]{1,0:T(8,128)(2,1)}, bf16[32,2048]{1,0:T(8,128)(2,1)S(1)}, u32[]{:S(2)}, u32[]{:S(2)}) collective-permute-start(bf16[32,2048]{1,0:T(8,128)(2,1)} %copy-done.91), channel_id=1, source_target_pairs={{0,12},{2,14},{4,8},{6,10},{8,4},{10,6},{12,0},{14,2},{1,13},{3,15... | collective-permute-start | bytes 393224 | tf_op jit(solution)/shard_map/ppermute | solution.py:47
  566.1 18.7 %collective-permute-start.110 = (bf16[144,2560]{1,0:T(8,128)(2,1)S(1)}, bf16[144,2560]{1,0:T(8,128)(2,1)}, u32[]{:S(2)}, u32[]{:S(2)}) collective-permute-start(bf16[144,2560]{1,0:T(8,128)(2,1)S(1)} %shard_map.302.refs_0_), channel_id=1, source_target_pairs={{0,4},{4,8},{8,12},{12,14},{14,10},{10,6},{6,2},{2,0},{1,5},{5,9},... | collective-permute-start | bytes 2211848 | tf_op jit(solution)/shard_map/ppermute | solution.py:225
  567.7 18.4 %collective-permute-start.111 = (bf16[144,2560]{1,0:T(8,128)(2,1)S(1)}, bf16[144,2560]{1,0:T(8,128)(2,1)}, u32[]{:S(2)}, u32[]{:S(2)}) collective-permute-start(bf16[144,2560]{1,0:T(8,128)(2,1)S(1)} %shard_map.302.refs_0_), channel_id=1, source_target_pairs={{4,0},{8,4},{12,8},{14,12},{10,14},{6,10},{2,6},{0,2},{5,1},{9,5},... | collective-permute-start | bytes 2211848 | tf_op jit(solution)/shard_map/ppermute | solution.py:226
  574.4 25.1 %collective-permute-start.114 = (bf16[512,768]{1,0:T(8,128)(2,1)}, bf16[512,768]{1,0:T(8,128)(2,1)}, u32[]{:S(2)}, u32[]{:S(2)}) collective-permute-start(bf16[512,768]{1,0:T(8,128)(2,1)} %shard_map.306), channel_id=1, source_target_pairs={{0,16},{16,0},{1,17},{17,1},{2,18},{18,2},{3,19},{19,3},{4,20},{20... | collective-permute-start | bytes 2359304 | tf_op jit(solution)/shard_map/ppermute | solution.py:38
  575.9 23.6 %collective-permute-start.115 = (bf16[512,2048]{1,0:T(8,128)(2,1)}, bf16[512,2048]{1,0:T(8,128)(2,1)S(1)}, u32[]{:S(2)}, u32[]{:S(2)}) collective-permute-start(bf16[512,2048]{1,0:T(8,128)(2,1)} %shard_map.307), channel_id=1, source_target_pairs={{0,16},{16,0},{1,17},{17,1},{2,18},{18,2},{3,19},{19,3},{4,20},{20... | collective-permute-start | bytes 6291464 | tf_op jit(solution)/shard_map/ppermute | solution.py:38
  586.9 23.2 %collective-permute-start.108 = (bf16[32,2048]{1,0:T(8,128)(2,1)}, bf16[32,2048]{1,0:T(8,128)(2,1)}, u32[]{:S(2)}, u32[]{:S(2)}) collective-permute-start(bf16[32,2048]{1,0:T(8,128)(2,1)} %broadcast_select_fusion.12), channel_id=1, source_target_pairs={{0,16},{16,0},{1,17},{17,1},{2,18},{18,2},{3,19},{19,3},{4,20},{20... | collective-permute-start | bytes 393224 | tf_op jit(solution)/shard_map/ppermute | solution.py:38
  587.4 20.6 %collective-permute-start.112 = (bf16[144,2560]{1,0:T(8,128)(2,1)}, bf16[144,2560]{1,0:T(8,128)(2,1)}, u32[]{:S(2)}, u32[]{:S(2)}) collective-permute-start(bf16[144,2560]{1,0:T(8,128)(2,1)} %collective-permute-done.110.refs_1_), channel_id=1, source_target_pairs={{0,4},{4,8},{8,12},{12,14},{14,10},{10,6},{6,2},{2,0},{1,5},{5,9},... | collective-permute-start | bytes 2211848 | tf_op jit(solution)/shard_map/ppermute | solution.py:225
  588.3 20.1 %collective-permute-start.113 = (bf16[144,2560]{1,0:T(8,128)(2,1)}, bf16[144,2560]{1,0:T(8,128)(2,1)}, u32[]{:S(2)}, u32[]{:S(2)}) collective-permute-start(bf16[144,2560]{1,0:T(8,128)(2,1)} %collective-permute-done.111.refs_2_), channel_id=1, source_target_pairs={{4,0},{8,4},{12,8},{14,12},{10,14},{6,10},{2,6},{0,2},{5,1},{9,5},... | collective-permute-start | bytes 2211848 | tf_op jit(solution)/shard_map/ppermute | solution.py:226
  594.6 41.3 %all-to-all-start.1 = ((bf16[8,160,256]{2,1,0:T(8,128)(2,1)}), bf16[8,160,256]{2,1,0:T(8,128)(2,1)S(1)}, u32[]{:S(2)}, u32[]{:S(2)}) async-start(bf16[8,160,256]{2,1,0:T(8,128)(2,1)} %fusion.4), calls=%async_computation.1 | async-start | bytes 1310720 | tf_op jit(solution)/shard_map/all_to_all | solution.py:1215
  608.0 22.9 %collective-permute-start.116 = (bf16[144,2560]{1,0:T(8,128)(2,1)}, bf16[144,2560]{1,0:T(8,128)(2,1)}, u32[]{:S(2)}, u32[]{:S(2)}) collective-permute-start(bf16[144,2560]{1,0:T(8,128)(2,1)} %collective-permute-done.112.refs_3_), channel_id=1, source_target_pairs={{0,4},{4,8},{8,12},{12,14},{14,10},{10,6},{6,2},{2,0},{1,5},{5,9},... | collective-permute-start | bytes 2211848 | tf_op jit(solution)/shard_map/ppermute | solution.py:225
  608.4 27.4 %collective-permute-start.117 = (bf16[144,2560]{1,0:T(8,128)(2,1)}, bf16[144,2560]{1,0:T(8,128)(2,1)S(1)}, u32[]{:S(2)}, u32[]{:S(2)}) collective-permute-start(bf16[144,2560]{1,0:T(8,128)(2,1)} %collective-permute-done.113.refs_4_), channel_id=1, source_target_pairs={{4,0},{8,4},{12,8},{14,12},{10,14},{6,10},{2,6},{0,2},{5,1},{9,5},... | collective-permute-start | bytes 2211848 | tf_op jit(solution)/shard_map/ppermute | solution.py:226
  611.0 24.9 %collective-permute-start.109 = (bf16[2,32,2048]{2,1,0:T(8,128)(2,1)S(1)}, bf16[2,32,2048]{2,1,0:T(8,128)(2,1)S(1)}, u32[]{:S(2)}, u32[]{:S(2)}) collective-permute-start(bf16[2,32,2048]{2,1,0:T(8,128)(2,1)S(1)} %pad_maximum_fusion.3), channel_id=1, source_target_pairs={{0,1},{1,0},{2,3},{3,2},{4,5},{5,4},{6,7},{7,6},{8,9},{9,8},{10,11... | collective-permute-start | bytes 786440 | tf_op jit(solution)/shard_map/ppermute | solution.py:42
  (206 other events, 3014.5 us)
